TPU v7x, 512 devices: a whole 4x4x16 slice. The times are simulated.
512 devices in a mesh: row: 32 (over z, core), col: 16 (over y, x).
Axes of the slice: x: 4, y: 4, z: 16, core: 2. Of those that a mesh axis runs over, the one named last changes fastest.
Arguments:
- z_slab: float32 [98304, 2048], P('row', 'col'), may hold values from -6 to 6
- v_first: float32 [98304, 256], P('row', 'col'), may hold values from -0.01953125 to 0.01953125
- v_second: float32 [98304, 256], P('row', 'col'), may hold values from -0.01953125 to 0.01953125
- t_first: float32 [256, 256], replicated, may hold values from -2.4 to 2.4, as said below
- t_second: float32 [256, 256], replicated, may hold values from -2.4 to 2.4, as said below
Outputs:
- z_result: float32 [98304, 2048], P('row', 'col')
Inputs may be any that keep to these rules, and one draw needn't show every extreme that they name: `t_first`: upper triangular; diagonal entries lie in 1.5 to 2. `t_second`: upper triangular; diagonal entries lie in 1.5 to 2.
All inputs are finite; a program needn't handle non-finite values.
Results may differ from a plain program's by a relative error of at most 0.00011.
Values sent between devices are 32-bit elements; how exact they have to be, the bound alone decides.
No kernel may reach another device: no remote copies, remote signals or barrier semaphores. Data moves between devices by JAX's collectives and lax.ppermute only.
A program may use at most 64 MiB of HBM per device.

v0:
```python
import jax
import jax.numpy as jnp
from jax import lax
from jax.sharding import PartitionSpec as P


def product(left, right):
    return jnp.dot(left, right, precision=lax.Precision.HIGHEST, preferred_element_type=jnp.float32)


def project(vectors, slab):
    return jnp.einsum(
        "nk,nm->km",
        vectors,
        slab,
        precision=lax.Precision.HIGHEST,
        preferred_element_type=jnp.float32,
    )


def body(z_slab, v_first, v_second, t_first, t_second):
    panel_two = lax.all_gather(v_second, "col", axis=1, tiled=True)
    coeff_two = lax.psum(project(panel_two, z_slab), "row")
    z_mid = z_slab - product(panel_two, product(t_second, coeff_two))
    panel_one = lax.all_gather(v_first, "col", axis=1, tiled=True)
    coeff_one = lax.psum(project(panel_one, z_mid), "row")
    return z_mid - product(panel_one, product(t_first, coeff_one))


def solution(mesh):
    placed = (P("row", "col"), P("row", "col"), P("row", "col"), P(), P())
    return jax.shard_map(
        body, mesh=mesh, in_specs=placed, out_specs=P("row", "col"), check_vma=False
    )
```

profile of v0, /device:TPU:1, one launch (start us, length us, event | category | flops | bytes accessed | tf_op | source)
XLA Modules:
  0.0 556.1 jit_solution(1661297677321923649)
XLA Ops:
  6.5 0.0 copy-start
  6.5 0.0 all-gather.3.cloned.1.call-start
  6.5 0.7 all-gather.3.cloned.1.call-update
  7.3 0.0 copy-start.1
  7.3 0.0 all-reduce.3.cloned.1.call-start
  7.3 71.3 %all-gather.3.cloned.1.call-done = f32[3072,256]{0,1:T(8,128)} async-done(((f32[3072,16]{0,1:T(8,128)}), f32[3072,256]{0,1:T(8,128)}) %all-gather.3.cloned.1.call-update) | async-done | bytes 3145744 | tf_op jit(solution)/shard_map/all_gather | solution.py:22
  78.7 5.6 %fusion.2 = f32[256,128]{1,0:T(8,128)} fusion(f32[3072,256]{0,1:T(8,128)} %all-gather.3.cloned.1.call-done, f32[3072,128]{1,0:T(8,128)} %param.5), kind=kOutput, calls=%fused_computation.5 | convolution fusion | flops 1207959552 | bytes 4849664 | tf_op jit(solution)/shard_map/nk,nm->km/dot_general | solution.py:12
  84.3 0.0 all-reduce.3.cloned.1.call-update
  84.3 0.0 all-gather.5.cloned.1.call-start
  84.4 0.7 all-gather.5.cloned.1.call-update
  85.1 0.0 all-reduce.5.cloned.1.call-start
  85.1 0.0 copy-done.1
  85.1 0.5 copy.6
  85.6 194.0 %all-reduce.3.cloned.1.call-done = f32[256,128]{1,0:T(8,128)} async-done(((f32[256,128]{1,0:T(8,128)}), f32[256,128]{1,0:T(8,128)}) %all-reduce.3.cloned.1.call-update) | async-done | bytes 131088 | tf_op jit(solution)/shard_map/psum | solution.py:23
  279.6 0.0 copy-done
  279.6 1.3 fusion.3
  280.9 3.7 fusion
  284.6 0.0 copy-start.2
  284.6 57.2 %all-gather.5.cloned.1.call-done = f32[3072,256]{0,1:T(8,128)} async-done(((f32[3072,16]{0,1:T(8,128)}), f32[3072,256]{0,1:T(8,128)}) %all-gather.5.cloned.1.call-update) | async-done | bytes 3145744 | tf_op jit(solution)/shard_map/all_gather | solution.py:25
  341.8 5.8 %convolution_bitcast_fusion.2 = f32[256,128]{0,1:T(8,128)} fusion(f32[3072,128]{0,1:T(8,128)S(1)} %fusion, f32[3072,256]{0,1:T(8,128)} %all-gather.5.cloned.1.call-done), kind=kOutput, calls=%fused_computation.4 | convolution fusion | flops 1207959552 | bytes 4849664 | tf_op jit(solution)/shard_map/nk,nm->km/dot_general | solution.py:12
  347.6 0.0 all-reduce.5.cloned.1.call-update
  347.6 195.3 %all-reduce.5.cloned.1.call-done = f32[256,128]{0,1:T(8,128)} async-done(((f32[256,128]{0,1:T(8,128)}), f32[256,128]{0,1:T(8,128)}) %all-reduce.5.cloned.1.call-update) | async-done | bytes 131088 | tf_op jit(solution)/shard_map/psum | solution.py:26
  543.0 0.0 copy-done.2
  543.0 1.3 fusion.4
  544.3 3.6 fusion.1
  547.9 1.6 copy.7
Async XLA Ops:
  6.5 273.1 %copy-start = (f32[256,256]{1,0:T(8,128)S(1)}, f32[256,256]{1,0:T(8,128)}, u32[]{:S(2)}) copy-start(f32[256,256]{1,0:T(8,128)} %param.9) | copy-start | bytes 786436
  6.5 72.1 %all-gather.3.cloned.1.call-start = ((), (), s32[]{:S(2)}) async-start(), calls=%async_computation | async-start | bytes 3342336 | tf_op jit(solution)/shard_map/all_gather | solution.py:22
  7.3 77.9 %copy-start.1 = (f32[3072,128]{1,0:T(8,128)S(1)}, f32[3072,128]{1,0:T(8,128)}, u32[]{:S(2)}) copy-start(f32[3072,128]{1,0:T(8,128)} %param.5) | copy-start | bytes 4718596
  7.3 272.4 %all-reduce.3.cloned.1.call-start = ((), (), s32[]{:S(2)}) async-start(), calls=%async_computation.1 | async-start | bytes 262144 | tf_op jit(solution)/shard_map/psum | solution.py:23
  84.3 257.5 %all-gather.5.cloned.1.call-start = ((), (), s32[]{:S(2)}) async-start(), calls=%async_computation.2 | async-start | bytes 3342336 | tf_op jit(solution)/shard_map/all_gather | solution.py:25
  85.1 457.9 %all-reduce.5.cloned.1.call-start = ((), (), s32[]{:S(2)}) async-start(), calls=%async_computation.3 | async-start | bytes 262144 | tf_op jit(solution)/shard_map/psum | solution.py:26
  284.6 258.4 %copy-start.2 = (f32[256,256]{1,0:T(8,128)S(1)}, f32[256,256]{1,0:T(8,128)}, u32[]{:S(2)}) copy-start(f32[256,256]{1,0:T(8,128)} %param.8) | copy-start | bytes 786436
Sparse Core Ops, SparseCore 0:
  10.4 68.2 all-gather.2
  84.5 195.1 all-reduce.2
  283.1 58.6 all-gather.4
  347.8 195.1 all-reduce.4
where the time goes:
time: 556 us
  waiting for transfers between devices  519 us (93%)
  matrix products  21.3 us (4%)
  between operations  13.2 us (2%)
    psum x1, waiting for transfers between devices, body(): coeff_one = lax.psum(project(panel_one, z_mid), 'row')  195 us
    psum x1, waiting for transfers between devices, body(): coeff_two = lax.psum(project(panel_two, z_slab), 'row')  194 us
    all_gather x1, waiting for transfers between devices, body(): panel_two = lax.all_gather(v_second, 'col', axis=1, tiled=True)  71.3 us
    all_gather x1, waiting for transfers between devices, body(): panel_one = lax.all_gather(v_first, 'col', axis=1, tiled=True)  57.2 us
    dot_general x2, matrix products, project(): jnp.einsum('nk,nm->km', vectors, slab, precision=lax.Precision.HIGHEST, p...  11.4 us
  transfers between devices with their start and end apart: 4, of which 4 were waited for; matrix products, arithmetic and copies ran while one was open for 1% of the time, Pallas kernels for 0%

commit v1 on v0

v1 whole, which is shorter than its diff:
```python
import jax
import jax.numpy as jnp
from jax import lax
from jax.sharding import PartitionSpec as P

NEAR = 8
FAR = 4
HIGHEST = lax.Precision.HIGHEST


def product(left, right):
    return jnp.dot(left, right, precision=HIGHEST, preferred_element_type=jnp.float32)


def sum_over_row(part):
    near = [[NEAR * g + i for i in range(NEAR)] for g in range(FAR)]
    far = [[i + NEAR * g for g in range(FAR)] for i in range(NEAR)]
    r, m = part.shape
    blocks = lax.all_to_all(part.reshape(NEAR, r // NEAR, m), "row", 0, 0, axis_index_groups=near, tiled=True)
    mine = jnp.sum(blocks, 0)
    far_blocks = lax.all_to_all(
        jnp.broadcast_to(mine[None], (FAR,) + mine.shape), "row", 0, 0, axis_index_groups=far, tiled=True
    )
    mine = jnp.sum(far_blocks, 0)
    full = lax.all_to_all(
        jnp.broadcast_to(mine[None], (NEAR,) + mine.shape), "row", 0, 0, axis_index_groups=near, tiled=True
    )
    return full.reshape(r, m)


def body(z_slab, v_first, v_second, t_first, t_second):
    n, w = v_first.shape
    m = z_slab.shape[1]
    k = t_first.shape[0]
    own = jnp.stack([v_first.T, v_second.T])
    panels = lax.all_gather(own, "col", axis=1, tiled=True)
    panel_one, panel_two = panels[0], panels[1]
    coeffs = jnp.einsum("kn,nm->km", panels.reshape(2 * k, n), z_slab, precision=HIGHEST)
    gram = jnp.einsum("kn,jn->kj", panel_one, panel_two, precision=HIGHEST)
    stacked = jnp.concatenate([coeffs, gram[:, :m], gram[:, m:]], 0)
    total = sum_over_row(stacked)
    gram = jnp.concatenate([total[2 * k : 3 * k], total[3 * k :]], 1)
    x_two = product(t_second, total[k : 2 * k])
    x_one = product(t_first, total[:k] - product(gram, x_two))
    x = jnp.concatenate([x_one, x_two], 0)
    return z_slab - jnp.einsum("kn,km->nm", panels.reshape(2 * k, n), x, precision=HIGHEST)


def solution(mesh):
    placed = (P("row", "col"), P("row", "col"), P("row", "col"), P(), P())
    return jax.shard_map(
        body, mesh=mesh, in_specs=placed, out_specs=P("row", "col"), check_vma=False
    )
```

time: 556 us -> 192 us (0.35)
  waiting for transfers between devices: 519 us -> 83.9 us
  blocking collectives: 0 us -> 67.1 us
    psum x2 -> x0, waiting for transfers between devices: 389 us -> none  [the longest x1 195 us: body(): coeff_one = lax.psum(project(panel_one, z_mid), 'row')]
    all_to_all x0 -> x3, blocking collectives: none -> 67.1 us  [the longest x1 25.1 us: sum_over_row(): lax.all_to_all(jnp.broadcast_to(mine[None], (FAR,) + mine.shape), 'row',...]
    all_gather x2 -> x1, waiting for transfers between devices: 129 us -> 83.9 us  [body(): panels = lax.all_gather(own, 'col', axis=1, tiled=True)]
  transfers between devices with their start and end apart: 4 -> 1, of which waited for: 4 -> 1; matrix products, arithmetic and copies ran while one was open for 1% -> 0% of each run, Pallas kernels for 0% -> 0%
where the time goes in v1:
time: 192 us; the launch traced here: 191 us
  waiting for transfers between devices  83.9 us (44%)
  blocking collectives  67.1 us (35%)
  matrix products  24.8 us (13%)
  between operations  13.5 us (7%)
  other arithmetic  2.01 us (1%)
    all_gather x1, waiting for transfers between devices, body(): panels = lax.all_gather(own, 'col', axis=1, tiled=True)  83.9 us
    all_to_all x1, blocking collectives, sum_over_row(): lax.all_to_all(jnp.broadcast_to(mine[None], (FAR,) + mine.shape), 'row',...  25.1 us
    all_to_all x1, blocking collectives, sum_over_row(): lax.all_to_all(jnp.broadcast_to(mine[None], (NEAR,) + mine.shape), 'row',...  22.3 us
    all_to_all x1, blocking collectives, sum_over_row(): lax.all_to_all(part.reshape(NEAR, r // NEAR, m), 'row', 0, 0, axis_index_...  19.7 us
    dot_general x1, matrix products, body(): jnp.einsum('kn,km->nm', panels.reshape(2 * k, n), x, precision=HIGHEST)  12.9 us
    dot_general x1, matrix products, body(): gram = jnp.einsum('kn,jn->kj', panel_one, panel_two, precision=HIGHEST)  5.67 us
    dot_general x1, matrix products, body(): jnp.einsum('kn,nm->km', panels.reshape(2 * k, n), z_slab, precision=HIGHEST)  5.06 us
  transfers between devices with their start and end apart: 1, of which 1 were waited for; matrix products, arithmetic and copies ran while one was open for 0% of the time, Pallas kernels for 0%

profile of v1, /device:TPU:1, one launch (start us, length us, event | category | flops | bytes accessed | tf_op | source)
XLA Modules:
  0.0 191.4 jit_solution(11743680919339025094)
XLA Ops:
  6.5 0.0 copy-start
  6.5 0.0 all-gather.2.cloned.1.call-start
  6.5 0.0 copy-start.2
  6.5 1.9 %pad_maximum_fusion.1 = f32[2,16,3072]{2,1,0:T(8,128)} fusion(f32[1,16,3072]{2,1,0:T(8,128)} %bitcast.37, f32[1,16,3072]{2,1,0:T(8,128)} %bitcast.38), kind=kLoop, calls=%fused_computation.7 | loop fusion | flops 98304 | bytes 786432 | tf_op jit(solution)/shard_map/stack | solution.py:35
  8.5 0.0 all-gather.2.cloned.1.call-update
  8.5 83.9 %all-gather.2.cloned.1.call-done = f32[2,256,3072]{2,1,0:T(8,128)} async-done(((f32[2,16,3072]{2,1,0:T(8,128)}), f32[2,256,3072]{2,1,0:T(8,128)}) %all-gather.2.cloned.1.call-update) | async-done | bytes 6291472 | tf_op jit(solution)/shard_map/all_gather | solution.py:36
  92.4 0.0 copy-start.1
  92.4 5.7 %fusion = f32[256,256]{1,0:T(8,128)S(1)} fusion(f32[2,256,3072]{2,1,0:T(8,128)} %all-gather.2.cloned.1.call-done), kind=kOutput, calls=%fused_computation.2 | convolution fusion | flops 2415919104 | bytes 6553600 | tf_op jit(solution)/shard_map/kn,jn->kj/dot_general | solution.py:39
  98.1 0.0 copy-done.2
  98.1 0.0 copy-done.1
  98.1 5.1 %fusion.11 = f32[512,128]{1,0:T(8,128)S(1)} fusion(f32[512,3072]{1,0:T(8,128)S(1)} %bitcast.30, f32[3072,128]{1,0:T(8,128)S(1)} %copy-done.2), kind=kOutput, calls=%fused_computation.18 | convolution fusion | flops 2415919104 | bytes 8126464 | tf_op jit(solution)/shard_map/kn,nm->km/dot_general | solution.py:38
  103.2 0.0 copy-start.3
  103.2 19.7 %all_to_all.15 = f32[8,128,128]{2,1,0:T(8,128)S(1)} all-to-all(f32[8,128,128]{2,1,0:T(8,128)S(1)} %bitcast.31), channel_id=1, replica_groups={{0,16,32,48,64,80,96,112},{128,144,160,176,192,208,224,240},{256,272,28..., dimensions={0} | all-to-all | bytes 1048576 | tf_op jit(solution)/shard_map/all_to_all | solution.py:19
  123.0 25.1 %all_to_all.16 = f32[4,128,128]{2,1,0:T(8,128)S(1)} all-to-all(f32[4,128,128]{2,1,0:T(8,128)S(1)} %broadcast_in_dim.4), channel_id=1, replica_groups={{0,128,256,384},{16,144,272,400},{32,160,288,416},{48,176,304,432},{64,..., dimensions={0} | all-to-all | bytes 524288 | tf_op jit(solution)/shard_map/all_to_all | solution.py:21
  148.1 22.3 %all_to_all.17 = f32[8,128,128]{2,1,0:T(8,128)S(1)} all-to-all(f32[8,128,128]{2,1,0:T(8,128)S(1)} %broadcast_in_dim.5), channel_id=1, replica_groups={{0,16,32,48,64,80,96,112},{128,144,160,176,192,208,224,240},{256,272,28..., dimensions={0} | all-to-all | bytes 1048576 | tf_op jit(solution)/shard_map/all_to_all | solution.py:25
  170.4 0.0 copy-done
  170.4 0.4 fusion.12
  170.9 0.4 convolution_subtract_fusion.1
  171.2 0.0 copy-done.3
  171.3 0.4 convolution_bitcast_fusion
  171.7 12.9 %convolution_subtract_fusion = f32[3072,128]{1,0:T(8,128)} fusion(f32[3072,128]{1,0:T(8,128)S(1)} %copy-done.2, f32[512,3072]{1,0:T(8,128)} %bitcast.29, f32[256,128]{0,1:T(8,128)S(1)} %bitcast.32, f32[256,128]{0,1:T(8,128)S(1)} %convolution_bitcast_fusion), kind=kOutput, calls=%fused_computation | convolution fusion | flops 2416377856 | bytes 9699328 | tf_op jit(solution)/shard_map/kn,km->nm/dot_general | solution.py:46
  (7 shorter events, 0.2 us)
Async XLA Ops:
  6.5 163.9 %copy-start = (f32[256,256]{1,0:T(8,128)S(1)}, f32[256,256]{1,0:T(8,128)}, u32[]{:S(2)}) copy-start(f32[256,256]{1,0:T(8,128)} %param.9) | copy-start | bytes 786436
  6.5 85.8 %all-gather.2.cloned.1.call-start = ((), (), s32[]{:S(2)}) async-start(), calls=%async_computation.3 | async-start | bytes 6684672 | tf_op jit(solution)/shard_map/all_gather | solution.py:36
  6.5 91.5 %copy-start.2 = (f32[3072,128]{1,0:T(8,128)S(1)}, f32[3072,128]{1,0:T(8,128)}, u32[]{:S(2)}) copy-start(f32[3072,128]{1,0:T(8,128)} %param.5) | copy-start | bytes 4718596
  92.4 5.7 %copy-start.1 = (f32[2,256,3072]{2,1,0:T(8,128)S(1)}, f32[2,256,3072]{2,1,0:T(8,128)}, u32[]{:S(2)}) copy-start(f32[2,256,3072]{2,1,0:T(8,128)} %all-gather.2.cloned.1.call-done) | copy-start | bytes 18874372
  103.2 68.0 %copy-start.3 = (f32[256,256]{1,0:T(8,128)S(1)}, f32[256,256]{1,0:T(8,128)}, u32[]{:S(2)}) copy-start(f32[256,256]{1,0:T(8,128)} %param.8) | copy-start | bytes 786436
Sparse Core Ops, SparseCore 0:
  10.4 81.9 all-gather.1

commit v2 on v1

v2 whole, which is shorter than its diff:
```python
import functools

import jax
import jax.numpy as jnp
from jax import lax
from jax.experimental import pallas as pl
from jax.experimental.pallas import tpu as pltpu
from jax.sharding import PartitionSpec as P

F32 = jnp.float32
BF16 = jnp.bfloat16
LANES = 128
XA, XB, YA, YB = 1, 3, 4, 12
SHARES = (7, 6, 6, 5)
PAIRS = 2
NEAR = 4
FAR = 4


def dot(left, right):
    return jnp.dot(left, right, preferred_element_type=F32)


def dot_t(left, right):
    return lax.dot_general(left, right, (((1,), (1,)), ((), ())), preferred_element_type=F32)


def exact(left, right):
    return jnp.dot(left, right, precision=lax.Precision.HIGHEST, preferred_element_type=F32)


def split(x):
    high = x.astype(BF16)
    return high, (x - high.astype(F32)).astype(BF16)


def swap(x, mask, size):
    return lax.ppermute(x, "col", [(i, i ^ mask) for i in range(size)])


def in_order(refs, masks, which, width):
    place = {}
    for ref, held in zip(refs, masks):
        for i, mask in enumerate(held):
            place[mask] = ref[which, i * width : (i + 1) * width, :]
    return jnp.concatenate([place[mask] for mask in sorted(place)], 0)


def project_kernel(masks, width, base, has_acc, *refs):
    refs = list(refs)
    acc_ref = refs.pop(0) if has_acc else None
    a_ref, b_ref, z_ref, out_ref = refs
    k = width * (len(masks[0]) + len(masks[1]))
    n = a_ref.shape[2]
    one_h, one_l = split(in_order((a_ref, b_ref), masks, 0, width))
    two_h, two_l = split(in_order((a_ref, b_ref), masks, 1, width))
    z_h, z_l = split(z_ref[base : base + n, :])
    z_both = jnp.concatenate([z_h, z_l], 1)
    m = z_h.shape[1]
    for row, high, low in ((0, one_h, one_l), (k, two_h, two_l)):
        wide = dot(high, z_both)
        part = wide[:, :m] + (wide[:, m:] + dot(low, z_h))
        if has_acc:
            part = part + acc_ref[row : row + k, :]
        out_ref[row : row + k, :] = part
    gram = dot_t(one_h, two_h) + (dot_t(one_h, two_l) + dot_t(one_l, two_h))
    for i in range(k // m):
        part = gram[:, i * m : (i + 1) * m]
        row = 2 * k + i * k
        if has_acc:
            part = part + acc_ref[row : row + k, :]
        out_ref[row : row + k, :] = part


def project(acc, piece, masks, z, base, k, width):
    m = z.shape[1]
    rows = 2 * k + k * k // m
    args = ([] if acc is None else [acc]) + list(piece) + [z]
    return pl.pallas_call(
        functools.partial(project_kernel, masks, width, base, acc is not None),
        out_shape=jax.ShapeDtypeStruct((rows, m), F32),
        in_specs=[pl.BlockSpec(memory_space=pltpu.VMEM)] * len(args),
        out_specs=pl.BlockSpec(memory_space=pltpu.VMEM),
        compiler_params=pltpu.CompilerParams(vmem_limit_bytes=32 << 20),
    )(*args)


def apply_kernel(all_masks, width, bases, col_ref, total_ref, t_one_ref, t_two_ref, z_ref, *refs):
    pieces, out_ref, true_ref, slot_ref = refs[:-3], refs[-3], refs[-2], refs[-1]
    k = t_one_ref.shape[0]
    m = z_ref.shape[1]
    blocks = k // width
    col = col_ref[0]

    def place(s):
        return pl.ds(pl.multiple_of(lax.bitwise_xor(col, s) * width, width), width)

    def solve(t_ref, coeff, row):
        for s in range(blocks):
            true_ref[place(s), :] = coeff[s * width : (s + 1) * width, :]
        true_ref[...] = exact(t_ref[...], true_ref[...])
        for s in range(blocks):
            slot_ref[row + s * width : row + (s + 1) * width, :] = true_ref[place(s), :]

    solve(t_two_ref, total_ref[k : 2 * k, :], k)
    coeff = total_ref[:k, :]
    for i in range(k // m):
        row = 2 * k + i * k
        coeff = coeff - exact(total_ref[row : row + k, :], slot_ref[k + i * m : k + (i + 1) * m, :])
    solve(t_one_ref, coeff, 0)
    x_h, x_l = split(slot_ref[...].T)
    x_both = jnp.concatenate([x_h, x_l], 0)
    for p, (base, masks) in enumerate(zip(bases, all_masks)):
        pair = pieces[2 * p : 2 * p + 2]
        n = pair[0].shape[2]
        both = jnp.concatenate([in_order(pair, masks, 0, width), in_order(pair, masks, 1, width)], 0)
        high, low = split(both)
        wide = dot(x_both, high)
        moved = wide[:m, :] + (wide[m:, :] + dot(x_h, low))
        out_ref[base : base + n, :] = z_ref[base : base + n, :] - moved.T


def apply(col, total, t_one, t_two, z, pieces, all_masks, bases, width):
    flat = [half for piece in pieces for half in piece]
    k = t_one.shape[0]
    vmem = pl.BlockSpec(memory_space=pltpu.VMEM)
    return pl.pallas_call(
        functools.partial(apply_kernel, all_masks, width, bases),
        out_shape=jax.ShapeDtypeStruct(z.shape, F32),
        in_specs=[pl.BlockSpec(memory_space=pltpu.SMEM)] + [vmem] * (4 + len(flat)),
        out_specs=vmem,
        scratch_shapes=[pltpu.VMEM((k, z.shape[1]), F32), pltpu.VMEM((2 * k, z.shape[1]), F32)],
        compiler_params=pltpu.CompilerParams(vmem_limit_bytes=40 << 20),
    )(col, total, t_one, t_two, z, *flat)


def gather_pieces(own, size):
    n = own.shape[2]
    unit = n // sum(SHARES)
    cuts = [unit * sum(SHARES[:i]) for i in range(len(SHARES) + 1)]

    def widen(held, mask):
        data, masks = held
        got = swap(data, mask, size)
        return jnp.concatenate([data, got], 1), masks + [m ^ mask for m in masks]

    def part(held, low, high):
        return held[0][:, :, low:high], held[1]

    first = (own[:, :, : cuts[2]], [0])
    second = (own[:, :, cuts[2] :], [0])
    first, second = widen(first, XA), widen(second, YA)
    first, second = widen(first, XB), widen(second, YB)
    parts = [
        (part(first, 0, cuts[1]), YA, YB),
        (part(first, cuts[1], cuts[2]), YB, YA),
        (part(second, 0, cuts[3] - cuts[2]), XA, XB),
        (part(second, cuts[3] - cuts[2], cuts[4] - cuts[2]), XB, XA),
    ]
    parts = [(widen(held, near), last) for held, near, last in parts]
    pieces, masks = [], []
    for (data, held), last in parts:
        pieces.append((data, swap(data, last, size)))
        masks.append((held, [m ^ last for m in held]))
    return pieces, masks, cuts


def sum_over_row(part):
    r, m = part.shape
    group = PAIRS * NEAR
    rows = group * FAR
    pair = [(i, i ^ 1) for i in range(rows)]
    near = [[group * g + PAIRS * i + c for i in range(NEAR)] for g in range(FAR) for c in range(PAIRS)]
    far = [[i + group * g for g in range(FAR)] for i in range(group)]
    core = lax.axis_index("row") % PAIRS
    half = r // PAIRS
    kept = lax.dynamic_slice_in_dim(part, core * half, half, 0)
    given = lax.dynamic_slice_in_dim(part, (1 - core) * half, half, 0)
    mine = kept + lax.ppermute(given, "row", pair)
    blocks = lax.all_to_all(mine.reshape(NEAR, half // NEAR, m), "row", 0, 0, axis_index_groups=near, tiled=True)
    mine = jnp.sum(blocks, 0)
    blocks = lax.all_to_all(
        jnp.broadcast_to(mine[None], (FAR,) + mine.shape), "row", 0, 0, axis_index_groups=far, tiled=True
    )
    mine = jnp.sum(blocks, 0)
    blocks = lax.all_to_all(
        jnp.broadcast_to(mine[None], (NEAR,) + mine.shape), "row", 0, 0, axis_index_groups=near, tiled=True
    )
    mine = blocks.reshape(half, m)
    other = lax.ppermute(mine, "row", pair)
    return jnp.where(core == 0, jnp.concatenate([mine, other], 0), jnp.concatenate([other, mine], 0))


def body(size, z_slab, v_first, v_second, t_first, t_second):
    n, width = v_first.shape
    k = t_first.shape[0]
    own = jnp.stack([v_first.T, v_second.T])
    pieces, masks, cuts = gather_pieces(own, size)
    part = None
    for piece, held, base in zip(pieces, masks, cuts):
        part = project(part, piece, held, z_slab, base, k, width)
    total = sum_over_row(part)
    col = lax.axis_index("col").astype(jnp.int32).reshape(1)
    return apply(col, total, t_first, t_second, z_slab, pieces, masks, cuts[:-1], width)


def solution(mesh):
    placed = (P("row", "col"), P("row", "col"), P("row", "col"), P(), P())
    return jax.shard_map(
        functools.partial(body, mesh.shape["col"]),
        mesh=mesh,
        in_specs=placed,
        out_specs=P("row", "col"),
        check_vma=False,
    )
```

time: 192 us -> 156 us (0.81)
  waiting for transfers between devices: 83.9 us -> 23.6 us
  starting transfers between devices: 0.01 us -> 52.5 us
  matrix products: 24.8 us -> 0 us
  Pallas kernels: 0 us -> 15.5 us
  blocking collectives: 67.1 us -> 52.1 us
  between operations: 13.5 us -> 0.37 us
  other arithmetic: 2.01 us -> 7.76 us
  local copies, waits for them, and re-layouts: 0.13 us -> 3.58 us
    all_gather x1 -> x0, waiting for transfers between devices: 83.9 us -> none  [body(): panels = lax.all_gather(own, 'col', axis=1, tiled=True)]
    ppermute x0 -> x14, starting transfers between devices: none -> 52.5 us  [the longest x12 37.8 us: swap(): return lax.ppermute(x, 'col', [(i, i ^ mask) for i in range(size)])]
    dot_general x6 -> x0, matrix products: 24.8 us -> none  [the longest x1 12.9 us: body(): jnp.einsum('kn,km->nm', panels.reshape(2 * k, n), x, precision=HIGHEST)]
    ppermute x0 -> x14, waiting for transfers between devices: none -> 23.6 us  [the longest x12 20.9 us: swap(): return lax.ppermute(x, 'col', [(i, i ^ mask) for i in range(size)])]
    pallas_call x0 -> x5, Pallas kernels: none -> 15.5 us  [the longest x4 8.63 us: project(): pl.pallas_call(functools.partial(project_kernel, masks, width, base, acc...]
    all_to_all x1, blocking collectives: 22.3 us -> 12.7 us  [sum_over_row(): lax.all_to_all(jnp.broadcast_to(mine[None], (NEAR,) + mine.shape), 'row',...]
    all_to_all x1, blocking collectives: 19.7 us -> 12.5 us  [sum_over_row(): lax.all_to_all(mine.reshape(NEAR, half // NEAR, m), 'row', 0, 0, axis_ind...]
    reduce_sum x1 -> x2, other arithmetic: 0.03 us -> 2.24 us  [sum_over_row(): mine = jnp.sum(blocks, 0)]
  transfers between devices with their start and end apart: 1 -> 14, of which waited for: 1 -> 7; matrix products, arithmetic and copies ran while one was open for 0% -> 1% of each run, Pallas kernels for 0% -> 4%
where the time goes in v2:
time: 156 us; the launch traced here: 155 us
  starting transfers between devices  52.5 us (34%)
  blocking collectives  52.1 us (33%)
  waiting for transfers between devices  23.6 us (15%)
  Pallas kernels  15.5 us (10%)
  other arithmetic  7.76 us (5%)
  local copies, waits for them, and re-layouts  3.58 us (2%)
    ppermute x12, starting transfers between devices, swap(): return lax.ppermute(x, 'col', [(i, i ^ mask) for i in range(size)])  37.8 us
    all_to_all x1, blocking collectives, sum_over_row(): lax.all_to_all(jnp.broadcast_to(mine[None], (FAR,) + mine.shape), 'row',...  27 us
    ppermute x12, waiting for transfers between devices, swap(): return lax.ppermute(x, 'col', [(i, i ^ mask) for i in range(size)])  20.9 us
    all_to_all x1, blocking collectives, sum_over_row(): lax.all_to_all(jnp.broadcast_to(mine[None], (NEAR,) + mine.shape), 'row',...  12.7 us
    all_to_all x1, blocking collectives, sum_over_row(): lax.all_to_all(mine.reshape(NEAR, half // NEAR, m), 'row', 0, 0, axis_ind...  12.5 us
    pallas_call x4, Pallas kernels, project(): pl.pallas_call(functools.partial(project_kernel, masks, width, base, acc...  8.63 us
    ppermute x1, starting transfers between devices, sum_over_row(): mine = kept + lax.ppermute(given, 'row', pair)  7.8 us
    ppermute x1, starting transfers between devices, sum_over_row(): other = lax.ppermute(mine, 'row', pair)  6.94 us
  transfers between devices with their start and end apart: 14, of which 7 were waited for; matrix products, arithmetic and copies ran while one was open for 1% of the time, Pallas kernels for 4%

profile of v2, /device:TPU:1, one launch (start us, length us, event | category | flops | bytes accessed | tf_op | source)
XLA Modules:
  0.0 155.5 jit_solution(10163573068120586166)
XLA Ops:
  0.0 0.0 copy-start.5
  0.0 0.0 copy-start.4
  0.0 1.0 fusion
  1.0 3.9 %collective-permute-start = (f32[2,16,1664]{2,1,0:T(8,128)S(1)}, f32[2,16,1664]{2,1,0:T(8,128)S(1)}, u32[]{:S(2)}, u32[]{:S(2)}) collective-permute-start(f32[2,16,1664]{2,1,0:T(8,128)S(1)} %fusion), channel_id=1, source_target_pairs={{0,1},{1,0},{2,3},{3,2},{4,5},{5,4},{6,7},{7,6},{8,9},{9,8},{10,11... | collective-permute-start | bytes 638984 | tf_op jit(solution)/shard_map/ppermute | solution.py:38
  5.0 3.2 %collective-permute-done = f32[2,16,1664]{2,1,0:T(8,128)S(1)} collective-permute-done((f32[2,16,1664]{2,1,0:T(8,128)S(1)}, f32[2,16,1664]{2,1,0:T(8,128)S(1)}, u32[]{:S(2)}, u32[]{:S(2)}) %collective-permute-start) | collective-permute-done | bytes 213024 | tf_op jit(solution)/shard_map/ppermute | solution.py:38
  8.2 6.1 %collective-permute-start.1 = (f32[2,32,1664]{2,1,0:T(8,128)S(1)}, f32[2,32,1664]{2,1,0:T(8,128)S(1)}, u32[]{:S(2)}, u32[]{:S(2)}) collective-permute-start(f32[2,32,1664]{2,1,0:T(8,128)S(1)} %pad_maximum_fusion.6), channel_id=1, source_target_pairs={{0,3},{1,2},{2,1},{3,0},{4,7},{5,6},{6,5},{7,4},{8,11},{9,10},{10,... | collective-permute-start | bytes 1277960 | tf_op jit(solution)/shard_map/ppermute | solution.py:38
  14.3 0.0 copy-done.5
  14.3 0.0 copy-done.4
  14.3 3.2 %collective-permute-start.6 = (f32[2,16,1408]{2,1,0:T(8,128)S(1)}, f32[2,16,1408]{2,1,0:T(8,128)S(1)}, u32[]{:S(2)}, u32[]{:S(2)}) collective-permute-start(f32[2,16,1408]{2,1,0:T(8,128)S(1)} %pad_maximum_fusion.10), channel_id=1, source_target_pairs={{0,4},{1,5},{2,6},{3,7},{4,0},{5,1},{6,2},{7,3},{8,12},{9,13},{10,... | collective-permute-start | bytes 540680 | tf_op jit(solution)/shard_map/ppermute | solution.py:38
  17.5 3.0 %collective-permute-done.6 = f32[2,16,1408]{2,1,0:T(8,128)S(1)} collective-permute-done((f32[2,16,1408]{2,1,0:T(8,128)S(1)}, f32[2,16,1408]{2,1,0:T(8,128)S(1)}, u32[]{:S(2)}, u32[]{:S(2)}) %collective-permute-start.6) | collective-permute-done | bytes 180256 | tf_op jit(solution)/shard_map/ppermute | solution.py:38
  20.6 4.9 %collective-permute-start.7 = (f32[2,32,1408]{2,1,0:T(8,128)S(1)}, f32[2,32,1408]{2,1,0:T(8,128)S(1)}, u32[]{:S(2)}, u32[]{:S(2)}) collective-permute-start(f32[2,32,1408]{2,1,0:T(8,128)S(1)} %pad_maximum_fusion.8), channel_id=1, source_target_pairs={{0,12},{1,13},{2,14},{3,15},{4,8},{5,9},{6,10},{7,11},{8,4},{9,5},... | collective-permute-start | bytes 1081352 | tf_op jit(solution)/shard_map/ppermute | solution.py:38
  25.5 0.0 collective-permute-done.1
  25.6 1.9 %collective-permute-start.4 = (f32[2,64,768]{2,1,0:T(8,128)S(1)}, f32[2,64,768]{2,1,0:T(8,128)S(1)}, u32[]{:S(2)}, u32[]{:S(2)}) collective-permute-start(f32[2,64,768]{2,1,0:T(8,128)S(1)} %pad_maximum_fusion.7), channel_id=1, source_target_pairs={{0,12},{1,13},{2,14},{3,15},{4,8},{5,9},{6,10},{7,11},{8,4},{9,5},... | collective-permute-start | bytes 1179656 | tf_op jit(solution)/shard_map/ppermute | solution.py:38
  27.5 0.1 pad_maximum_fusion.1
  27.6 1.9 %collective-permute-start.2 = (f32[2,64,896]{2,1,0:T(8,128)S(1)}, f32[2,64,896]{2,1,0:T(8,128)S(1)}, u32[]{:S(2)}, u32[]{:S(2)}) collective-permute-start(f32[2,64,896]{2,1,0:T(8,128)S(1)} %slice.26), channel_id=1, source_target_pairs={{0,4},{1,5},{2,6},{3,7},{4,0},{5,1},{6,2},{7,3},{8,12},{9,13},{10,... | collective-permute-start | bytes 1376264 | tf_op jit(solution)/shard_map/ppermute | solution.py:38
  29.6 1.0 collective-permute-done.7
  30.6 1.9 %collective-permute-start.8 = (f32[2,64,768]{2,1,0:T(8,128)S(1)}, f32[2,64,768]{2,1,0:T(8,128)S(1)}, u32[]{:S(2)}, u32[]{:S(2)}) collective-permute-start(f32[2,64,768]{2,1,0:T(8,128)S(1)} %slice.27), channel_id=1, source_target_pairs={{0,1},{1,0},{2,3},{3,2},{4,5},{5,4},{6,7},{7,6},{8,9},{9,8},{10,11... | collective-permute-start | bytes 1179656 | tf_op jit(solution)/shard_map/ppermute | solution.py:38
  32.6 3.3 %collective-permute-start.10 = (f32[2,64,640]{2,1,0:T(8,128)S(1)}, f32[2,64,640]{2,1,0:T(8,128)S(1)}, u32[]{:S(2)}, u32[]{:S(2)}) collective-permute-start(f32[2,64,640]{2,1,0:T(8,128)S(1)} %pad_maximum_fusion.9), channel_id=1, source_target_pairs={{0,3},{1,2},{2,1},{3,0},{4,7},{5,6},{6,5},{7,4},{8,11},{9,10},{10,... | collective-permute-start | bytes 983048 | tf_op jit(solution)/shard_map/ppermute | solution.py:38
  35.9 3.9 %collective-permute-done.4 = f32[2,64,768]{2,1,0:T(8,128)S(1)} collective-permute-done((f32[2,64,768]{2,1,0:T(8,128)S(1)}, f32[2,64,768]{2,1,0:T(8,128)S(1)}, u32[]{:S(2)}, u32[]{:S(2)}) %collective-permute-start.4) | collective-permute-done | bytes 393248 | tf_op jit(solution)/shard_map/ppermute | solution.py:38
  39.8 0.1 pad_maximum_fusion.2.refs_1_.refs_2_
  39.9 1.9 %collective-permute-start.5 = (f32[2,128,768]{2,1,0:T(8,128)S(1)}, f32[2,128,768]{2,1,0:T(8,128)}, u32[]{:S(2)}, u32[]{:S(2)}) collective-permute-start(f32[2,128,768]{2,1,0:T(8,128)S(1)} %pad_maximum_fusion.2.refs_1_.refs_2_), channel_id=1, source_target_pairs={{0,4},{1,5},{2,6},{3,7},{4,0},{5,1},{6,2},{7,3},{8,12},{9,13},{10,... | collective-permute-start | bytes 2359304 | tf_op jit(solution)/shard_map/ppermute | solution.py:38
  41.8 0.0 collective-permute-done.2
  41.8 0.1 pad_maximum_fusion.refs_0_
  41.9 0.0 copy-start
  41.9 4.6 %collective-permute-start.3 = (f32[2,128,896]{2,1,0:T(8,128)S(1)}, f32[2,128,896]{2,1,0:T(8,128)}, u32[]{:S(2)}, u32[]{:S(2)}) collective-permute-start(f32[2,128,896]{2,1,0:T(8,128)S(1)} %pad_maximum_fusion.refs_0_), channel_id=1, source_target_pairs={{0,12},{1,13},{2,14},{3,15},{4,8},{5,9},{6,10},{7,11},{8,4},{9,5},... | collective-permute-start | bytes 2752520 | tf_op jit(solution)/shard_map/ppermute | solution.py:38
  46.5 0.0 collective-permute-done.8
  46.5 0.9 pad_maximum_fusion.3.refs_1_.refs_4_
  47.5 1.9 %collective-permute-start.9 = (f32[2,128,768]{2,1,0:T(8,128)}, f32[2,128,768]{2,1,0:T(8,128)}, u32[]{:S(2)}, u32[]{:S(2)}) collective-permute-start(f32[2,128,768]{2,1,0:T(8,128)} %pad_maximum_fusion.3.refs_1_.refs_4_), channel_id=1, source_target_pairs={{0,3},{1,2},{2,1},{3,0},{4,7},{5,6},{6,5},{7,4},{8,11},{9,10},{10,... | collective-permute-start | bytes 2359304 | tf_op jit(solution)/shard_map/ppermute | solution.py:38
  49.4 0.0 collective-permute-done.10
  49.4 0.9 pad_maximum_fusion.5.refs_1_.refs_6_
  50.3 2.1 %collective-permute-start.11 = (f32[2,128,640]{2,1,0:T(8,128)}, f32[2,128,640]{2,1,0:T(8,128)}, u32[]{:S(2)}, u32[]{:S(2)}) collective-permute-start(f32[2,128,640]{2,1,0:T(8,128)} %pad_maximum_fusion.5.refs_1_.refs_6_), channel_id=1, source_target_pairs={{0,1},{1,0},{2,3},{3,2},{4,5},{5,4},{6,7},{7,6},{8,9},{9,8},{10,11... | collective-permute-start | bytes 1966088 | tf_op jit(solution)/shard_map/ppermute | solution.py:38
  52.4 9.7 %collective-permute-done.3.refs_1_ = f32[2,128,896]{2,1,0:T(8,128)} collective-permute-done((f32[2,128,896]{2,1,0:T(8,128)S(1)}, f32[2,128,896]{2,1,0:T(8,128)}, u32[]{:S(2)}, u32[]{:S(2)}) %collective-permute-start.3) | collective-permute-done | bytes 917536 | tf_op jit(solution)/shard_map/ppermute | solution.py:38
  62.1 0.0 copy-done
  62.1 2.3 %shard_map.55.refs_0_ = f32[1024,128]{1,0:T(8,128)S(1)} custom-call(f32[2,128,896]{2,1,0:T(8,128)S(1)} %pad_maximum_fusion.refs_0_, f32[2,128,896]{2,1,0:T(8,128)} %collective-permute-done.3.refs_1_, f32[3072,128]{1,0:T(8,128)S(1)} %copy-done), custom_call_target="tpu_custom_call" | custom-call | tf_op jit(solution)/shard_map/pallas_call | solution.py:79
  64.4 0.0 collective-permute-done.5.refs_2_.refs_3_
  64.4 2.0 %shard_map.56.refs_0_ = f32[1024,128]{1,0:T(8,128)S(1)} custom-call(f32[1024,128]{1,0:T(8,128)S(1)} %shard_map.55.refs_0_, f32[2,128,768]{2,1,0:T(8,128)S(1)} %pad_maximum_fusion.2.refs_1_.refs_2_, f32[2,128,768]{2,1,0:T(8,128)} %collective-permute-done.5.refs_2_.refs_3_, f32[3072,128]{1,0:T(8,128)S(1)} %copy-done), custom_call_target="tpu_custom_call" | custom-call | tf_op jit(solution)/shard_map/pallas_call | solution.py:79
  66.4 0.0 collective-permute-done.9.refs_2_.refs_5_
  66.4 2.2 %shard_map.57.refs_0_ = f32[1024,128]{1,0:T(8,128)S(1)} custom-call(f32[1024,128]{1,0:T(8,128)S(1)} %shard_map.56.refs_0_, f32[2,128,768]{2,1,0:T(8,128)} %pad_maximum_fusion.3.refs_1_.refs_4_, f32[2,128,768]{2,1,0:T(8,128)} %collective-permute-done.9.refs_2_.refs_5_, f32[3072,128]{1,0:T(8,128)S(1)} %copy-done), custom_call_target="tpu_custom_call" | custom-call | tf_op jit(solution)/shard_map/pallas_call | solution.py:79
  68.7 0.0 collective-permute-done.11.refs_2_.refs_7_
  68.7 2.1 %shard_map.58 = f32[1024,128]{1,0:T(8,128)S(1)} custom-call(f32[1024,128]{1,0:T(8,128)S(1)} %shard_map.57.refs_0_, f32[2,128,640]{2,1,0:T(8,128)} %pad_maximum_fusion.5.refs_1_.refs_6_, f32[2,128,640]{2,1,0:T(8,128)} %collective-permute-done.11.refs_2_.refs_7_, f32[3072,128]{1,0:T(8,128)S(1)} %copy-done), custom_call_target="tpu_custom_call" | custom-call | tf_op jit(solution)/shard_map/pallas_call | solution.py:79
  70.8 0.0 copy-start.1
  70.8 0.8 copy-done.1
  71.6 7.8 %collective-permute-start.12 = (f32[512,128]{1,0:T(8,128)S(1)}, f32[512,128]{1,0:T(8,128)}, u32[]{:S(2)}, u32[]{:S(2)}) collective-permute-start(f32[512,128]{1,0:T(8,128)S(1)} %constant_dynamic-slice_fusion), channel_id=1, source_target_pairs={{0,16},{16,0},{32,48},{48,32},{64,80},{80,64},{96,112},{112,96},{1... | collective-permute-start | bytes 786440 | tf_op jit(solution)/shard_map/ppermute | solution.py:179
  79.5 1.3 collective-permute-done.12
  80.7 1.1 dynamic-slice_add_fusion
  81.8 12.5 %all_to_all.15 = f32[4,128,128]{2,1,0:T(8,128)S(1)} all-to-all(f32[4,128,128]{2,1,0:T(8,128)S(1)} %bitcast.9), channel_id=1, replica_groups={{0,32,64,96},{16,48,80,112},{128,160,192,224},{144,176,208,240},{256,28..., dimensions={0} | all-to-all | bytes 524288 | tf_op jit(solution)/shard_map/all_to_all | solution.py:180
  94.3 0.6 reduce_sum.18
  94.9 0.0 copy-start.2
  94.9 0.9 broadcast_in_dim.4
  95.8 27.0 %all_to_all.16 = f32[4,128,128]{2,1,0:T(8,128)} all-to-all(f32[4,128,128]{2,1,0:T(8,128)S(1)} %broadcast_in_dim.4), channel_id=1, replica_groups={{0,128,256,384},{16,144,272,400},{32,160,288,416},{48,176,304,432},{64,..., dimensions={0} | all-to-all | bytes 524288 | tf_op jit(solution)/shard_map/all_to_all | solution.py:182
  122.8 1.6 %reduce_sum.19 = f32[128,128]{1,0:T(8,128)} reduce(f32[4,128,128]{2,1,0:T(8,128)} %all_to_all.16, f32[]{:T(128)} %constant.29.clone.1), dimensions={0}, to_apply=%region_1.2 | reduce | flops 49152 | bytes 327684 | tf_op jit(solution)/shard_map/reduce_sum | solution.py:185
  124.4 0.9 broadcast_in_dim.5
  125.3 12.7 %all_to_all.17 = f32[4,128,128]{2,1,0:T(8,128)} all-to-all(f32[4,128,128]{2,1,0:T(8,128)S(1)} %broadcast_in_dim.5), channel_id=1, replica_groups={{0,32,64,96},{16,48,80,112},{128,160,192,224},{144,176,208,240},{256,28..., dimensions={0} | all-to-all | bytes 524288 | tf_op jit(solution)/shard_map/all_to_all | solution.py:186
  137.9 6.9 %collective-permute-start.13 = (f32[512,128]{1,0:T(8,128)}, f32[512,128]{1,0:T(8,128)}, u32[]{:S(2)}, u32[]{:S(2)}) collective-permute-start(f32[512,128]{1,0:T(8,128)} %bitcast.6), channel_id=1, source_target_pairs={{0,16},{16,0},{32,48},{48,32},{64,80},{80,64},{96,112},{112,96},{1... | collective-permute-start | bytes 786440 | tf_op jit(solution)/shard_map/ppermute | solution.py:190
  144.9 1.5 collective-permute-done.13
  146.4 1.3 maximum_select_fusion.total_ref
  147.6 0.0 copy-done.2
  147.6 0.0 copy-start.3
  147.7 0.9 copy-done.3
  148.6 6.9 %shard_map.59 = f32[3072,128]{1,0:T(8,128)} custom-call(s32[1]{0:T(128)} %bitcast.col_ref, f32[1024,128]{1,0:T(8,128)S(1)} %maximum_select_fusion.total_ref, f32[256,256]{1,0:T(8,128)S(1)} %copy-done.2, f32[256,256]{1,0:T(8,128)S(1)} %copy-done.3, f32[3072,128]{1,0:T(8,128)S(1)} %copy-done, f32[2,128,896]{2,1,0:T(8,128)S(1)} %pad_maximum_fusion.refs_0_, ...), custom_call_target="tpu_custom_call" | custom-call | tf_op jit(solution)/shard_map/pallas_call | solution.py:127
  (9 shorter events, 0.2 us)
Async XLA Ops:
  0.0 14.3 %copy-start.5 = (f32[3072,16]{0,1:T(8,128)S(1)}, f32[3072,16]{0,1:T(8,128)}, u32[]{:S(2)}) copy-start(f32[3072,16]{0,1:T(8,128)} %param.7) | copy-start | bytes 589828
  0.0 14.3 %copy-start.4 = (f32[3072,16]{0,1:T(8,128)S(1)}, f32[3072,16]{0,1:T(8,128)}, u32[]{:S(2)}) copy-start(f32[3072,16]{0,1:T(8,128)} %param.6) | copy-start | bytes 589828
  1.0 7.2 %collective-permute-start = (f32[2,16,1664]{2,1,0:T(8,128)S(1)}, f32[2,16,1664]{2,1,0:T(8,128)S(1)}, u32[]{:S(2)}, u32[]{:S(2)}) collective-permute-start(f32[2,16,1664]{2,1,0:T(8,128)S(1)} %fusion), channel_id=1, source_target_pairs={{0,1},{1,0},{2,3},{3,2},{4,5},{5,4},{6,7},{7,6},{8,9},{9,8},{10,11... | collective-permute-start | bytes 638984 | tf_op jit(solution)/shard_map/ppermute | solution.py:38
  8.2 17.3 %collective-permute-start.1 = (f32[2,32,1664]{2,1,0:T(8,128)S(1)}, f32[2,32,1664]{2,1,0:T(8,128)S(1)}, u32[]{:S(2)}, u32[]{:S(2)}) collective-permute-start(f32[2,32,1664]{2,1,0:T(8,128)S(1)} %pad_maximum_fusion.6), channel_id=1, source_target_pairs={{0,3},{1,2},{2,1},{3,0},{4,7},{5,6},{6,5},{7,4},{8,11},{9,10},{10,... | collective-permute-start | bytes 1277960 | tf_op jit(solution)/shard_map/ppermute | solution.py:38
  14.3 6.2 %collective-permute-start.6 = (f32[2,16,1408]{2,1,0:T(8,128)S(1)}, f32[2,16,1408]{2,1,0:T(8,128)S(1)}, u32[]{:S(2)}, u32[]{:S(2)}) collective-permute-start(f32[2,16,1408]{2,1,0:T(8,128)S(1)} %pad_maximum_fusion.10), channel_id=1, source_target_pairs={{0,4},{1,5},{2,6},{3,7},{4,0},{5,1},{6,2},{7,3},{8,12},{9,13},{10,... | collective-permute-start | bytes 540680 | tf_op jit(solution)/shard_map/ppermute | solution.py:38
  20.6 9.9 %collective-permute-start.7 = (f32[2,32,1408]{2,1,0:T(8,128)S(1)}, f32[2,32,1408]{2,1,0:T(8,128)S(1)}, u32[]{:S(2)}, u32[]{:S(2)}) collective-permute-start(f32[2,32,1408]{2,1,0:T(8,128)S(1)} %pad_maximum_fusion.8), channel_id=1, source_target_pairs={{0,12},{1,13},{2,14},{3,15},{4,8},{5,9},{6,10},{7,11},{8,4},{9,5},... | collective-permute-start | bytes 1081352 | tf_op jit(solution)/shard_map/ppermute | solution.py:38
  25.6 14.2 %collective-permute-start.4 = (f32[2,64,768]{2,1,0:T(8,128)S(1)}, f32[2,64,768]{2,1,0:T(8,128)S(1)}, u32[]{:S(2)}, u32[]{:S(2)}) collective-permute-start(f32[2,64,768]{2,1,0:T(8,128)S(1)} %pad_maximum_fusion.7), channel_id=1, source_target_pairs={{0,12},{1,13},{2,14},{3,15},{4,8},{5,9},{6,10},{7,11},{8,4},{9,5},... | collective-permute-start | bytes 1179656 | tf_op jit(solution)/shard_map/ppermute | solution.py:38
  27.6 14.2 %collective-permute-start.2 = (f32[2,64,896]{2,1,0:T(8,128)S(1)}, f32[2,64,896]{2,1,0:T(8,128)S(1)}, u32[]{:S(2)}, u32[]{:S(2)}) collective-permute-start(f32[2,64,896]{2,1,0:T(8,128)S(1)} %slice.26), channel_id=1, source_target_pairs={{0,4},{1,5},{2,6},{3,7},{4,0},{5,1},{6,2},{7,3},{8,12},{9,13},{10,... | collective-permute-start | bytes 1376264 | tf_op jit(solution)/shard_map/ppermute | solution.py:38
  30.6 15.9 %collective-permute-start.8 = (f32[2,64,768]{2,1,0:T(8,128)S(1)}, f32[2,64,768]{2,1,0:T(8,128)S(1)}, u32[]{:S(2)}, u32[]{:S(2)}) collective-permute-start(f32[2,64,768]{2,1,0:T(8,128)S(1)} %slice.27), channel_id=1, source_target_pairs={{0,1},{1,0},{2,3},{3,2},{4,5},{5,4},{6,7},{7,6},{8,9},{9,8},{10,11... | collective-permute-start | bytes 1179656 | tf_op jit(solution)/shard_map/ppermute | solution.py:38
  32.6 16.8 %collective-permute-start.10 = (f32[2,64,640]{2,1,0:T(8,128)S(1)}, f32[2,64,640]{2,1,0:T(8,128)S(1)}, u32[]{:S(2)}, u32[]{:S(2)}) collective-permute-start(f32[2,64,640]{2,1,0:T(8,128)S(1)} %pad_maximum_fusion.9), channel_id=1, source_target_pairs={{0,3},{1,2},{2,1},{3,0},{4,7},{5,6},{6,5},{7,4},{8,11},{9,10},{10,... | collective-permute-start | bytes 983048 | tf_op jit(solution)/shard_map/ppermute | solution.py:38
  39.9 24.5 %collective-permute-start.5 = (f32[2,128,768]{2,1,0:T(8,128)S(1)}, f32[2,128,768]{2,1,0:T(8,128)}, u32[]{:S(2)}, u32[]{:S(2)}) collective-permute-start(f32[2,128,768]{2,1,0:T(8,128)S(1)} %pad_maximum_fusion.2.refs_1_.refs_2_), channel_id=1, source_target_pairs={{0,4},{1,5},{2,6},{3,7},{4,0},{5,1},{6,2},{7,3},{8,12},{9,13},{10,... | collective-permute-start | bytes 2359304 | tf_op jit(solution)/shard_map/ppermute | solution.py:38
  41.9 20.2 %copy-start = (f32[3072,128]{1,0:T(8,128)S(1)}, f32[3072,128]{1,0:T(8,128)}, u32[]{:S(2)}) copy-start(f32[3072,128]{1,0:T(8,128)} %z_ref.1) | copy-start | bytes 4718596
  41.9 20.2 %collective-permute-start.3 = (f32[2,128,896]{2,1,0:T(8,128)S(1)}, f32[2,128,896]{2,1,0:T(8,128)}, u32[]{:S(2)}, u32[]{:S(2)}) collective-permute-start(f32[2,128,896]{2,1,0:T(8,128)S(1)} %pad_maximum_fusion.refs_0_), channel_id=1, source_target_pairs={{0,12},{1,13},{2,14},{3,15},{4,8},{5,9},{6,10},{7,11},{8,4},{9,5},... | collective-permute-start | bytes 2752520 | tf_op jit(solution)/shard_map/ppermute | solution.py:38
  47.5 19.0 %collective-permute-start.9 = (f32[2,128,768]{2,1,0:T(8,128)}, f32[2,128,768]{2,1,0:T(8,128)}, u32[]{:S(2)}, u32[]{:S(2)}) collective-permute-start(f32[2,128,768]{2,1,0:T(8,128)} %pad_maximum_fusion.3.refs_1_.refs_4_), channel_id=1, source_target_pairs={{0,3},{1,2},{2,1},{3,0},{4,7},{5,6},{6,5},{7,4},{8,11},{9,10},{10,... | collective-permute-start | bytes 2359304 | tf_op jit(solution)/shard_map/ppermute | solution.py:38
  50.3 18.4 %collective-permute-start.11 = (f32[2,128,640]{2,1,0:T(8,128)}, f32[2,128,640]{2,1,0:T(8,128)}, u32[]{:S(2)}, u32[]{:S(2)}) collective-permute-start(f32[2,128,640]{2,1,0:T(8,128)} %pad_maximum_fusion.5.refs_1_.refs_6_), channel_id=1, source_target_pairs={{0,1},{1,0},{2,3},{3,2},{4,5},{5,4},{6,7},{7,6},{8,9},{9,8},{10,11... | collective-permute-start | bytes 1966088 | tf_op jit(solution)/shard_map/ppermute | solution.py:38
  70.8 0.8 copy-start.1
  71.6 9.1 %collective-permute-start.12 = (f32[512,128]{1,0:T(8,128)S(1)}, f32[512,128]{1,0:T(8,128)}, u32[]{:S(2)}, u32[]{:S(2)}) collective-permute-start(f32[512,128]{1,0:T(8,128)S(1)} %constant_dynamic-slice_fusion), channel_id=1, source_target_pairs={{0,16},{16,0},{32,48},{48,32},{64,80},{80,64},{96,112},{112,96},{1... | collective-permute-start | bytes 786440 | tf_op jit(solution)/shard_map/ppermute | solution.py:179
  94.9 52.7 %copy-start.2 = (f32[256,256]{1,0:T(8,128)S(1)}, f32[256,256]{1,0:T(8,128)}, u32[]{:S(2)}) copy-start(f32[256,256]{1,0:T(8,128)} %t_one_ref.1) | copy-start | bytes 786436
  137.9 8.4 %collective-permute-start.13 = (f32[512,128]{1,0:T(8,128)}, f32[512,128]{1,0:T(8,128)}, u32[]{:S(2)}, u32[]{:S(2)}) collective-permute-start(f32[512,128]{1,0:T(8,128)} %bitcast.6), channel_id=1, source_target_pairs={{0,16},{16,0},{32,48},{48,32},{64,80},{80,64},{96,112},{112,96},{1... | collective-permute-start | bytes 786440 | tf_op jit(solution)/shard_map/ppermute | solution.py:190
  147.6 1.0 copy-start.3

commit v3 on v2

--- a/solution.py
+++ b/solution.py
@@ -11,10 +11,13 @@
 BF16 = jnp.bfloat16
 LANES = 128
 XA, XB, YA, YB = 1, 3, 4, 12
-SHARES = (7, 6, 6, 5)
+SHARES = (7, 5, 7, 5)
 PAIRS = 2
 NEAR = 4
 FAR = 4
+EARLY_VMEM = 24 << 20
+LATE_VMEM = 16 << 20
+APPLY_VMEM = 24 << 20
 
 
 def dot(left, right):
@@ -38,55 +41,112 @@
     return lax.ppermute(x, "col", [(i, i ^ mask) for i in range(size)])
 
 
-def in_order(refs, masks, which, width):
-    place = {}
-    for ref, held in zip(refs, masks):
+def in_order(pair, masks, row, width):
+    blocks = {}
+    for half, held in zip(pair, masks):
         for i, mask in enumerate(held):
-            place[mask] = ref[which, i * width : (i + 1) * width, :]
-    return jnp.concatenate([place[mask] for mask in sorted(place)], 0)
-
-
-def project_kernel(masks, width, base, has_acc, *refs):
-    refs = list(refs)
-    acc_ref = refs.pop(0) if has_acc else None
-    a_ref, b_ref, z_ref, out_ref = refs
-    k = width * (len(masks[0]) + len(masks[1]))
-    n = a_ref.shape[2]
-    one_h, one_l = split(in_order((a_ref, b_ref), masks, 0, width))
-    two_h, two_l = split(in_order((a_ref, b_ref), masks, 1, width))
-    z_h, z_l = split(z_ref[base : base + n, :])
-    z_both = jnp.concatenate([z_h, z_l], 1)
-    m = z_h.shape[1]
-    for row, high, low in ((0, one_h, one_l), (k, two_h, two_l)):
-        wide = dot(high, z_both)
-        part = wide[:, :m] + (wide[:, m:] + dot(low, z_h))
-        if has_acc:
-            part = part + acc_ref[row : row + k, :]
-        out_ref[row : row + k, :] = part
+            low = row * len(held) * width + i * width
+            blocks[mask] = half[low : low + width, :]
+    return jnp.concatenate([blocks[mask] for mask in sorted(blocks)], 0)
+
+
+def scatter_rows(part, held, k, width):
+    count = len(held)
+    for which in range(2):
+        for i, mask in enumerate(held):
+            low = (which * count + i) * width
+            yield which * k + mask * width, part[low : low + width, :]
+
+
+def split_half(ref, high_ref, low_ref):
+    rows = ref.shape[1]
+    for which in range(2):
+        high, low = split(ref[which])
+        high_ref[which * rows : (which + 1) * rows, :] = high
+        low_ref[which * rows : (which + 1) * rows, :] = low
+
+
+def half_coeffs(high, low, z_both):
+    m = z_both.shape[1] // 2
+    wide = dot(high, z_both)
+    return wide[:, :m] + (wide[:, m:] + dot(low, z_both[:, :m]))
+
+
+def early_kernel(all_masks, width, bases, k, z_ref, *refs):
+    count = len(bases)
+    halves, acc_ref, zb_ref, out = refs[:count], refs[count], refs[count + 1], refs[count + 2 :]
+    m = z_ref.shape[1]
+    acc_ref[...] = jnp.zeros_like(acc_ref)
+    for p, base in enumerate(bases):
+        n = halves[p].shape[2]
+        z_h, z_l = split(z_ref[base : base + n, :])
+        zb_ref[base : base + n, :m] = z_h
+        zb_ref[base : base + n, m:] = z_l
+        split_half(halves[p], out[2 * p], out[2 * p + 1])
+        part = half_coeffs(out[2 * p][...], out[2 * p + 1][...], zb_ref[base : base + n, :])
+        for place, rows in scatter_rows(part, all_masks[p][0], k, width):
+            acc_ref[place : place + width, :] += rows
+
+
+def split_shapes(half):
+    shape = jax.ShapeDtypeStruct((half.shape[0] * half.shape[1], half.shape[2]), BF16)
+    return [shape, shape]
+
+
+def vmem_specs(count):
+    return [pl.BlockSpec(memory_space=pltpu.VMEM)] * count
+
+
+def early(z, halves, all_masks, bases, k, width):
+    n, m = z.shape
+    shapes = [jax.ShapeDtypeStruct((2 * k, m), F32), jax.ShapeDtypeStruct((n, 2 * m), BF16)]
+    for half in halves:
+        shapes += split_shapes(half)
+    out = pl.pallas_call(
+        functools.partial(early_kernel, all_masks, width, bases, k),
+        out_shape=shapes,
+        in_specs=vmem_specs(1 + len(halves)),
+        out_specs=vmem_specs(len(shapes)),
+        compiler_params=pltpu.CompilerParams(vmem_limit_bytes=EARLY_VMEM),
+        cost_estimate=pl.CostEstimate(flops=6 * k * n * m, bytes_accessed=12 << 20, transcendentals=0),
+    )(z, *halves)
+    return out[0], out[1], [(out[2 + 2 * p], out[3 + 2 * p]) for p in range(len(halves))]
+
+
+def late_kernel(masks, width, base, k, first, acc_ref, got_ref, first_h, first_l, zb_ref, out_ref, got_h, got_l):
+    n = got_ref.shape[2]
+    m = zb_ref.shape[1] // 2
+    split_half(got_ref, got_h, got_l)
+    part = half_coeffs(got_h[...], got_l[...], zb_ref[base : base + n, :])
+    added = {place: rows for place, rows in scatter_rows(part, masks[1], k, width)}
+    for place in range(0, 2 * k, width):
+        rows = acc_ref[place : place + width, :]
+        out_ref[place : place + width, :] = rows + added[place] if place in added else rows
+    one_h = in_order((first_h, got_h), masks, 0, width)
+    one_l = in_order((first_l, got_l), masks, 0, width)
+    two_h = in_order((first_h, got_h), masks, 1, width)
+    two_l = in_order((first_l, got_l), masks, 1, width)
     gram = dot_t(one_h, two_h) + (dot_t(one_h, two_l) + dot_t(one_l, two_h))
     for i in range(k // m):
+        row = 2 * k + i * k
         part = gram[:, i * m : (i + 1) * m]
-        row = 2 * k + i * k
-        if has_acc:
-            part = part + acc_ref[row : row + k, :]
-        out_ref[row : row + k, :] = part
-
-
-def project(acc, piece, masks, z, base, k, width):
-    m = z.shape[1]
-    rows = 2 * k + k * k // m
-    args = ([] if acc is None else [acc]) + list(piece) + [z]
+        out_ref[row : row + k, :] = part if first else acc_ref[row : row + k, :] + part
+
+
+def late(acc, got, firsts, zb, masks, base, first, k, width):
+    m = zb.shape[1] // 2
+    shapes = [jax.ShapeDtypeStruct((2 * k + k * k // m, m), F32)] + split_shapes(got)
     return pl.pallas_call(
-        functools.partial(project_kernel, masks, width, base, acc is not None),
-        out_shape=jax.ShapeDtypeStruct((rows, m), F32),
-        in_specs=[pl.BlockSpec(memory_space=pltpu.VMEM)] * len(args),
-        out_specs=pl.BlockSpec(memory_space=pltpu.VMEM),
-        compiler_params=pltpu.CompilerParams(vmem_limit_bytes=32 << 20),
-    )(*args)
+        functools.partial(late_kernel, masks, width, base, k, first),
+        out_shape=shapes,
+        in_specs=vmem_specs(5),
+        out_specs=vmem_specs(3),
+        compiler_params=pltpu.CompilerParams(vmem_limit_bytes=LATE_VMEM),
+    )(acc, got, *firsts, zb)
 
 
 def apply_kernel(all_masks, width, bases, col_ref, total_ref, t_one_ref, t_two_ref, z_ref, *refs):
-    pieces, out_ref, true_ref, slot_ref = refs[:-3], refs[-3], refs[-2], refs[-1]
+    halves, out_ref, true_ref, slot_ref = refs[:-3], refs[-3], refs[-2], refs[-1]
     k = t_one_ref.shape[0]
     m = z_ref.shape[1]
     blocks = k // width
@@ -111,27 +171,25 @@
     x_h, x_l = split(slot_ref[...].T)
     x_both = jnp.concatenate([x_h, x_l], 0)
     for p, (base, masks) in enumerate(zip(bases, all_masks)):
-        pair = pieces[2 * p : 2 * p + 2]
-        n = pair[0].shape[2]
-        both = jnp.concatenate([in_order(pair, masks, 0, width), in_order(pair, masks, 1, width)], 0)
-        high, low = split(both)
+        first_h, first_l, got_h, got_l = halves[4 * p : 4 * p + 4]
+        n = first_h.shape[1]
+        high = jnp.concatenate([in_order((first_h, got_h), masks, w, width) for w in range(2)], 0)
+        low = jnp.concatenate([in_order((first_l, got_l), masks, w, width) for w in range(2)], 0)
         wide = dot(x_both, high)
         moved = wide[:m, :] + (wide[m:, :] + dot(x_h, low))
         out_ref[base : base + n, :] = z_ref[base : base + n, :] - moved.T
 
 
-def apply(col, total, t_one, t_two, z, pieces, all_masks, bases, width):
-    flat = [half for piece in pieces for half in piece]
+def apply(col, total, t_one, t_two, z, halves, all_masks, bases, width):
     k = t_one.shape[0]
-    vmem = pl.BlockSpec(memory_space=pltpu.VMEM)
     return pl.pallas_call(
         functools.partial(apply_kernel, all_masks, width, bases),
         out_shape=jax.ShapeDtypeStruct(z.shape, F32),
-        in_specs=[pl.BlockSpec(memory_space=pltpu.SMEM)] + [vmem] * (4 + len(flat)),
-        out_specs=vmem,
+        in_specs=[pl.BlockSpec(memory_space=pltpu.SMEM)] + vmem_specs(4 + len(halves)),
+        out_specs=pl.BlockSpec(memory_space=pltpu.VMEM),
         scratch_shapes=[pltpu.VMEM((k, z.shape[1]), F32), pltpu.VMEM((2 * k, z.shape[1]), F32)],
-        compiler_params=pltpu.CompilerParams(vmem_limit_bytes=40 << 20),
-    )(col, total, t_one, t_two, z, *flat)
+        compiler_params=pltpu.CompilerParams(vmem_limit_bytes=APPLY_VMEM),
+    )(col, total, t_one, t_two, z, *halves)
 
 
 def gather_pieces(own, size):
@@ -194,14 +252,17 @@
 def body(size, z_slab, v_first, v_second, t_first, t_second):
     n, width = v_first.shape
     k = t_first.shape[0]
-    own = jnp.stack([v_first.T, v_second.T])
+    own = lax.optimization_barrier(jnp.stack([v_first.T, v_second.T]))
     pieces, masks, cuts = gather_pieces(own, size)
-    part = None
-    for piece, held, base in zip(pieces, masks, cuts):
-        part = project(part, piece, held, z_slab, base, k, width)
+    bases = cuts[:-1]
+    part, z_both, firsts = early(z_slab, [piece[0] for piece in pieces], masks, bases, k, width)
+    halves = []
+    for p, base in enumerate(bases):
+        part, *got = late(part, pieces[p][1], firsts[p], z_both, masks[p], base, p == 0, k, width)
+        halves += [*firsts[p], *got]
     total = sum_over_row(part)
     col = lax.axis_index("col").astype(jnp.int32).reshape(1)
-    return apply(col, total, t_first, t_second, z_slab, pieces, masks, cuts[:-1], width)
+    return apply(col, total, t_first, t_second, z_slab, halves, masks, bases, width)
 
 
 def solution(mesh):

time: 156 us -> 159 us (1.019)
  local copies, waits for them, and re-layouts: 3.58 us -> 16.9 us
  waiting for transfers between devices: 23.6 us -> 11.9 us
  starting transfers between devices: 52.5 us -> 55.9 us
  other arithmetic: 7.76 us -> 5.53 us
    unnamed x12 -> x70, local copies, waits for them, and re-layouts: 1.75 us -> 16.8 us
    ppermute x12, waiting for transfers between devices: 20.9 us -> 9.26 us  [swap(): return lax.ppermute(x, 'col', [(i, i ^ mask) for i in range(size)])]
    ppermute x12, starting transfers between devices: 37.8 us -> 43.2 us  [swap(): return lax.ppermute(x, 'col', [(i, i ^ mask) for i in range(size)])]
    pallas_call x1, Pallas kernels: 6.9 us -> 4.72 us  [apply(): pl.pallas_call(functools.partial(apply_kernel, all_masks, width, bases),...]
    ppermute x1, starting transfers between devices: 7.8 us -> 5.79 us  [sum_over_row(): mine = kept + lax.ppermute(given, 'row', pair)]
    pallas_call x4 -> x5, Pallas kernels: 8.63 us -> 10.6 us  [the longest x4 8.13 us: late(): pl.pallas_call(functools.partial(late_kernel, masks, width, base, k, firs...]
  transfers between devices with their start and end apart: 14 -> 14, of which waited for: 7 -> 5; matrix products, arithmetic and copies ran while one was open for 1% -> 1% of each run, Pallas kernels for 4% -> 5%
where the time goes in v3:
time: 159 us; the launch traced here: 158 us
  starting transfers between devices  55.9 us (35%)
  blocking collectives  51.5 us (32%)
  local copies, waits for them, and re-layouts  16.9 us (11%)
  Pallas kernels  15.3 us (10%)
  waiting for transfers between devices  11.9 us (7%)
  other arithmetic  5.53 us (3%)
    ppermute x12, starting transfers between devices, swap(): return lax.ppermute(x, 'col', [(i, i ^ mask) for i in range(size)])  43.2 us
    all_to_all x1, blocking collectives, sum_over_row(): lax.all_to_all(jnp.broadcast_to(mine[None], (FAR,) + mine.shape), 'row',...  27.1 us
    unnamed x70, local copies, waits for them, and re-layouts  16.8 us
    all_to_all x1, blocking collectives, sum_over_row(): lax.all_to_all(jnp.broadcast_to(mine[None], (NEAR,) + mine.shape), 'row',...  12.7 us
    all_to_all x1, blocking collectives, sum_over_row(): lax.all_to_all(mine.reshape(NEAR, half // NEAR, m), 'row', 0, 0, axis_ind...  11.8 us
    ppermute x12, waiting for transfers between devices, swap(): return lax.ppermute(x, 'col', [(i, i ^ mask) for i in range(size)])  9.26 us
    pallas_call x4, Pallas kernels, late(): pl.pallas_call(functools.partial(late_kernel, masks, width, base, k, firs...  8.13 us
    ppermute x1, starting transfers between devices, sum_over_row(): other = lax.ppermute(mine, 'row', pair)  6.94 us
  transfers between devices with their start and end apart: 14, of which 5 were waited for; matrix products, arithmetic and copies ran while one was open for 1% of the time, Pallas kernels for 5%

profile of v3, /device:TPU:1, one launch (start us, length us, event | category | flops | bytes accessed | tf_op | source)
XLA Modules:
  0.0 157.7 jit_solution(9849816923276130210)
XLA Ops:
  0.0 1.0 pad_maximum_fusion.6
  1.1 3.9 %collective-permute-start = (f32[2,16,1536]{2,1,0:T(8,128)S(1)}, f32[2,16,1536]{2,1,0:T(8,128)S(1)}, u32[]{:S(2)}, u32[]{:S(2)}) collective-permute-start(f32[2,16,1536]{2,1,0:T(8,128)S(1)} %get-tuple-element.50), channel_id=1, source_target_pairs={{0,1},{1,0},{2,3},{3,2},{4,5},{5,4},{6,7},{7,6},{8,9},{9,8},{10,11... | collective-permute-start | bytes 589832 | tf_op jit(solution)/shard_map/ppermute | solution.py:41
  5.0 3.2 %collective-permute-start.4 = (f32[2,16,1536]{2,1,0:T(8,128)S(1)}, f32[2,16,1536]{2,1,0:T(8,128)S(1)}, u32[]{:S(2)}, u32[]{:S(2)}) collective-permute-start(f32[2,16,1536]{2,1,0:T(8,128)S(1)} %get-tuple-element.49), channel_id=1, source_target_pairs={{0,4},{1,5},{2,6},{3,7},{4,0},{5,1},{6,2},{7,3},{8,12},{9,13},{10,... | collective-permute-start | bytes 589832 | tf_op jit(solution)/shard_map/ppermute | solution.py:41
  8.3 0.0 collective-permute-done
  8.3 5.7 %collective-permute-start.1 = (f32[2,32,1536]{2,1,0:T(8,128)S(1)}, f32[2,32,1536]{2,1,0:T(8,128)S(1)}, u32[]{:S(2)}, u32[]{:S(2)}) collective-permute-start(f32[2,32,1536]{2,1,0:T(8,128)S(1)} %pad_maximum_fusion.7), channel_id=1, source_target_pairs={{0,3},{1,2},{2,1},{3,0},{4,7},{5,6},{6,5},{7,4},{8,11},{9,10},{10,... | collective-permute-start | bytes 1179656 | tf_op jit(solution)/shard_map/ppermute | solution.py:41
  14.0 0.0 collective-permute-done.4
  14.1 4.6 %collective-permute-start.5 = (f32[2,32,1536]{2,1,0:T(8,128)S(1)}, f32[2,32,1536]{2,1,0:T(8,128)S(1)}, u32[]{:S(2)}, u32[]{:S(2)}) collective-permute-start(f32[2,32,1536]{2,1,0:T(8,128)S(1)} %pad_maximum_fusion.8), channel_id=1, source_target_pairs={{0,12},{1,13},{2,14},{3,15},{4,8},{5,9},{6,10},{7,11},{8,4},{9,5},... | collective-permute-start | bytes 1179656 | tf_op jit(solution)/shard_map/ppermute | solution.py:41
  18.7 0.5 collective-permute-done.1
  19.2 0.1 pad_maximum_fusion.2
  19.3 4.9 %collective-permute-start.2 = (f32[2,64,896]{2,1,0:T(8,128)S(1)}, f32[2,64,896]{2,1,0:T(8,128)S(1)}, u32[]{:S(2)}, u32[]{:S(2)}) collective-permute-start(f32[2,64,896]{2,1,0:T(8,128)S(1)} %slice.25), channel_id=1, source_target_pairs={{0,4},{1,5},{2,6},{3,7},{4,0},{5,1},{6,2},{7,3},{8,12},{9,13},{10,... | collective-permute-start | bytes 1376264 | tf_op jit(solution)/shard_map/ppermute | solution.py:41
  24.2 1.1 collective-permute-done.5
  25.3 0.1 pad_maximum_fusion.3
  25.4 1.9 %collective-permute-start.6 = (f32[2,64,896]{2,1,0:T(8,128)S(1)}, f32[2,64,896]{2,1,0:T(8,128)S(1)}, u32[]{:S(2)}, u32[]{:S(2)}) collective-permute-start(f32[2,64,896]{2,1,0:T(8,128)S(1)} %slice.27), channel_id=1, source_target_pairs={{0,1},{1,0},{2,3},{3,2},{4,5},{5,4},{6,7},{7,6},{8,9},{9,8},{10,11... | collective-permute-start | bytes 1376264 | tf_op jit(solution)/shard_map/ppermute | solution.py:41
  27.3 5.3 %collective-permute-start.3 = (f32[2,64,640]{2,1,0:T(8,128)S(1)}, f32[2,64,640]{2,1,0:T(8,128)S(1)}, u32[]{:S(2)}, u32[]{:S(2)}) collective-permute-start(f32[2,64,640]{2,1,0:T(8,128)S(1)} %pad_maximum_fusion.10), channel_id=1, source_target_pairs={{0,12},{1,13},{2,14},{3,15},{4,8},{5,9},{6,10},{7,11},{8,4},{9,5},... | collective-permute-start | bytes 983048 | tf_op jit(solution)/shard_map/ppermute | solution.py:41
  32.7 3.0 %collective-permute-start.7 = (f32[2,64,640]{2,1,0:T(8,128)S(1)}, f32[2,64,640]{2,1,0:T(8,128)S(1)}, u32[]{:S(2)}, u32[]{:S(2)}) collective-permute-start(f32[2,64,640]{2,1,0:T(8,128)S(1)} %pad_maximum_fusion.9), channel_id=1, source_target_pairs={{0,3},{1,2},{2,1},{3,0},{4,7},{5,6},{6,5},{7,4},{8,11},{9,10},{10,... | collective-permute-start | bytes 983048 | tf_op jit(solution)/shard_map/ppermute | solution.py:41
  35.7 0.0 collective-permute-done.2
  35.7 0.1 pad_maximum_fusion.refs_0_
  35.7 2.4 %collective-permute-start.8 = (f32[2,128,896]{2,1,0:T(8,128)S(1)}, f32[2,128,896]{2,1,0:T(8,128)}, u32[]{:S(2)}, u32[]{:S(2)}) collective-permute-start(f32[2,128,896]{2,1,0:T(8,128)S(1)} %pad_maximum_fusion.refs_0_), channel_id=1, source_target_pairs={{0,12},{1,13},{2,14},{3,15},{4,8},{5,9},{6,10},{7,11},{8,4},{9,5},... | collective-permute-start | bytes 2752520 | tf_op jit(solution)/shard_map/ppermute | solution.py:41
  38.2 0.0 collective-permute-done.6
  38.2 0.1 pad_maximum_fusion.1.refs_2_
  38.3 0.0 copy-start
  38.3 4.4 %collective-permute-start.10 = (f32[2,128,896]{2,1,0:T(8,128)S(1)}, f32[2,128,896]{2,1,0:T(8,128)}, u32[]{:S(2)}, u32[]{:S(2)}) collective-permute-start(f32[2,128,896]{2,1,0:T(8,128)S(1)} %pad_maximum_fusion.1.refs_2_), channel_id=1, source_target_pairs={{0,3},{1,2},{2,1},{3,0},{4,7},{5,6},{6,5},{7,4},{8,11},{9,10},{10,... | collective-permute-start | bytes 2752520 | tf_op jit(solution)/shard_map/ppermute | solution.py:41
  42.7 0.9 pad_maximum_fusion.4.refs_1_
  43.5 1.9 %collective-permute-start.9 = (f32[2,128,640]{2,1,0:T(8,128)}, f32[2,128,640]{2,1,0:T(8,128)}, u32[]{:S(2)}, u32[]{:S(2)}) collective-permute-start(f32[2,128,640]{2,1,0:T(8,128)} %pad_maximum_fusion.4.refs_1_), channel_id=1, source_target_pairs={{0,4},{1,5},{2,6},{3,7},{4,0},{5,1},{6,2},{7,3},{8,12},{9,13},{10,... | collective-permute-start | bytes 1966088 | tf_op jit(solution)/shard_map/ppermute | solution.py:41
  45.5 0.0 collective-permute-done.7
  45.5 0.9 pad_maximum_fusion.5.refs_3_
  46.4 1.9 %collective-permute-start.11 = (f32[2,128,640]{2,1,0:T(8,128)}, f32[2,128,640]{2,1,0:T(8,128)}, u32[]{:S(2)}, u32[]{:S(2)}) collective-permute-start(f32[2,128,640]{2,1,0:T(8,128)} %pad_maximum_fusion.5.refs_3_), channel_id=1, source_target_pairs={{0,1},{1,0},{2,3},{3,2},{4,5},{5,4},{6,7},{7,6},{8,9},{9,8},{10,11... | collective-permute-start | bytes 1966088 | tf_op jit(solution)/shard_map/ppermute | solution.py:41
  48.3 2.5 %shard_map.55 = (f32[512,128]{1,0:T(8,128)S(1)}, bf16[3072,256]{1,0:T(8,128)(2,1)S(1)}, bf16[256,896]{1,0:T(8,128)(2,1)S(1)}, bf16[256,896]{1,0:T(8,128)(2,1)S(1...) custom-call(f32[3072,128]{1,0:T(8,128)S(1)} %copy-done, ...), custom_call_target="tpu_custom_call" | custom-call | flops 603979776 | bytes 12582912 | tf_op jit(solution)/shard_map/pallas_call | solution.py:105
  50.9 7.7 %collective-permute-done.8.got_ref = f32[2,128,896]{2,1,0:T(8,128)} collective-permute-done((f32[2,128,896]{2,1,0:T(8,128)S(1)}, f32[2,128,896]{2,1,0:T(8,128)}, u32[]{:S(2)}, u32[]{:S(2)}) %collective-permute-start.8) | collective-permute-done | bytes 917536 | tf_op jit(solution)/shard_map/ppermute | solution.py:41
  58.5 2.0 %shard_map.56 = (f32[1024,128]{1,0:T(8,128)S(1)}, bf16[256,896]{1,0:T(8,128)(2,1)S(1)}, bf16[256,896]{1,0:T(8,128)(2,1)S(1)}) custom-call(f32[512,128]{1,0:T(8,128)S(1)} %get-tuple-element.27.acc_ref, f32[2,128,896]{2,1,0:T(8,128)} %collective-permute-done.8.got_ref, bf16[256,896]{1,0:T(8,128)(2,1)S(1)} %get-tuple-element.28.first_h.refs_0_, ...), custom_call_target="tpu_custom_call" | custom-call | tf_op jit(solution)/shard_map/pallas_call | solution.py:139
  60.6 0.8 copy-done.17
  61.3 0.0 collective-permute-done.9.got_ref
  61.3 1.9 %shard_map.57 = (f32[1024,128]{1,0:T(8,128)S(1)}, bf16[256,640]{1,0:T(8,128)(2,1)S(1)}, bf16[256,640]{1,0:T(8,128)(2,1)S(1)}) custom-call(f32[1024,128]{1,0:T(8,128)S(1)} %get-tuple-element.31.acc_ref, f32[2,128,640]{2,1,0:T(8,128)} %collective-permute-done.9.got_ref, bf16[256,640]{1,0:T(8,128)(2,1)S(1)} %get-tuple-element.32.first_h.refs_4_, ...), custom_call_target="tpu_custom_call" | custom-call | tf_op jit(solution)/shard_map/pallas_call | solution.py:139
  63.3 0.7 copy-done.25
  64.0 2.2 %shard_map.58 = (f32[1024,128]{1,0:T(8,128)S(1)}, bf16[256,896]{1,0:T(8,128)(2,1)S(1)}, bf16[256,896]{1,0:T(8,128)(2,1)S(1)}) custom-call(f32[1024,128]{1,0:T(8,128)S(1)} %get-tuple-element.34.acc_ref, f32[2,128,896]{2,1,0:T(8,128)} %collective-permute-done.10.got_ref, bf16[256,896]{1,0:T(8,128)(2,1)S(1)} %get-tuple-element.35.first_h.refs_8_, ...), custom_call_target="tpu_custom_call" | custom-call | tf_op jit(solution)/shard_map/pallas_call | solution.py:139
  66.2 0.0 copy-start.21
  66.2 0.0 collective-permute-done.11.got_ref
  66.2 2.0 %shard_map.59 = (f32[1024,128]{1,0:T(8,128)S(1)}, bf16[256,640]{1,0:T(8,128)(2,1)S(1)}, bf16[256,640]{1,0:T(8,128)(2,1)S(1)}) custom-call(f32[1024,128]{1,0:T(8,128)S(1)} %get-tuple-element.37.acc_ref, f32[2,128,640]{2,1,0:T(8,128)} %collective-permute-done.11.got_ref, bf16[256,640]{1,0:T(8,128)(2,1)S(1)} %get-tuple-element.38.first_h.refs_12_, ...), custom_call_target="tpu_custom_call" | custom-call | tf_op jit(solution)/shard_map/pallas_call | solution.py:139
  68.3 0.7 copy-done.29
  69.0 0.7 copy-done.31
  69.8 5.8 %collective-permute-start.12 = (f32[512,128]{1,0:T(8,128)S(1)}, f32[512,128]{1,0:T(8,128)S(1)}, u32[]{:S(2)}, u32[]{:S(2)}) collective-permute-start(f32[512,128]{1,0:T(8,128)S(1)} %constant_dynamic-slice_fusion), channel_id=1, source_target_pairs={{0,16},{16,0},{32,48},{48,32},{64,80},{80,64},{96,112},{112,96},{1... | collective-permute-start | bytes 786440 | tf_op jit(solution)/shard_map/ppermute | solution.py:237
  75.6 1.1 collective-permute-done.12
  76.8 11.8 %all_to_all.15 = f32[4,128,128]{2,1,0:T(8,128)S(1)} all-to-all(f32[4,128,128]{2,1,0:T(8,128)S(1)} %bitcast.9), channel_id=1, replica_groups={{0,32,64,96},{16,48,80,112},{128,160,192,224},{144,176,208,240},{256,28..., dimensions={0} | all-to-all | bytes 524288 | tf_op jit(solution)/shard_map/all_to_all | solution.py:238
  88.6 27.1 %all_to_all.16 = f32[4,128,128]{2,1,0:T(8,128)} all-to-all(f32[4,128,128]{2,1,0:T(8,128)S(1)} %broadcast_in_dim.4), channel_id=1, replica_groups={{0,128,256,384},{16,144,272,400},{32,160,288,416},{48,176,304,432},{64,..., dimensions={0} | all-to-all | bytes 524288 | tf_op jit(solution)/shard_map/all_to_all | solution.py:240
  115.7 1.0 reduce_sum.19
  116.7 12.7 %all_to_all.17 = f32[4,128,128]{2,1,0:T(8,128)} all-to-all(f32[4,128,128]{2,1,0:T(8,128)S(1)} %broadcast_in_dim.5), channel_id=1, replica_groups={{0,32,64,96},{16,48,80,112},{128,160,192,224},{144,176,208,240},{256,28..., dimensions={0} | all-to-all | bytes 524288 | tf_op jit(solution)/shard_map/all_to_all | solution.py:244
  129.4 6.9 %collective-permute-start.13 = (f32[512,128]{1,0:T(8,128)}, f32[512,128]{1,0:T(8,128)}, u32[]{:S(2)}, u32[]{:S(2)}) collective-permute-start(f32[512,128]{1,0:T(8,128)} %bitcast.6), channel_id=1, source_target_pairs={{0,16},{16,0},{32,48},{48,32},{64,80},{80,64},{96,112},{112,96},{1... | collective-permute-start | bytes 786440 | tf_op jit(solution)/shard_map/ppermute | solution.py:248
  136.3 1.5 collective-permute-done.13
  137.8 1.4 maximum_select_fusion.total_ref
  139.2 1.0 copy-done.10
  140.2 1.0 copy-done.12
  141.2 1.0 copy-done.14
  142.1 1.0 copy-done.16
  143.1 1.0 copy-done.18
  144.1 1.0 copy-done.20
  145.2 1.0 copy-done.22
  146.2 1.0 copy-done.24
  147.2 1.0 copy-done.26
  148.2 1.0 copy-done.28
  149.1 1.0 copy-done.30
  150.1 1.0 copy-done.32
  151.1 0.9 copy-done.33
  152.0 0.9 copy-done.34
  153.0 4.7 %shard_map.60 = f32[3072,128]{1,0:T(8,128)} custom-call(s32[1]{0:T(128)} %bitcast.col_ref, f32[1024,128]{1,0:T(8,128)S(1)} %maximum_select_fusion.total_ref, f32[256,256]{1,0:T(8,128)S(1)} %copy-done.33, f32[256,256]{1,0:T(8,128)S(1)} %copy-done.34, f32[3072,128]{1,0:T(8,128)S(1)} %copy-done, bf16[256,896]{1,0:T(8,128)(2,1)S(1)} %copy-done.2, ...), custom_call_target="tpu_custom_call" | custom-call | tf_op jit(solution)/shard_map/pallas_call | solution.py:185
  (64 shorter events, 0.4 us)
Async XLA Ops:
  1.1 7.2 %collective-permute-start = (f32[2,16,1536]{2,1,0:T(8,128)S(1)}, f32[2,16,1536]{2,1,0:T(8,128)S(1)}, u32[]{:S(2)}, u32[]{:S(2)}) collective-permute-start(f32[2,16,1536]{2,1,0:T(8,128)S(1)} %get-tuple-element.50), channel_id=1, source_target_pairs={{0,1},{1,0},{2,3},{3,2},{4,5},{5,4},{6,7},{7,6},{8,9},{9,8},{10,11... | collective-permute-start | bytes 589832 | tf_op jit(solution)/shard_map/ppermute | solution.py:41
  5.0 9.0 %collective-permute-start.4 = (f32[2,16,1536]{2,1,0:T(8,128)S(1)}, f32[2,16,1536]{2,1,0:T(8,128)S(1)}, u32[]{:S(2)}, u32[]{:S(2)}) collective-permute-start(f32[2,16,1536]{2,1,0:T(8,128)S(1)} %get-tuple-element.49), channel_id=1, source_target_pairs={{0,4},{1,5},{2,6},{3,7},{4,0},{5,1},{6,2},{7,3},{8,12},{9,13},{10,... | collective-permute-start | bytes 589832 | tf_op jit(solution)/shard_map/ppermute | solution.py:41
  8.3 10.9 %collective-permute-start.1 = (f32[2,32,1536]{2,1,0:T(8,128)S(1)}, f32[2,32,1536]{2,1,0:T(8,128)S(1)}, u32[]{:S(2)}, u32[]{:S(2)}) collective-permute-start(f32[2,32,1536]{2,1,0:T(8,128)S(1)} %pad_maximum_fusion.7), channel_id=1, source_target_pairs={{0,3},{1,2},{2,1},{3,0},{4,7},{5,6},{6,5},{7,4},{8,11},{9,10},{10,... | collective-permute-start | bytes 1179656 | tf_op jit(solution)/shard_map/ppermute | solution.py:41
  14.1 11.2 %collective-permute-start.5 = (f32[2,32,1536]{2,1,0:T(8,128)S(1)}, f32[2,32,1536]{2,1,0:T(8,128)S(1)}, u32[]{:S(2)}, u32[]{:S(2)}) collective-permute-start(f32[2,32,1536]{2,1,0:T(8,128)S(1)} %pad_maximum_fusion.8), channel_id=1, source_target_pairs={{0,12},{1,13},{2,14},{3,15},{4,8},{5,9},{6,10},{7,11},{8,4},{9,5},... | collective-permute-start | bytes 1179656 | tf_op jit(solution)/shard_map/ppermute | solution.py:41
  19.3 16.4 %collective-permute-start.2 = (f32[2,64,896]{2,1,0:T(8,128)S(1)}, f32[2,64,896]{2,1,0:T(8,128)S(1)}, u32[]{:S(2)}, u32[]{:S(2)}) collective-permute-start(f32[2,64,896]{2,1,0:T(8,128)S(1)} %slice.25), channel_id=1, source_target_pairs={{0,4},{1,5},{2,6},{3,7},{4,0},{5,1},{6,2},{7,3},{8,12},{9,13},{10,... | collective-permute-start | bytes 1376264 | tf_op jit(solution)/shard_map/ppermute | solution.py:41
  25.4 12.8 %collective-permute-start.6 = (f32[2,64,896]{2,1,0:T(8,128)S(1)}, f32[2,64,896]{2,1,0:T(8,128)S(1)}, u32[]{:S(2)}, u32[]{:S(2)}) collective-permute-start(f32[2,64,896]{2,1,0:T(8,128)S(1)} %slice.27), channel_id=1, source_target_pairs={{0,1},{1,0},{2,3},{3,2},{4,5},{5,4},{6,7},{7,6},{8,9},{9,8},{10,11... | collective-permute-start | bytes 1376264 | tf_op jit(solution)/shard_map/ppermute | solution.py:41
  27.3 15.3 %collective-permute-start.3 = (f32[2,64,640]{2,1,0:T(8,128)S(1)}, f32[2,64,640]{2,1,0:T(8,128)S(1)}, u32[]{:S(2)}, u32[]{:S(2)}) collective-permute-start(f32[2,64,640]{2,1,0:T(8,128)S(1)} %pad_maximum_fusion.10), channel_id=1, source_target_pairs={{0,12},{1,13},{2,14},{3,15},{4,8},{5,9},{6,10},{7,11},{8,4},{9,5},... | collective-permute-start | bytes 983048 | tf_op jit(solution)/shard_map/ppermute | solution.py:41
  32.7 12.8 %collective-permute-start.7 = (f32[2,64,640]{2,1,0:T(8,128)S(1)}, f32[2,64,640]{2,1,0:T(8,128)S(1)}, u32[]{:S(2)}, u32[]{:S(2)}) collective-permute-start(f32[2,64,640]{2,1,0:T(8,128)S(1)} %pad_maximum_fusion.9), channel_id=1, source_target_pairs={{0,3},{1,2},{2,1},{3,0},{4,7},{5,6},{6,5},{7,4},{8,11},{9,10},{10,... | collective-permute-start | bytes 983048 | tf_op jit(solution)/shard_map/ppermute | solution.py:41
  35.7 22.8 %collective-permute-start.8 = (f32[2,128,896]{2,1,0:T(8,128)S(1)}, f32[2,128,896]{2,1,0:T(8,128)}, u32[]{:S(2)}, u32[]{:S(2)}) collective-permute-start(f32[2,128,896]{2,1,0:T(8,128)S(1)} %pad_maximum_fusion.refs_0_), channel_id=1, source_target_pairs={{0,12},{1,13},{2,14},{3,15},{4,8},{5,9},{6,10},{7,11},{8,4},{9,5},... | collective-permute-start | bytes 2752520 | tf_op jit(solution)/shard_map/ppermute | solution.py:41
  38.3 10.0 %copy-start = (f32[3072,128]{1,0:T(8,128)S(1)}, f32[3072,128]{1,0:T(8,128)}, u32[]{:S(2)}) copy-start(f32[3072,128]{1,0:T(8,128)} %z_ref.3) | copy-start | bytes 4718596
  38.3 25.7 %collective-permute-start.10 = (f32[2,128,896]{2,1,0:T(8,128)S(1)}, f32[2,128,896]{2,1,0:T(8,128)}, u32[]{:S(2)}, u32[]{:S(2)}) collective-permute-start(f32[2,128,896]{2,1,0:T(8,128)S(1)} %pad_maximum_fusion.1.refs_2_), channel_id=1, source_target_pairs={{0,3},{1,2},{2,1},{3,0},{4,7},{5,6},{6,5},{7,4},{8,11},{9,10},{10,... | collective-permute-start | bytes 2752520 | tf_op jit(solution)/shard_map/ppermute | solution.py:41
  43.5 17.8 %collective-permute-start.9 = (f32[2,128,640]{2,1,0:T(8,128)}, f32[2,128,640]{2,1,0:T(8,128)}, u32[]{:S(2)}, u32[]{:S(2)}) collective-permute-start(f32[2,128,640]{2,1,0:T(8,128)} %pad_maximum_fusion.4.refs_1_), channel_id=1, source_target_pairs={{0,4},{1,5},{2,6},{3,7},{4,0},{5,1},{6,2},{7,3},{8,12},{9,13},{10,... | collective-permute-start | bytes 1966088 | tf_op jit(solution)/shard_map/ppermute | solution.py:41
  46.4 19.8 %collective-permute-start.11 = (f32[2,128,640]{2,1,0:T(8,128)}, f32[2,128,640]{2,1,0:T(8,128)}, u32[]{:S(2)}, u32[]{:S(2)}) collective-permute-start(f32[2,128,640]{2,1,0:T(8,128)} %pad_maximum_fusion.5.refs_3_), channel_id=1, source_target_pairs={{0,1},{1,0},{2,3},{3,2},{4,5},{5,4},{6,7},{7,6},{8,9},{9,8},{10,11... | collective-permute-start | bytes 1966088 | tf_op jit(solution)/shard_map/ppermute | solution.py:41
  50.8 9.8 %copy-start.1 = (bf16[256,896]{1,0:T(8,128)(2,1)}, bf16[256,896]{1,0:T(8,128)(2,1)S(1)}, u32[]{:S(2)}) copy-start(bf16[256,896]{1,0:T(8,128)(2,1)S(1)} %get-tuple-element.28.first_h.refs_0_) | copy-start | bytes 1376260
  50.8 9.8 %copy-start.3 = (bf16[256,896]{1,0:T(8,128)(2,1)}, bf16[256,896]{1,0:T(8,128)(2,1)S(1)}, u32[]{:S(2)}) copy-start(bf16[256,896]{1,0:T(8,128)(2,1)S(1)} %get-tuple-element.29.first_l.refs_1_) | copy-start | bytes 1376260
  50.8 10.5 %copy-start.9 = (bf16[256,640]{1,0:T(8,128)(2,1)}, bf16[256,640]{1,0:T(8,128)(2,1)S(1)}, u32[]{:S(2)}) copy-start(bf16[256,640]{1,0:T(8,128)(2,1)S(1)} %get-tuple-element.32.first_h.refs_4_) | copy-start | bytes 983044
  50.8 10.5 %copy-start.11 = (bf16[256,640]{1,0:T(8,128)(2,1)}, bf16[256,640]{1,0:T(8,128)(2,1)S(1)}, u32[]{:S(2)}) copy-start(bf16[256,640]{1,0:T(8,128)(2,1)S(1)} %get-tuple-element.33.first_l.refs_5_) | copy-start | bytes 983044
  50.8 13.2 %copy-start.5 = (bf16[256,896]{1,0:T(8,128)(2,1)}, bf16[256,896]{1,0:T(8,128)(2,1)S(1)}, u32[]{:S(2)}) copy-start(bf16[256,896]{1,0:T(8,128)(2,1)S(1)} %get-tuple-element.35.first_h.refs_8_) | copy-start | bytes 1376260
  50.8 13.2 %copy-start.7 = (bf16[256,896]{1,0:T(8,128)(2,1)}, bf16[256,896]{1,0:T(8,128)(2,1)S(1)}, u32[]{:S(2)}) copy-start(bf16[256,896]{1,0:T(8,128)(2,1)S(1)} %get-tuple-element.36.first_l.refs_9_) | copy-start | bytes 1376260
  50.8 15.4 %copy-start.13 = (bf16[256,640]{1,0:T(8,128)(2,1)}, bf16[256,640]{1,0:T(8,128)(2,1)S(1)}, u32[]{:S(2)}) copy-start(bf16[256,640]{1,0:T(8,128)(2,1)S(1)} %get-tuple-element.38.first_h.refs_12_) | copy-start | bytes 983044
  50.8 15.4 %copy-start.15 = (bf16[256,640]{1,0:T(8,128)(2,1)}, bf16[256,640]{1,0:T(8,128)(2,1)S(1)}, u32[]{:S(2)}) copy-start(bf16[256,640]{1,0:T(8,128)(2,1)S(1)} %get-tuple-element.39.first_l.refs_13_) | copy-start | bytes 983044
  60.6 0.8 copy-start.17
  61.3 1.9 %copy-start.19 = (bf16[256,896]{1,0:T(8,128)(2,1)}, bf16[256,896]{1,0:T(8,128)(2,1)S(1)}, u32[]{:S(2)}) copy-start(bf16[256,896]{1,0:T(8,128)(2,1)S(1)} %get-tuple-element.42.refs_3_) | copy-start | bytes 1376260
  63.3 0.7 copy-start.25
  64.0 2.2 %copy-start.27 = (bf16[256,640]{1,0:T(8,128)(2,1)}, bf16[256,640]{1,0:T(8,128)(2,1)S(1)}, u32[]{:S(2)}) copy-start(bf16[256,640]{1,0:T(8,128)(2,1)S(1)} %get-tuple-element.44.refs_7_) | copy-start | bytes 983044
  66.2 2.1 %copy-start.21 = (bf16[256,896]{1,0:T(8,128)(2,1)}, bf16[256,896]{1,0:T(8,128)(2,1)S(1)}, u32[]{:S(2)}) copy-start(bf16[256,896]{1,0:T(8,128)(2,1)S(1)} %get-tuple-element.45.refs_10_) | copy-start | bytes 1376260
  66.2 2.1 %copy-start.23 = (bf16[256,896]{1,0:T(8,128)(2,1)}, bf16[256,896]{1,0:T(8,128)(2,1)S(1)}, u32[]{:S(2)}) copy-start(bf16[256,896]{1,0:T(8,128)(2,1)S(1)} %get-tuple-element.46.refs_11_) | copy-start | bytes 1376260
  68.3 0.7 copy-start.29
  69.0 0.7 copy-start.31
  69.8 6.9 %collective-permute-start.12 = (f32[512,128]{1,0:T(8,128)S(1)}, f32[512,128]{1,0:T(8,128)S(1)}, u32[]{:S(2)}, u32[]{:S(2)}) collective-permute-start(f32[512,128]{1,0:T(8,128)S(1)} %constant_dynamic-slice_fusion), channel_id=1, source_target_pairs={{0,16},{16,0},{32,48},{48,32},{64,80},{80,64},{96,112},{112,96},{1... | collective-permute-start | bytes 786440 | tf_op jit(solution)/shard_map/ppermute | solution.py:237
  88.5 50.6 %copy-start.2 = (bf16[256,896]{1,0:T(8,128)(2,1)S(1)}, bf16[256,896]{1,0:T(8,128)(2,1)}, u32[]{:S(2)}) copy-start(bf16[256,896]{1,0:T(8,128)(2,1)} %copy-done.1) | copy-start | bytes 1376260
  88.6 50.6 %copy-start.4 = (bf16[256,896]{1,0:T(8,128)(2,1)S(1)}, bf16[256,896]{1,0:T(8,128)(2,1)}, u32[]{:S(2)}) copy-start(bf16[256,896]{1,0:T(8,128)(2,1)} %copy-done.3) | copy-start | bytes 1376260
  88.6 50.6 %copy-start.6 = (bf16[256,896]{1,0:T(8,128)(2,1)S(1)}, bf16[256,896]{1,0:T(8,128)(2,1)}, u32[]{:S(2)}) copy-start(bf16[256,896]{1,0:T(8,128)(2,1)} %copy-done.5) | copy-start | bytes 1376260
  88.6 50.6 %copy-start.8 = (bf16[256,896]{1,0:T(8,128)(2,1)S(1)}, bf16[256,896]{1,0:T(8,128)(2,1)}, u32[]{:S(2)}) copy-start(bf16[256,896]{1,0:T(8,128)(2,1)} %copy-done.7) | copy-start | bytes 1376260
  129.4 8.4 %collective-permute-start.13 = (f32[512,128]{1,0:T(8,128)}, f32[512,128]{1,0:T(8,128)}, u32[]{:S(2)}, u32[]{:S(2)}) collective-permute-start(f32[512,128]{1,0:T(8,128)} %bitcast.6), channel_id=1, source_target_pairs={{0,16},{16,0},{32,48},{48,32},{64,80},{80,64},{96,112},{112,96},{1... | collective-permute-start | bytes 786440 | tf_op jit(solution)/shard_map/ppermute | solution.py:248
  139.2 1.0 copy-start.10
  140.2 1.0 copy-start.12
  141.2 1.0 copy-start.14
  142.1 1.0 copy-start.16
  143.1 1.0 copy-start.18
  144.1 1.0 copy-start.20
  145.2 1.0 copy-start.22
  146.2 1.0 copy-start.24
  147.2 1.0 copy-start.26
  148.2 1.0 copy-start.28
  149.1 1.0 copy-start.30
  150.1 1.0 copy-start.32
  151.1 0.9 copy-start.33
  152.0 0.9 copy-start.34

commit v4 on v3

--- a/solution.py
+++ b/solution.py
@@ -74,8 +74,10 @@
 
 def early_kernel(all_masks, width, bases, k, z_ref, *refs):
     count = len(bases)
-    halves, acc_ref, zb_ref, out = refs[:count], refs[count], refs[count + 1], refs[count + 2 :]
+    halves, acc_ref, zb_ref, out = refs[:count], refs[count], refs[count + 1], refs[count + 2 : 3 * count + 2]
+    kept, sems = refs[3 * count + 2 : -1], refs[-1]
     m = z_ref.shape[1]
+    copies = []
     acc_ref[...] = jnp.zeros_like(acc_ref)
     for p, base in enumerate(bases):
         n = halves[p].shape[2]
@@ -83,9 +85,14 @@
         zb_ref[base : base + n, :m] = z_h
         zb_ref[base : base + n, m:] = z_l
         split_half(halves[p], out[2 * p], out[2 * p + 1])
+        for i in (2 * p, 2 * p + 1):
+            copies.append(pltpu.make_async_copy(out[i], kept[i], sems.at[i]))
+            copies[-1].start()
         part = half_coeffs(out[2 * p][...], out[2 * p + 1][...], zb_ref[base : base + n, :])
         for place, rows in scatter_rows(part, all_masks[p][0], k, width):
             acc_ref[place : place + width, :] += rows
+    for copy in copies:
+        copy.wait()
 
 
 def split_shapes(half):
@@ -97,26 +104,35 @@
     return [pl.BlockSpec(memory_space=pltpu.VMEM)] * count
 
 
+def hbm_specs(count):
+    return [pl.BlockSpec(memory_space=pltpu.HBM)] * count
+
+
 def early(z, halves, all_masks, bases, k, width):
     n, m = z.shape
     shapes = [jax.ShapeDtypeStruct((2 * k, m), F32), jax.ShapeDtypeStruct((n, 2 * m), BF16)]
-    for half in halves:
-        shapes += split_shapes(half)
+    split_halves = [shape for half in halves for shape in split_shapes(half)]
+    count = len(split_halves)
     out = pl.pallas_call(
         functools.partial(early_kernel, all_masks, width, bases, k),
-        out_shape=shapes,
+        out_shape=shapes + split_halves + split_halves,
         in_specs=vmem_specs(1 + len(halves)),
-        out_specs=vmem_specs(len(shapes)),
+        out_specs=vmem_specs(2 + count) + hbm_specs(count),
+        scratch_shapes=[pltpu.SemaphoreType.DMA((count,))],
         compiler_params=pltpu.CompilerParams(vmem_limit_bytes=EARLY_VMEM),
         cost_estimate=pl.CostEstimate(flops=6 * k * n * m, bytes_accessed=12 << 20, transcendentals=0),
     )(z, *halves)
-    return out[0], out[1], [(out[2 + 2 * p], out[3 + 2 * p]) for p in range(len(halves))]
-
-
-def late_kernel(masks, width, base, k, first, acc_ref, got_ref, first_h, first_l, zb_ref, out_ref, got_h, got_l):
+    return out[0], out[1], out[2 : 2 + count], out[2 + count :]
+
+
+def late_kernel(masks, width, base, k, first, acc_ref, got_ref, first_h, first_l, zb_ref, out_ref, *refs):
+    kept, (got_h, got_l, sems) = refs[:2], refs[2:]
     n = got_ref.shape[2]
     m = zb_ref.shape[1] // 2
     split_half(got_ref, got_h, got_l)
+    copies = [pltpu.make_async_copy(half, kept[i], sems.at[i]) for i, half in enumerate((got_h, got_l))]
+    for copy in copies:
+        copy.start()
     part = half_coeffs(got_h[...], got_l[...], zb_ref[base : base + n, :])
     added = {place: rows for place, rows in scatter_rows(part, masks[1], k, width)}
     for place in range(0, 2 * k, width):
@@ -131,26 +147,44 @@
         row = 2 * k + i * k
         part = gram[:, i * m : (i + 1) * m]
         out_ref[row : row + k, :] = part if first else acc_ref[row : row + k, :] + part
+    for copy in copies:
+        copy.wait()
 
 
 def late(acc, got, firsts, zb, masks, base, first, k, width):
     m = zb.shape[1] // 2
-    shapes = [jax.ShapeDtypeStruct((2 * k + k * k // m, m), F32)] + split_shapes(got)
+    split_got = split_shapes(got)
     return pl.pallas_call(
         functools.partial(late_kernel, masks, width, base, k, first),
-        out_shape=shapes,
+        out_shape=[jax.ShapeDtypeStruct((2 * k + k * k // m, m), F32)] + split_got,
         in_specs=vmem_specs(5),
-        out_specs=vmem_specs(3),
+        out_specs=vmem_specs(1) + hbm_specs(2),
+        scratch_shapes=[pltpu.VMEM(shape.shape, BF16) for shape in split_got] + [pltpu.SemaphoreType.DMA((2,))],
         compiler_params=pltpu.CompilerParams(vmem_limit_bytes=LATE_VMEM),
     )(acc, got, *firsts, zb)
 
 
-def apply_kernel(all_masks, width, bases, col_ref, total_ref, t_one_ref, t_two_ref, z_ref, *refs):
-    halves, out_ref, true_ref, slot_ref = refs[:-3], refs[-3], refs[-2], refs[-1]
+def apply_kernel(all_masks, width, bases, place_ref, mine_ref, other_ref, t_one_ref, t_two_ref, z_ref, *refs):
+    count = 4 * len(bases)
+    halves, out_ref, held = refs[:count], refs[count], refs[count + 1 : 2 * count + 1]
+    z_held, out_held, total_ref, true_ref, slot_ref, sems, z_sems, out_sems = refs[2 * count + 1 :]
     k = t_one_ref.shape[0]
     m = z_ref.shape[1]
     blocks = k // width
-    col = col_ref[0]
+    ends = bases[1:] + [z_ref.shape[0]]
+    loads = [pltpu.make_async_copy(half, held[i], sems.at[i]) for i, half in enumerate(halves)]
+    z_loads = []
+    for p, (base, end) in enumerate(zip(bases, ends)):
+        rows = pl.ds(base, end - base)
+        z_loads.append(pltpu.make_async_copy(z_ref.at[rows, :], z_held.at[rows, :], z_sems.at[p]))
+    for p in range(len(bases)):
+        for i in range(4 * p, 4 * p + 4):
+            loads[i].start()
+        z_loads[p].start()
+    col, core = place_ref[0], place_ref[1]
+    half = mine_ref.shape[0]
+    total_ref[pl.ds(pl.multiple_of(core * half, half), half), :] = mine_ref[...]
+    total_ref[pl.ds(pl.multiple_of((1 - core) * half, half), half), :] = other_ref[...]
 
     def place(s):
         return pl.ds(pl.multiple_of(lax.bitwise_xor(col, s) * width, width), width)
@@ -170,26 +204,37 @@
     solve(t_one_ref, coeff, 0)
     x_h, x_l = split(slot_ref[...].T)
     x_both = jnp.concatenate([x_h, x_l], 0)
-    for p, (base, masks) in enumerate(zip(bases, all_masks)):
-        first_h, first_l, got_h, got_l = halves[4 * p : 4 * p + 4]
-        n = first_h.shape[1]
+    stores = []
+    for p, (base, end, masks) in enumerate(zip(bases, ends, all_masks)):
+        for load in loads[4 * p : 4 * p + 4] + [z_loads[p]]:
+            load.wait()
+        first_h, first_l, got_h, got_l = held[4 * p : 4 * p + 4]
         high = jnp.concatenate([in_order((first_h, got_h), masks, w, width) for w in range(2)], 0)
         low = jnp.concatenate([in_order((first_l, got_l), masks, w, width) for w in range(2)], 0)
         wide = dot(x_both, high)
         moved = wide[:m, :] + (wide[m:, :] + dot(x_h, low))
-        out_ref[base : base + n, :] = z_ref[base : base + n, :] - moved.T
-
-
-def apply(col, total, t_one, t_two, z, halves, all_masks, bases, width):
-    k = t_one.shape[0]
+        out_held[base:end, :] = z_held[base:end, :] - moved.T
+        rows = pl.ds(base, end - base)
+        stores.append(pltpu.make_async_copy(out_held.at[rows, :], out_ref.at[rows, :], out_sems.at[p]))
+        stores[-1].start()
+    for store in stores:
+        store.wait()
+
+
+def apply(place, mine, other, t_one, t_two, z, halves, all_masks, bases, width):
+    k, m = t_one.shape[0], z.shape[1]
+    rows = pltpu.VMEM(z.shape, F32)
+    dma = pltpu.SemaphoreType.DMA
     return pl.pallas_call(
         functools.partial(apply_kernel, all_masks, width, bases),
         out_shape=jax.ShapeDtypeStruct(z.shape, F32),
-        in_specs=[pl.BlockSpec(memory_space=pltpu.SMEM)] + vmem_specs(4 + len(halves)),
-        out_specs=pl.BlockSpec(memory_space=pltpu.VMEM),
-        scratch_shapes=[pltpu.VMEM((k, z.shape[1]), F32), pltpu.VMEM((2 * k, z.shape[1]), F32)],
+        in_specs=[pl.BlockSpec(memory_space=pltpu.SMEM)] + vmem_specs(4) + hbm_specs(1 + len(halves)),
+        out_specs=pl.BlockSpec(memory_space=pltpu.HBM),
+        scratch_shapes=[pltpu.VMEM(half.shape, BF16) for half in halves]
+        + [rows, rows, pltpu.VMEM((2 * mine.shape[0], m), F32), pltpu.VMEM((k, m), F32), pltpu.VMEM((2 * k, m), F32)]
+        + [dma((len(halves),)), dma((len(bases),)), dma((len(bases),))],
         compiler_params=pltpu.CompilerParams(vmem_limit_bytes=APPLY_VMEM),
-    )(col, total, t_one, t_two, z, *halves)
+    )(place, mine, other, t_one, t_two, z, *halves)
 
 
 def gather_pieces(own, size):
@@ -245,8 +290,7 @@
         jnp.broadcast_to(mine[None], (NEAR,) + mine.shape), "row", 0, 0, axis_index_groups=near, tiled=True
     )
     mine = blocks.reshape(half, m)
-    other = lax.ppermute(mine, "row", pair)
-    return jnp.where(core == 0, jnp.concatenate([mine, other], 0), jnp.concatenate([other, mine], 0))
+    return mine, lax.ppermute(mine, "row", pair), core
 
 
 def body(size, z_slab, v_first, v_second, t_first, t_second):
@@ -255,14 +299,15 @@
     own = lax.optimization_barrier(jnp.stack([v_first.T, v_second.T]))
     pieces, masks, cuts = gather_pieces(own, size)
     bases = cuts[:-1]
-    part, z_both, firsts = early(z_slab, [piece[0] for piece in pieces], masks, bases, k, width)
+    part, z_both, firsts, kept = early(z_slab, [piece[0] for piece in pieces], masks, bases, k, width)
     halves = []
     for p, base in enumerate(bases):
-        part, *got = late(part, pieces[p][1], firsts[p], z_both, masks[p], base, p == 0, k, width)
-        halves += [*firsts[p], *got]
-    total = sum_over_row(part)
-    col = lax.axis_index("col").astype(jnp.int32).reshape(1)
-    return apply(col, total, t_first, t_second, z_slab, halves, masks, bases, width)
+        two = slice(2 * p, 2 * p + 2)
+        part, *got = late(part, pieces[p][1], firsts[two], z_both, masks[p], base, p == 0, k, width)
+        halves += [*kept[two], *got]
+    mine, other, core = sum_over_row(part)
+    place = jnp.stack([lax.axis_index("col"), core]).astype(jnp.int32)
+    return apply(place, mine, other, t_first, t_second, z_slab, halves, masks, bases, width)
 
 
 def solution(mesh):

time: 159 us -> 168 us (1.057)
  Pallas kernels: 15.3 us -> 26.1 us
  waiting for transfers between devices: 11.9 us -> 7.69 us
  local copies, waits for them, and re-layouts: 16.9 us -> 20 us
    pallas_call x1, Pallas kernels: 4.72 us -> 10.5 us  [apply(): pl.pallas_call(functools.partial(apply_kernel, all_masks, width, bases),...]
    ppermute x12, waiting for transfers between devices: 9.26 us -> 5.55 us  [swap(): return lax.ppermute(x, 'col', [(i, i ^ mask) for i in range(size)])]
    pallas_call x1, Pallas kernels: 2.47 us -> 5.48 us  [early(): pl.pallas_call(functools.partial(early_kernel, all_masks, width, bases, k...]
    pallas_call x4, Pallas kernels: 8.13 us -> 10.1 us  [late(): pl.pallas_call(functools.partial(late_kernel, masks, width, base, k, firs...]
  transfers between devices with their start and end apart: 14 -> 14, of which waited for: 5 -> 5; matrix products, arithmetic and copies ran while one was open for 1% -> 1% of each run, Pallas kernels for 5% -> 8%
where the time goes in v4:
time: 168 us; the launch traced here: 167 us
  starting transfers between devices  56.1 us (33%)
  blocking collectives  51.3 us (31%)
  Pallas kernels  26.1 us (16%)
  local copies, waits for them, and re-layouts  20 us (12%)
  waiting for transfers between devices  7.69 us (5%)
  other arithmetic  4.54 us (3%)
    ppermute x12, starting transfers between devices, swap(): return lax.ppermute(x, 'col', [(i, i ^ mask) for i in range(size)])  43.2 us
    all_to_all x1, blocking collectives, sum_over_row(): lax.all_to_all(jnp.broadcast_to(mine[None], (FAR,) + mine.shape), 'row',...  26.9 us
    unnamed x70, local copies, waits for them, and re-layouts  18.2 us
    all_to_all x1, blocking collectives, sum_over_row(): lax.all_to_all(jnp.broadcast_to(mine[None], (NEAR,) + mine.shape), 'row',...  12.6 us
    all_to_all x1, blocking collectives, sum_over_row(): lax.all_to_all(mine.reshape(NEAR, half // NEAR, m), 'row', 0, 0, axis_ind...  11.9 us
    pallas_call x1, Pallas kernels, apply(): pl.pallas_call(functools.partial(apply_kernel, all_masks, width, bases),...  10.5 us
    pallas_call x4, Pallas kernels, late(): pl.pallas_call(functools.partial(late_kernel, masks, width, base, k, firs...  10.1 us
    ppermute x1, starting transfers between devices, sum_over_row(): return (mine, lax.ppermute(mine, 'row', pair), core)  7.12 us
  transfers between devices with their start and end apart: 14, of which 5 were waited for; matrix products, arithmetic and copies ran while one was open for 1% of the time, Pallas kernels for 8%

profile of v4, /device:TPU:1, one launch (start us, length us, event | category | flops | bytes accessed | tf_op | source)
XLA Modules:
  0.0 166.5 jit_solution(11587283533271694912)
XLA Ops:
  0.0 1.0 pad_maximum_fusion.6
  1.1 3.9 %collective-permute-start = (f32[2,16,1536]{2,1,0:T(8,128)S(1)}, f32[2,16,1536]{2,1,0:T(8,128)S(1)}, u32[]{:S(2)}, u32[]{:S(2)}) collective-permute-start(f32[2,16,1536]{2,1,0:T(8,128)S(1)} %get-tuple-element.66), channel_id=1, source_target_pairs={{0,1},{1,0},{2,3},{3,2},{4,5},{5,4},{6,7},{7,6},{8,9},{9,8},{10,11... | collective-permute-start | bytes 589832 | tf_op jit(solution)/shard_map/ppermute | solution.py:41
  5.0 3.2 %collective-permute-start.4 = (f32[2,16,1536]{2,1,0:T(8,128)S(1)}, f32[2,16,1536]{2,1,0:T(8,128)S(1)}, u32[]{:S(2)}, u32[]{:S(2)}) collective-permute-start(f32[2,16,1536]{2,1,0:T(8,128)S(1)} %get-tuple-element.65), channel_id=1, source_target_pairs={{0,4},{1,5},{2,6},{3,7},{4,0},{5,1},{6,2},{7,3},{8,12},{9,13},{10,... | collective-permute-start | bytes 589832 | tf_op jit(solution)/shard_map/ppermute | solution.py:41
  8.3 0.0 collective-permute-done
  8.3 5.7 %collective-permute-start.1 = (f32[2,32,1536]{2,1,0:T(8,128)S(1)}, f32[2,32,1536]{2,1,0:T(8,128)S(1)}, u32[]{:S(2)}, u32[]{:S(2)}) collective-permute-start(f32[2,32,1536]{2,1,0:T(8,128)S(1)} %pad_maximum_fusion.7), channel_id=1, source_target_pairs={{0,3},{1,2},{2,1},{3,0},{4,7},{5,6},{6,5},{7,4},{8,11},{9,10},{10,... | collective-permute-start | bytes 1179656 | tf_op jit(solution)/shard_map/ppermute | solution.py:41
  14.1 4.6 %collective-permute-start.5 = (f32[2,32,1536]{2,1,0:T(8,128)S(1)}, f32[2,32,1536]{2,1,0:T(8,128)S(1)}, u32[]{:S(2)}, u32[]{:S(2)}) collective-permute-start(f32[2,32,1536]{2,1,0:T(8,128)S(1)} %pad_maximum_fusion.8), channel_id=1, source_target_pairs={{0,12},{1,13},{2,14},{3,15},{4,8},{5,9},{6,10},{7,11},{8,4},{9,5},... | collective-permute-start | bytes 1179656 | tf_op jit(solution)/shard_map/ppermute | solution.py:41
  18.7 0.5 collective-permute-done.1
  19.2 0.1 pad_maximum_fusion.2
  19.3 4.9 %collective-permute-start.2 = (f32[2,64,896]{2,1,0:T(8,128)S(1)}, f32[2,64,896]{2,1,0:T(8,128)S(1)}, u32[]{:S(2)}, u32[]{:S(2)}) collective-permute-start(f32[2,64,896]{2,1,0:T(8,128)S(1)} %slice.25), channel_id=1, source_target_pairs={{0,4},{1,5},{2,6},{3,7},{4,0},{5,1},{6,2},{7,3},{8,12},{9,13},{10,... | collective-permute-start | bytes 1376264 | tf_op jit(solution)/shard_map/ppermute | solution.py:41
  24.2 1.1 collective-permute-done.5
  25.3 0.1 pad_maximum_fusion.3
  25.4 1.9 %collective-permute-start.6 = (f32[2,64,896]{2,1,0:T(8,128)S(1)}, f32[2,64,896]{2,1,0:T(8,128)S(1)}, u32[]{:S(2)}, u32[]{:S(2)}) collective-permute-start(f32[2,64,896]{2,1,0:T(8,128)S(1)} %slice.27), channel_id=1, source_target_pairs={{0,1},{1,0},{2,3},{3,2},{4,5},{5,4},{6,7},{7,6},{8,9},{9,8},{10,11... | collective-permute-start | bytes 1376264 | tf_op jit(solution)/shard_map/ppermute | solution.py:41
  27.3 5.3 %collective-permute-start.3 = (f32[2,64,640]{2,1,0:T(8,128)S(1)}, f32[2,64,640]{2,1,0:T(8,128)S(1)}, u32[]{:S(2)}, u32[]{:S(2)}) collective-permute-start(f32[2,64,640]{2,1,0:T(8,128)S(1)} %pad_maximum_fusion.10), channel_id=1, source_target_pairs={{0,12},{1,13},{2,14},{3,15},{4,8},{5,9},{6,10},{7,11},{8,4},{9,5},... | collective-permute-start | bytes 983048 | tf_op jit(solution)/shard_map/ppermute | solution.py:41
  32.7 3.0 %collective-permute-start.7 = (f32[2,64,640]{2,1,0:T(8,128)S(1)}, f32[2,64,640]{2,1,0:T(8,128)S(1)}, u32[]{:S(2)}, u32[]{:S(2)}) collective-permute-start(f32[2,64,640]{2,1,0:T(8,128)S(1)} %pad_maximum_fusion.9), channel_id=1, source_target_pairs={{0,3},{1,2},{2,1},{3,0},{4,7},{5,6},{6,5},{7,4},{8,11},{9,10},{10,... | collective-permute-start | bytes 983048 | tf_op jit(solution)/shard_map/ppermute | solution.py:41
  35.7 0.0 collective-permute-done.2
  35.7 0.1 pad_maximum_fusion.refs_0_
  35.7 2.4 %collective-permute-start.8 = (f32[2,128,896]{2,1,0:T(8,128)S(1)}, f32[2,128,896]{2,1,0:T(8,128)}, u32[]{:S(2)}, u32[]{:S(2)}) collective-permute-start(f32[2,128,896]{2,1,0:T(8,128)S(1)} %pad_maximum_fusion.refs_0_), channel_id=1, source_target_pairs={{0,12},{1,13},{2,14},{3,15},{4,8},{5,9},{6,10},{7,11},{8,4},{9,5},... | collective-permute-start | bytes 2752520 | tf_op jit(solution)/shard_map/ppermute | solution.py:41
  38.2 0.1 pad_maximum_fusion.1.refs_2_
  38.3 0.0 copy-start
  38.3 4.4 %collective-permute-start.10 = (f32[2,128,896]{2,1,0:T(8,128)S(1)}, f32[2,128,896]{2,1,0:T(8,128)}, u32[]{:S(2)}, u32[]{:S(2)}) collective-permute-start(f32[2,128,896]{2,1,0:T(8,128)S(1)} %pad_maximum_fusion.1.refs_2_), channel_id=1, source_target_pairs={{0,3},{1,2},{2,1},{3,0},{4,7},{5,6},{6,5},{7,4},{8,11},{9,10},{10,... | collective-permute-start | bytes 2752520 | tf_op jit(solution)/shard_map/ppermute | solution.py:41
  42.7 0.9 pad_maximum_fusion.4.refs_1_
  43.5 1.9 %collective-permute-start.9 = (f32[2,128,640]{2,1,0:T(8,128)}, f32[2,128,640]{2,1,0:T(8,128)}, u32[]{:S(2)}, u32[]{:S(2)}) collective-permute-start(f32[2,128,640]{2,1,0:T(8,128)} %pad_maximum_fusion.4.refs_1_), channel_id=1, source_target_pairs={{0,4},{1,5},{2,6},{3,7},{4,0},{5,1},{6,2},{7,3},{8,12},{9,13},{10,... | collective-permute-start | bytes 1966088 | tf_op jit(solution)/shard_map/ppermute | solution.py:41
  45.5 0.9 pad_maximum_fusion.5.refs_3_
  46.4 1.9 %collective-permute-start.11 = (f32[2,128,640]{2,1,0:T(8,128)}, f32[2,128,640]{2,1,0:T(8,128)}, u32[]{:S(2)}, u32[]{:S(2)}) collective-permute-start(f32[2,128,640]{2,1,0:T(8,128)} %pad_maximum_fusion.5.refs_3_), channel_id=1, source_target_pairs={{0,1},{1,0},{2,3},{3,2},{4,5},{5,4},{6,7},{7,6},{8,9},{9,8},{10,11... | collective-permute-start | bytes 1966088 | tf_op jit(solution)/shard_map/ppermute | solution.py:41
  48.3 5.5 %shard_map.55 = (f32[512,128]{1,0:T(8,128)S(1)}, bf16[3072,256]{1,0:T(8,128)(2,1)S(1)}, bf16[256,896]{1,0:T(8,128)(2,1)S(1)}, bf16[256,896]{1,0:T(8,128)(2,1)S(1...) custom-call(f32[3072,128]{1,0:T(8,128)S(1)} %copy-done, ...), custom_call_target="tpu_custom_call" | custom-call | flops 603979776 | bytes 12582912 | tf_op jit(solution)/shard_map/pallas_call | solution.py:116
  53.8 0.7 copy-done.23
  54.6 3.9 %collective-permute-done.8.got_ref = f32[2,128,896]{2,1,0:T(8,128)} collective-permute-done((f32[2,128,896]{2,1,0:T(8,128)S(1)}, f32[2,128,896]{2,1,0:T(8,128)}, u32[]{:S(2)}, u32[]{:S(2)}) %collective-permute-start.8) | collective-permute-done | bytes 917536 | tf_op jit(solution)/shard_map/ppermute | solution.py:41
  58.5 2.7 %shard_map.56 = (f32[1024,128]{1,0:T(8,128)S(1)}, bf16[256,896]{1,0:T(8,128)(2,1)S(1)}, bf16[256,896]{1,0:T(8,128)(2,1)S(1)}) custom-call(f32[512,128]{1,0:T(8,128)S(1)} %get-tuple-element.35.acc_ref, f32[2,128,896]{2,1,0:T(8,128)} %collective-permute-done.8.got_ref, bf16[256,896]{1,0:T(8,128)(2,1)S(1)} %get-tuple-element.36.first_h, ...), custom_call_target="tpu_custom_call" | custom-call | tf_op jit(solution)/shard_map/pallas_call | solution.py:157
  61.3 2.4 %shard_map.57 = (f32[1024,128]{1,0:T(8,128)S(1)}, bf16[256,640]{1,0:T(8,128)(2,1)S(1)}, bf16[256,640]{1,0:T(8,128)(2,1)S(1)}) custom-call(f32[1024,128]{1,0:T(8,128)S(1)} %get-tuple-element.39.acc_ref, f32[2,128,640]{2,1,0:T(8,128)} %collective-permute-done.9.got_ref, bf16[256,640]{1,0:T(8,128)(2,1)S(1)} %get-tuple-element.40.first_h, ...), custom_call_target="tpu_custom_call" | custom-call | tf_op jit(solution)/shard_map/pallas_call | solution.py:157
  63.8 0.7 copy-done.25
  64.5 0.7 copy-done.27
  65.2 2.7 %shard_map.58 = (f32[1024,128]{1,0:T(8,128)S(1)}, bf16[256,896]{1,0:T(8,128)(2,1)S(1)}, bf16[256,896]{1,0:T(8,128)(2,1)S(1)}) custom-call(f32[1024,128]{1,0:T(8,128)S(1)} %get-tuple-element.42.acc_ref, f32[2,128,896]{2,1,0:T(8,128)} %collective-permute-done.10.got_ref, bf16[256,896]{1,0:T(8,128)(2,1)S(1)} %get-tuple-element.43.first_h, ...), custom_call_target="tpu_custom_call" | custom-call | tf_op jit(solution)/shard_map/pallas_call | solution.py:157
  67.9 0.0 copy-start.13
  67.9 0.8 copy-done.13
  68.7 2.2 %shard_map.59 = (f32[1024,128]{1,0:T(8,128)S(1)}, bf16[256,640]{1,0:T(8,128)(2,1)S(1)}, bf16[256,640]{1,0:T(8,128)(2,1)S(1)}) custom-call(f32[1024,128]{1,0:T(8,128)S(1)} %get-tuple-element.45.acc_ref, f32[2,128,640]{2,1,0:T(8,128)} %collective-permute-done.11.got_ref, bf16[256,640]{1,0:T(8,128)(2,1)S(1)} %get-tuple-element.46.first_h, ...), custom_call_target="tpu_custom_call" | custom-call | tf_op jit(solution)/shard_map/pallas_call | solution.py:157
  71.0 0.7 copy-done.29
  71.7 0.7 copy-done.31
  72.5 5.8 %collective-permute-start.12 = (f32[512,128]{1,0:T(8,128)S(1)}, f32[512,128]{1,0:T(8,128)S(1)}, u32[]{:S(2)}, u32[]{:S(2)}) collective-permute-start(f32[512,128]{1,0:T(8,128)S(1)} %constant_dynamic-slice_fusion), channel_id=1, source_target_pairs={{0,16},{16,0},{32,48},{48,32},{64,80},{80,64},{96,112},{112,96},{1... | collective-permute-start | bytes 786440 | tf_op jit(solution)/shard_map/ppermute | solution.py:282
  78.3 1.1 collective-permute-done.12
  79.5 11.9 %all_to_all.15 = f32[4,128,128]{2,1,0:T(8,128)S(1)} all-to-all(f32[4,128,128]{2,1,0:T(8,128)S(1)} %bitcast.12), channel_id=1, replica_groups={{0,32,64,96},{16,48,80,112},{128,160,192,224},{144,176,208,240},{256,28..., dimensions={0} | all-to-all | bytes 524288 | tf_op jit(solution)/shard_map/all_to_all | solution.py:283
  91.4 0.6 reduce_sum.18
  92.0 0.9 broadcast_in_dim.4
  92.9 26.9 %all_to_all.16 = f32[4,128,128]{2,1,0:T(8,128)S(1)} all-to-all(f32[4,128,128]{2,1,0:T(8,128)S(1)} %broadcast_in_dim.4), channel_id=1, replica_groups={{0,128,256,384},{16,144,272,400},{32,160,288,416},{48,176,304,432},{64,..., dimensions={0} | all-to-all | bytes 524288 | tf_op jit(solution)/shard_map/all_to_all | solution.py:285
  119.7 0.6 reduce_sum.19
  120.4 0.9 broadcast_in_dim.5
  121.2 12.6 %all_to_all.17 = f32[4,128,128]{2,1,0:T(8,128)S(1)} all-to-all(f32[4,128,128]{2,1,0:T(8,128)S(1)} %broadcast_in_dim.5), channel_id=1, replica_groups={{0,32,64,96},{16,48,80,112},{128,160,192,224},{144,176,208,240},{256,28..., dimensions={0} | all-to-all | bytes 524288 | tf_op jit(solution)/shard_map/all_to_all | solution.py:289
  133.8 7.1 %collective-permute-start.13 = (f32[512,128]{1,0:T(8,128)S(1)}, f32[512,128]{1,0:T(8,128)}, u32[]{:S(2)}, u32[]{:S(2)}) collective-permute-start(f32[512,128]{1,0:T(8,128)S(1)} %bitcast.10), channel_id=1, source_target_pairs={{0,16},{16,0},{32,48},{48,32},{64,80},{80,64},{96,112},{112,96},{1... | collective-permute-start | bytes 786440 | tf_op jit(solution)/shard_map/ppermute | solution.py:293
  140.9 0.1 pad_add_fusion.place_ref
  141.0 1.0 collective-permute-done.13.other_ref
  142.0 1.0 copy-done.8
  143.0 1.0 copy-done.10
  144.1 1.0 copy-done.12
  145.1 1.0 copy-done.14
  146.1 1.0 copy-done.16
  147.1 1.0 copy-done.20
  148.1 1.0 copy-done.22
  149.1 1.0 copy-done.24
  150.0 1.0 copy-done.26
  151.0 1.0 copy-done.28
  152.0 1.0 copy-done.30
  152.9 1.0 copy-done.32
  153.9 0.9 copy-done.33
  154.9 0.9 copy-done.34
  155.8 10.5 %shard_map.60 = f32[3072,128]{1,0:T(8,128)} custom-call(s32[2]{0:T(128)S(1)} %pad_add_fusion.place_ref, f32[512,128]{1,0:T(8,128)S(1)} %bitcast.11, f32[512,128]{1,0:T(8,128)} %collective-permute-done.13.other_ref, f32[256,256]{1,0:T(8,128)S(1)} %copy-done.33, f32[256,256]{1,0:T(8,128)S(1)} %copy-done.34, f32[3072,128]{1,0:T(8,128)S(1)} %copy-done, ...), custom_call_target="tpu_custom_call" | custom-call | tf_op jit(solution)/shard_map/pallas_call | solution.py:228
  (64 shorter events, 0.4 us)
Async XLA Ops:
  1.1 7.2 %collective-permute-start = (f32[2,16,1536]{2,1,0:T(8,128)S(1)}, f32[2,16,1536]{2,1,0:T(8,128)S(1)}, u32[]{:S(2)}, u32[]{:S(2)}) collective-permute-start(f32[2,16,1536]{2,1,0:T(8,128)S(1)} %get-tuple-element.66), channel_id=1, source_target_pairs={{0,1},{1,0},{2,3},{3,2},{4,5},{5,4},{6,7},{7,6},{8,9},{9,8},{10,11... | collective-permute-start | bytes 589832 | tf_op jit(solution)/shard_map/ppermute | solution.py:41
  5.0 9.0 %collective-permute-start.4 = (f32[2,16,1536]{2,1,0:T(8,128)S(1)}, f32[2,16,1536]{2,1,0:T(8,128)S(1)}, u32[]{:S(2)}, u32[]{:S(2)}) collective-permute-start(f32[2,16,1536]{2,1,0:T(8,128)S(1)} %get-tuple-element.65), channel_id=1, source_target_pairs={{0,4},{1,5},{2,6},{3,7},{4,0},{5,1},{6,2},{7,3},{8,12},{9,13},{10,... | collective-permute-start | bytes 589832 | tf_op jit(solution)/shard_map/ppermute | solution.py:41
  8.3 10.9 %collective-permute-start.1 = (f32[2,32,1536]{2,1,0:T(8,128)S(1)}, f32[2,32,1536]{2,1,0:T(8,128)S(1)}, u32[]{:S(2)}, u32[]{:S(2)}) collective-permute-start(f32[2,32,1536]{2,1,0:T(8,128)S(1)} %pad_maximum_fusion.7), channel_id=1, source_target_pairs={{0,3},{1,2},{2,1},{3,0},{4,7},{5,6},{6,5},{7,4},{8,11},{9,10},{10,... | collective-permute-start | bytes 1179656 | tf_op jit(solution)/shard_map/ppermute | solution.py:41
  14.1 11.2 %collective-permute-start.5 = (f32[2,32,1536]{2,1,0:T(8,128)S(1)}, f32[2,32,1536]{2,1,0:T(8,128)S(1)}, u32[]{:S(2)}, u32[]{:S(2)}) collective-permute-start(f32[2,32,1536]{2,1,0:T(8,128)S(1)} %pad_maximum_fusion.8), channel_id=1, source_target_pairs={{0,12},{1,13},{2,14},{3,15},{4,8},{5,9},{6,10},{7,11},{8,4},{9,5},... | collective-permute-start | bytes 1179656 | tf_op jit(solution)/shard_map/ppermute | solution.py:41
  19.3 16.4 %collective-permute-start.2 = (f32[2,64,896]{2,1,0:T(8,128)S(1)}, f32[2,64,896]{2,1,0:T(8,128)S(1)}, u32[]{:S(2)}, u32[]{:S(2)}) collective-permute-start(f32[2,64,896]{2,1,0:T(8,128)S(1)} %slice.25), channel_id=1, source_target_pairs={{0,4},{1,5},{2,6},{3,7},{4,0},{5,1},{6,2},{7,3},{8,12},{9,13},{10,... | collective-permute-start | bytes 1376264 | tf_op jit(solution)/shard_map/ppermute | solution.py:41
  25.4 12.8 %collective-permute-start.6 = (f32[2,64,896]{2,1,0:T(8,128)S(1)}, f32[2,64,896]{2,1,0:T(8,128)S(1)}, u32[]{:S(2)}, u32[]{:S(2)}) collective-permute-start(f32[2,64,896]{2,1,0:T(8,128)S(1)} %slice.27), channel_id=1, source_target_pairs={{0,1},{1,0},{2,3},{3,2},{4,5},{5,4},{6,7},{7,6},{8,9},{9,8},{10,11... | collective-permute-start | bytes 1376264 | tf_op jit(solution)/shard_map/ppermute | solution.py:41
  27.3 15.3 %collective-permute-start.3 = (f32[2,64,640]{2,1,0:T(8,128)S(1)}, f32[2,64,640]{2,1,0:T(8,128)S(1)}, u32[]{:S(2)}, u32[]{:S(2)}) collective-permute-start(f32[2,64,640]{2,1,0:T(8,128)S(1)} %pad_maximum_fusion.10), channel_id=1, source_target_pairs={{0,12},{1,13},{2,14},{3,15},{4,8},{5,9},{6,10},{7,11},{8,4},{9,5},... | collective-permute-start | bytes 983048 | tf_op jit(solution)/shard_map/ppermute | solution.py:41
  32.7 12.8 %collective-permute-start.7 = (f32[2,64,640]{2,1,0:T(8,128)S(1)}, f32[2,64,640]{2,1,0:T(8,128)S(1)}, u32[]{:S(2)}, u32[]{:S(2)}) collective-permute-start(f32[2,64,640]{2,1,0:T(8,128)S(1)} %pad_maximum_fusion.9), channel_id=1, source_target_pairs={{0,3},{1,2},{2,1},{3,0},{4,7},{5,6},{6,5},{7,4},{8,11},{9,10},{10,... | collective-permute-start | bytes 983048 | tf_op jit(solution)/shard_map/ppermute | solution.py:41
  35.7 22.8 %collective-permute-start.8 = (f32[2,128,896]{2,1,0:T(8,128)S(1)}, f32[2,128,896]{2,1,0:T(8,128)}, u32[]{:S(2)}, u32[]{:S(2)}) collective-permute-start(f32[2,128,896]{2,1,0:T(8,128)S(1)} %pad_maximum_fusion.refs_0_), channel_id=1, source_target_pairs={{0,12},{1,13},{2,14},{3,15},{4,8},{5,9},{6,10},{7,11},{8,4},{9,5},... | collective-permute-start | bytes 2752520 | tf_op jit(solution)/shard_map/ppermute | solution.py:41
  38.3 10.0 %copy-start = (f32[3072,128]{1,0:T(8,128)S(1)}, f32[3072,128]{1,0:T(8,128)}, u32[]{:S(2)}) copy-start(f32[3072,128]{1,0:T(8,128)} %z_ref.3) | copy-start | bytes 4718596
  38.3 26.9 %collective-permute-start.10 = (f32[2,128,896]{2,1,0:T(8,128)S(1)}, f32[2,128,896]{2,1,0:T(8,128)}, u32[]{:S(2)}, u32[]{:S(2)}) collective-permute-start(f32[2,128,896]{2,1,0:T(8,128)S(1)} %pad_maximum_fusion.1.refs_2_), channel_id=1, source_target_pairs={{0,3},{1,2},{2,1},{3,0},{4,7},{5,6},{6,5},{7,4},{8,11},{9,10},{10,... | collective-permute-start | bytes 2752520 | tf_op jit(solution)/shard_map/ppermute | solution.py:41
  43.5 17.8 %collective-permute-start.9 = (f32[2,128,640]{2,1,0:T(8,128)}, f32[2,128,640]{2,1,0:T(8,128)}, u32[]{:S(2)}, u32[]{:S(2)}) collective-permute-start(f32[2,128,640]{2,1,0:T(8,128)} %pad_maximum_fusion.4.refs_1_), channel_id=1, source_target_pairs={{0,4},{1,5},{2,6},{3,7},{4,0},{5,1},{6,2},{7,3},{8,12},{9,13},{10,... | collective-permute-start | bytes 1966088 | tf_op jit(solution)/shard_map/ppermute | solution.py:41
  46.4 22.3 %collective-permute-start.11 = (f32[2,128,640]{2,1,0:T(8,128)}, f32[2,128,640]{2,1,0:T(8,128)}, u32[]{:S(2)}, u32[]{:S(2)}) collective-permute-start(f32[2,128,640]{2,1,0:T(8,128)} %pad_maximum_fusion.5.refs_3_), channel_id=1, source_target_pairs={{0,1},{1,0},{2,3},{3,2},{4,5},{5,4},{6,7},{7,6},{8,9},{9,8},{10,11... | collective-permute-start | bytes 1966088 | tf_op jit(solution)/shard_map/ppermute | solution.py:41
  53.8 0.7 copy-start.23
  54.5 6.7 %copy-start.1 = (bf16[256,896]{1,0:T(8,128)(2,1)}, bf16[256,896]{1,0:T(8,128)(2,1)S(1)}, u32[]{:S(2)}) copy-start(bf16[256,896]{1,0:T(8,128)(2,1)S(1)} %get-tuple-element.49.refs_0_) | copy-start | bytes 1376260
  54.5 6.7 %copy-start.3 = (bf16[256,896]{1,0:T(8,128)(2,1)}, bf16[256,896]{1,0:T(8,128)(2,1)S(1)}, u32[]{:S(2)}) copy-start(bf16[256,896]{1,0:T(8,128)(2,1)S(1)} %get-tuple-element.50.refs_1_) | copy-start | bytes 1376260
  54.5 6.7 %copy-start.5 = (bf16[256,896]{1,0:T(8,128)(2,1)}, bf16[256,896]{1,0:T(8,128)(2,1)S(1)}, u32[]{:S(2)}) copy-start(bf16[256,896]{1,0:T(8,128)(2,1)S(1)} %get-tuple-element.57.refs_8_) | copy-start | bytes 1376260
  54.5 6.7 %copy-start.7 = (bf16[256,896]{1,0:T(8,128)(2,1)}, bf16[256,896]{1,0:T(8,128)(2,1)S(1)}, u32[]{:S(2)}) copy-start(bf16[256,896]{1,0:T(8,128)(2,1)S(1)} %get-tuple-element.58.refs_9_) | copy-start | bytes 1376260
  54.5 6.7 %copy-start.17 = (bf16[256,640]{1,0:T(8,128)(2,1)}, bf16[256,640]{1,0:T(8,128)(2,1)S(1)}, u32[]{:S(2)}) copy-start(bf16[256,640]{1,0:T(8,128)(2,1)S(1)} %get-tuple-element.53.refs_4_) | copy-start | bytes 983044
  54.5 6.7 %copy-start.19 = (bf16[256,640]{1,0:T(8,128)(2,1)}, bf16[256,640]{1,0:T(8,128)(2,1)S(1)}, u32[]{:S(2)}) copy-start(bf16[256,640]{1,0:T(8,128)(2,1)S(1)} %get-tuple-element.54.refs_5_) | copy-start | bytes 983044
  54.6 6.7 %copy-start.21 = (bf16[256,640]{1,0:T(8,128)(2,1)}, bf16[256,640]{1,0:T(8,128)(2,1)S(1)}, u32[]{:S(2)}) copy-start(bf16[256,640]{1,0:T(8,128)(2,1)S(1)} %get-tuple-element.61.refs_12_) | copy-start | bytes 983044
  61.3 2.4 %copy-start.9 = (bf16[256,896]{1,0:T(8,128)(2,1)}, bf16[256,896]{1,0:T(8,128)(2,1)S(1)}, u32[]{:S(2)}) copy-start(bf16[256,896]{1,0:T(8,128)(2,1)S(1)} %get-tuple-element.51.refs_2_) | copy-start | bytes 1376260
  61.3 2.4 %copy-start.11 = (bf16[256,896]{1,0:T(8,128)(2,1)}, bf16[256,896]{1,0:T(8,128)(2,1)S(1)}, u32[]{:S(2)}) copy-start(bf16[256,896]{1,0:T(8,128)(2,1)S(1)} %get-tuple-element.52.refs_3_) | copy-start | bytes 1376260
  63.8 0.7 copy-start.25
  64.5 0.7 copy-start.27
  67.9 0.8 copy-start.13
  68.7 2.2 %copy-start.15 = (bf16[256,896]{1,0:T(8,128)(2,1)}, bf16[256,896]{1,0:T(8,128)(2,1)S(1)}, u32[]{:S(2)}) copy-start(bf16[256,896]{1,0:T(8,128)(2,1)S(1)} %get-tuple-element.60.refs_11_) | copy-start | bytes 1376260
  71.0 0.7 copy-start.29
  71.7 0.7 copy-start.31
  72.5 6.9 %collective-permute-start.12 = (f32[512,128]{1,0:T(8,128)S(1)}, f32[512,128]{1,0:T(8,128)S(1)}, u32[]{:S(2)}, u32[]{:S(2)}) collective-permute-start(f32[512,128]{1,0:T(8,128)S(1)} %constant_dynamic-slice_fusion), channel_id=1, source_target_pairs={{0,16},{16,0},{32,48},{48,32},{64,80},{80,64},{96,112},{112,96},{1... | collective-permute-start | bytes 786440 | tf_op jit(solution)/shard_map/ppermute | solution.py:282
  79.4 62.6 %copy-start.2 = (bf16[256,896]{1,0:T(8,128)(2,1)S(1)}, bf16[256,896]{1,0:T(8,128)(2,1)}, u32[]{:S(2)}) copy-start(bf16[256,896]{1,0:T(8,128)(2,1)} %copy-done.1) | copy-start | bytes 1376260
  79.4 62.6 %copy-start.4 = (bf16[256,896]{1,0:T(8,128)(2,1)S(1)}, bf16[256,896]{1,0:T(8,128)(2,1)}, u32[]{:S(2)}) copy-start(bf16[256,896]{1,0:T(8,128)(2,1)} %copy-done.3) | copy-start | bytes 1376260
  79.4 62.6 %copy-start.6 = (bf16[256,896]{1,0:T(8,128)(2,1)S(1)}, bf16[256,896]{1,0:T(8,128)(2,1)}, u32[]{:S(2)}) copy-start(bf16[256,896]{1,0:T(8,128)(2,1)} %copy-done.5) | copy-start | bytes 1376260
  79.5 62.5 %copy-start.18 = (bf16[256,640]{1,0:T(8,128)(2,1)S(1)}, bf16[256,640]{1,0:T(8,128)(2,1)}, u32[]{:S(2)}) copy-start(bf16[256,640]{1,0:T(8,128)(2,1)} %copy-done.17) | copy-start | bytes 983044
  133.8 8.2 %collective-permute-start.13 = (f32[512,128]{1,0:T(8,128)S(1)}, f32[512,128]{1,0:T(8,128)}, u32[]{:S(2)}, u32[]{:S(2)}) collective-permute-start(f32[512,128]{1,0:T(8,128)S(1)} %bitcast.10), channel_id=1, source_target_pairs={{0,16},{16,0},{32,48},{48,32},{64,80},{80,64},{96,112},{112,96},{1... | collective-permute-start | bytes 786440 | tf_op jit(solution)/shard_map/ppermute | solution.py:293
  142.0 1.0 copy-start.8
  143.0 1.0 copy-start.10
  144.0 1.0 copy-start.12
  145.1 1.0 copy-start.14
  146.1 1.0 copy-start.16
  147.1 1.0 copy-start.20
  148.1 1.0 copy-start.22
  149.1 1.0 copy-start.24
  150.0 1.0 copy-start.26
  151.0 1.0 copy-start.28
  152.0 1.0 copy-start.30
  152.9 1.0 copy-start.32
  153.9 0.9 copy-start.33
  154.9 0.9 copy-start.34

commit v5 on v4

--- a/solution.py
+++ b/solution.py
@@ -17,7 +17,7 @@
 FAR = 4
 EARLY_VMEM = 24 << 20
 LATE_VMEM = 16 << 20
-APPLY_VMEM = 24 << 20
+APPLY_VMEM = 56 << 20
 
 
 def dot(left, right):
@@ -72,10 +72,17 @@
     return wide[:, :m] + (wide[:, m:] + dot(low, z_both[:, :m]))
 
 
+def keep(half, kept, place, base, sem):
+    rows, n = half.shape
+    copy = pltpu.make_async_copy(half, kept.at[pl.ds(place * rows, rows), pl.ds(base, n)], sem)
+    copy.start()
+    return copy
+
+
 def early_kernel(all_masks, width, bases, k, z_ref, *refs):
     count = len(bases)
     halves, acc_ref, zb_ref, out = refs[:count], refs[count], refs[count + 1], refs[count + 2 : 3 * count + 2]
-    kept, sems = refs[3 * count + 2 : -1], refs[-1]
+    kept, sems = refs[3 * count + 2 :]
     m = z_ref.shape[1]
     copies = []
     acc_ref[...] = jnp.zeros_like(acc_ref)
@@ -85,9 +92,8 @@
         zb_ref[base : base + n, :m] = z_h
         zb_ref[base : base + n, m:] = z_l
         split_half(halves[p], out[2 * p], out[2 * p + 1])
-        for i in (2 * p, 2 * p + 1):
-            copies.append(pltpu.make_async_copy(out[i], kept[i], sems.at[i]))
-            copies[-1].start()
+        for i in range(2):
+            copies.append(keep(out[2 * p + i], kept, 2 * i, base, sems.at[2 * p + i]))
         part = half_coeffs(out[2 * p][...], out[2 * p + 1][...], zb_ref[base : base + n, :])
         for place, rows in scatter_rows(part, all_masks[p][0], k, width):
             acc_ref[place : place + width, :] += rows
@@ -104,8 +110,8 @@
     return [pl.BlockSpec(memory_space=pltpu.VMEM)] * count
 
 
-def hbm_specs(count):
-    return [pl.BlockSpec(memory_space=pltpu.HBM)] * count
+def any_specs(count):
+    return [pl.BlockSpec(memory_space=pl.ANY)] * count
 
 
 def early(z, halves, all_masks, bases, k, width):
@@ -115,24 +121,22 @@
     count = len(split_halves)
     out = pl.pallas_call(
         functools.partial(early_kernel, all_masks, width, bases, k),
-        out_shape=shapes + split_halves + split_halves,
+        out_shape=shapes + split_halves + [jax.ShapeDtypeStruct((4 * k, n), BF16)],
         in_specs=vmem_specs(1 + len(halves)),
-        out_specs=vmem_specs(2 + count) + hbm_specs(count),
+        out_specs=vmem_specs(2 + count) + any_specs(1),
         scratch_shapes=[pltpu.SemaphoreType.DMA((count,))],
         compiler_params=pltpu.CompilerParams(vmem_limit_bytes=EARLY_VMEM),
         cost_estimate=pl.CostEstimate(flops=6 * k * n * m, bytes_accessed=12 << 20, transcendentals=0),
     )(z, *halves)
-    return out[0], out[1], out[2 : 2 + count], out[2 + count :]
-
-
-def late_kernel(masks, width, base, k, first, acc_ref, got_ref, first_h, first_l, zb_ref, out_ref, *refs):
-    kept, (got_h, got_l, sems) = refs[:2], refs[2:]
+    return out[0], out[1], out[2 : 2 + count], out[2 + count]
+
+
+def late_kernel(masks, width, base, k, first, acc_ref, got_ref, first_h, first_l, zb_ref, _, *refs):
+    out_ref, kept, got_h, got_l, sems = refs
     n = got_ref.shape[2]
     m = zb_ref.shape[1] // 2
     split_half(got_ref, got_h, got_l)
-    copies = [pltpu.make_async_copy(half, kept[i], sems.at[i]) for i, half in enumerate((got_h, got_l))]
-    for copy in copies:
-        copy.start()
+    copies = [keep(half, kept, 2 * i + 1, base, sems.at[i]) for i, half in enumerate((got_h, got_l))]
     part = half_coeffs(got_h[...], got_l[...], zb_ref[base : base + n, :])
     added = {place: rows for place, rows in scatter_rows(part, masks[1], k, width)}
     for place in range(0, 2 * k, width):
@@ -151,35 +155,32 @@
         copy.wait()
 
 
-def late(acc, got, firsts, zb, masks, base, first, k, width):
+def late(acc, got, firsts, zb, kept, masks, base, first, k, width):
     m = zb.shape[1] // 2
     split_got = split_shapes(got)
     return pl.pallas_call(
         functools.partial(late_kernel, masks, width, base, k, first),
-        out_shape=[jax.ShapeDtypeStruct((2 * k + k * k // m, m), F32)] + split_got,
-        in_specs=vmem_specs(5),
-        out_specs=vmem_specs(1) + hbm_specs(2),
+        out_shape=[jax.ShapeDtypeStruct((2 * k + k * k // m, m), F32), jax.ShapeDtypeStruct(kept.shape, BF16)],
+        in_specs=vmem_specs(5) + any_specs(1),
+        out_specs=vmem_specs(1) + any_specs(1),
+        input_output_aliases={5: 1},
         scratch_shapes=[pltpu.VMEM(shape.shape, BF16) for shape in split_got] + [pltpu.SemaphoreType.DMA((2,))],
         compiler_params=pltpu.CompilerParams(vmem_limit_bytes=LATE_VMEM),
-    )(acc, got, *firsts, zb)
-
-
-def apply_kernel(all_masks, width, bases, place_ref, mine_ref, other_ref, t_one_ref, t_two_ref, z_ref, *refs):
-    count = 4 * len(bases)
-    halves, out_ref, held = refs[:count], refs[count], refs[count + 1 : 2 * count + 1]
-    z_held, out_held, total_ref, true_ref, slot_ref, sems, z_sems, out_sems = refs[2 * count + 1 :]
+    )(acc, got, *firsts, zb, kept)
+
+
+def apply_kernel(all_masks, width, bases, place_ref, mine_ref, other_ref, t_one_ref, t_two_ref, z_ref, kept_ref, *refs):
+    out_ref, held, z_held, out_held, total_ref, true_ref, slot_ref, sems, z_sems, out_sems = refs
     k = t_one_ref.shape[0]
     m = z_ref.shape[1]
     blocks = k // width
     ends = bases[1:] + [z_ref.shape[0]]
-    loads = [pltpu.make_async_copy(half, held[i], sems.at[i]) for i, half in enumerate(halves)]
-    z_loads = []
+    loads, z_loads = [], []
     for p, (base, end) in enumerate(zip(bases, ends)):
-        rows = pl.ds(base, end - base)
+        rows, lanes = pl.ds(base, end - base), (slice(None), pl.ds(base, end - base))
+        loads.append(pltpu.make_async_copy(kept_ref.at[lanes], held.at[lanes], sems.at[p]))
         z_loads.append(pltpu.make_async_copy(z_ref.at[rows, :], z_held.at[rows, :], z_sems.at[p]))
-    for p in range(len(bases)):
-        for i in range(4 * p, 4 * p + 4):
-            loads[i].start()
+        loads[p].start()
         z_loads[p].start()
     col, core = place_ref[0], place_ref[1]
     half = mine_ref.shape[0]
@@ -206,9 +207,9 @@
     x_both = jnp.concatenate([x_h, x_l], 0)
     stores = []
     for p, (base, end, masks) in enumerate(zip(bases, ends, all_masks)):
-        for load in loads[4 * p : 4 * p + 4] + [z_loads[p]]:
-            load.wait()
-        first_h, first_l, got_h, got_l = held[4 * p : 4 * p + 4]
+        loads[p].wait()
+        z_loads[p].wait()
+        first_h, got_h, first_l, got_l = [held.at[pl.ds(i * k, k), pl.ds(base, end - base)] for i in range(4)]
         high = jnp.concatenate([in_order((first_h, got_h), masks, w, width) for w in range(2)], 0)
         low = jnp.concatenate([in_order((first_l, got_l), masks, w, width) for w in range(2)], 0)
         wide = dot(x_both, high)
@@ -221,20 +222,19 @@
         store.wait()
 
 
-def apply(place, mine, other, t_one, t_two, z, halves, all_masks, bases, width):
+def apply(place, mine, other, t_one, t_two, z, kept, all_masks, bases, width):
     k, m = t_one.shape[0], z.shape[1]
     rows = pltpu.VMEM(z.shape, F32)
     dma = pltpu.SemaphoreType.DMA
     return pl.pallas_call(
         functools.partial(apply_kernel, all_masks, width, bases),
         out_shape=jax.ShapeDtypeStruct(z.shape, F32),
-        in_specs=[pl.BlockSpec(memory_space=pltpu.SMEM)] + vmem_specs(4) + hbm_specs(1 + len(halves)),
-        out_specs=pl.BlockSpec(memory_space=pltpu.HBM),
-        scratch_shapes=[pltpu.VMEM(half.shape, BF16) for half in halves]
-        + [rows, rows, pltpu.VMEM((2 * mine.shape[0], m), F32), pltpu.VMEM((k, m), F32), pltpu.VMEM((2 * k, m), F32)]
-        + [dma((len(halves),)), dma((len(bases),)), dma((len(bases),))],
+        in_specs=[pl.BlockSpec(memory_space=pltpu.SMEM)] + vmem_specs(4) + any_specs(2),
+        out_specs=pl.BlockSpec(memory_space=pl.ANY),
+        scratch_shapes=[pltpu.VMEM(kept.shape, BF16), rows, rows, pltpu.VMEM((2 * mine.shape[0], m), F32), pltpu.VMEM((k, m), F32), pltpu.VMEM((2 * k, m), F32)]
+        + [dma((len(bases),))] * 3,
         compiler_params=pltpu.CompilerParams(vmem_limit_bytes=APPLY_VMEM),
-    )(place, mine, other, t_one, t_two, z, *halves)
+    )(place, mine, other, t_one, t_two, z, kept)
 
 
 def gather_pieces(own, size):
@@ -300,14 +300,12 @@
     pieces, masks, cuts = gather_pieces(own, size)
     bases = cuts[:-1]
     part, z_both, firsts, kept = early(z_slab, [piece[0] for piece in pieces], masks, bases, k, width)
-    halves = []
     for p, base in enumerate(bases):
         two = slice(2 * p, 2 * p + 2)
-        part, *got = late(part, pieces[p][1], firsts[two], z_both, masks[p], base, p == 0, k, width)
-        halves += [*kept[two], *got]
+        part, kept = late(part, pieces[p][1], firsts[two], z_both, kept, masks[p], base, p == 0, k, width)
     mine, other, core = sum_over_row(part)
     place = jnp.stack([lax.axis_index("col"), core]).astype(jnp.int32)
-    return apply(place, mine, other, t_first, t_second, z_slab, halves, masks, bases, width)
+    return apply(place, mine, other, t_first, t_second, z_slab, kept, masks, bases, width)
 
 
 def solution(mesh):

time: 168 us -> 146 us (0.87)
  local copies, waits for them, and re-layouts: 20 us -> 3.53 us
  Pallas kernels: 26.1 us -> 21.3 us
    unnamed x70 -> x8, local copies, waits for them, and re-layouts: 18.2 us -> 3.37 us
    pallas_call x1, Pallas kernels: 10.5 us -> 8.5 us  [apply(): pl.pallas_call(functools.partial(apply_kernel, all_masks, width, bases),...]
    ppermute x12, waiting for transfers between devices: 5.55 us -> 7.34 us  [swap(): return lax.ppermute(x, 'col', [(i, i ^ mask) for i in range(size)])]
  transfers between devices with their start and end apart: 14 -> 14, of which waited for: 5 -> 5; matrix products, arithmetic and copies ran while one was open for 1% -> 2% of each run, Pallas kernels for 8% -> 7%
where the time goes in v5:
time: 146 us; the launch traced here: 145 us
  starting transfers between devices  56.2 us (38%)
  blocking collectives  51.2 us (35%)
  Pallas kernels  21.3 us (15%)
  waiting for transfers between devices  8.76 us (6%)
  other arithmetic  3.88 us (3%)
  local copies, waits for them, and re-layouts  3.53 us (2%)
    ppermute x12, starting transfers between devices, swap(): return lax.ppermute(x, 'col', [(i, i ^ mask) for i in range(size)])  43.3 us
    all_to_all x1, blocking collectives, sum_over_row(): lax.all_to_all(jnp.broadcast_to(mine[None], (FAR,) + mine.shape), 'row',...  26.9 us
    all_to_all x1, blocking collectives, sum_over_row(): lax.all_to_all(jnp.broadcast_to(mine[None], (NEAR,) + mine.shape), 'row',...  12.6 us
    all_to_all x1, blocking collectives, sum_over_row(): lax.all_to_all(mine.reshape(NEAR, half // NEAR, m), 'row', 0, 0, axis_ind...  11.8 us
    pallas_call x1, Pallas kernels, apply(): pl.pallas_call(functools.partial(apply_kernel, all_masks, width, bases),...  8.5 us
    pallas_call x4, Pallas kernels, late(): pl.pallas_call(functools.partial(late_kernel, masks, width, base, k, firs...  8.49 us
    ppermute x12, waiting for transfers between devices, swap(): return lax.ppermute(x, 'col', [(i, i ^ mask) for i in range(size)])  7.34 us
    ppermute x1, starting transfers between devices, sum_over_row(): return (mine, lax.ppermute(mine, 'row', pair), core)  7.11 us
  transfers between devices with their start and end apart: 14, of which 5 were waited for; matrix products, arithmetic and copies ran while one was open for 2% of the time, Pallas kernels for 7%

profile of v5, /device:TPU:1, one launch (start us, length us, event | category | flops | bytes accessed | tf_op | source)
XLA Modules:
  0.0 145.5 jit_solution(1053884392096116477)
XLA Ops:
  0.0 1.0 pad_maximum_fusion.6
  1.1 3.9 %collective-permute-start = (f32[2,16,1536]{2,1,0:T(8,128)S(1)}, f32[2,16,1536]{2,1,0:T(8,128)S(1)}, u32[]{:S(2)}, u32[]{:S(2)}) collective-permute-start(f32[2,16,1536]{2,1,0:T(8,128)S(1)} %get-tuple-element.44), channel_id=1, source_target_pairs={{0,1},{1,0},{2,3},{3,2},{4,5},{5,4},{6,7},{7,6},{8,9},{9,8},{10,11... | collective-permute-start | bytes 589832 | tf_op jit(solution)/shard_map/ppermute | solution.py:41
  5.0 3.2 %collective-permute-start.4 = (f32[2,16,1536]{2,1,0:T(8,128)S(1)}, f32[2,16,1536]{2,1,0:T(8,128)S(1)}, u32[]{:S(2)}, u32[]{:S(2)}) collective-permute-start(f32[2,16,1536]{2,1,0:T(8,128)S(1)} %get-tuple-element.43), channel_id=1, source_target_pairs={{0,4},{1,5},{2,6},{3,7},{4,0},{5,1},{6,2},{7,3},{8,12},{9,13},{10,... | collective-permute-start | bytes 589832 | tf_op jit(solution)/shard_map/ppermute | solution.py:41
  8.3 0.0 collective-permute-done
  8.3 5.7 %collective-permute-start.1 = (f32[2,32,1536]{2,1,0:T(8,128)S(1)}, f32[2,32,1536]{2,1,0:T(8,128)S(1)}, u32[]{:S(2)}, u32[]{:S(2)}) collective-permute-start(f32[2,32,1536]{2,1,0:T(8,128)S(1)} %pad_maximum_fusion.7), channel_id=1, source_target_pairs={{0,3},{1,2},{2,1},{3,0},{4,7},{5,6},{6,5},{7,4},{8,11},{9,10},{10,... | collective-permute-start | bytes 1179656 | tf_op jit(solution)/shard_map/ppermute | solution.py:41
  14.0 0.0 collective-permute-done.4
  14.1 4.6 %collective-permute-start.5 = (f32[2,32,1536]{2,1,0:T(8,128)S(1)}, f32[2,32,1536]{2,1,0:T(8,128)S(1)}, u32[]{:S(2)}, u32[]{:S(2)}) collective-permute-start(f32[2,32,1536]{2,1,0:T(8,128)S(1)} %pad_maximum_fusion.8), channel_id=1, source_target_pairs={{0,12},{1,13},{2,14},{3,15},{4,8},{5,9},{6,10},{7,11},{8,4},{9,5},... | collective-permute-start | bytes 1179656 | tf_op jit(solution)/shard_map/ppermute | solution.py:41
  18.7 0.5 collective-permute-done.1
  19.2 0.1 pad_maximum_fusion.2
  19.2 0.0 copy-start.1
  19.3 5.0 %collective-permute-start.2 = (f32[2,64,896]{2,1,0:T(8,128)S(1)}, f32[2,64,896]{2,1,0:T(8,128)S(1)}, u32[]{:S(2)}, u32[]{:S(2)}) collective-permute-start(f32[2,64,896]{2,1,0:T(8,128)S(1)} %slice.25), channel_id=1, source_target_pairs={{0,4},{1,5},{2,6},{3,7},{4,0},{5,1},{6,2},{7,3},{8,12},{9,13},{10,... | collective-permute-start | bytes 1376264 | tf_op jit(solution)/shard_map/ppermute | solution.py:41
  24.3 1.0 collective-permute-done.5
  25.3 0.1 pad_maximum_fusion.3
  25.4 1.9 %collective-permute-start.6 = (f32[2,64,896]{2,1,0:T(8,128)S(1)}, f32[2,64,896]{2,1,0:T(8,128)S(1)}, u32[]{:S(2)}, u32[]{:S(2)}) collective-permute-start(f32[2,64,896]{2,1,0:T(8,128)S(1)} %slice.27), channel_id=1, source_target_pairs={{0,1},{1,0},{2,3},{3,2},{4,5},{5,4},{6,7},{7,6},{8,9},{9,8},{10,11... | collective-permute-start | bytes 1376264 | tf_op jit(solution)/shard_map/ppermute | solution.py:41
  27.3 5.3 %collective-permute-start.3 = (f32[2,64,640]{2,1,0:T(8,128)S(1)}, f32[2,64,640]{2,1,0:T(8,128)S(1)}, u32[]{:S(2)}, u32[]{:S(2)}) collective-permute-start(f32[2,64,640]{2,1,0:T(8,128)S(1)} %pad_maximum_fusion.10), channel_id=1, source_target_pairs={{0,12},{1,13},{2,14},{3,15},{4,8},{5,9},{6,10},{7,11},{8,4},{9,5},... | collective-permute-start | bytes 983048 | tf_op jit(solution)/shard_map/ppermute | solution.py:41
  32.7 3.0 %collective-permute-start.7 = (f32[2,64,640]{2,1,0:T(8,128)S(1)}, f32[2,64,640]{2,1,0:T(8,128)S(1)}, u32[]{:S(2)}, u32[]{:S(2)}) collective-permute-start(f32[2,64,640]{2,1,0:T(8,128)S(1)} %pad_maximum_fusion.9), channel_id=1, source_target_pairs={{0,3},{1,2},{2,1},{3,0},{4,7},{5,6},{6,5},{7,4},{8,11},{9,10},{10,... | collective-permute-start | bytes 983048 | tf_op jit(solution)/shard_map/ppermute | solution.py:41
  35.7 0.0 collective-permute-done.2
  35.7 0.1 pad_maximum_fusion.refs_0_
  35.7 2.6 %collective-permute-start.8 = (f32[2,128,896]{2,1,0:T(8,128)S(1)}, f32[2,128,896]{2,1,0:T(8,128)}, u32[]{:S(2)}, u32[]{:S(2)}) collective-permute-start(f32[2,128,896]{2,1,0:T(8,128)S(1)} %pad_maximum_fusion.refs_0_), channel_id=1, source_target_pairs={{0,12},{1,13},{2,14},{3,15},{4,8},{5,9},{6,10},{7,11},{8,4},{9,5},... | collective-permute-start | bytes 2752520 | tf_op jit(solution)/shard_map/ppermute | solution.py:41
  38.3 0.0 collective-permute-done.6
  38.3 0.1 pad_maximum_fusion.1.refs_2_
  38.4 4.2 %collective-permute-start.10 = (f32[2,128,896]{2,1,0:T(8,128)S(1)}, f32[2,128,896]{2,1,0:T(8,128)}, u32[]{:S(2)}, u32[]{:S(2)}) collective-permute-start(f32[2,128,896]{2,1,0:T(8,128)S(1)} %pad_maximum_fusion.1.refs_2_), channel_id=1, source_target_pairs={{0,3},{1,2},{2,1},{3,0},{4,7},{5,6},{6,5},{7,4},{8,11},{9,10},{10,... | collective-permute-start | bytes 2752520 | tf_op jit(solution)/shard_map/ppermute | solution.py:41
  42.6 0.0 collective-permute-done.3
  42.7 0.9 pad_maximum_fusion.4.refs_1_
  43.5 1.9 %collective-permute-start.9 = (f32[2,128,640]{2,1,0:T(8,128)}, f32[2,128,640]{2,1,0:T(8,128)}, u32[]{:S(2)}, u32[]{:S(2)}) collective-permute-start(f32[2,128,640]{2,1,0:T(8,128)} %pad_maximum_fusion.4.refs_1_), channel_id=1, source_target_pairs={{0,4},{1,5},{2,6},{3,7},{4,0},{5,1},{6,2},{7,3},{8,12},{9,13},{10,... | collective-permute-start | bytes 1966088 | tf_op jit(solution)/shard_map/ppermute | solution.py:41
  45.5 0.0 collective-permute-done.7
  45.5 0.9 pad_maximum_fusion.5.refs_3_
  46.4 1.9 %collective-permute-start.11 = (f32[2,128,640]{2,1,0:T(8,128)}, f32[2,128,640]{2,1,0:T(8,128)}, u32[]{:S(2)}, u32[]{:S(2)}) collective-permute-start(f32[2,128,640]{2,1,0:T(8,128)} %pad_maximum_fusion.5.refs_3_), channel_id=1, source_target_pairs={{0,1},{1,0},{2,3},{3,2},{4,5},{5,4},{6,7},{7,6},{8,9},{9,8},{10,11... | collective-permute-start | bytes 1966088 | tf_op jit(solution)/shard_map/ppermute | solution.py:41
  48.3 0.0 copy-done.1
  48.3 4.3 %shard_map.55 = (f32[512,128]{1,0:T(8,128)S(1)}, bf16[3072,256]{1,0:T(8,128)(2,1)S(1)}, bf16[256,896]{1,0:T(8,128)(2,1)S(1)}, bf16[256,896]{1,0:T(8,128)(2,1)S(1...) custom-call(f32[3072,128]{1,0:T(8,128)S(1)} %copy-done.1, ...), custom_call_target="tpu_custom_call" | custom-call | flops 603979776 | bytes 12582912 | tf_op jit(solution)/shard_map/pallas_call | solution.py:122
  52.6 5.9 %collective-permute-done.8.got_ref = f32[2,128,896]{2,1,0:T(8,128)} collective-permute-done((f32[2,128,896]{2,1,0:T(8,128)S(1)}, f32[2,128,896]{2,1,0:T(8,128)}, u32[]{:S(2)}, u32[]{:S(2)}) %collective-permute-start.8) | collective-permute-done | bytes 917536 | tf_op jit(solution)/shard_map/ppermute | solution.py:41
  58.5 2.3 %shard_map.56 = (f32[1024,128]{1,0:T(8,128)S(1)}, bf16[1024,3072]{1,0:T(8,128)(2,1)S(1)}) custom-call(f32[512,128]{1,0:T(8,128)S(1)} %get-tuple-element.24.acc_ref, f32[2,128,896]{2,1,0:T(8,128)} %collective-permute-done.8.got_ref, bf16[256,896]{1,0:T(8,128)(2,1)S(1)} %get-tuple-element.25.first_h, ...), custom_call_target="tpu_custom_call", output_to_operand_aliasing={{1}: (5, {})} | custom-call | tf_op jit(solution)/shard_map/pallas_call | solution.py:161
  60.8 0.0 collective-permute-done.9.got_ref
  60.8 1.9 %shard_map.57 = (f32[1024,128]{1,0:T(8,128)S(1)}, bf16[1024,3072]{1,0:T(8,128)(2,1)S(1)}) custom-call(f32[1024,128]{1,0:T(8,128)S(1)} %get-tuple-element.29.acc_ref, f32[2,128,640]{2,1,0:T(8,128)} %collective-permute-done.9.got_ref, bf16[256,640]{1,0:T(8,128)(2,1)S(1)} %get-tuple-element.30.first_h, ...), custom_call_target="tpu_custom_call", output_to_operand_aliasing={{1}: (5, {})} | custom-call | tf_op jit(solution)/shard_map/pallas_call | solution.py:161
  62.8 0.0 collective-permute-done.10.got_ref
  62.8 2.3 %shard_map.58 = (f32[1024,128]{1,0:T(8,128)S(1)}, bf16[1024,3072]{1,0:T(8,128)(2,1)S(1)}) custom-call(f32[1024,128]{1,0:T(8,128)S(1)} %get-tuple-element.33.acc_ref, f32[2,128,896]{2,1,0:T(8,128)} %collective-permute-done.10.got_ref, bf16[256,896]{1,0:T(8,128)(2,1)S(1)} %get-tuple-element.34.first_h, ...), custom_call_target="tpu_custom_call", output_to_operand_aliasing={{1}: (5, {})} | custom-call | tf_op jit(solution)/shard_map/pallas_call | solution.py:161
  65.1 0.0 collective-permute-done.11.got_ref
  65.1 1.9 %shard_map.59 = (f32[1024,128]{1,0:T(8,128)S(1)}, bf16[1024,3072]{1,0:T(8,128)(2,1)S(1)}) custom-call(f32[1024,128]{1,0:T(8,128)S(1)} %get-tuple-element.37.acc_ref, f32[2,128,640]{2,1,0:T(8,128)} %collective-permute-done.11.got_ref, bf16[256,640]{1,0:T(8,128)(2,1)S(1)} %get-tuple-element.38.first_h, ...), custom_call_target="tpu_custom_call", output_to_operand_aliasing={{1}: (5, {})} | custom-call | tf_op jit(solution)/shard_map/pallas_call | solution.py:161
  67.1 0.0 copy-start
  67.1 2.6 %copy-done = bf16[1024,3072]{1,0:T(8,128)(2,1)} copy-done((bf16[1024,3072]{1,0:T(8,128)(2,1)}, bf16[1024,3072]{1,0:T(8,128)(2,1)S(1)}, u32[]{:S(2)}) %copy-start) | copy-done | bytes 6291480
  69.7 5.8 %collective-permute-start.12 = (f32[512,128]{1,0:T(8,128)S(1)}, f32[512,128]{1,0:T(8,128)S(1)}, u32[]{:S(2)}, u32[]{:S(2)}) collective-permute-start(f32[512,128]{1,0:T(8,128)S(1)} %constant_dynamic-slice_fusion), channel_id=1, source_target_pairs={{0,16},{16,0},{32,48},{48,32},{64,80},{80,64},{96,112},{112,96},{1... | collective-permute-start | bytes 786440 | tf_op jit(solution)/shard_map/ppermute | solution.py:282
  75.5 1.1 collective-permute-done.12
  76.7 11.8 %all_to_all.15 = f32[4,128,128]{2,1,0:T(8,128)S(1)} all-to-all(f32[4,128,128]{2,1,0:T(8,128)S(1)} %bitcast.10), channel_id=1, replica_groups={{0,32,64,96},{16,48,80,112},{128,160,192,224},{144,176,208,240},{256,28..., dimensions={0} | all-to-all | bytes 524288 | tf_op jit(solution)/shard_map/all_to_all | solution.py:283
  88.5 26.9 %all_to_all.16 = f32[4,128,128]{2,1,0:T(8,128)S(1)} all-to-all(f32[4,128,128]{2,1,0:T(8,128)S(1)} %broadcast_in_dim.4), channel_id=1, replica_groups={{0,128,256,384},{16,144,272,400},{32,160,288,416},{48,176,304,432},{64,..., dimensions={0} | all-to-all | bytes 524288 | tf_op jit(solution)/shard_map/all_to_all | solution.py:285
  115.4 12.6 %all_to_all.17 = f32[4,128,128]{2,1,0:T(8,128)S(1)} all-to-all(f32[4,128,128]{2,1,0:T(8,128)S(1)} %broadcast_in_dim.5), channel_id=1, replica_groups={{0,32,64,96},{16,48,80,112},{128,160,192,224},{144,176,208,240},{256,28..., dimensions={0} | all-to-all | bytes 524288 | tf_op jit(solution)/shard_map/all_to_all | solution.py:289
  128.0 0.0 copy-start.2
  128.0 7.1 %collective-permute-start.13 = (f32[512,128]{1,0:T(8,128)S(1)}, f32[512,128]{1,0:T(8,128)S(1)}, u32[]{:S(2)}, u32[]{:S(2)}) collective-permute-start(f32[512,128]{1,0:T(8,128)S(1)} %bitcast.11), channel_id=1, source_target_pairs={{0,16},{16,0},{32,48},{48,32},{64,80},{80,64},{96,112},{112,96},{1... | collective-permute-start | bytes 786440 | tf_op jit(solution)/shard_map/ppermute | solution.py:293
  135.1 0.7 pad_add_fusion.place_ref
  135.8 0.3 collective-permute-done.13.other_ref
  136.1 0.0 copy-start.3
  136.1 0.0 copy-done.2
  136.1 0.7 copy-done.3
  136.8 8.5 %shard_map.60 = f32[3072,128]{1,0:T(8,128)} custom-call(s32[2]{0:T(128)} %pad_add_fusion.place_ref, f32[512,128]{1,0:T(8,128)} %bitcast.12, f32[512,128]{1,0:T(8,128)} %copy-done.3, f32[256,256]{1,0:T(8,128)} %t_one_ref.1, f32[256,256]{1,0:T(8,128)} %t_two_ref.1, f32[3072,128]{1,0:T(8,128)} %z_ref.3, bf16[1024,3072]{1,0:T(8,128)(2,1)} %copy-done), custom_call_target="tpu_custom_call" | custom-call | tf_op jit(solution)/shard_map/pallas_call | solution.py:229
  (13 shorter events, 0.3 us)
Async XLA Ops:
  1.1 7.2 %collective-permute-start = (f32[2,16,1536]{2,1,0:T(8,128)S(1)}, f32[2,16,1536]{2,1,0:T(8,128)S(1)}, u32[]{:S(2)}, u32[]{:S(2)}) collective-permute-start(f32[2,16,1536]{2,1,0:T(8,128)S(1)} %get-tuple-element.44), channel_id=1, source_target_pairs={{0,1},{1,0},{2,3},{3,2},{4,5},{5,4},{6,7},{7,6},{8,9},{9,8},{10,11... | collective-permute-start | bytes 589832 | tf_op jit(solution)/shard_map/ppermute | solution.py:41
  5.0 9.0 %collective-permute-start.4 = (f32[2,16,1536]{2,1,0:T(8,128)S(1)}, f32[2,16,1536]{2,1,0:T(8,128)S(1)}, u32[]{:S(2)}, u32[]{:S(2)}) collective-permute-start(f32[2,16,1536]{2,1,0:T(8,128)S(1)} %get-tuple-element.43), channel_id=1, source_target_pairs={{0,4},{1,5},{2,6},{3,7},{4,0},{5,1},{6,2},{7,3},{8,12},{9,13},{10,... | collective-permute-start | bytes 589832 | tf_op jit(solution)/shard_map/ppermute | solution.py:41
  8.3 10.9 %collective-permute-start.1 = (f32[2,32,1536]{2,1,0:T(8,128)S(1)}, f32[2,32,1536]{2,1,0:T(8,128)S(1)}, u32[]{:S(2)}, u32[]{:S(2)}) collective-permute-start(f32[2,32,1536]{2,1,0:T(8,128)S(1)} %pad_maximum_fusion.7), channel_id=1, source_target_pairs={{0,3},{1,2},{2,1},{3,0},{4,7},{5,6},{6,5},{7,4},{8,11},{9,10},{10,... | collective-permute-start | bytes 1179656 | tf_op jit(solution)/shard_map/ppermute | solution.py:41
  14.1 11.2 %collective-permute-start.5 = (f32[2,32,1536]{2,1,0:T(8,128)S(1)}, f32[2,32,1536]{2,1,0:T(8,128)S(1)}, u32[]{:S(2)}, u32[]{:S(2)}) collective-permute-start(f32[2,32,1536]{2,1,0:T(8,128)S(1)} %pad_maximum_fusion.8), channel_id=1, source_target_pairs={{0,12},{1,13},{2,14},{3,15},{4,8},{5,9},{6,10},{7,11},{8,4},{9,5},... | collective-permute-start | bytes 1179656 | tf_op jit(solution)/shard_map/ppermute | solution.py:41
  19.2 29.1 %copy-start.1 = (f32[3072,128]{1,0:T(8,128)S(1)}, f32[3072,128]{1,0:T(8,128)}, u32[]{:S(2)}) copy-start(f32[3072,128]{1,0:T(8,128)} %z_ref.3) | copy-start | bytes 4718596
  19.3 16.4 %collective-permute-start.2 = (f32[2,64,896]{2,1,0:T(8,128)S(1)}, f32[2,64,896]{2,1,0:T(8,128)S(1)}, u32[]{:S(2)}, u32[]{:S(2)}) collective-permute-start(f32[2,64,896]{2,1,0:T(8,128)S(1)} %slice.25), channel_id=1, source_target_pairs={{0,4},{1,5},{2,6},{3,7},{4,0},{5,1},{6,2},{7,3},{8,12},{9,13},{10,... | collective-permute-start | bytes 1376264 | tf_op jit(solution)/shard_map/ppermute | solution.py:41
  25.4 13.0 %collective-permute-start.6 = (f32[2,64,896]{2,1,0:T(8,128)S(1)}, f32[2,64,896]{2,1,0:T(8,128)S(1)}, u32[]{:S(2)}, u32[]{:S(2)}) collective-permute-start(f32[2,64,896]{2,1,0:T(8,128)S(1)} %slice.27), channel_id=1, source_target_pairs={{0,1},{1,0},{2,3},{3,2},{4,5},{5,4},{6,7},{7,6},{8,9},{9,8},{10,11... | collective-permute-start | bytes 1376264 | tf_op jit(solution)/shard_map/ppermute | solution.py:41
  27.3 15.3 %collective-permute-start.3 = (f32[2,64,640]{2,1,0:T(8,128)S(1)}, f32[2,64,640]{2,1,0:T(8,128)S(1)}, u32[]{:S(2)}, u32[]{:S(2)}) collective-permute-start(f32[2,64,640]{2,1,0:T(8,128)S(1)} %pad_maximum_fusion.10), channel_id=1, source_target_pairs={{0,12},{1,13},{2,14},{3,15},{4,8},{5,9},{6,10},{7,11},{8,4},{9,5},... | collective-permute-start | bytes 983048 | tf_op jit(solution)/shard_map/ppermute | solution.py:41
  32.7 12.8 %collective-permute-start.7 = (f32[2,64,640]{2,1,0:T(8,128)S(1)}, f32[2,64,640]{2,1,0:T(8,128)S(1)}, u32[]{:S(2)}, u32[]{:S(2)}) collective-permute-start(f32[2,64,640]{2,1,0:T(8,128)S(1)} %pad_maximum_fusion.9), channel_id=1, source_target_pairs={{0,3},{1,2},{2,1},{3,0},{4,7},{5,6},{6,5},{7,4},{8,11},{9,10},{10,... | collective-permute-start | bytes 983048 | tf_op jit(solution)/shard_map/ppermute | solution.py:41
  35.7 22.8 %collective-permute-start.8 = (f32[2,128,896]{2,1,0:T(8,128)S(1)}, f32[2,128,896]{2,1,0:T(8,128)}, u32[]{:S(2)}, u32[]{:S(2)}) collective-permute-start(f32[2,128,896]{2,1,0:T(8,128)S(1)} %pad_maximum_fusion.refs_0_), channel_id=1, source_target_pairs={{0,12},{1,13},{2,14},{3,15},{4,8},{5,9},{6,10},{7,11},{8,4},{9,5},... | collective-permute-start | bytes 2752520 | tf_op jit(solution)/shard_map/ppermute | solution.py:41
  38.4 24.4 %collective-permute-start.10 = (f32[2,128,896]{2,1,0:T(8,128)S(1)}, f32[2,128,896]{2,1,0:T(8,128)}, u32[]{:S(2)}, u32[]{:S(2)}) collective-permute-start(f32[2,128,896]{2,1,0:T(8,128)S(1)} %pad_maximum_fusion.1.refs_2_), channel_id=1, source_target_pairs={{0,3},{1,2},{2,1},{3,0},{4,7},{5,6},{6,5},{7,4},{8,11},{9,10},{10,... | collective-permute-start | bytes 2752520 | tf_op jit(solution)/shard_map/ppermute | solution.py:41
  43.5 17.3 %collective-permute-start.9 = (f32[2,128,640]{2,1,0:T(8,128)}, f32[2,128,640]{2,1,0:T(8,128)}, u32[]{:S(2)}, u32[]{:S(2)}) collective-permute-start(f32[2,128,640]{2,1,0:T(8,128)} %pad_maximum_fusion.4.refs_1_), channel_id=1, source_target_pairs={{0,4},{1,5},{2,6},{3,7},{4,0},{5,1},{6,2},{7,3},{8,12},{9,13},{10,... | collective-permute-start | bytes 1966088 | tf_op jit(solution)/shard_map/ppermute | solution.py:41
  46.4 18.7 %collective-permute-start.11 = (f32[2,128,640]{2,1,0:T(8,128)}, f32[2,128,640]{2,1,0:T(8,128)}, u32[]{:S(2)}, u32[]{:S(2)}) collective-permute-start(f32[2,128,640]{2,1,0:T(8,128)} %pad_maximum_fusion.5.refs_3_), channel_id=1, source_target_pairs={{0,1},{1,0},{2,3},{3,2},{4,5},{5,4},{6,7},{7,6},{8,9},{9,8},{10,11... | collective-permute-start | bytes 1966088 | tf_op jit(solution)/shard_map/ppermute | solution.py:41
  67.1 2.7 %copy-start = (bf16[1024,3072]{1,0:T(8,128)(2,1)}, bf16[1024,3072]{1,0:T(8,128)(2,1)S(1)}, u32[]{:S(2)}) copy-start(bf16[1024,3072]{1,0:T(8,128)(2,1)S(1)} %get-tuple-element.42.kept_ref) | copy-start | bytes 18874372
  69.7 6.9 %collective-permute-start.12 = (f32[512,128]{1,0:T(8,128)S(1)}, f32[512,128]{1,0:T(8,128)S(1)}, u32[]{:S(2)}, u32[]{:S(2)}) collective-permute-start(f32[512,128]{1,0:T(8,128)S(1)} %constant_dynamic-slice_fusion), channel_id=1, source_target_pairs={{0,16},{16,0},{32,48},{48,32},{64,80},{80,64},{96,112},{112,96},{1... | collective-permute-start | bytes 786440 | tf_op jit(solution)/shard_map/ppermute | solution.py:282
  128.0 8.1 %copy-start.2 = (f32[4,128,128]{2,1,0:T(8,128)}, f32[4,128,128]{2,1,0:T(8,128)S(1)}, u32[]{:S(2)}) copy-start(f32[4,128,128]{2,1,0:T(8,128)S(1)} %all_to_all.17) | copy-start | bytes 786436
  128.0 8.1 %collective-permute-start.13 = (f32[512,128]{1,0:T(8,128)S(1)}, f32[512,128]{1,0:T(8,128)S(1)}, u32[]{:S(2)}, u32[]{:S(2)}) collective-permute-start(f32[512,128]{1,0:T(8,128)S(1)} %bitcast.11), channel_id=1, source_target_pairs={{0,16},{16,0},{32,48},{48,32},{64,80},{80,64},{96,112},{112,96},{1... | collective-permute-start | bytes 786440 | tf_op jit(solution)/shard_map/ppermute | solution.py:293
  136.1 0.7 copy-start.3

commit v6 on v0

v6 whole, which is shorter than its diff:
```python
import functools

import jax
import jax.numpy as jnp
from jax import lax
from jax.experimental import pallas as pl
from jax.experimental.pallas import tpu as pltpu
from jax.sharding import PartitionSpec as P

F32 = jnp.float32
BF16 = jnp.bfloat16
NEXT, BACK = 1, 3
SIDE = 4
SHARES = (7, 5, 7, 5)
PAIRS = 2
NEAR = 4
FAR = 4
GRANT = 32 << 20
PLANES = 6


def dot(left, right):
    return jnp.dot(left, right, preferred_element_type=F32)


def dot_t(left, right):
    return lax.dot_general(left, right, (((1,), (1,)), ((), ())), preferred_element_type=F32)


def exact(left, right):
    return jnp.dot(left, right, precision=lax.Precision.HIGHEST, preferred_element_type=F32)


def split(x):
    high = x.astype(BF16)
    return high, (x - high.astype(F32)).astype(BF16)


class Piece:
    def __init__(self, base, size, x_first, steps):
        self.base, self.size, self.x_first, self.steps = base, size, x_first, steps
        self.masks = [0, steps[0], steps[1], steps[0] ^ steps[1]]

    def chunk(self, place_ref, pos):
        y, x = place_ref[0], place_ref[1]
        mask, other = self.masks[pos // SIDE], pos % SIDE
        if self.x_first:
            return lax.bitwise_xor(y, mask) * SIDE + other
        return other * SIDE + lax.bitwise_xor(x, mask)


def block(place, width, base=0):
    return pl.ds(pl.multiple_of(base + place * width, width), width)


def half_coeffs(high, low, z_both):
    m = z_both.shape[1] // 2
    wide = dot(high, z_both)
    return wide[:, :m] + (wide[:, m:] + dot(low, z_both[:, :m]))


def add_coeffs(out_ref, part, place_ref, piece, first, k, width):
    for i in range(part.shape[0] // (2 * width)):
        chunk = piece.chunk(place_ref, first + i)
        for which in range(2):
            low = (2 * i + which) * width
            out_ref[block(chunk, width, which * k), :] += part[low : low + width, :]


def keep(half, kept, row, base, sem):
    rows, n = half.shape
    copy = pltpu.make_async_copy(half, kept.at[0, pl.ds(row, rows), pl.ds(base, n)], sem)
    copy.start()
    return copy


def early_kernel(pieces, k, width, place_ref, z_ref, *refs):
    count = len(pieces)
    halves, acc_ref, zb_ref, out = refs[:count], refs[count], refs[count + 1], refs[count + 2 : 3 * count + 2]
    kept, sems = refs[3 * count + 2 :]
    m = z_ref.shape[1]
    acc_ref[...] = jnp.zeros_like(acc_ref)
    copies = []
    for p, piece in enumerate(pieces):
        rows = slice(piece.base, piece.base + piece.size)
        zb_ref[rows, :m], zb_ref[rows, m:] = split(z_ref[rows, :])
        out[2 * p][...], out[2 * p + 1][...] = split(halves[p][...])
        for i in range(2):
            copies.append(keep(out[2 * p + i], kept, 2 * i * k, piece.base, sems.at[2 * p + i]))
        part = half_coeffs(out[2 * p][...], out[2 * p + 1][...], zb_ref[rows, :])
        add_coeffs(acc_ref, part, place_ref, piece, 0, k, width)
    for copy in copies:
        copy.wait()


def vmem_specs(count):
    return [pl.BlockSpec(memory_space=pltpu.VMEM)] * count


def any_specs(count):
    return [pl.BlockSpec(memory_space=pl.ANY)] * count


SMEM = [pl.BlockSpec(memory_space=pltpu.SMEM)]


def early(place, z, halves, pieces, k, width):
    n, m = z.shape
    pairs = [jax.ShapeDtypeStruct(half.shape, BF16) for half in halves for _ in range(2)]
    shapes = [jax.ShapeDtypeStruct((2 * k, m), F32), jax.ShapeDtypeStruct((n, 2 * m), BF16)] + pairs
    out = pl.pallas_call(
        functools.partial(early_kernel, pieces, k, width),
        out_shape=shapes + [jax.ShapeDtypeStruct((PLANES, 4 * k, n), BF16)],
        in_specs=SMEM + vmem_specs(1 + len(halves)),
        out_specs=vmem_specs(len(shapes)) + any_specs(1),
        scratch_shapes=[pltpu.SemaphoreType.DMA((len(pairs),))],
        compiler_params=pltpu.CompilerParams(vmem_limit_bytes=GRANT),
        cost_estimate=pl.CostEstimate(flops=6 * k * n * m, bytes_accessed=12 << 20, transcendentals=0),
    )(place, z, *halves)
    return out[0], out[1], out[2:-1], out[-1]


def late_kernel(piece, first, k, width, place_ref, acc_ref, got_ref, first_h, first_l, zb_ref, _, *refs):
    out_ref, kept, got_h, got_l, two_h, two_l, sems = refs
    m = zb_ref.shape[1] // 2
    got_h[...], got_l[...] = split(got_ref[...])
    copies = [keep(half, kept, (2 * i + 1) * k, piece.base, sems.at[i]) for i, half in enumerate((got_h, got_l))]
    half = k // (2 * width)
    chunks = [piece.chunk(place_ref, pos) for pos in range(2 * half)]
    one = []
    for own, got, two in ((first_h, got_h, two_h), (first_l, got_l, two_l)):
        blocks = []
        for pos, chunk in enumerate(chunks):
            ref, low = (own, got)[pos // half], pos % half * 2 * width
            blocks.append(ref[low : low + width, :])
            two[block(chunk, width), :] = ref[low + width : low + 2 * width, :]
        one.append(jnp.concatenate(blocks, 0))
    out_ref[: 2 * k, :] = acc_ref[: 2 * k, :]
    part = half_coeffs(got_h[...], got_l[...], zb_ref[piece.base : piece.base + piece.size, :])
    add_coeffs(out_ref, part, place_ref, piece, half, k, width)
    high = two_h[...]
    gram = dot_t(one[0], high) + (dot_t(one[0], two_l[...]) + dot_t(one[1], high))
    for pos, chunk in enumerate(chunks):
        for i in range(k // m):
            part = gram[pos * width : (pos + 1) * width, i * m : (i + 1) * m]
            rows = block(chunk, width, (2 + i) * k)
            out_ref[rows, :] = part if first else acc_ref[rows, :] + part
    for copy in copies:
        copy.wait()


def late(place, acc, got, firsts, zb, kept, piece, first, k, width):
    m = zb.shape[1] // 2
    rows = pltpu.VMEM(got.shape, BF16)
    return pl.pallas_call(
        functools.partial(late_kernel, piece, first, k, width),
        out_shape=[jax.ShapeDtypeStruct((2 * k + k * k // m, m), F32), jax.ShapeDtypeStruct(kept.shape, BF16)],
        in_specs=SMEM + vmem_specs(5) + any_specs(1),
        out_specs=vmem_specs(1) + any_specs(1),
        input_output_aliases={6: 1},
        scratch_shapes=[rows] * 4 + [pltpu.SemaphoreType.DMA((2,))],
        compiler_params=pltpu.CompilerParams(vmem_limit_bytes=GRANT),
    )(place, acc, got, *firsts, zb, kept)


def apply_kernel(pieces, width, place_ref, mine_ref, other_ref, t_one_ref, t_two_ref, z_ref, kept_ref, *refs):
    out_ref, held, z_held, out_held, total_ref, x_ref, slot_ref, sems, z_sems, out_sems = refs
    k = t_one_ref.shape[0]
    m = z_ref.shape[1]
    loads, z_loads = [], []
    for p, piece in enumerate(pieces):
        lanes = pl.ds(piece.base, piece.size)
        loads.append(pltpu.make_async_copy(kept_ref.at[0, :, lanes], held.at[:, lanes], sems.at[p]))
        z_loads.append(pltpu.make_async_copy(z_ref.at[lanes, :], z_held.at[lanes, :], z_sems.at[p]))
        loads[p].start()
        z_loads[p].start()
    core = place_ref[2]
    half = mine_ref.shape[0]
    total_ref[block(core, half), :] = mine_ref[...]
    total_ref[block(1 - core, half), :] = other_ref[...]
    x_ref[k:, :] = exact(t_two_ref[...], total_ref[k : 2 * k, :])
    coeff = total_ref[:k, :]
    for i in range(k // m):
        row = (2 + i) * k
        coeff = coeff - exact(total_ref[row : row + k, :], x_ref[k + i * m : k + (i + 1) * m, :])
    x_ref[:k, :] = exact(t_one_ref[...], coeff)
    stores = []
    for p, piece in enumerate(pieces):
        for pos in range(k // width):
            chunk = piece.chunk(place_ref, pos)
            for which in range(2):
                low = (2 * pos + which) * width
                slot_ref[low : low + width, :] = x_ref[block(chunk, width, which * k), :]
        x_h, x_l = split(slot_ref[...].T)
        x_both = jnp.concatenate([x_h, x_l], 0)
        loads[p].wait()
        z_loads[p].wait()
        rows = slice(piece.base, piece.base + piece.size)
        wide = dot(x_both, held[: 2 * k, rows])
        moved = wide[:m, :] + (wide[m:, :] + dot(x_h, held[2 * k :, rows]))
        out_held[rows, :] = z_held[rows, :] - moved.T
        lanes = pl.ds(piece.base, piece.size)
        stores.append(pltpu.make_async_copy(out_held.at[lanes, :], out_ref.at[lanes, :], out_sems.at[p]))
        stores[-1].start()
    for store in stores:
        store.wait()


def apply(place, mine, other, t_one, t_two, z, kept, pieces, width):
    k, m = t_one.shape[0], z.shape[1]
    rows = pltpu.VMEM(z.shape, F32)
    coeffs = pltpu.VMEM((2 * k, m), F32)
    return pl.pallas_call(
        functools.partial(apply_kernel, pieces, width),
        out_shape=jax.ShapeDtypeStruct(z.shape, F32),
        in_specs=SMEM + vmem_specs(4) + any_specs(2),
        out_specs=pl.BlockSpec(memory_space=pl.ANY),
        scratch_shapes=[pltpu.VMEM(kept.shape[1:], BF16), rows, rows, pltpu.VMEM((2 * mine.shape[0], m), F32)]
        + [coeffs, coeffs]
        + [pltpu.SemaphoreType.DMA((len(pieces),))] * 3,
        compiler_params=pltpu.CompilerParams(vmem_limit_bytes=GRANT),
    )(place, mine, other, t_one, t_two, z, kept)


def line(along_x):
    if along_x:
        return [[SIDE * y + x for x in range(SIDE)] for y in range(SIDE)]
    return [[SIDE * y + x for y in range(SIDE)] for x in range(SIDE)]


def gather_line(data, along_x):
    spread = jnp.broadcast_to(data[None], (SIDE,) + data.shape)
    got = lax.all_to_all(spread, "col", 0, 0, axis_index_groups=line(along_x), tiled=True)
    return got.reshape(SIDE * data.shape[0], data.shape[1])


def swap(data, mask, along_x):
    mask = mask if along_x else SIDE * mask
    return lax.ppermute(data, "col", [(i, i ^ mask) for i in range(SIDE * SIDE)])


def gather_pieces(own):
    unit = own.shape[1] // sum(SHARES)
    sizes = [unit * share for share in SHARES]
    pieces, halves = [], []
    for pair, x_first in ((0, True), (2, False)):
        base = sum(sizes[:pair])
        whole = gather_line(own[:, base : base + sizes[pair] + sizes[pair + 1]], x_first)
        for i, steps in ((0, (NEXT, BACK)), (1, (BACK, NEXT))):
            low = i * sizes[pair]
            piece = Piece(base + low, sizes[pair + i], x_first, steps)
            data = whole[:, low : low + piece.size]
            data = jnp.concatenate([data, swap(data, steps[0], not x_first)], 0)
            pieces.append(piece)
            halves.append((data, swap(data, steps[1], not x_first)))
    return pieces, halves


def sum_over_row(part):
    r, m = part.shape
    group = PAIRS * NEAR
    rows = group * FAR
    pair = [(i, i ^ 1) for i in range(rows)]
    near = [[group * g + PAIRS * i + c for i in range(NEAR)] for g in range(FAR) for c in range(PAIRS)]
    far = [[i + group * g for g in range(FAR)] for i in range(group)]
    core = lax.axis_index("row") % PAIRS
    half = r // PAIRS
    kept = lax.dynamic_slice_in_dim(part, core * half, half, 0)
    given = lax.dynamic_slice_in_dim(part, (1 - core) * half, half, 0)
    mine = kept + lax.ppermute(given, "row", pair)
    blocks = lax.all_to_all(mine.reshape(NEAR, half // NEAR, m), "row", 0, 0, axis_index_groups=near, tiled=True)
    mine = jnp.sum(blocks, 0)
    blocks = lax.all_to_all(
        jnp.broadcast_to(mine[None], (FAR,) + mine.shape), "row", 0, 0, axis_index_groups=far, tiled=True
    )
    mine = jnp.sum(blocks, 0)
    blocks = lax.all_to_all(
        jnp.broadcast_to(mine[None], (NEAR,) + mine.shape), "row", 0, 0, axis_index_groups=near, tiled=True
    )
    mine = blocks.reshape(half, m)
    return mine, lax.ppermute(mine, "row", pair)


def body(z_slab, v_first, v_second, t_first, t_second):
    width = v_first.shape[1]
    k = t_first.shape[0]
    own = lax.optimization_barrier(jnp.concatenate([v_first.T, v_second.T], 0))
    pieces, halves = gather_pieces(own)
    col, row = lax.axis_index("col"), lax.axis_index("row")
    place = lax.optimization_barrier(jnp.stack([col // SIDE, col % SIDE, row % PAIRS]).astype(jnp.int32))
    part, z_both, firsts, kept = early(place, z_slab, [half[0] for half in halves], pieces, k, width)
    for p, piece in enumerate(pieces):
        two = firsts[2 * p : 2 * p + 2]
        part, kept = late(place, part, halves[p][1], two, z_both, kept, piece, p == 0, k, width)
    mine, other = sum_over_row(part)
    return apply(place, mine, other, t_first, t_second, z_slab, kept, pieces, width)


def solution(mesh):
    placed = (P("row", "col"), P("row", "col"), P("row", "col"), P(), P())
    return jax.shard_map(
        body,
        mesh=mesh,
        in_specs=placed,
        out_specs=P("row", "col"),
        check_vma=False,
    )
```

time: 556 us -> 152 us (0.27)
  waiting for transfers between devices: 519 us -> 19.3 us
  blocking collectives: 0 us -> 64.8 us
  starting transfers between devices: 0.12 us -> 41.7 us
  matrix products: 21.3 us -> 0 us
  Pallas kernels: 0 us -> 21.2 us
  between operations: 13.2 us -> 0.34 us
    psum x2 -> x0, waiting for transfers between devices: 389 us -> none  [the longest x1 195 us: body(): coeff_one = lax.psum(project(panel_one, z_mid), 'row')]
    all_gather x2 -> x0, waiting for transfers between devices: 129 us -> none  [the longest x1 71.3 us: body(): panel_two = lax.all_gather(v_second, 'col', axis=1, tiled=True)]
    all_to_all x0 -> x4, blocking collectives: none -> 64.8 us  [the longest x1 26.9 us: sum_over_row(): lax.all_to_all(jnp.broadcast_to(mine[None], (FAR,) + mine.shape), 'row',...]
    ppermute x0 -> x10, starting transfers between devices: none -> 34.5 us  [the longest x8 21.5 us: swap(): lax.ppermute(data, 'col', [(i, i ^ mask) for i in range(SIDE * SIDE)])]
    dot_general x6 -> x0, matrix products: 21.3 us -> none  [the longest x2 11.4 us: project(): jnp.einsum('nk,nm->km', vectors, slab, precision=lax.Precision.HIGHEST, p...]
    pallas_call x0 -> x6, Pallas kernels: none -> 21.2 us  [the longest x4 11 us: late(): pl.pallas_call(functools.partial(late_kernel, piece, first, k, width), ou...]
    ppermute x0 -> x10, waiting for transfers between devices: none -> 12.8 us  [the longest x8 10.5 us: swap(): lax.ppermute(data, 'col', [(i, i ^ mask) for i in range(SIDE * SIDE)])]
    all_to_all x0 -> x1, starting transfers between devices: none -> 7.22 us  [gather_line(): lax.all_to_all(spread, 'col', 0, 0, axis_index_groups=line(along_x), tile...]
  transfers between devices with their start and end apart: 4 -> 11, of which waited for: 4 -> 5; matrix products, arithmetic and copies ran while one was open for 1% -> 0% of each run, Pallas kernels for 0% -> 8%
where the time goes in v6:
time: 152 us; the launch traced here: 151 us
  blocking collectives  64.8 us (43%)
  starting transfers between devices  41.7 us (27%)
  Pallas kernels  21.2 us (14%)
  waiting for transfers between devices  19.3 us (13%)
  local copies, waits for them, and re-layouts  2.67 us (2%)
    all_to_all x1, blocking collectives, sum_over_row(): lax.all_to_all(jnp.broadcast_to(mine[None], (FAR,) + mine.shape), 'row',...  26.9 us
    ppermute x8, starting transfers between devices, swap(): lax.ppermute(data, 'col', [(i, i ^ mask) for i in range(SIDE * SIDE)])  21.5 us
    all_to_all x1, blocking collectives, gather_line(): lax.all_to_all(spread, 'col', 0, 0, axis_index_groups=line(along_x), tile...  13 us
    all_to_all x1, blocking collectives, sum_over_row(): lax.all_to_all(jnp.broadcast_to(mine[None], (NEAR,) + mine.shape), 'row',...  12.6 us
    all_to_all x1, blocking collectives, sum_over_row(): lax.all_to_all(mine.reshape(NEAR, half // NEAR, m), 'row', 0, 0, axis_ind...  12.4 us
    pallas_call x4, Pallas kernels, late(): pl.pallas_call(functools.partial(late_kernel, piece, first, k, width), ou...  11 us
    ppermute x8, waiting for transfers between devices, swap(): lax.ppermute(data, 'col', [(i, i ^ mask) for i in range(SIDE * SIDE)])  10.5 us
    all_to_all x1, starting transfers between devices, gather_line(): lax.all_to_all(spread, 'col', 0, 0, axis_index_groups=line(along_x), tile...  7.22 us
  transfers between devices with their start and end apart: 11, of which 5 were waited for; matrix products, arithmetic and copies ran while one was open for 0% of the time, Pallas kernels for 8%

profile of v6, /device:TPU:1, one launch (start us, length us, event | category | flops | bytes accessed | tf_op | source)
XLA Modules:
  0.0 151.5 jit_solution(17805451701224169572)
XLA Ops:
  0.0 1.0 pad_maximum_fusion.4
  1.1 0.1 broadcast_in_dim.8
  1.2 13.0 %all_to_all.25 = f32[4,32,1536]{2,1,0:T(8,128)S(1)} all-to-all(f32[4,32,1536]{2,1,0:T(8,128)S(1)} %broadcast_in_dim.8), channel_id=1, replica_groups={{0,1,2,3},{4,5,6,7},{8,9,10,11},{12,13,14,15},{16,17,18,19},{20,21,22,2..., dimensions={0} | all-to-all | bytes 1572864 | tf_op jit(solution)/shard_map/all_to_all | solution.py:233
  14.1 1.0 broadcast_in_dim.9
  15.1 7.2 %all-to-all-start.1 = ((f32[4,32,1536]{2,1,0:T(8,128)}), f32[4,32,1536]{2,1,0:T(8,128)S(1)}, u32[]{:S(2)}, u32[]{:S(2)}) async-start(f32[4,32,1536]{2,1,0:T(8,128)} %broadcast_in_dim.9), calls=%async_computation.1 | async-start | bytes 1572864 | tf_op jit(solution)/shard_map/all_to_all | solution.py:233
  22.4 3.4 %collective-permute-start = (f32[128,896]{1,0:T(8,128)S(1)}, f32[128,896]{1,0:T(8,128)S(1)}, u32[]{:S(2)}, u32[]{:S(2)}) collective-permute-start(f32[128,896]{1,0:T(8,128)S(1)} %slice.25), channel_id=1, source_target_pairs={{0,4},{1,5},{2,6},{3,7},{4,0},{5,1},{6,2},{7,3},{8,12},{9,13},{10,... | collective-permute-start | bytes 1376264 | tf_op jit(solution)/shard_map/ppermute | solution.py:239
  25.7 6.5 %all-to-all-done.1 = f32[4,32,1536]{2,1,0:T(8,128)S(1)} async-done(((f32[4,32,1536]{2,1,0:T(8,128)}), f32[4,32,1536]{2,1,0:T(8,128)S(1)}, u32[]{:S(2)}, u32[]{:S(2)}) %all-to-all-start.1) | async-done | bytes 786464 | tf_op jit(solution)/shard_map/all_to_all | solution.py:233
  32.2 2.2 %collective-permute-start.2 = (f32[128,896]{1,0:T(8,128)S(1)}, f32[128,896]{1,0:T(8,128)S(1)}, u32[]{:S(2)}, u32[]{:S(2)}) collective-permute-start(f32[128,896]{1,0:T(8,128)S(1)} %slice.28), channel_id=1, source_target_pairs={{0,1},{1,0},{2,3},{3,2},{4,5},{5,4},{6,7},{7,6},{8,9},{9,8},{10,11... | collective-permute-start | bytes 1376264 | tf_op jit(solution)/shard_map/ppermute | solution.py:239
  34.5 2.8 %collective-permute-start.1 = (f32[128,640]{1,0:T(8,128)S(1)}, f32[128,640]{1,0:T(8,128)S(1)}, u32[]{:S(2)}, u32[]{:S(2)}) collective-permute-start(f32[128,640]{1,0:T(8,128)S(1)} %slice.26), channel_id=1, source_target_pairs={{0,12},{1,13},{2,14},{3,15},{4,8},{5,9},{6,10},{7,11},{8,4},{9,5},... | collective-permute-start | bytes 983048 | tf_op jit(solution)/shard_map/ppermute | solution.py:239
  37.3 2.5 %collective-permute-start.3 = (f32[128,640]{1,0:T(8,128)S(1)}, f32[128,640]{1,0:T(8,128)S(1)}, u32[]{:S(2)}, u32[]{:S(2)}) collective-permute-start(f32[128,640]{1,0:T(8,128)S(1)} %slice.29), channel_id=1, source_target_pairs={{0,3},{1,2},{2,1},{3,0},{4,7},{5,6},{6,5},{7,4},{8,11},{9,10},{10,... | collective-permute-start | bytes 983048 | tf_op jit(solution)/shard_map/ppermute | solution.py:239
  39.9 1.0 collective-permute-done
  40.8 0.1 pad_maximum_fusion.refs_0_
  40.9 3.7 %collective-permute-start.4 = (f32[256,896]{1,0:T(8,128)S(1)}, f32[256,896]{1,0:T(8,128)}, u32[]{:S(2)}, u32[]{:S(2)}) collective-permute-start(f32[256,896]{1,0:T(8,128)S(1)} %pad_maximum_fusion.refs_0_), channel_id=1, source_target_pairs={{0,12},{1,13},{2,14},{3,15},{4,8},{5,9},{6,10},{7,11},{8,4},{9,5},... | collective-permute-start | bytes 2752520 | tf_op jit(solution)/shard_map/ppermute | solution.py:239
  44.6 0.0 collective-permute-done.2
  44.6 0.1 pad_maximum_fusion.1.refs_2_
  44.7 3.0 %collective-permute-start.6 = (f32[256,896]{1,0:T(8,128)S(1)}, f32[256,896]{1,0:T(8,128)}, u32[]{:S(2)}, u32[]{:S(2)}) collective-permute-start(f32[256,896]{1,0:T(8,128)S(1)} %pad_maximum_fusion.1.refs_2_), channel_id=1, source_target_pairs={{0,3},{1,2},{2,1},{3,0},{4,7},{5,6},{6,5},{7,4},{8,11},{9,10},{10,... | collective-permute-start | bytes 2752520 | tf_op jit(solution)/shard_map/ppermute | solution.py:239
  47.7 0.0 collective-permute-done.1
  47.8 2.0 %collective-permute-start.5 = (f32[256,640]{1,0:T(8,128)S(1)}, f32[256,640]{1,0:T(8,128)}, u32[]{:S(2)}, u32[]{:S(2)}) collective-permute-start(f32[256,640]{1,0:T(8,128)S(1)} %pad_maximum_fusion.2.refs_1_), channel_id=1, source_target_pairs={{0,4},{1,5},{2,6},{3,7},{4,0},{5,1},{6,2},{7,3},{8,12},{9,13},{10,... | collective-permute-start | bytes 1966088 | tf_op jit(solution)/shard_map/ppermute | solution.py:239
  49.7 0.0 collective-permute-done.3
  49.8 1.9 %collective-permute-start.7 = (f32[256,640]{1,0:T(8,128)S(1)}, f32[256,640]{1,0:T(8,128)}, u32[]{:S(2)}, u32[]{:S(2)}) collective-permute-start(f32[256,640]{1,0:T(8,128)S(1)} %pad_maximum_fusion.3.refs_3_), channel_id=1, source_target_pairs={{0,1},{1,0},{2,3},{3,2},{4,5},{5,4},{6,7},{7,6},{8,9},{9,8},{10,11... | collective-permute-start | bytes 1966088 | tf_op jit(solution)/shard_map/ppermute | solution.py:239
  51.8 0.1 pad_add_fusion.place_ref
  51.8 0.0 copy-start
  51.8 1.4 copy-done
  53.3 3.4 %shard_map.55 = (f32[512,128]{1,0:T(8,128)S(1)}, bf16[3072,256]{1,0:T(8,128)(2,1)S(1)}, bf16[256,896]{1,0:T(8,128)(2,1)S(1)}, bf16[256,896]{1,0:T(8,128)(2,1)S(1...) custom-call(s32[3]{0:T(128)S(1)} %pad_add_fusion.place_ref, ...), custom_call_target="tpu_custom_call" | custom-call | flops 603979776 | bytes 12582912 | tf_op jit(solution)/shard_map/pallas_call | solution.py:111
  56.7 9.5 %collective-permute-done.4.got_ref = f32[256,896]{1,0:T(8,128)} collective-permute-done((f32[256,896]{1,0:T(8,128)S(1)}, f32[256,896]{1,0:T(8,128)}, u32[]{:S(2)}, u32[]{:S(2)}) %collective-permute-start.4) | collective-permute-done | bytes 917536 | tf_op jit(solution)/shard_map/ppermute | solution.py:239
  66.2 2.8 %shard_map.56 = (f32[1024,128]{1,0:T(8,128)S(1)}, bf16[6,1024,3072]{2,1,0:T(8,128)(2,1)}) custom-call(s32[3]{0:T(128)S(1)} %pad_add_fusion.place_ref, f32[512,128]{1,0:T(8,128)S(1)} %get-tuple-element.24.acc_ref, f32[256,896]{1,0:T(8,128)} %collective-permute-done.4.got_ref, ...), custom_call_target="tpu_custom_call", output_to_operand_aliasing={{1}: (6, {})} | custom-call | tf_op jit(solution)/shard_map/pallas_call | solution.py:155
  69.1 0.0 collective-permute-done.5.got_ref
  69.1 2.6 %shard_map.57 = (f32[1024,128]{1,0:T(8,128)S(1)}, bf16[6,1024,3072]{2,1,0:T(8,128)(2,1)}) custom-call(s32[3]{0:T(128)S(1)} %pad_add_fusion.place_ref, f32[1024,128]{1,0:T(8,128)S(1)} %get-tuple-element.29.acc_ref, f32[256,640]{1,0:T(8,128)} %collective-permute-done.5.got_ref, ...), custom_call_target="tpu_custom_call", output_to_operand_aliasing={{1}: (6, {})} | custom-call | tf_op jit(solution)/shard_map/pallas_call | solution.py:155
  71.7 0.0 collective-permute-done.6.got_ref
  71.7 0.0 copy-start.1
  71.7 0.0 copy-start.2
  71.7 0.0 copy-start.3
  71.7 3.0 %shard_map.58 = (f32[1024,128]{1,0:T(8,128)S(1)}, bf16[6,1024,3072]{2,1,0:T(8,128)(2,1)}) custom-call(s32[3]{0:T(128)S(1)} %pad_add_fusion.place_ref, f32[1024,128]{1,0:T(8,128)S(1)} %get-tuple-element.33.acc_ref, f32[256,896]{1,0:T(8,128)} %collective-permute-done.6.got_ref, ...), custom_call_target="tpu_custom_call", output_to_operand_aliasing={{1}: (6, {})} | custom-call | tf_op jit(solution)/shard_map/pallas_call | solution.py:155
  74.7 0.0 collective-permute-done.7.got_ref
  74.7 2.6 %shard_map.59 = (f32[1024,128]{1,0:T(8,128)S(1)}, bf16[6,1024,3072]{2,1,0:T(8,128)(2,1)}) custom-call(s32[3]{0:T(128)S(1)} %pad_add_fusion.place_ref, f32[1024,128]{1,0:T(8,128)S(1)} %get-tuple-element.37.acc_ref, f32[256,640]{1,0:T(8,128)} %collective-permute-done.7.got_ref, ...), custom_call_target="tpu_custom_call", output_to_operand_aliasing={{1}: (6, {})} | custom-call | tf_op jit(solution)/shard_map/pallas_call | solution.py:155
  77.4 6.1 %collective-permute-start.8 = (f32[512,128]{1,0:T(8,128)S(1)}, f32[512,128]{1,0:T(8,128)S(1)}, u32[]{:S(2)}, u32[]{:S(2)}) collective-permute-start(f32[512,128]{1,0:T(8,128)S(1)} %constant_dynamic-slice_fusion), channel_id=1, source_target_pairs={{0,16},{16,0},{32,48},{48,32},{64,80},{80,64},{96,112},{112,96},{1... | collective-permute-start | bytes 786440 | tf_op jit(solution)/shard_map/ppermute | solution.py:270
  83.5 1.1 collective-permute-done.8
  84.6 12.4 %all_to_all.26 = f32[4,128,128]{2,1,0:T(8,128)S(1)} all-to-all(f32[4,128,128]{2,1,0:T(8,128)S(1)} %bitcast.15), channel_id=1, replica_groups={{0,32,64,96},{16,48,80,112},{128,160,192,224},{144,176,208,240},{256,28..., dimensions={0} | all-to-all | bytes 524288 | tf_op jit(solution)/shard_map/all_to_all | solution.py:271
  97.1 26.9 %all_to_all.27 = f32[4,128,128]{2,1,0:T(8,128)S(1)} all-to-all(f32[4,128,128]{2,1,0:T(8,128)S(1)} %broadcast_in_dim.10), channel_id=1, replica_groups={{0,128,256,384},{16,144,272,400},{32,160,288,416},{48,176,304,432},{64,..., dimensions={0} | all-to-all | bytes 524288 | tf_op jit(solution)/shard_map/all_to_all | solution.py:273
  124.0 12.6 %all_to_all.28 = f32[4,128,128]{2,1,0:T(8,128)S(1)} all-to-all(f32[4,128,128]{2,1,0:T(8,128)S(1)} %broadcast_in_dim.11), channel_id=1, replica_groups={{0,32,64,96},{16,48,80,112},{128,160,192,224},{144,176,208,240},{256,28..., dimensions={0} | all-to-all | bytes 524288 | tf_op jit(solution)/shard_map/all_to_all | solution.py:277
  136.6 6.9 %collective-permute-start.9 = (f32[512,128]{1,0:T(8,128)S(1)}, f32[512,128]{1,0:T(8,128)S(1)}, u32[]{:S(2)}, u32[]{:S(2)}) collective-permute-start(f32[512,128]{1,0:T(8,128)S(1)} %bitcast.9), channel_id=1, source_target_pairs={{0,16},{16,0},{32,48},{48,32},{64,80},{80,64},{96,112},{112,96},{1... | collective-permute-start | bytes 786440 | tf_op jit(solution)/shard_map/ppermute | solution.py:281
  143.5 1.1 collective-permute-done.9.other_ref
  144.7 0.0 copy-done.1
  144.7 0.0 copy-done.2
  144.7 0.0 copy-done.3
  144.7 6.8 %shard_map.60 = f32[3072,128]{1,0:T(8,128)} custom-call(s32[3]{0:T(128)S(1)} %pad_add_fusion.place_ref, f32[512,128]{1,0:T(8,128)S(1)} %bitcast.10, f32[512,128]{1,0:T(8,128)S(1)} %collective-permute-done.9.other_ref, f32[256,256]{1,0:T(8,128)S(1)} %copy-done.2, f32[256,256]{1,0:T(8,128)S(1)} %copy-done.3, f32[3072,128]{1,0:T(8,128)S(1)} %copy-done.1, ...), custom_call_target="tpu_custom_call" | custom-call | tf_op jit(solution)/shard_map/pallas_call | solution.py:213
  (13 shorter events, 0.4 us)
Async XLA Ops:
  15.1 17.1 %all-to-all-start.1 = ((f32[4,32,1536]{2,1,0:T(8,128)}), f32[4,32,1536]{2,1,0:T(8,128)S(1)}, u32[]{:S(2)}, u32[]{:S(2)}) async-start(f32[4,32,1536]{2,1,0:T(8,128)} %broadcast_in_dim.9), calls=%async_computation.1 | async-start | bytes 1572864 | tf_op jit(solution)/shard_map/all_to_all | solution.py:233
  22.4 18.5 %collective-permute-start = (f32[128,896]{1,0:T(8,128)S(1)}, f32[128,896]{1,0:T(8,128)S(1)}, u32[]{:S(2)}, u32[]{:S(2)}) collective-permute-start(f32[128,896]{1,0:T(8,128)S(1)} %slice.25), channel_id=1, source_target_pairs={{0,4},{1,5},{2,6},{3,7},{4,0},{5,1},{6,2},{7,3},{8,12},{9,13},{10,... | collective-permute-start | bytes 1376264 | tf_op jit(solution)/shard_map/ppermute | solution.py:239
  32.2 12.4 %collective-permute-start.2 = (f32[128,896]{1,0:T(8,128)S(1)}, f32[128,896]{1,0:T(8,128)S(1)}, u32[]{:S(2)}, u32[]{:S(2)}) collective-permute-start(f32[128,896]{1,0:T(8,128)S(1)} %slice.28), channel_id=1, source_target_pairs={{0,1},{1,0},{2,3},{3,2},{4,5},{5,4},{6,7},{7,6},{8,9},{9,8},{10,11... | collective-permute-start | bytes 1376264 | tf_op jit(solution)/shard_map/ppermute | solution.py:239
  34.5 13.2 %collective-permute-start.1 = (f32[128,640]{1,0:T(8,128)S(1)}, f32[128,640]{1,0:T(8,128)S(1)}, u32[]{:S(2)}, u32[]{:S(2)}) collective-permute-start(f32[128,640]{1,0:T(8,128)S(1)} %slice.26), channel_id=1, source_target_pairs={{0,12},{1,13},{2,14},{3,15},{4,8},{5,9},{6,10},{7,11},{8,4},{9,5},... | collective-permute-start | bytes 983048 | tf_op jit(solution)/shard_map/ppermute | solution.py:239
  37.3 12.4 %collective-permute-start.3 = (f32[128,640]{1,0:T(8,128)S(1)}, f32[128,640]{1,0:T(8,128)S(1)}, u32[]{:S(2)}, u32[]{:S(2)}) collective-permute-start(f32[128,640]{1,0:T(8,128)S(1)} %slice.29), channel_id=1, source_target_pairs={{0,3},{1,2},{2,1},{3,0},{4,7},{5,6},{6,5},{7,4},{8,11},{9,10},{10,... | collective-permute-start | bytes 983048 | tf_op jit(solution)/shard_map/ppermute | solution.py:239
  40.9 25.3 %collective-permute-start.4 = (f32[256,896]{1,0:T(8,128)S(1)}, f32[256,896]{1,0:T(8,128)}, u32[]{:S(2)}, u32[]{:S(2)}) collective-permute-start(f32[256,896]{1,0:T(8,128)S(1)} %pad_maximum_fusion.refs_0_), channel_id=1, source_target_pairs={{0,12},{1,13},{2,14},{3,15},{4,8},{5,9},{6,10},{7,11},{8,4},{9,5},... | collective-permute-start | bytes 2752520 | tf_op jit(solution)/shard_map/ppermute | solution.py:239
  44.7 27.0 %collective-permute-start.6 = (f32[256,896]{1,0:T(8,128)S(1)}, f32[256,896]{1,0:T(8,128)}, u32[]{:S(2)}, u32[]{:S(2)}) collective-permute-start(f32[256,896]{1,0:T(8,128)S(1)} %pad_maximum_fusion.1.refs_2_), channel_id=1, source_target_pairs={{0,3},{1,2},{2,1},{3,0},{4,7},{5,6},{6,5},{7,4},{8,11},{9,10},{10,... | collective-permute-start | bytes 2752520 | tf_op jit(solution)/shard_map/ppermute | solution.py:239
  47.8 21.3 %collective-permute-start.5 = (f32[256,640]{1,0:T(8,128)S(1)}, f32[256,640]{1,0:T(8,128)}, u32[]{:S(2)}, u32[]{:S(2)}) collective-permute-start(f32[256,640]{1,0:T(8,128)S(1)} %pad_maximum_fusion.2.refs_1_), channel_id=1, source_target_pairs={{0,4},{1,5},{2,6},{3,7},{4,0},{5,1},{6,2},{7,3},{8,12},{9,13},{10,... | collective-permute-start | bytes 1966088 | tf_op jit(solution)/shard_map/ppermute | solution.py:239
  49.8 24.9 %collective-permute-start.7 = (f32[256,640]{1,0:T(8,128)S(1)}, f32[256,640]{1,0:T(8,128)}, u32[]{:S(2)}, u32[]{:S(2)}) collective-permute-start(f32[256,640]{1,0:T(8,128)S(1)} %pad_maximum_fusion.3.refs_3_), channel_id=1, source_target_pairs={{0,1},{1,0},{2,3},{3,2},{4,5},{5,4},{6,7},{7,6},{8,9},{9,8},{10,11... | collective-permute-start | bytes 1966088 | tf_op jit(solution)/shard_map/ppermute | solution.py:239
  51.8 1.4 copy-start
  71.7 73.0 %copy-start.1 = (f32[3072,128]{1,0:T(8,128)S(1)}, f32[3072,128]{1,0:T(8,128)}, u32[]{:S(2)}) copy-start(f32[3072,128]{1,0:T(8,128)} %z_ref.3) | copy-start | bytes 4718596
  71.7 73.0 %copy-start.2 = (f32[256,256]{1,0:T(8,128)S(1)}, f32[256,256]{1,0:T(8,128)}, u32[]{:S(2)}) copy-start(f32[256,256]{1,0:T(8,128)} %t_one_ref.1) | copy-start | bytes 786436
  71.7 73.0 %copy-start.3 = (f32[256,256]{1,0:T(8,128)S(1)}, f32[256,256]{1,0:T(8,128)}, u32[]{:S(2)}) copy-start(f32[256,256]{1,0:T(8,128)} %t_two_ref.1) | copy-start | bytes 786436
  77.4 7.2 %collective-permute-start.8 = (f32[512,128]{1,0:T(8,128)S(1)}, f32[512,128]{1,0:T(8,128)S(1)}, u32[]{:S(2)}, u32[]{:S(2)}) collective-permute-start(f32[512,128]{1,0:T(8,128)S(1)} %constant_dynamic-slice_fusion), channel_id=1, source_target_pairs={{0,16},{16,0},{32,48},{48,32},{64,80},{80,64},{96,112},{112,96},{1... | collective-permute-start | bytes 786440 | tf_op jit(solution)/shard_map/ppermute | solution.py:270
  136.6 8.1 %collective-permute-start.9 = (f32[512,128]{1,0:T(8,128)S(1)}, f32[512,128]{1,0:T(8,128)S(1)}, u32[]{:S(2)}, u32[]{:S(2)}) collective-permute-start(f32[512,128]{1,0:T(8,128)S(1)} %bitcast.9), channel_id=1, source_target_pairs={{0,16},{16,0},{32,48},{48,32},{64,80},{80,64},{96,112},{112,96},{1... | collective-permute-start | bytes 786440 | tf_op jit(solution)/shard_map/ppermute | solution.py:281

commit v7 on v6

v7 whole, which is shorter than its diff:
```python
import functools

import jax
import jax.numpy as jnp
from jax import lax
from jax.experimental import pallas as pl
from jax.experimental.pallas import tpu as pltpu
from jax.sharding import PartitionSpec as P

F32 = jnp.float32
BF16 = jnp.bfloat16
XA, XB, YA, YB = 1, 3, 4, 12
SHARES = (7, 5, 7, 5)
PAIRS = 2
NEAR = 4
FAR = 4
GRANT = 32 << 20
PLANES = 6


def dot(left, right):
    return jnp.dot(left, right, preferred_element_type=F32)


def dot_t(left, right):
    return lax.dot_general(left, right, (((1,), (1,)), ((), ())), preferred_element_type=F32)


def exact(left, right):
    return jnp.dot(left, right, precision=lax.Precision.HIGHEST, preferred_element_type=F32)


def split(x):
    high = x.astype(BF16)
    return high, (x - high.astype(F32)).astype(BF16)


class Piece:
    def __init__(self, base, size, masks):
        self.base, self.size, self.masks = base, size, masks


def block(place, width, base=0):
    return pl.ds(pl.multiple_of(base + place * width, width), width)


def half_coeffs(high, low, z_both):
    m = z_both.shape[1] // 2
    wide = dot(high, z_both)
    return wide[:, :m] + (wide[:, m:] + dot(low, z_both[:, :m]))


def add_coeffs(out_ref, part, masks, k, width):
    for i, mask in enumerate(masks):
        for which in range(2):
            low, place = (2 * i + which) * width, which * k + mask * width
            out_ref[place : place + width, :] += part[low : low + width, :]


def keep(half, kept, row, base, sem):
    rows, n = half.shape
    copy = pltpu.make_async_copy(half, kept.at[0, pl.ds(row, rows), pl.ds(base, n)], sem)
    copy.start()
    return copy


def early_kernel(pieces, k, width, z_ref, *refs):
    count = len(pieces)
    halves, acc_ref, zb_ref, out = refs[:count], refs[count], refs[count + 1], refs[count + 2 : 3 * count + 2]
    kept, sems = refs[3 * count + 2 :]
    m = z_ref.shape[1]
    acc_ref[...] = jnp.zeros_like(acc_ref)
    copies = []
    for p, piece in enumerate(pieces):
        rows = slice(piece.base, piece.base + piece.size)
        zb_ref[rows, :m], zb_ref[rows, m:] = split(z_ref[rows, :])
        out[2 * p][...], out[2 * p + 1][...] = split(halves[p][...])
        for i in range(2):
            copies.append(keep(out[2 * p + i], kept, 2 * i * k, piece.base, sems.at[2 * p + i]))
        part = half_coeffs(out[2 * p][...], out[2 * p + 1][...], zb_ref[rows, :])
        add_coeffs(acc_ref, part, piece.masks[: len(piece.masks) // 2], k, width)
    for copy in copies:
        copy.wait()


def vmem_specs(count):
    return [pl.BlockSpec(memory_space=pltpu.VMEM)] * count


def any_specs(count):
    return [pl.BlockSpec(memory_space=pl.ANY)] * count


SMEM = [pl.BlockSpec(memory_space=pltpu.SMEM)]


def early(z, halves, pieces, k, width):
    n, m = z.shape
    pairs = [jax.ShapeDtypeStruct(half.shape, BF16) for half in halves for _ in range(2)]
    shapes = [jax.ShapeDtypeStruct((2 * k, m), F32), jax.ShapeDtypeStruct((n, 2 * m), BF16)] + pairs
    out = pl.pallas_call(
        functools.partial(early_kernel, pieces, k, width),
        out_shape=shapes + [jax.ShapeDtypeStruct((PLANES, 4 * k, n), BF16)],
        in_specs=vmem_specs(1 + len(halves)),
        out_specs=vmem_specs(len(shapes)) + any_specs(1),
        scratch_shapes=[pltpu.SemaphoreType.DMA((len(pairs),))],
        compiler_params=pltpu.CompilerParams(vmem_limit_bytes=GRANT),
        cost_estimate=pl.CostEstimate(flops=6 * k * n * m, bytes_accessed=12 << 20, transcendentals=0),
    )(z, *halves)
    return out[0], out[1], out[2:-1], out[-1]


def late_kernel(piece, first, k, width, acc_ref, got_ref, first_h, first_l, zb_ref, _, *refs):
    out_ref, kept, got_h, got_l, sems = refs
    m = zb_ref.shape[1] // 2
    got_h[...], got_l[...] = split(got_ref[...])
    copies = [keep(half, kept, (2 * i + 1) * k, piece.base, sems.at[i]) for i, half in enumerate((got_h, got_l))]
    half = k // (2 * width)

    def panel(which, own, got):
        blocks = [None] * (2 * half)
        for pos, mask in enumerate(piece.masks):
            ref, low = (own, got)[pos // half], (pos % half * 2 + which) * width
            blocks[mask] = ref[low : low + width, :]
        return jnp.concatenate(blocks, 0)

    out_ref[: 2 * k, :] = acc_ref[: 2 * k, :]
    part = half_coeffs(got_h[...], got_l[...], zb_ref[piece.base : piece.base + piece.size, :])
    add_coeffs(out_ref, part, piece.masks[half:], k, width)
    one_h, one_l, two_h, two_l = [panel(i, *pair) for i in range(2) for pair in ((first_h, got_h), (first_l, got_l))]
    gram = dot_t(one_h, two_h) + (dot_t(one_h, two_l) + dot_t(one_l, two_h))
    for i in range(k // m):
        rows, part = slice((2 + i) * k, (3 + i) * k), gram[:, i * m : (i + 1) * m]
        out_ref[rows, :] = part if first else acc_ref[rows, :] + part
    for copy in copies:
        copy.wait()


def late(acc, got, firsts, zb, kept, piece, first, k, width):
    m = zb.shape[1] // 2
    rows = pltpu.VMEM(got.shape, BF16)
    return pl.pallas_call(
        functools.partial(late_kernel, piece, first, k, width),
        out_shape=[jax.ShapeDtypeStruct((2 * k + k * k // m, m), F32), jax.ShapeDtypeStruct(kept.shape, BF16)],
        in_specs=vmem_specs(5) + any_specs(1),
        out_specs=vmem_specs(1) + any_specs(1),
        input_output_aliases={5: 1},
        scratch_shapes=[rows] * 2 + [pltpu.SemaphoreType.DMA((2,))],
        compiler_params=pltpu.CompilerParams(vmem_limit_bytes=GRANT),
    )(acc, got, *firsts, zb, kept)


def apply_kernel(pieces, width, place_ref, mine_ref, other_ref, t_one_ref, t_two_ref, z_ref, kept_ref, *refs):
    out_ref, held, z_held, out_held, total_ref, x_ref, slot_ref, sems, z_sems, out_sems = refs
    k = t_one_ref.shape[0]
    m = z_ref.shape[1]
    loads, z_loads = [], []
    for p, piece in enumerate(pieces):
        lanes = pl.ds(piece.base, piece.size)
        loads.append(pltpu.make_async_copy(kept_ref.at[0, :, lanes], held.at[:, lanes], sems.at[p]))
        z_loads.append(pltpu.make_async_copy(z_ref.at[lanes, :], z_held.at[lanes, :], z_sems.at[p]))
        loads[p].start()
        z_loads[p].start()
    core = place_ref[1]
    half = mine_ref.shape[0]
    total_ref[block(core, half), :] = mine_ref[...]
    total_ref[block(1 - core, half), :] = other_ref[...]
    col = place_ref[0]

    def solve(t_ref, coeff, row):
        for mask in range(k // width):
            slot_ref[block(lax.bitwise_xor(col, mask), width), :] = coeff[mask * width : (mask + 1) * width, :]
        slot_ref[:k, :] = exact(t_ref[...], slot_ref[:k, :])
        for mask in range(k // width):
            x_ref[row + mask * width : row + (mask + 1) * width, :] = slot_ref[block(lax.bitwise_xor(col, mask), width), :]

    solve(t_two_ref, total_ref[k : 2 * k, :], k)
    coeff = total_ref[:k, :]
    for i in range(k // m):
        row = (2 + i) * k
        coeff = coeff - exact(total_ref[row : row + k, :], x_ref[k + i * m : k + (i + 1) * m, :])
    solve(t_one_ref, coeff, 0)
    stores = []
    for p, piece in enumerate(pieces):
        for pos, mask in enumerate(piece.masks):
            for which in range(2):
                low, row = (2 * pos + which) * width, which * k + mask * width
                slot_ref[low : low + width, :] = x_ref[row : row + width, :]
        x_h, x_l = split(slot_ref[...].T)
        x_both = jnp.concatenate([x_h, x_l], 0)
        loads[p].wait()
        z_loads[p].wait()
        rows = slice(piece.base, piece.base + piece.size)
        wide = dot(x_both, held[: 2 * k, rows])
        moved = wide[:m, :] + (wide[m:, :] + dot(x_h, held[2 * k :, rows]))
        out_held[rows, :] = z_held[rows, :] - moved.T
        lanes = pl.ds(piece.base, piece.size)
        stores.append(pltpu.make_async_copy(out_held.at[lanes, :], out_ref.at[lanes, :], out_sems.at[p]))
        stores[-1].start()
    for store in stores:
        store.wait()


def apply(place, mine, other, t_one, t_two, z, kept, pieces, width):
    k, m = t_one.shape[0], z.shape[1]
    rows = pltpu.VMEM(z.shape, F32)
    coeffs = pltpu.VMEM((2 * k, m), F32)
    return pl.pallas_call(
        functools.partial(apply_kernel, pieces, width),
        out_shape=jax.ShapeDtypeStruct(z.shape, F32),
        in_specs=SMEM + vmem_specs(4) + any_specs(2),
        out_specs=pl.BlockSpec(memory_space=pl.ANY),
        scratch_shapes=[pltpu.VMEM(kept.shape[1:], BF16), rows, rows, pltpu.VMEM((2 * mine.shape[0], m), F32)]
        + [coeffs, coeffs]
        + [pltpu.SemaphoreType.DMA((len(pieces),))] * 3,
        compiler_params=pltpu.CompilerParams(vmem_limit_bytes=GRANT),
    )(place, mine, other, t_one, t_two, z, kept)


def widen(data, masks, mask, size):
    got = lax.ppermute(data, "col", [(i, i ^ mask) for i in range(size)])
    return got, masks + [m ^ mask for m in masks]


def gather_pieces(own, size):
    unit = own.shape[1] // sum(SHARES)
    sizes = [unit * share for share in SHARES]
    pieces, halves = [], []
    for pair, early_steps, late_steps in ((0, (XA, XB), (YA, YB)), (2, (YA, YB), (XA, XB))):
        base = sum(sizes[:pair])
        data, masks = own[:, base : base + sizes[pair] + sizes[pair + 1]], [0]
        for step in early_steps:
            got, masks = widen(data, masks, step, size)
            data = jnp.concatenate([data, got], 0)
        for i, steps in ((0, late_steps), (1, late_steps[::-1])):
            low = i * sizes[pair]
            part = data[:, low : low + sizes[pair + i]]
            got, held = widen(part, masks, steps[0], size)
            part = jnp.concatenate([part, got], 0)
            got, held = widen(part, held, steps[1], size)
            pieces.append(Piece(base + low, sizes[pair + i], held))
            halves.append((part, got))
    return pieces, halves


def sum_over_row(part):
    r, m = part.shape
    group = PAIRS * NEAR
    rows = group * FAR
    pair = [(i, i ^ 1) for i in range(rows)]
    near = [[group * g + PAIRS * i + c for i in range(NEAR)] for g in range(FAR) for c in range(PAIRS)]
    far = [[i + group * g for g in range(FAR)] for i in range(group)]
    core = lax.axis_index("row") % PAIRS
    half = r // PAIRS
    kept = lax.dynamic_slice_in_dim(part, core * half, half, 0)
    given = lax.dynamic_slice_in_dim(part, (1 - core) * half, half, 0)
    mine = kept + lax.ppermute(given, "row", pair)
    blocks = lax.all_to_all(mine.reshape(NEAR, half // NEAR, m), "row", 0, 0, axis_index_groups=near, tiled=True)
    mine = jnp.sum(blocks, 0)
    blocks = lax.all_to_all(
        jnp.broadcast_to(mine[None], (FAR,) + mine.shape), "row", 0, 0, axis_index_groups=far, tiled=True
    )
    mine = jnp.sum(blocks, 0)
    blocks = lax.all_to_all(
        jnp.broadcast_to(mine[None], (NEAR,) + mine.shape), "row", 0, 0, axis_index_groups=near, tiled=True
    )
    mine = blocks.reshape(half, m)
    return mine, lax.ppermute(mine, "row", pair)


def body(size, z_slab, v_first, v_second, t_first, t_second):
    width = v_first.shape[1]
    k = t_first.shape[0]
    own = lax.optimization_barrier(jnp.concatenate([v_first.T, v_second.T], 0))
    pieces, halves = gather_pieces(own, size)
    place = jnp.stack([lax.axis_index("col"), lax.axis_index("row") % PAIRS]).astype(jnp.int32)
    place = lax.optimization_barrier(place)
    part, z_both, firsts, kept = early(z_slab, [half[0] for half in halves], pieces, k, width)
    for p, piece in enumerate(pieces):
        two = firsts[2 * p : 2 * p + 2]
        part, kept = late(part, halves[p][1], two, z_both, kept, piece, p == 0, k, width)
    mine, other = sum_over_row(part)
    return apply(place, mine, other, t_first, t_second, z_slab, kept, pieces, width)


def solution(mesh):
    placed = (P("row", "col"), P("row", "col"), P("row", "col"), P(), P())
    return jax.shard_map(
        functools.partial(body, mesh.shape["col"]),
        mesh=mesh,
        in_specs=placed,
        out_specs=P("row", "col"),
        check_vma=False,
    )
```

time: 152 us -> 143 us (0.941)
  starting transfers between devices: 41.7 us -> 55.8 us
  blocking collectives: 64.8 us -> 51.2 us
  waiting for transfers between devices: 19.3 us -> 11.8 us
    ppermute x8 -> x12, starting transfers between devices: 21.5 us -> 43.1 us  [widen(): got = lax.ppermute(data, 'col', [(i, i ^ mask) for i in range(size)])]
    all_to_all x1 -> x0, blocking collectives: 13 us -> none  [gather_line(): lax.all_to_all(spread, 'col', 0, 0, axis_index_groups=line(along_x), tile...]
    all_to_all x1 -> x0, starting transfers between devices: 7.22 us -> none  [gather_line(): lax.all_to_all(spread, 'col', 0, 0, axis_index_groups=line(along_x), tile...]
    all_to_all x1 -> x0, waiting for transfers between devices: 6.46 us -> none  [gather_line(): lax.all_to_all(spread, 'col', 0, 0, axis_index_groups=line(along_x), tile...]
    ppermute x8 -> x12, waiting for transfers between devices: 10.5 us -> 9.6 us  [widen(): got = lax.ppermute(data, 'col', [(i, i ^ mask) for i in range(size)])]
  transfers between devices with their start and end apart: 11 -> 14, of which waited for: 5 -> 5; matrix products, arithmetic and copies ran while one was open for 0% -> 0% of each run, Pallas kernels for 8% -> 8%
where the time goes in v7:
time: 143 us; the launch traced here: 142 us
  starting transfers between devices  55.8 us (39%)
  blocking collectives  51.2 us (36%)
  Pallas kernels  19.9 us (14%)
  waiting for transfers between devices  11.8 us (8%)
  other arithmetic  1.61 us (1%)
  local copies, waits for them, and re-layouts  1.59 us (1%)
    ppermute x12, starting transfers between devices, widen(): got = lax.ppermute(data, 'col', [(i, i ^ mask) for i in range(size)])  43.1 us
    all_to_all x1, blocking collectives, sum_over_row(): lax.all_to_all(jnp.broadcast_to(mine[None], (FAR,) + mine.shape), 'row',...  26.9 us
    all_to_all x1, blocking collectives, sum_over_row(): lax.all_to_all(jnp.broadcast_to(mine[None], (NEAR,) + mine.shape), 'row',...  12.6 us
    all_to_all x1, blocking collectives, sum_over_row(): lax.all_to_all(mine.reshape(NEAR, half // NEAR, m), 'row', 0, 0, axis_ind...  11.8 us
    pallas_call x4, Pallas kernels, late(): pl.pallas_call(functools.partial(late_kernel, piece, first, k, width), ou...  10.4 us
    ppermute x12, waiting for transfers between devices, widen(): got = lax.ppermute(data, 'col', [(i, i ^ mask) for i in range(size)])  9.6 us
    ppermute x1, starting transfers between devices, sum_over_row(): return (mine, lax.ppermute(mine, 'row', pair))  6.93 us
    pallas_call x1, Pallas kernels, apply(): pl.pallas_call(functools.partial(apply_kernel, pieces, width), out_shape=...  6.93 us
  transfers between devices with their start and end apart: 14, of which 5 were waited for; matrix products, arithmetic and copies ran while one was open for 0% of the time, Pallas kernels for 8%

profile of v7, /device:TPU:1, one launch (start us, length us, event | category | flops | bytes accessed | tf_op | source)
XLA Modules:
  0.0 142.3 jit_solution(11401741167195025488)
XLA Ops:
  0.0 1.0 pad_maximum_fusion.6
  1.1 3.9 %collective-permute-start = (f32[32,1536]{1,0:T(8,128)S(1)}, f32[32,1536]{1,0:T(8,128)S(1)}, u32[]{:S(2)}, u32[]{:S(2)}) collective-permute-start(f32[32,1536]{1,0:T(8,128)S(1)} %get-tuple-element.44), channel_id=1, source_target_pairs={{0,1},{1,0},{2,3},{3,2},{4,5},{5,4},{6,7},{7,6},{8,9},{9,8},{10,11... | collective-permute-start | bytes 589832 | tf_op jit(solution)/shard_map/ppermute | solution.py:221
  5.0 3.2 %collective-permute-start.4 = (f32[32,1536]{1,0:T(8,128)S(1)}, f32[32,1536]{1,0:T(8,128)S(1)}, u32[]{:S(2)}, u32[]{:S(2)}) collective-permute-start(f32[32,1536]{1,0:T(8,128)S(1)} %get-tuple-element.43), channel_id=1, source_target_pairs={{0,4},{1,5},{2,6},{3,7},{4,0},{5,1},{6,2},{7,3},{8,12},{9,13},{10,... | collective-permute-start | bytes 589832 | tf_op jit(solution)/shard_map/ppermute | solution.py:221
  8.3 0.0 collective-permute-done
  8.3 5.7 %collective-permute-start.1 = (f32[64,1536]{1,0:T(8,128)S(1)}, f32[64,1536]{1,0:T(8,128)S(1)}, u32[]{:S(2)}, u32[]{:S(2)}) collective-permute-start(f32[64,1536]{1,0:T(8,128)S(1)} %pad_maximum_fusion.7), channel_id=1, source_target_pairs={{0,3},{1,2},{2,1},{3,0},{4,7},{5,6},{6,5},{7,4},{8,11},{9,10},{10,... | collective-permute-start | bytes 1179656 | tf_op jit(solution)/shard_map/ppermute | solution.py:221
  14.0 0.0 collective-permute-done.4
  14.1 4.6 %collective-permute-start.5 = (f32[64,1536]{1,0:T(8,128)S(1)}, f32[64,1536]{1,0:T(8,128)S(1)}, u32[]{:S(2)}, u32[]{:S(2)}) collective-permute-start(f32[64,1536]{1,0:T(8,128)S(1)} %pad_maximum_fusion.8), channel_id=1, source_target_pairs={{0,12},{1,13},{2,14},{3,15},{4,8},{5,9},{6,10},{7,11},{8,4},{9,5},... | collective-permute-start | bytes 1179656 | tf_op jit(solution)/shard_map/ppermute | solution.py:221
  18.7 0.5 collective-permute-done.1
  19.2 0.1 pad_maximum_fusion.2
  19.3 4.9 %collective-permute-start.2 = (f32[128,896]{1,0:T(8,128)S(1)}, f32[128,896]{1,0:T(8,128)S(1)}, u32[]{:S(2)}, u32[]{:S(2)}) collective-permute-start(f32[128,896]{1,0:T(8,128)S(1)} %slice.25), channel_id=1, source_target_pairs={{0,4},{1,5},{2,6},{3,7},{4,0},{5,1},{6,2},{7,3},{8,12},{9,13},{10,... | collective-permute-start | bytes 1376264 | tf_op jit(solution)/shard_map/ppermute | solution.py:221
  24.2 1.1 collective-permute-done.5
  25.3 0.1 pad_maximum_fusion.3
  25.4 1.9 %collective-permute-start.6 = (f32[128,896]{1,0:T(8,128)S(1)}, f32[128,896]{1,0:T(8,128)S(1)}, u32[]{:S(2)}, u32[]{:S(2)}) collective-permute-start(f32[128,896]{1,0:T(8,128)S(1)} %slice.27), channel_id=1, source_target_pairs={{0,1},{1,0},{2,3},{3,2},{4,5},{5,4},{6,7},{7,6},{8,9},{9,8},{10,11... | collective-permute-start | bytes 1376264 | tf_op jit(solution)/shard_map/ppermute | solution.py:221
  27.3 5.3 %collective-permute-start.3 = (f32[128,640]{1,0:T(8,128)S(1)}, f32[128,640]{1,0:T(8,128)S(1)}, u32[]{:S(2)}, u32[]{:S(2)}) collective-permute-start(f32[128,640]{1,0:T(8,128)S(1)} %pad_maximum_fusion.10), channel_id=1, source_target_pairs={{0,12},{1,13},{2,14},{3,15},{4,8},{5,9},{6,10},{7,11},{8,4},{9,5},... | collective-permute-start | bytes 983048 | tf_op jit(solution)/shard_map/ppermute | solution.py:221
  32.7 3.0 %collective-permute-start.7 = (f32[128,640]{1,0:T(8,128)S(1)}, f32[128,640]{1,0:T(8,128)S(1)}, u32[]{:S(2)}, u32[]{:S(2)}) collective-permute-start(f32[128,640]{1,0:T(8,128)S(1)} %pad_maximum_fusion.9), channel_id=1, source_target_pairs={{0,3},{1,2},{2,1},{3,0},{4,7},{5,6},{6,5},{7,4},{8,11},{9,10},{10,... | collective-permute-start | bytes 983048 | tf_op jit(solution)/shard_map/ppermute | solution.py:221
  35.7 0.0 collective-permute-done.2
  35.7 0.1 pad_maximum_fusion.refs_0_
  35.7 2.4 %collective-permute-start.8 = (f32[256,896]{1,0:T(8,128)S(1)}, f32[256,896]{1,0:T(8,128)}, u32[]{:S(2)}, u32[]{:S(2)}) collective-permute-start(f32[256,896]{1,0:T(8,128)S(1)} %pad_maximum_fusion.refs_0_), channel_id=1, source_target_pairs={{0,12},{1,13},{2,14},{3,15},{4,8},{5,9},{6,10},{7,11},{8,4},{9,5},... | collective-permute-start | bytes 2752520 | tf_op jit(solution)/shard_map/ppermute | solution.py:221
  38.2 0.0 collective-permute-done.6
  38.2 0.1 pad_maximum_fusion.1.refs_2_
  38.3 4.2 %collective-permute-start.10 = (f32[256,896]{1,0:T(8,128)S(1)}, f32[256,896]{1,0:T(8,128)}, u32[]{:S(2)}, u32[]{:S(2)}) collective-permute-start(f32[256,896]{1,0:T(8,128)S(1)} %pad_maximum_fusion.1.refs_2_), channel_id=1, source_target_pairs={{0,3},{1,2},{2,1},{3,0},{4,7},{5,6},{6,5},{7,4},{8,11},{9,10},{10,... | collective-permute-start | bytes 2752520 | tf_op jit(solution)/shard_map/ppermute | solution.py:221
  42.5 0.0 collective-permute-done.3
  42.6 1.9 %collective-permute-start.9 = (f32[256,640]{1,0:T(8,128)S(1)}, f32[256,640]{1,0:T(8,128)}, u32[]{:S(2)}, u32[]{:S(2)}) collective-permute-start(f32[256,640]{1,0:T(8,128)S(1)} %pad_maximum_fusion.4.refs_1_), channel_id=1, source_target_pairs={{0,4},{1,5},{2,6},{3,7},{4,0},{5,1},{6,2},{7,3},{8,12},{9,13},{10,... | collective-permute-start | bytes 1966088 | tf_op jit(solution)/shard_map/ppermute | solution.py:221
  44.5 0.0 collective-permute-done.7
  44.6 1.9 %collective-permute-start.11 = (f32[256,640]{1,0:T(8,128)S(1)}, f32[256,640]{1,0:T(8,128)}, u32[]{:S(2)}, u32[]{:S(2)}) collective-permute-start(f32[256,640]{1,0:T(8,128)S(1)} %pad_maximum_fusion.5.refs_3_), channel_id=1, source_target_pairs={{0,1},{1,0},{2,3},{3,2},{4,5},{5,4},{6,7},{7,6},{8,9},{9,8},{10,11... | collective-permute-start | bytes 1966088 | tf_op jit(solution)/shard_map/ppermute | solution.py:221
  46.5 0.0 copy-start
  46.5 1.4 copy-done
  47.9 2.6 %shard_map.55 = (f32[512,128]{1,0:T(8,128)S(1)}, bf16[3072,256]{1,0:T(8,128)(2,1)S(1)}, bf16[256,896]{1,0:T(8,128)(2,1)S(1)}, bf16[256,896]{1,0:T(8,128)(2,1)S(1...) custom-call(f32[3072,128]{1,0:T(8,128)S(1)} %copy-done, ...), custom_call_target="tpu_custom_call" | custom-call | flops 603979776 | bytes 12582912 | tf_op jit(solution)/shard_map/pallas_call | solution.py:101
  50.5 8.0 %collective-permute-done.8.got_ref = f32[256,896]{1,0:T(8,128)} collective-permute-done((f32[256,896]{1,0:T(8,128)S(1)}, f32[256,896]{1,0:T(8,128)}, u32[]{:S(2)}, u32[]{:S(2)}) %collective-permute-start.8) | collective-permute-done | bytes 917536 | tf_op jit(solution)/shard_map/ppermute | solution.py:221
  58.5 2.9 %shard_map.56 = (f32[1024,128]{1,0:T(8,128)S(1)}, bf16[6,1024,3072]{2,1,0:T(8,128)(2,1)}) custom-call(f32[512,128]{1,0:T(8,128)S(1)} %get-tuple-element.24.acc_ref, f32[256,896]{1,0:T(8,128)} %collective-permute-done.8.got_ref, bf16[256,896]{1,0:T(8,128)(2,1)S(1)} %get-tuple-element.25.first_h, ...), custom_call_target="tpu_custom_call", output_to_operand_aliasing={{1}: (5, {})} | custom-call | tf_op jit(solution)/shard_map/pallas_call | solution.py:142
  61.4 0.0 collective-permute-done.9.got_ref
  61.5 2.2 %shard_map.57 = (f32[1024,128]{1,0:T(8,128)S(1)}, bf16[6,1024,3072]{2,1,0:T(8,128)(2,1)}) custom-call(f32[1024,128]{1,0:T(8,128)S(1)} %get-tuple-element.29.acc_ref, f32[256,640]{1,0:T(8,128)} %collective-permute-done.9.got_ref, bf16[256,640]{1,0:T(8,128)(2,1)S(1)} %get-tuple-element.30.first_h, ...), custom_call_target="tpu_custom_call", output_to_operand_aliasing={{1}: (5, {})} | custom-call | tf_op jit(solution)/shard_map/pallas_call | solution.py:142
  63.7 0.0 collective-permute-done.10.got_ref
  63.7 0.0 copy-start.1
  63.7 0.0 copy-start.2
  63.7 0.0 copy-start.3
  63.7 3.0 %shard_map.58 = (f32[1024,128]{1,0:T(8,128)S(1)}, bf16[6,1024,3072]{2,1,0:T(8,128)(2,1)}) custom-call(f32[1024,128]{1,0:T(8,128)S(1)} %get-tuple-element.33.acc_ref, f32[256,896]{1,0:T(8,128)} %collective-permute-done.10.got_ref, bf16[256,896]{1,0:T(8,128)(2,1)S(1)} %get-tuple-element.34.first_h, ...), custom_call_target="tpu_custom_call", output_to_operand_aliasing={{1}: (5, {})} | custom-call | tf_op jit(solution)/shard_map/pallas_call | solution.py:142
  66.8 0.0 collective-permute-done.11.got_ref
  66.8 2.2 %shard_map.59 = (f32[1024,128]{1,0:T(8,128)S(1)}, bf16[6,1024,3072]{2,1,0:T(8,128)(2,1)}) custom-call(f32[1024,128]{1,0:T(8,128)S(1)} %get-tuple-element.37.acc_ref, f32[256,640]{1,0:T(8,128)} %collective-permute-done.11.got_ref, bf16[256,640]{1,0:T(8,128)(2,1)S(1)} %get-tuple-element.38.first_h, ...), custom_call_target="tpu_custom_call", output_to_operand_aliasing={{1}: (5, {})} | custom-call | tf_op jit(solution)/shard_map/pallas_call | solution.py:142
  69.0 5.8 %collective-permute-start.12 = (f32[512,128]{1,0:T(8,128)S(1)}, f32[512,128]{1,0:T(8,128)S(1)}, u32[]{:S(2)}, u32[]{:S(2)}) collective-permute-start(f32[512,128]{1,0:T(8,128)S(1)} %constant_dynamic-slice_fusion), channel_id=1, source_target_pairs={{0,16},{16,0},{32,48},{48,32},{64,80},{80,64},{96,112},{112,96},{1... | collective-permute-start | bytes 786440 | tf_op jit(solution)/shard_map/ppermute | solution.py:257
  74.8 1.1 collective-permute-done.12
  76.0 11.8 %all_to_all.15 = f32[4,128,128]{2,1,0:T(8,128)S(1)} all-to-all(f32[4,128,128]{2,1,0:T(8,128)S(1)} %bitcast.8), channel_id=1, replica_groups={{0,32,64,96},{16,48,80,112},{128,160,192,224},{144,176,208,240},{256,28..., dimensions={0} | all-to-all | bytes 524288 | tf_op jit(solution)/shard_map/all_to_all | solution.py:258
  87.8 26.9 %all_to_all.16 = f32[4,128,128]{2,1,0:T(8,128)S(1)} all-to-all(f32[4,128,128]{2,1,0:T(8,128)S(1)} %broadcast_in_dim.4), channel_id=1, replica_groups={{0,128,256,384},{16,144,272,400},{32,160,288,416},{48,176,304,432},{64,..., dimensions={0} | all-to-all | bytes 524288 | tf_op jit(solution)/shard_map/all_to_all | solution.py:260
  114.7 12.6 %all_to_all.17 = f32[4,128,128]{2,1,0:T(8,128)S(1)} all-to-all(f32[4,128,128]{2,1,0:T(8,128)S(1)} %broadcast_in_dim.5), channel_id=1, replica_groups={{0,32,64,96},{16,48,80,112},{128,160,192,224},{144,176,208,240},{256,28..., dimensions={0} | all-to-all | bytes 524288 | tf_op jit(solution)/shard_map/all_to_all | solution.py:264
  127.3 6.9 %collective-permute-start.13 = (f32[512,128]{1,0:T(8,128)S(1)}, f32[512,128]{1,0:T(8,128)S(1)}, u32[]{:S(2)}, u32[]{:S(2)}) collective-permute-start(f32[512,128]{1,0:T(8,128)S(1)} %bitcast.6), channel_id=1, source_target_pairs={{0,16},{16,0},{32,48},{48,32},{64,80},{80,64},{96,112},{112,96},{1... | collective-permute-start | bytes 786440 | tf_op jit(solution)/shard_map/ppermute | solution.py:268
  134.2 0.1 pad_add_fusion.place_ref
  134.3 1.1 collective-permute-done.13.other_ref
  135.3 0.0 copy-done.1
  135.4 0.0 copy-done.2
  135.4 0.0 copy-done.3
  135.4 6.9 %shard_map.60 = f32[3072,128]{1,0:T(8,128)} custom-call(s32[2]{0:T(128)S(1)} %pad_add_fusion.place_ref, f32[512,128]{1,0:T(8,128)S(1)} %bitcast.7, f32[512,128]{1,0:T(8,128)S(1)} %collective-permute-done.13.other_ref, f32[256,256]{1,0:T(8,128)S(1)} %copy-done.2, f32[256,256]{1,0:T(8,128)S(1)} %copy-done.3, f32[3072,128]{1,0:T(8,128)S(1)} %copy-done.1, ...), custom_call_target="tpu_custom_call" | custom-call | tf_op jit(solution)/shard_map/pallas_call | solution.py:208
  (15 shorter events, 0.4 us)
Async XLA Ops:
  1.1 7.2 %collective-permute-start = (f32[32,1536]{1,0:T(8,128)S(1)}, f32[32,1536]{1,0:T(8,128)S(1)}, u32[]{:S(2)}, u32[]{:S(2)}) collective-permute-start(f32[32,1536]{1,0:T(8,128)S(1)} %get-tuple-element.44), channel_id=1, source_target_pairs={{0,1},{1,0},{2,3},{3,2},{4,5},{5,4},{6,7},{7,6},{8,9},{9,8},{10,11... | collective-permute-start | bytes 589832 | tf_op jit(solution)/shard_map/ppermute | solution.py:221
  5.0 9.0 %collective-permute-start.4 = (f32[32,1536]{1,0:T(8,128)S(1)}, f32[32,1536]{1,0:T(8,128)S(1)}, u32[]{:S(2)}, u32[]{:S(2)}) collective-permute-start(f32[32,1536]{1,0:T(8,128)S(1)} %get-tuple-element.43), channel_id=1, source_target_pairs={{0,4},{1,5},{2,6},{3,7},{4,0},{5,1},{6,2},{7,3},{8,12},{9,13},{10,... | collective-permute-start | bytes 589832 | tf_op jit(solution)/shard_map/ppermute | solution.py:221
  8.3 10.9 %collective-permute-start.1 = (f32[64,1536]{1,0:T(8,128)S(1)}, f32[64,1536]{1,0:T(8,128)S(1)}, u32[]{:S(2)}, u32[]{:S(2)}) collective-permute-start(f32[64,1536]{1,0:T(8,128)S(1)} %pad_maximum_fusion.7), channel_id=1, source_target_pairs={{0,3},{1,2},{2,1},{3,0},{4,7},{5,6},{6,5},{7,4},{8,11},{9,10},{10,... | collective-permute-start | bytes 1179656 | tf_op jit(solution)/shard_map/ppermute | solution.py:221
  14.1 11.2 %collective-permute-start.5 = (f32[64,1536]{1,0:T(8,128)S(1)}, f32[64,1536]{1,0:T(8,128)S(1)}, u32[]{:S(2)}, u32[]{:S(2)}) collective-permute-start(f32[64,1536]{1,0:T(8,128)S(1)} %pad_maximum_fusion.8), channel_id=1, source_target_pairs={{0,12},{1,13},{2,14},{3,15},{4,8},{5,9},{6,10},{7,11},{8,4},{9,5},... | collective-permute-start | bytes 1179656 | tf_op jit(solution)/shard_map/ppermute | solution.py:221
  19.3 16.4 %collective-permute-start.2 = (f32[128,896]{1,0:T(8,128)S(1)}, f32[128,896]{1,0:T(8,128)S(1)}, u32[]{:S(2)}, u32[]{:S(2)}) collective-permute-start(f32[128,896]{1,0:T(8,128)S(1)} %slice.25), channel_id=1, source_target_pairs={{0,4},{1,5},{2,6},{3,7},{4,0},{5,1},{6,2},{7,3},{8,12},{9,13},{10,... | collective-permute-start | bytes 1376264 | tf_op jit(solution)/shard_map/ppermute | solution.py:221
  25.4 12.8 %collective-permute-start.6 = (f32[128,896]{1,0:T(8,128)S(1)}, f32[128,896]{1,0:T(8,128)S(1)}, u32[]{:S(2)}, u32[]{:S(2)}) collective-permute-start(f32[128,896]{1,0:T(8,128)S(1)} %slice.27), channel_id=1, source_target_pairs={{0,1},{1,0},{2,3},{3,2},{4,5},{5,4},{6,7},{7,6},{8,9},{9,8},{10,11... | collective-permute-start | bytes 1376264 | tf_op jit(solution)/shard_map/ppermute | solution.py:221
  27.3 15.2 %collective-permute-start.3 = (f32[128,640]{1,0:T(8,128)S(1)}, f32[128,640]{1,0:T(8,128)S(1)}, u32[]{:S(2)}, u32[]{:S(2)}) collective-permute-start(f32[128,640]{1,0:T(8,128)S(1)} %pad_maximum_fusion.10), channel_id=1, source_target_pairs={{0,12},{1,13},{2,14},{3,15},{4,8},{5,9},{6,10},{7,11},{8,4},{9,5},... | collective-permute-start | bytes 983048 | tf_op jit(solution)/shard_map/ppermute | solution.py:221
  32.7 11.8 %collective-permute-start.7 = (f32[128,640]{1,0:T(8,128)S(1)}, f32[128,640]{1,0:T(8,128)S(1)}, u32[]{:S(2)}, u32[]{:S(2)}) collective-permute-start(f32[128,640]{1,0:T(8,128)S(1)} %pad_maximum_fusion.9), channel_id=1, source_target_pairs={{0,3},{1,2},{2,1},{3,0},{4,7},{5,6},{6,5},{7,4},{8,11},{9,10},{10,... | collective-permute-start | bytes 983048 | tf_op jit(solution)/shard_map/ppermute | solution.py:221
  35.7 22.8 %collective-permute-start.8 = (f32[256,896]{1,0:T(8,128)S(1)}, f32[256,896]{1,0:T(8,128)}, u32[]{:S(2)}, u32[]{:S(2)}) collective-permute-start(f32[256,896]{1,0:T(8,128)S(1)} %pad_maximum_fusion.refs_0_), channel_id=1, source_target_pairs={{0,12},{1,13},{2,14},{3,15},{4,8},{5,9},{6,10},{7,11},{8,4},{9,5},... | collective-permute-start | bytes 2752520 | tf_op jit(solution)/shard_map/ppermute | solution.py:221
  38.3 25.4 %collective-permute-start.10 = (f32[256,896]{1,0:T(8,128)S(1)}, f32[256,896]{1,0:T(8,128)}, u32[]{:S(2)}, u32[]{:S(2)}) collective-permute-start(f32[256,896]{1,0:T(8,128)S(1)} %pad_maximum_fusion.1.refs_2_), channel_id=1, source_target_pairs={{0,3},{1,2},{2,1},{3,0},{4,7},{5,6},{6,5},{7,4},{8,11},{9,10},{10,... | collective-permute-start | bytes 2752520 | tf_op jit(solution)/shard_map/ppermute | solution.py:221
  42.6 18.9 %collective-permute-start.9 = (f32[256,640]{1,0:T(8,128)S(1)}, f32[256,640]{1,0:T(8,128)}, u32[]{:S(2)}, u32[]{:S(2)}) collective-permute-start(f32[256,640]{1,0:T(8,128)S(1)} %pad_maximum_fusion.4.refs_1_), channel_id=1, source_target_pairs={{0,4},{1,5},{2,6},{3,7},{4,0},{5,1},{6,2},{7,3},{8,12},{9,13},{10,... | collective-permute-start | bytes 1966088 | tf_op jit(solution)/shard_map/ppermute | solution.py:221
  44.6 22.2 %collective-permute-start.11 = (f32[256,640]{1,0:T(8,128)S(1)}, f32[256,640]{1,0:T(8,128)}, u32[]{:S(2)}, u32[]{:S(2)}) collective-permute-start(f32[256,640]{1,0:T(8,128)S(1)} %pad_maximum_fusion.5.refs_3_), channel_id=1, source_target_pairs={{0,1},{1,0},{2,3},{3,2},{4,5},{5,4},{6,7},{7,6},{8,9},{9,8},{10,11... | collective-permute-start | bytes 1966088 | tf_op jit(solution)/shard_map/ppermute | solution.py:221
  46.5 1.4 copy-start
  63.7 71.7 %copy-start.1 = (f32[3072,128]{1,0:T(8,128)S(1)}, f32[3072,128]{1,0:T(8,128)}, u32[]{:S(2)}) copy-start(f32[3072,128]{1,0:T(8,128)} %z_ref.3) | copy-start | bytes 4718596
  63.7 71.7 %copy-start.2 = (f32[256,256]{1,0:T(8,128)S(1)}, f32[256,256]{1,0:T(8,128)}, u32[]{:S(2)}) copy-start(f32[256,256]{1,0:T(8,128)} %t_one_ref.1) | copy-start | bytes 786436
  63.7 71.6 %copy-start.3 = (f32[256,256]{1,0:T(8,128)S(1)}, f32[256,256]{1,0:T(8,128)}, u32[]{:S(2)}) copy-start(f32[256,256]{1,0:T(8,128)} %t_two_ref.1) | copy-start | bytes 786436
  69.0 6.9 %collective-permute-start.12 = (f32[512,128]{1,0:T(8,128)S(1)}, f32[512,128]{1,0:T(8,128)S(1)}, u32[]{:S(2)}, u32[]{:S(2)}) collective-permute-start(f32[512,128]{1,0:T(8,128)S(1)} %constant_dynamic-slice_fusion), channel_id=1, source_target_pairs={{0,16},{16,0},{32,48},{48,32},{64,80},{80,64},{96,112},{112,96},{1... | collective-permute-start | bytes 786440 | tf_op jit(solution)/shard_map/ppermute | solution.py:257
  127.3 8.1 %collective-permute-start.13 = (f32[512,128]{1,0:T(8,128)S(1)}, f32[512,128]{1,0:T(8,128)S(1)}, u32[]{:S(2)}, u32[]{:S(2)}) collective-permute-start(f32[512,128]{1,0:T(8,128)S(1)} %bitcast.6), channel_id=1, source_target_pairs={{0,16},{16,0},{32,48},{48,32},{64,80},{80,64},{96,112},{112,96},{1... | collective-permute-start | bytes 786440 | tf_op jit(solution)/shard_map/ppermute | solution.py:268

commit v8 on v7

--- a/solution.py
+++ b/solution.py
@@ -26,13 +26,15 @@
     return lax.dot_general(left, right, (((1,), (1,)), ((), ())), preferred_element_type=F32)
 
 
-def exact(left, right):
-    return jnp.dot(left, right, precision=lax.Precision.HIGHEST, preferred_element_type=F32)
-
-
 def split(x):
     high = x.astype(BF16)
     return high, (x - high.astype(F32)).astype(BF16)
+
+
+def thrice(left, right):
+    left_h, left_l = split(left)
+    right_h, right_l = split(right)
+    return dot(left_h, right_h) + (dot(left_h, right_l) + dot(left_l, right_h))
 
 
 class Piece:
@@ -110,44 +112,58 @@
     return out[0], out[1], out[2:-1], out[-1]
 
 
-def late_kernel(piece, first, k, width, acc_ref, got_ref, first_h, first_l, zb_ref, _, *refs):
-    out_ref, kept, got_h, got_l, sems = refs
+def late_kernel(pieces, k, width, acc_ref, zb_ref, *refs):
+    count = len(pieces)
+    firsts, gots, out_ref, kept = refs[: 2 * count], refs[2 * count : 3 * count], refs[3 * count + 1], refs[3 * count + 2]
+    scratch = refs[3 * count + 3 :]
+    raw, pairs, load_sems, sems = scratch[:count], scratch[count : 3 * count], scratch[-2], scratch[-1]
     m = zb_ref.shape[1] // 2
-    got_h[...], got_l[...] = split(got_ref[...])
-    copies = [keep(half, kept, (2 * i + 1) * k, piece.base, sems.at[i]) for i, half in enumerate((got_h, got_l))]
     half = k // (2 * width)
-
-    def panel(which, own, got):
-        blocks = [None] * (2 * half)
-        for pos, mask in enumerate(piece.masks):
-            ref, low = (own, got)[pos // half], (pos % half * 2 + which) * width
-            blocks[mask] = ref[low : low + width, :]
-        return jnp.concatenate(blocks, 0)
-
-    out_ref[: 2 * k, :] = acc_ref[: 2 * k, :]
-    part = half_coeffs(got_h[...], got_l[...], zb_ref[piece.base : piece.base + piece.size, :])
-    add_coeffs(out_ref, part, piece.masks[half:], k, width)
-    one_h, one_l, two_h, two_l = [panel(i, *pair) for i in range(2) for pair in ((first_h, got_h), (first_l, got_l))]
-    gram = dot_t(one_h, two_h) + (dot_t(one_h, two_l) + dot_t(one_l, two_h))
-    for i in range(k // m):
-        rows, part = slice((2 + i) * k, (3 + i) * k), gram[:, i * m : (i + 1) * m]
-        out_ref[rows, :] = part if first else acc_ref[rows, :] + part
+    loads = [pltpu.make_async_copy(gots[p], raw[p], load_sems.at[p]) for p in range(count)]
+    for load in loads:
+        load.start()
+    out_ref[: 2 * k, :] = acc_ref[...]
+    copies = []
+    for p, piece in enumerate(pieces):
+        got = pairs[2 * p : 2 * p + 2]
+        loads[p].wait()
+        got[0][...], got[1][...] = split(raw[p][...])
+        for i in range(2):
+            copies.append(keep(got[i], kept, (2 * i + 1) * k, piece.base, sems.at[2 * p + i]))
+
+        def panel(which, i):
+            blocks = [None] * (2 * half)
+            for pos, mask in enumerate(piece.masks):
+                ref, low = (firsts[2 * p + i], got[i])[pos // half], (pos % half * 2 + which) * width
+                blocks[mask] = ref[low : low + width, :]
+            return jnp.concatenate(blocks, 0)
+
+        part = half_coeffs(got[0][...], got[1][...], zb_ref[piece.base : piece.base + piece.size, :])
+        add_coeffs(out_ref, part, piece.masks[half:], k, width)
+        one_h, one_l, two_h, two_l = [panel(which, i) for which in range(2) for i in range(2)]
+        gram = dot_t(one_h, two_h) + (dot_t(one_h, two_l) + dot_t(one_l, two_h))
+        for i in range(k // m):
+            rows, part = slice((2 + i) * k, (3 + i) * k), gram[:, i * m : (i + 1) * m]
+            out_ref[rows, :] = part if p == 0 else out_ref[rows, :] + part
     for copy in copies:
         copy.wait()
 
 
-def late(acc, got, firsts, zb, kept, piece, first, k, width):
+def late(acc, zb, firsts, gots, kept, pieces, k, width):
     m = zb.shape[1] // 2
-    rows = pltpu.VMEM(got.shape, BF16)
+    count = len(pieces)
+    dma = pltpu.SemaphoreType.DMA
     return pl.pallas_call(
-        functools.partial(late_kernel, piece, first, k, width),
+        functools.partial(late_kernel, pieces, k, width),
         out_shape=[jax.ShapeDtypeStruct((2 * k + k * k // m, m), F32), jax.ShapeDtypeStruct(kept.shape, BF16)],
-        in_specs=vmem_specs(5) + any_specs(1),
+        in_specs=vmem_specs(2 + 2 * count) + any_specs(count + 1),
         out_specs=vmem_specs(1) + any_specs(1),
-        input_output_aliases={5: 1},
-        scratch_shapes=[rows] * 2 + [pltpu.SemaphoreType.DMA((2,))],
+        input_output_aliases={2 + 3 * count: 1},
+        scratch_shapes=[pltpu.VMEM(got.shape, F32) for got in gots]
+        + [pltpu.VMEM(got.shape, BF16) for got in gots for _ in range(2)]
+        + [dma((count,)), dma((2 * count,))],
         compiler_params=pltpu.CompilerParams(vmem_limit_bytes=GRANT),
-    )(acc, got, *firsts, zb, kept)
+    )(acc, zb, *firsts, *gots, kept)
 
 
 def apply_kernel(pieces, width, place_ref, mine_ref, other_ref, t_one_ref, t_two_ref, z_ref, kept_ref, *refs):
@@ -170,7 +186,7 @@
     def solve(t_ref, coeff, row):
         for mask in range(k // width):
             slot_ref[block(lax.bitwise_xor(col, mask), width), :] = coeff[mask * width : (mask + 1) * width, :]
-        slot_ref[:k, :] = exact(t_ref[...], slot_ref[:k, :])
+        slot_ref[:k, :] = thrice(t_ref[...], slot_ref[:k, :])
         for mask in range(k // width):
             x_ref[row + mask * width : row + (mask + 1) * width, :] = slot_ref[block(lax.bitwise_xor(col, mask), width), :]
 
@@ -178,7 +194,7 @@
     coeff = total_ref[:k, :]
     for i in range(k // m):
         row = (2 + i) * k
-        coeff = coeff - exact(total_ref[row : row + k, :], x_ref[k + i * m : k + (i + 1) * m, :])
+        coeff = coeff - thrice(total_ref[row : row + k, :], x_ref[k + i * m : k + (i + 1) * m, :])
     solve(t_one_ref, coeff, 0)
     stores = []
     for p, piece in enumerate(pieces):
@@ -276,9 +292,7 @@
     place = jnp.stack([lax.axis_index("col"), lax.axis_index("row") % PAIRS]).astype(jnp.int32)
     place = lax.optimization_barrier(place)
     part, z_both, firsts, kept = early(z_slab, [half[0] for half in halves], pieces, k, width)
-    for p, piece in enumerate(pieces):
-        two = firsts[2 * p : 2 * p + 2]
-        part, kept = late(part, halves[p][1], two, z_both, kept, piece, p == 0, k, width)
+    part, kept = late(part, z_both, firsts, [half[1] for half in halves], kept, pieces, k, width)
     mine, other = sum_over_row(part)
     return apply(place, mine, other, t_first, t_second, z_slab, kept, pieces, width)
 

time: 143 us -> 141 us (0.986)
  Pallas kernels: 19.9 us -> 14.9 us
  waiting for transfers between devices: 11.8 us -> 13.8 us
  other arithmetic: 1.61 us -> 3.29 us
    pallas_call x4 -> x1, Pallas kernels: 10.4 us -> 5.4 us  [late(): pl.pallas_call(functools.partial(late_kernel, pieces, k, width), out_shap...]
    ppermute x12, waiting for transfers between devices: 9.6 us -> 11.6 us  [widen(): got = lax.ppermute(data, 'col', [(i, i ^ mask) for i in range(size)])]
    concatenate x4, other arithmetic: 0.21 us -> 1.89 us  [gather_pieces(): part = jnp.concatenate([part, got], 0)]
  transfers between devices with their start and end apart: 14 -> 14, of which waited for: 5 -> 7; matrix products, arithmetic and copies ran while one was open for 0% -> 2% of each run, Pallas kernels for 8% -> 3%
where the time goes in v8:
time: 141 us; the launch traced here: 140 us
  starting transfers between devices  55.8 us (40%)
  blocking collectives  52 us (37%)
  Pallas kernels  14.9 us (11%)
  waiting for transfers between devices  13.8 us (10%)
  other arithmetic  3.29 us (2%)
    ppermute x12, starting transfers between devices, widen(): got = lax.ppermute(data, 'col', [(i, i ^ mask) for i in range(size)])  42.8 us
    all_to_all x1, blocking collectives, sum_over_row(): lax.all_to_all(jnp.broadcast_to(mine[None], (FAR,) + mine.shape), 'row',...  26.9 us
    all_to_all x1, blocking collectives, sum_over_row(): lax.all_to_all(mine.reshape(NEAR, half // NEAR, m), 'row', 0, 0, axis_ind...  12.6 us
    all_to_all x1, blocking collectives, sum_over_row(): lax.all_to_all(jnp.broadcast_to(mine[None], (NEAR,) + mine.shape), 'row',...  12.6 us
    ppermute x12, waiting for transfers between devices, widen(): got = lax.ppermute(data, 'col', [(i, i ^ mask) for i in range(size)])  11.6 us
    ppermute x1, starting transfers between devices, sum_over_row(): return (mine, lax.ppermute(mine, 'row', pair))  6.93 us
    ppermute x1, starting transfers between devices, sum_over_row(): mine = kept + lax.ppermute(given, 'row', pair)  6.05 us
    pallas_call x1, Pallas kernels, apply(): pl.pallas_call(functools.partial(apply_kernel, pieces, width), out_shape=...  5.82 us
  transfers between devices with their start and end apart: 14, of which 7 were waited for; matrix products, arithmetic and copies ran while one was open for 2% of the time, Pallas kernels for 3%

profile of v8, /device:TPU:1, one launch (start us, length us, event | category | flops | bytes accessed | tf_op | source)
XLA Modules:
  0.0 140.3 jit_solution(8247621404116531150)
XLA Ops:
  0.0 1.0 pad_maximum_fusion.6
  1.1 4.0 %collective-permute-start.4 = (f32[32,1536]{1,0:T(8,128)S(1)}, f32[32,1536]{1,0:T(8,128)S(1)}, u32[]{:S(2)}, u32[]{:S(2)}) collective-permute-start(f32[32,1536]{1,0:T(8,128)S(1)} %get-tuple-element.31), channel_id=1, source_target_pairs={{0,4},{1,5},{2,6},{3,7},{4,0},{5,1},{6,2},{7,3},{8,12},{9,13},{10,... | collective-permute-start | bytes 589832 | tf_op jit(solution)/shard_map/ppermute | solution.py:237
  5.1 3.1 %collective-permute-start = (f32[32,1536]{1,0:T(8,128)S(1)}, f32[32,1536]{1,0:T(8,128)S(1)}, u32[]{:S(2)}, u32[]{:S(2)}) collective-permute-start(f32[32,1536]{1,0:T(8,128)S(1)} %get-tuple-element.32), channel_id=1, source_target_pairs={{0,1},{1,0},{2,3},{3,2},{4,5},{5,4},{6,7},{7,6},{8,9},{9,8},{10,11... | collective-permute-start | bytes 589832 | tf_op jit(solution)/shard_map/ppermute | solution.py:237
  8.3 0.0 collective-permute-done.4
  8.3 6.0 %collective-permute-start.5 = (f32[64,1536]{1,0:T(8,128)S(1)}, f32[64,1536]{1,0:T(8,128)S(1)}, u32[]{:S(2)}, u32[]{:S(2)}) collective-permute-start(f32[64,1536]{1,0:T(8,128)S(1)} %pad_maximum_fusion.8), channel_id=1, source_target_pairs={{0,12},{1,13},{2,14},{3,15},{4,8},{5,9},{6,10},{7,11},{8,4},{9,5},... | collective-permute-start | bytes 1179656 | tf_op jit(solution)/shard_map/ppermute | solution.py:237
  14.3 0.0 collective-permute-done
  14.3 4.4 %collective-permute-start.1 = (f32[64,1536]{1,0:T(8,128)S(1)}, f32[64,1536]{1,0:T(8,128)S(1)}, u32[]{:S(2)}, u32[]{:S(2)}) collective-permute-start(f32[64,1536]{1,0:T(8,128)S(1)} %pad_maximum_fusion.7), channel_id=1, source_target_pairs={{0,3},{1,2},{2,1},{3,0},{4,7},{5,6},{6,5},{7,4},{8,11},{9,10},{10,... | collective-permute-start | bytes 1179656 | tf_op jit(solution)/shard_map/ppermute | solution.py:237
  18.7 1.0 collective-permute-done.5
  19.7 0.1 pad_maximum_fusion.3
  19.8 4.5 %collective-permute-start.6 = (f32[128,896]{1,0:T(8,128)S(1)}, f32[128,896]{1,0:T(8,128)S(1)}, u32[]{:S(2)}, u32[]{:S(2)}) collective-permute-start(f32[128,896]{1,0:T(8,128)S(1)} %slice.27), channel_id=1, source_target_pairs={{0,1},{1,0},{2,3},{3,2},{4,5},{5,4},{6,7},{7,6},{8,9},{9,8},{10,11... | collective-permute-start | bytes 1376264 | tf_op jit(solution)/shard_map/ppermute | solution.py:237
  24.3 0.9 collective-permute-done.1
  25.3 0.1 pad_maximum_fusion.2
  25.4 1.9 %collective-permute-start.2 = (f32[128,896]{1,0:T(8,128)S(1)}, f32[128,896]{1,0:T(8,128)S(1)}, u32[]{:S(2)}, u32[]{:S(2)}) collective-permute-start(f32[128,896]{1,0:T(8,128)S(1)} %slice.25), channel_id=1, source_target_pairs={{0,4},{1,5},{2,6},{3,7},{4,0},{5,1},{6,2},{7,3},{8,12},{9,13},{10,... | collective-permute-start | bytes 1376264 | tf_op jit(solution)/shard_map/ppermute | solution.py:237
  27.3 5.3 %collective-permute-start.7 = (f32[128,640]{1,0:T(8,128)S(1)}, f32[128,640]{1,0:T(8,128)S(1)}, u32[]{:S(2)}, u32[]{:S(2)}) collective-permute-start(f32[128,640]{1,0:T(8,128)S(1)} %pad_maximum_fusion.9), channel_id=1, source_target_pairs={{0,3},{1,2},{2,1},{3,0},{4,7},{5,6},{6,5},{7,4},{8,11},{9,10},{10,... | collective-permute-start | bytes 983048 | tf_op jit(solution)/shard_map/ppermute | solution.py:237
  32.7 3.0 %collective-permute-start.3 = (f32[128,640]{1,0:T(8,128)S(1)}, f32[128,640]{1,0:T(8,128)S(1)}, u32[]{:S(2)}, u32[]{:S(2)}) collective-permute-start(f32[128,640]{1,0:T(8,128)S(1)} %pad_maximum_fusion.10), channel_id=1, source_target_pairs={{0,12},{1,13},{2,14},{3,15},{4,8},{5,9},{6,10},{7,11},{8,4},{9,5},... | collective-permute-start | bytes 983048 | tf_op jit(solution)/shard_map/ppermute | solution.py:237
  35.7 0.0 collective-permute-done.6
  35.7 0.1 pad_maximum_fusion.1.refs_2_
  35.7 2.6 %collective-permute-start.10 = (f32[256,896]{1,0:T(8,128)S(1)}, f32[256,896]{1,0:T(8,128)}, u32[]{:S(2)}, u32[]{:S(2)}) collective-permute-start(f32[256,896]{1,0:T(8,128)S(1)} %pad_maximum_fusion.1.refs_2_), channel_id=1, source_target_pairs={{0,3},{1,2},{2,1},{3,0},{4,7},{5,6},{6,5},{7,4},{8,11},{9,10},{10,... | collective-permute-start | bytes 2752520 | tf_op jit(solution)/shard_map/ppermute | solution.py:237
  38.4 0.0 collective-permute-done.2
  38.4 0.1 pad_maximum_fusion.refs_0_
  38.4 0.0 copy-start
  38.5 4.2 %collective-permute-start.8 = (f32[256,896]{1,0:T(8,128)S(1)}, f32[256,896]{1,0:T(8,128)}, u32[]{:S(2)}, u32[]{:S(2)}) collective-permute-start(f32[256,896]{1,0:T(8,128)S(1)} %pad_maximum_fusion.refs_0_), channel_id=1, source_target_pairs={{0,12},{1,13},{2,14},{3,15},{4,8},{5,9},{6,10},{7,11},{8,4},{9,5},... | collective-permute-start | bytes 2752520 | tf_op jit(solution)/shard_map/ppermute | solution.py:237
  42.7 0.0 collective-permute-done.7
  42.7 0.9 pad_maximum_fusion.5.refs_3_
  43.5 1.9 %collective-permute-start.11 = (f32[256,640]{1,0:T(8,128)}, f32[256,640]{1,0:T(8,128)}, u32[]{:S(2)}, u32[]{:S(2)}) collective-permute-start(f32[256,640]{1,0:T(8,128)} %pad_maximum_fusion.5.refs_3_), channel_id=1, source_target_pairs={{0,1},{1,0},{2,3},{3,2},{4,5},{5,4},{6,7},{7,6},{8,9},{9,8},{10,11... | collective-permute-start | bytes 1966088 | tf_op jit(solution)/shard_map/ppermute | solution.py:237
  45.5 0.0 collective-permute-done.3
  45.5 0.9 pad_maximum_fusion.4.refs_1_
  46.4 1.9 %collective-permute-start.9 = (f32[256,640]{1,0:T(8,128)}, f32[256,640]{1,0:T(8,128)}, u32[]{:S(2)}, u32[]{:S(2)}) collective-permute-start(f32[256,640]{1,0:T(8,128)} %pad_maximum_fusion.4.refs_1_), channel_id=1, source_target_pairs={{0,4},{1,5},{2,6},{3,7},{4,0},{5,1},{6,2},{7,3},{8,12},{9,13},{10,... | collective-permute-start | bytes 1966088 | tf_op jit(solution)/shard_map/ppermute | solution.py:237
  48.3 0.0 copy-done
  48.3 3.7 %shard_map.55 = (f32[512,128]{1,0:T(8,128)S(1)}, bf16[3072,256]{1,0:T(8,128)(2,1)S(1)}, bf16[256,896]{1,0:T(8,128)(2,1)S(1)}, bf16[256,896]{1,0:T(8,128)(2,1)S(1...) custom-call(f32[3072,128]{1,0:T(8,128)S(1)} %copy-done, ...), custom_call_target="tpu_custom_call" | custom-call | flops 603979776 | bytes 12582912 | tf_op jit(solution)/shard_map/pallas_call | solution.py:103
  52.0 5.7 %collective-permute-done.11.refs_11_ = f32[256,640]{1,0:T(8,128)} collective-permute-done((f32[256,640]{1,0:T(8,128)}, f32[256,640]{1,0:T(8,128)}, u32[]{:S(2)}, u32[]{:S(2)}) %collective-permute-start.11) | collective-permute-done | bytes 655392 | tf_op jit(solution)/shard_map/ppermute | solution.py:237
  57.7 2.8 %collective-permute-done.9.refs_9_ = f32[256,640]{1,0:T(8,128)} collective-permute-done((f32[256,640]{1,0:T(8,128)}, f32[256,640]{1,0:T(8,128)}, u32[]{:S(2)}, u32[]{:S(2)}) %collective-permute-start.9) | collective-permute-done | bytes 655392 | tf_op jit(solution)/shard_map/ppermute | solution.py:237
  60.5 0.0 collective-permute-done.10.refs_10_
  60.5 1.1 collective-permute-done.8.refs_8_
  61.6 5.4 %shard_map.56 = (f32[1024,128]{1,0:T(8,128)S(1)}, bf16[6,1024,3072]{2,1,0:T(8,128)(2,1)}) custom-call(f32[512,128]{1,0:T(8,128)S(1)} %get-tuple-element.18.acc_ref, bf16[3072,256]{1,0:T(8,128)(2,1)S(1)} %get-tuple-element.19.zb_ref, bf16[256,896]{1,0:T(8,128)(2,1)S(1)} %get-tuple-element.20.refs_0_, ...), custom_call_target="tpu_custom_call", output_to_operand_aliasing={{1}: (14, {})} | custom-call | tf_op jit(solution)/shard_map/pallas_call | solution.py:156
  67.1 6.1 %collective-permute-start.12 = (f32[512,128]{1,0:T(8,128)S(1)}, f32[512,128]{1,0:T(8,128)S(1)}, u32[]{:S(2)}, u32[]{:S(2)}) collective-permute-start(f32[512,128]{1,0:T(8,128)S(1)} %constant_dynamic-slice_fusion), channel_id=1, source_target_pairs={{0,16},{16,0},{32,48},{48,32},{64,80},{80,64},{96,112},{112,96},{1... | collective-permute-start | bytes 786440 | tf_op jit(solution)/shard_map/ppermute | solution.py:273
  73.2 1.1 collective-permute-done.12
  74.3 0.0 copy-start.1
  74.3 0.0 copy-start.2
  74.3 12.6 %all_to_all.15 = f32[4,128,128]{2,1,0:T(8,128)S(1)} all-to-all(f32[4,128,128]{2,1,0:T(8,128)S(1)} %bitcast.8), channel_id=1, replica_groups={{0,32,64,96},{16,48,80,112},{128,160,192,224},{144,176,208,240},{256,28..., dimensions={0} | all-to-all | bytes 524288 | tf_op jit(solution)/shard_map/all_to_all | solution.py:274
  87.0 26.9 %all_to_all.16 = f32[4,128,128]{2,1,0:T(8,128)S(1)} all-to-all(f32[4,128,128]{2,1,0:T(8,128)S(1)} %broadcast_in_dim.4), channel_id=1, replica_groups={{0,128,256,384},{16,144,272,400},{32,160,288,416},{48,176,304,432},{64,..., dimensions={0} | all-to-all | bytes 524288 | tf_op jit(solution)/shard_map/all_to_all | solution.py:276
  113.9 12.6 %all_to_all.17 = f32[4,128,128]{2,1,0:T(8,128)S(1)} all-to-all(f32[4,128,128]{2,1,0:T(8,128)S(1)} %broadcast_in_dim.5), channel_id=1, replica_groups={{0,32,64,96},{16,48,80,112},{128,160,192,224},{144,176,208,240},{256,28..., dimensions={0} | all-to-all | bytes 524288 | tf_op jit(solution)/shard_map/all_to_all | solution.py:280
  126.4 6.9 %collective-permute-start.13 = (f32[512,128]{1,0:T(8,128)S(1)}, f32[512,128]{1,0:T(8,128)S(1)}, u32[]{:S(2)}, u32[]{:S(2)}) collective-permute-start(f32[512,128]{1,0:T(8,128)S(1)} %bitcast.6), channel_id=1, source_target_pairs={{0,16},{16,0},{32,48},{48,32},{64,80},{80,64},{96,112},{112,96},{1... | collective-permute-start | bytes 786440 | tf_op jit(solution)/shard_map/ppermute | solution.py:284
  133.4 0.1 pad_add_fusion.place_ref
  133.4 1.1 collective-permute-done.13.other_ref
  134.5 0.0 copy-done.1
  134.5 0.0 copy-done.2
  134.5 5.8 %shard_map.57 = f32[3072,128]{1,0:T(8,128)} custom-call(s32[2]{0:T(128)S(1)} %pad_add_fusion.place_ref, f32[512,128]{1,0:T(8,128)S(1)} %bitcast.7, f32[512,128]{1,0:T(8,128)S(1)} %collective-permute-done.13.other_ref, f32[256,256]{1,0:T(8,128)S(1)} %copy-done.1, f32[256,256]{1,0:T(8,128)S(1)} %copy-done.2, f32[3072,128]{1,0:T(8,128)S(1)} %copy-done, ...), custom_call_target="tpu_custom_call" | custom-call | tf_op jit(solution)/shard_map/pallas_call | solution.py:224
  (13 shorter events, 0.3 us)
Async XLA Ops:
  1.1 7.2 %collective-permute-start.4 = (f32[32,1536]{1,0:T(8,128)S(1)}, f32[32,1536]{1,0:T(8,128)S(1)}, u32[]{:S(2)}, u32[]{:S(2)}) collective-permute-start(f32[32,1536]{1,0:T(8,128)S(1)} %get-tuple-element.31), channel_id=1, source_target_pairs={{0,4},{1,5},{2,6},{3,7},{4,0},{5,1},{6,2},{7,3},{8,12},{9,13},{10,... | collective-permute-start | bytes 589832 | tf_op jit(solution)/shard_map/ppermute | solution.py:237
  5.1 9.1 %collective-permute-start = (f32[32,1536]{1,0:T(8,128)S(1)}, f32[32,1536]{1,0:T(8,128)S(1)}, u32[]{:S(2)}, u32[]{:S(2)}) collective-permute-start(f32[32,1536]{1,0:T(8,128)S(1)} %get-tuple-element.32), channel_id=1, source_target_pairs={{0,1},{1,0},{2,3},{3,2},{4,5},{5,4},{6,7},{7,6},{8,9},{9,8},{10,11... | collective-permute-start | bytes 589832 | tf_op jit(solution)/shard_map/ppermute | solution.py:237
  8.3 11.4 %collective-permute-start.5 = (f32[64,1536]{1,0:T(8,128)S(1)}, f32[64,1536]{1,0:T(8,128)S(1)}, u32[]{:S(2)}, u32[]{:S(2)}) collective-permute-start(f32[64,1536]{1,0:T(8,128)S(1)} %pad_maximum_fusion.8), channel_id=1, source_target_pairs={{0,12},{1,13},{2,14},{3,15},{4,8},{5,9},{6,10},{7,11},{8,4},{9,5},... | collective-permute-start | bytes 1179656 | tf_op jit(solution)/shard_map/ppermute | solution.py:237
  14.3 11.0 %collective-permute-start.1 = (f32[64,1536]{1,0:T(8,128)S(1)}, f32[64,1536]{1,0:T(8,128)S(1)}, u32[]{:S(2)}, u32[]{:S(2)}) collective-permute-start(f32[64,1536]{1,0:T(8,128)S(1)} %pad_maximum_fusion.7), channel_id=1, source_target_pairs={{0,3},{1,2},{2,1},{3,0},{4,7},{5,6},{6,5},{7,4},{8,11},{9,10},{10,... | collective-permute-start | bytes 1179656 | tf_op jit(solution)/shard_map/ppermute | solution.py:237
  19.8 15.9 %collective-permute-start.6 = (f32[128,896]{1,0:T(8,128)S(1)}, f32[128,896]{1,0:T(8,128)S(1)}, u32[]{:S(2)}, u32[]{:S(2)}) collective-permute-start(f32[128,896]{1,0:T(8,128)S(1)} %slice.27), channel_id=1, source_target_pairs={{0,1},{1,0},{2,3},{3,2},{4,5},{5,4},{6,7},{7,6},{8,9},{9,8},{10,11... | collective-permute-start | bytes 1376264 | tf_op jit(solution)/shard_map/ppermute | solution.py:237
  25.4 13.0 %collective-permute-start.2 = (f32[128,896]{1,0:T(8,128)S(1)}, f32[128,896]{1,0:T(8,128)S(1)}, u32[]{:S(2)}, u32[]{:S(2)}) collective-permute-start(f32[128,896]{1,0:T(8,128)S(1)} %slice.25), channel_id=1, source_target_pairs={{0,4},{1,5},{2,6},{3,7},{4,0},{5,1},{6,2},{7,3},{8,12},{9,13},{10,... | collective-permute-start | bytes 1376264 | tf_op jit(solution)/shard_map/ppermute | solution.py:237
  27.3 15.3 %collective-permute-start.7 = (f32[128,640]{1,0:T(8,128)S(1)}, f32[128,640]{1,0:T(8,128)S(1)}, u32[]{:S(2)}, u32[]{:S(2)}) collective-permute-start(f32[128,640]{1,0:T(8,128)S(1)} %pad_maximum_fusion.9), channel_id=1, source_target_pairs={{0,3},{1,2},{2,1},{3,0},{4,7},{5,6},{6,5},{7,4},{8,11},{9,10},{10,... | collective-permute-start | bytes 983048 | tf_op jit(solution)/shard_map/ppermute | solution.py:237
  32.7 12.8 %collective-permute-start.3 = (f32[128,640]{1,0:T(8,128)S(1)}, f32[128,640]{1,0:T(8,128)S(1)}, u32[]{:S(2)}, u32[]{:S(2)}) collective-permute-start(f32[128,640]{1,0:T(8,128)S(1)} %pad_maximum_fusion.10), channel_id=1, source_target_pairs={{0,12},{1,13},{2,14},{3,15},{4,8},{5,9},{6,10},{7,11},{8,4},{9,5},... | collective-permute-start | bytes 983048 | tf_op jit(solution)/shard_map/ppermute | solution.py:237
  35.7 24.8 %collective-permute-start.10 = (f32[256,896]{1,0:T(8,128)S(1)}, f32[256,896]{1,0:T(8,128)}, u32[]{:S(2)}, u32[]{:S(2)}) collective-permute-start(f32[256,896]{1,0:T(8,128)S(1)} %pad_maximum_fusion.1.refs_2_), channel_id=1, source_target_pairs={{0,3},{1,2},{2,1},{3,0},{4,7},{5,6},{6,5},{7,4},{8,11},{9,10},{10,... | collective-permute-start | bytes 2752520 | tf_op jit(solution)/shard_map/ppermute | solution.py:237
  38.4 9.9 %copy-start = (f32[3072,128]{1,0:T(8,128)S(1)}, f32[3072,128]{1,0:T(8,128)}, u32[]{:S(2)}) copy-start(f32[3072,128]{1,0:T(8,128)} %z_ref.3) | copy-start | bytes 4718596
  38.5 23.2 %collective-permute-start.8 = (f32[256,896]{1,0:T(8,128)S(1)}, f32[256,896]{1,0:T(8,128)}, u32[]{:S(2)}, u32[]{:S(2)}) collective-permute-start(f32[256,896]{1,0:T(8,128)S(1)} %pad_maximum_fusion.refs_0_), channel_id=1, source_target_pairs={{0,12},{1,13},{2,14},{3,15},{4,8},{5,9},{6,10},{7,11},{8,4},{9,5},... | collective-permute-start | bytes 2752520 | tf_op jit(solution)/shard_map/ppermute | solution.py:237
  43.5 14.2 %collective-permute-start.11 = (f32[256,640]{1,0:T(8,128)}, f32[256,640]{1,0:T(8,128)}, u32[]{:S(2)}, u32[]{:S(2)}) collective-permute-start(f32[256,640]{1,0:T(8,128)} %pad_maximum_fusion.5.refs_3_), channel_id=1, source_target_pairs={{0,1},{1,0},{2,3},{3,2},{4,5},{5,4},{6,7},{7,6},{8,9},{9,8},{10,11... | collective-permute-start | bytes 1966088 | tf_op jit(solution)/shard_map/ppermute | solution.py:237
  46.4 14.2 %collective-permute-start.9 = (f32[256,640]{1,0:T(8,128)}, f32[256,640]{1,0:T(8,128)}, u32[]{:S(2)}, u32[]{:S(2)}) collective-permute-start(f32[256,640]{1,0:T(8,128)} %pad_maximum_fusion.4.refs_1_), channel_id=1, source_target_pairs={{0,4},{1,5},{2,6},{3,7},{4,0},{5,1},{6,2},{7,3},{8,12},{9,13},{10,... | collective-permute-start | bytes 1966088 | tf_op jit(solution)/shard_map/ppermute | solution.py:237
  67.1 7.2 %collective-permute-start.12 = (f32[512,128]{1,0:T(8,128)S(1)}, f32[512,128]{1,0:T(8,128)S(1)}, u32[]{:S(2)}, u32[]{:S(2)}) collective-permute-start(f32[512,128]{1,0:T(8,128)S(1)} %constant_dynamic-slice_fusion), channel_id=1, source_target_pairs={{0,16},{16,0},{32,48},{48,32},{64,80},{80,64},{96,112},{112,96},{1... | collective-permute-start | bytes 786440 | tf_op jit(solution)/shard_map/ppermute | solution.py:273
  74.3 60.2 %copy-start.1 = (f32[256,256]{1,0:T(8,128)S(1)}, f32[256,256]{1,0:T(8,128)}, u32[]{:S(2)}) copy-start(f32[256,256]{1,0:T(8,128)} %t_one_ref.1) | copy-start | bytes 786436
  74.3 60.2 %copy-start.2 = (f32[256,256]{1,0:T(8,128)S(1)}, f32[256,256]{1,0:T(8,128)}, u32[]{:S(2)}) copy-start(f32[256,256]{1,0:T(8,128)} %t_two_ref.1) | copy-start | bytes 786436
  126.4 8.1 %collective-permute-start.13 = (f32[512,128]{1,0:T(8,128)S(1)}, f32[512,128]{1,0:T(8,128)S(1)}, u32[]{:S(2)}, u32[]{:S(2)}) collective-permute-start(f32[512,128]{1,0:T(8,128)S(1)} %bitcast.6), channel_id=1, source_target_pairs={{0,16},{16,0},{32,48},{48,32},{64,80},{80,64},{96,112},{112,96},{1... | collective-permute-start | bytes 786440 | tf_op jit(solution)/shard_map/ppermute | solution.py:284

commit v9 on v8

v9 whole, which is shorter than its diff:
```python
import functools

import jax
import jax.numpy as jnp
from jax import lax
from jax.experimental import pallas as pl
from jax.experimental.pallas import tpu as pltpu
from jax.sharding import PartitionSpec as P

F32 = jnp.float32
BF16 = jnp.bfloat16
XA, XB, YA, YB = 1, 3, 4, 12
RANGES = (14, 10)
PARTS = 2
PAIRS = 2
NEAR = 4
FAR = 4
GRANT = 32 << 20
PLANES = 6


def dot(left, right):
    return jnp.dot(left, right, preferred_element_type=F32)


def dot_t(left, right):
    return lax.dot_general(left, right, (((1,), (1,)), ((), ())), preferred_element_type=F32)


def split(x):
    high = x.astype(BF16)
    return high, (x - high.astype(F32)).astype(BF16)


def thrice(left, right):
    left_h, left_l = split(left)
    right_h, right_l = split(right)
    return dot(left_h, right_h) + (dot(left_h, right_l) + dot(left_l, right_h))


class Piece:
    def __init__(self, panel, base, size, masks):
        self.panel, self.base, self.size, self.masks = panel, base, size, masks


def block(place, width, base=0):
    return pl.ds(pl.multiple_of(base + place * width, width), width)


def half_coeffs(high, low, z_both):
    m = z_both.shape[1] // 2
    wide = dot(high, z_both)
    return wide[:, :m] + (wide[:, m:] + dot(low, z_both[:, :m]))


def add_coeffs(out_ref, part, masks, row, width):
    for i, mask in enumerate(masks):
        place = row + mask * width
        out_ref[place : place + width, :] += part[i * width : (i + 1) * width, :]


def keep(half, kept, row, base, sem):
    rows, n = half.shape
    copy = pltpu.make_async_copy(half, kept.at[0, pl.ds(row, rows), pl.ds(base, n)], sem)
    copy.start()
    return copy


def early_kernel(pieces, k, width, z_ref, *refs):
    count = len(pieces)
    halves, acc_ref, zb_ref, out = refs[:count], refs[count], refs[count + 1], refs[count + 2 : 3 * count + 2]
    kept, sems = refs[3 * count + 2 :]
    m = z_ref.shape[1]
    acc_ref[...] = jnp.zeros_like(acc_ref)
    zb_ref[:, :m], zb_ref[:, m:] = split(z_ref[...])
    copies = []
    for p, piece in enumerate(pieces):
        rows = slice(piece.base, piece.base + piece.size)
        pair = out[2 * p : 2 * p + 2]
        pair[0][...], pair[1][...] = split(halves[p][...])
        for i in range(2):
            copies.append(keep(pair[i], kept, (2 * i + piece.panel) * k, piece.base, sems.at[2 * p + i]))
        part = half_coeffs(pair[0][...], pair[1][...], zb_ref[rows, :])
        add_coeffs(acc_ref, part, piece.masks[: len(piece.masks) // 2], piece.panel * k, width)
    for copy in copies:
        copy.wait()


def vmem_specs(count):
    return [pl.BlockSpec(memory_space=pltpu.VMEM)] * count


def any_specs(count):
    return [pl.BlockSpec(memory_space=pl.ANY)] * count


SMEM = [pl.BlockSpec(memory_space=pltpu.SMEM)]


def early(z, halves, pieces, k, width):
    n, m = z.shape
    pairs = [jax.ShapeDtypeStruct(half.shape, BF16) for half in halves for _ in range(2)]
    shapes = [jax.ShapeDtypeStruct((2 * k, m), F32), jax.ShapeDtypeStruct((n, 2 * m), BF16)] + pairs
    out = pl.pallas_call(
        functools.partial(early_kernel, pieces, k, width),
        out_shape=shapes + [jax.ShapeDtypeStruct((PLANES, 4 * k, n), BF16)],
        in_specs=vmem_specs(1 + len(halves)),
        out_specs=vmem_specs(len(shapes)) + any_specs(1),
        scratch_shapes=[pltpu.SemaphoreType.DMA((len(pairs),))],
        compiler_params=pltpu.CompilerParams(vmem_limit_bytes=GRANT),
        cost_estimate=pl.CostEstimate(flops=6 * k * n * m, bytes_accessed=12 << 20, transcendentals=0),
    )(z, *halves)
    return out[0], out[1], out[2:-1], out[-1]


def late_kernel(pieces, first, k, width, acc_ref, zb_ref, *refs):
    firsts, gots, out_ref, kept = refs[:4], refs[4:6], refs[7], refs[8]
    raw, pairs, load_sems, sems = refs[9:11], refs[11:15], refs[15], refs[16]
    m = zb_ref.shape[1] // 2
    half = k // (2 * width)
    loads = [pltpu.make_async_copy(gots[p], raw[p], load_sems.at[p]) for p in range(2)]
    for load in loads:
        load.start()
    done = acc_ref.shape[0]
    out_ref[:done, :] = acc_ref[...]
    copies, panels = [], []
    for p, piece in enumerate(pieces):
        own, got = firsts[2 * p : 2 * p + 2], pairs[2 * p : 2 * p + 2]
        loads[p].wait()
        got[0][...], got[1][...] = split(raw[p][...])
        for i in range(2):
            row = (2 * i + piece.panel) * k + k // 2
            copies.append(keep(got[i], kept, row, piece.base, sems.at[2 * p + i]))
        part = half_coeffs(got[0][...], got[1][...], zb_ref[piece.base : piece.base + piece.size, :])
        add_coeffs(out_ref, part, piece.masks[half:], piece.panel * k, width)
        for i in range(2):
            blocks = [None] * (2 * half)
            for pos, mask in enumerate(piece.masks):
                ref, low = (own[i], got[i])[pos // half], pos % half * width
                blocks[mask] = ref[low : low + width, :]
            panels.append(jnp.concatenate(blocks, 0))
    one_h, one_l, two_h, two_l = panels
    gram = dot_t(one_h, two_h) + (dot_t(one_h, two_l) + dot_t(one_l, two_h))
    for i in range(k // m):
        rows, part = slice((2 + i) * k, (3 + i) * k), gram[:, i * m : (i + 1) * m]
        out_ref[rows, :] = part if first else out_ref[rows, :] + part
    for copy in copies:
        copy.wait()


def late(acc, zb, firsts, gots, kept, pieces, first, k, width):
    m = zb.shape[1] // 2
    dma = pltpu.SemaphoreType.DMA
    return pl.pallas_call(
        functools.partial(late_kernel, pieces, first, k, width),
        out_shape=[jax.ShapeDtypeStruct((2 * k + k * k // m, m), F32), jax.ShapeDtypeStruct(kept.shape, BF16)],
        in_specs=vmem_specs(6) + any_specs(3),
        out_specs=vmem_specs(1) + any_specs(1),
        input_output_aliases={8: 1},
        scratch_shapes=[pltpu.VMEM(got.shape, F32) for got in gots]
        + [pltpu.VMEM(got.shape, BF16) for got in gots for _ in range(2)]
        + [dma((2,)), dma((4,))],
        compiler_params=pltpu.CompilerParams(vmem_limit_bytes=GRANT),
    )(acc, zb, *firsts, *gots, kept)


def apply_kernel(parts, width, place_ref, mine_ref, other_ref, t_one_ref, t_two_ref, z_ref, kept_ref, *refs):
    out_ref, held, z_held, out_held, total_ref, x_ref, slot_ref, sems, z_sems, out_sems = refs
    k = t_one_ref.shape[0]
    m = z_ref.shape[1]
    loads, z_loads = [], []
    for p, (base, size, _) in enumerate(parts):
        lanes = pl.ds(base, size)
        loads.append(pltpu.make_async_copy(kept_ref.at[0, :, lanes], held.at[:, lanes], sems.at[p]))
        z_loads.append(pltpu.make_async_copy(z_ref.at[lanes, :], z_held.at[lanes, :], z_sems.at[p]))
        loads[p].start()
        z_loads[p].start()
    core = place_ref[1]
    half = mine_ref.shape[0]
    total_ref[block(core, half), :] = mine_ref[...]
    total_ref[block(1 - core, half), :] = other_ref[...]
    col = place_ref[0]

    def solve(t_ref, coeff, row):
        for mask in range(k // width):
            slot_ref[block(lax.bitwise_xor(col, mask), width), :] = coeff[mask * width : (mask + 1) * width, :]
        slot_ref[:k, :] = thrice(t_ref[...], slot_ref[:k, :])
        for mask in range(k // width):
            x_ref[row + mask * width : row + (mask + 1) * width, :] = slot_ref[block(lax.bitwise_xor(col, mask), width), :]

    solve(t_two_ref, total_ref[k : 2 * k, :], k)
    coeff = total_ref[:k, :]
    for i in range(k // m):
        row = (2 + i) * k
        coeff = coeff - thrice(total_ref[row : row + k, :], x_ref[k + i * m : k + (i + 1) * m, :])
    solve(t_one_ref, coeff, 0)
    stores = []
    for p, (base, size, orders) in enumerate(parts):
        if orders is not None:
            for which, masks in enumerate(orders):
                for pos, mask in enumerate(masks):
                    low, row = which * k + pos * width, which * k + mask * width
                    slot_ref[low : low + width, :] = x_ref[row : row + width, :]
            x_h, x_l = split(slot_ref[...].T)
            x_both = jnp.concatenate([x_h, x_l], 0)
        loads[p].wait()
        z_loads[p].wait()
        rows, lanes = slice(base, base + size), pl.ds(base, size)
        wide = dot(x_both, held[: 2 * k, rows])
        moved = wide[:m, :] + (wide[m:, :] + dot(x_h, held[2 * k :, rows]))
        out_held[rows, :] = z_held[rows, :] - moved.T
        stores.append(pltpu.make_async_copy(out_held.at[lanes, :], out_ref.at[lanes, :], out_sems.at[p]))
        stores[-1].start()
    for store in stores:
        store.wait()


def apply(place, mine, other, t_one, t_two, z, kept, parts, width):
    k, m = t_one.shape[0], z.shape[1]
    rows = pltpu.VMEM(z.shape, F32)
    coeffs = pltpu.VMEM((2 * k, m), F32)
    return pl.pallas_call(
        functools.partial(apply_kernel, parts, width),
        out_shape=jax.ShapeDtypeStruct(z.shape, F32),
        in_specs=SMEM + vmem_specs(4) + any_specs(2),
        out_specs=pl.BlockSpec(memory_space=pl.ANY),
        scratch_shapes=[pltpu.VMEM(kept.shape[1:], BF16), rows, rows, pltpu.VMEM((2 * mine.shape[0], m), F32)]
        + [coeffs, coeffs]
        + [pltpu.SemaphoreType.DMA((len(parts),))] * 3,
        compiler_params=pltpu.CompilerParams(vmem_limit_bytes=GRANT),
    )(place, mine, other, t_one, t_two, z, kept)


def widen(data, masks, mask, size):
    got = lax.ppermute(data, "col", [(i, i ^ mask) for i in range(size)])
    return got, masks + [m ^ mask for m in masks]


def gather_pieces(owns, size):
    unit = owns[0].shape[1] // sum(RANGES)
    cut = unit * RANGES[0]
    pieces, halves = [], []
    for panel, early_steps, late_steps in ((0, (XA, XB), (YA, YB)), (1, (YA, YB), (XA, XB))):
        data, masks = owns[panel], [0]
        for step in early_steps:
            got, masks = widen(data, masks, step, size)
            data = jnp.concatenate([data, got], 0)
        for low, high, steps in ((0, cut, late_steps), (cut, data.shape[1], late_steps[::-1])):
            part = data[:, low:high]
            got, held = widen(part, masks, steps[0], size)
            part = jnp.concatenate([part, got], 0)
            got, held = widen(part, held, steps[1], size)
            pieces.append(Piece(panel, low, high - low, held))
            halves.append((part, got))
    return pieces, halves


def sum_over_row(part):
    r, m = part.shape
    group = PAIRS * NEAR
    rows = group * FAR
    pair = [(i, i ^ 1) for i in range(rows)]
    near = [[group * g + PAIRS * i + c for i in range(NEAR)] for g in range(FAR) for c in range(PAIRS)]
    far = [[i + group * g for g in range(FAR)] for i in range(group)]
    core = lax.axis_index("row") % PAIRS
    half = r // PAIRS
    kept = lax.dynamic_slice_in_dim(part, core * half, half, 0)
    given = lax.dynamic_slice_in_dim(part, (1 - core) * half, half, 0)
    mine = kept + lax.ppermute(given, "row", pair)
    blocks = lax.all_to_all(mine.reshape(NEAR, half // NEAR, m), "row", 0, 0, axis_index_groups=near, tiled=True)
    mine = jnp.sum(blocks, 0)
    blocks = lax.all_to_all(
        jnp.broadcast_to(mine[None], (FAR,) + mine.shape), "row", 0, 0, axis_index_groups=far, tiled=True
    )
    mine = jnp.sum(blocks, 0)
    blocks = lax.all_to_all(
        jnp.broadcast_to(mine[None], (NEAR,) + mine.shape), "row", 0, 0, axis_index_groups=near, tiled=True
    )
    mine = blocks.reshape(half, m)
    return mine, lax.ppermute(mine, "row", pair)


def body(size, z_slab, v_first, v_second, t_first, t_second):
    width = v_first.shape[1]
    k = t_first.shape[0]
    pieces, halves = gather_pieces((v_first.T, v_second.T), size)
    place = jnp.stack([lax.axis_index("col"), lax.axis_index("row") % PAIRS]).astype(jnp.int32)
    place = lax.optimization_barrier(place)
    part, z_both, firsts, kept = early(z_slab, [half[0] for half in halves], pieces, k, width)
    parts = []
    for r in range(len(RANGES)):
        both = (r, len(RANGES) + r)
        pair = [pieces[p] for p in both]
        two = [half for p in both for half in firsts[2 * p : 2 * p + 2]]
        part, kept = late(part, z_both, two, [halves[p][1] for p in both], kept, pair, r == 0, k, width)
        step = pair[0].size // PARTS
        parts += [(pair[0].base + i * step, step, None if i else [piece.masks for piece in pair]) for i in range(PARTS)]
    mine, other = sum_over_row(part)
    return apply(place, mine, other, t_first, t_second, z_slab, kept, parts, width)


def solution(mesh):
    placed = (P("row", "col"), P("row", "col"), P("row", "col"), P(), P())
    return jax.shard_map(
        functools.partial(body, mesh.shape["col"]),
        mesh=mesh,
        in_specs=placed,
        out_specs=P("row", "col"),
        check_vma=False,
    )
```

time: 141 us -> 147 us (1.043)
  other arithmetic: 3.29 us -> 6.04 us
  local copies, waits for them, and re-layouts: 0.18 us -> 2.49 us
    concatenate x4, other arithmetic: 0.16 us -> 3.87 us  [gather_pieces(): data = jnp.concatenate([data, got], 0)]
    unnamed x6 -> x8, local copies, waits for them, and re-layouts: 0.02 us -> 2.36 us
    slice x2, other arithmetic: 0.05 us -> 1.82 us  [gather_pieces(): part = data[:, low:high]]
    concatenate x4, other arithmetic: 1.89 us -> 0.21 us  [gather_pieces(): part = jnp.concatenate([part, got], 0)]
    pallas_call x2 -> x3, Pallas kernels: 11.2 us -> 12.7 us  [the longest x2 6.93 us: late(): pl.pallas_call(functools.partial(late_kernel, pieces, first, k, width), o...]
  transfers between devices with their start and end apart: 14 -> 14, of which waited for: 7 -> 7; matrix products, arithmetic and copies ran while one was open for 2% -> 4% of each run, Pallas kernels for 3% -> 4%
where the time goes in v9:
time: 147 us; the launch traced here: 146 us
  starting transfers between devices  55.1 us (37%)
  blocking collectives  52.6 us (36%)
  Pallas kernels  15.2 us (10%)
  waiting for transfers between devices  14.5 us (10%)
  other arithmetic  6.04 us (4%)
  local copies, waits for them, and re-layouts  2.49 us (2%)
    ppermute x12, starting transfers between devices, widen(): got = lax.ppermute(data, 'col', [(i, i ^ mask) for i in range(size)])  41.9 us
    all_to_all x1, blocking collectives, sum_over_row(): lax.all_to_all(jnp.broadcast_to(mine[None], (FAR,) + mine.shape), 'row',...  26.9 us
    all_to_all x1, blocking collectives, sum_over_row(): lax.all_to_all(mine.reshape(NEAR, half // NEAR, m), 'row', 0, 0, axis_ind...  13.2 us
    all_to_all x1, blocking collectives, sum_over_row(): lax.all_to_all(jnp.broadcast_to(mine[None], (NEAR,) + mine.shape), 'row',...  12.6 us
    ppermute x12, waiting for transfers between devices, widen(): got = lax.ppermute(data, 'col', [(i, i ^ mask) for i in range(size)])  12.3 us
    ppermute x1, starting transfers between devices, sum_over_row(): return (mine, lax.ppermute(mine, 'row', pair))  6.93 us
    pallas_call x2, Pallas kernels, late(): pl.pallas_call(functools.partial(late_kernel, pieces, first, k, width), o...  6.93 us
    ppermute x1, starting transfers between devices, sum_over_row(): mine = kept + lax.ppermute(given, 'row', pair)  6.29 us
  transfers between devices with their start and end apart: 14, of which 7 were waited for; matrix products, arithmetic and copies ran while one was open for 4% of the time, Pallas kernels for 4%

profile of v9, /device:TPU:1, one launch (start us, length us, event | category | flops | bytes accessed | tf_op | source)
XLA Modules:
  0.0 146.3 jit_solution(13007683514588393900)
XLA Ops:
  0.0 4.0 %collective-permute-start.4 = (f32[16,3072]{1,0:T(8,128)}, f32[16,3072]{1,0:T(8,128)S(1)}, u32[]{:S(2)}, u32[]{:S(2)}) collective-permute-start(f32[16,3072]{1,0:T(8,128)} %bitcast.12), channel_id=1, source_target_pairs={{0,4},{1,5},{2,6},{3,7},{4,0},{5,1},{6,2},{7,3},{8,12},{9,13},{10,... | collective-permute-start | bytes 589832 | tf_op jit(solution)/shard_map/ppermute | solution.py:235
  4.0 3.1 %collective-permute-start = (f32[16,3072]{1,0:T(8,128)}, f32[16,3072]{1,0:T(8,128)S(1)}, u32[]{:S(2)}, u32[]{:S(2)}) collective-permute-start(f32[16,3072]{1,0:T(8,128)} %bitcast.8), channel_id=1, source_target_pairs={{0,1},{1,0},{2,3},{3,2},{4,5},{5,4},{6,7},{7,6},{8,9},{9,8},{10,11... | collective-permute-start | bytes 589832 | tf_op jit(solution)/shard_map/ppermute | solution.py:235
  7.2 0.1 collective-permute-done.4
  7.3 1.0 pad_maximum_fusion.7
  8.2 6.0 %collective-permute-start.5 = (f32[32,3072]{1,0:T(8,128)S(1)}, f32[32,3072]{1,0:T(8,128)S(1)}, u32[]{:S(2)}, u32[]{:S(2)}) collective-permute-start(f32[32,3072]{1,0:T(8,128)S(1)} %pad_maximum_fusion.7), channel_id=1, source_target_pairs={{0,12},{1,13},{2,14},{3,15},{4,8},{5,9},{6,10},{7,11},{8,4},{9,5},... | collective-permute-start | bytes 1179656 | tf_op jit(solution)/shard_map/ppermute | solution.py:235
  14.3 0.0 collective-permute-done
  14.3 1.0 pad_maximum_fusion.6
  15.3 4.4 %collective-permute-start.1 = (f32[32,3072]{1,0:T(8,128)S(1)}, f32[32,3072]{1,0:T(8,128)S(1)}, u32[]{:S(2)}, u32[]{:S(2)}) collective-permute-start(f32[32,3072]{1,0:T(8,128)S(1)} %pad_maximum_fusion.6), channel_id=1, source_target_pairs={{0,3},{1,2},{2,1},{3,0},{4,7},{5,6},{6,5},{7,4},{8,11},{9,10},{10,... | collective-permute-start | bytes 1179656 | tf_op jit(solution)/shard_map/ppermute | solution.py:235
  19.7 0.1 collective-permute-done.5
  19.7 1.0 pad_maximum_fusion.3
  20.8 4.5 %collective-permute-start.6 = (f32[64,1792]{1,0:T(8,128)S(1)}, f32[64,1792]{1,0:T(8,128)S(1)}, u32[]{:S(2)}, u32[]{:S(2)}) collective-permute-start(f32[64,1792]{1,0:T(8,128)S(1)} %slice.17), channel_id=1, source_target_pairs={{0,1},{1,0},{2,3},{3,2},{4,5},{5,4},{6,7},{7,6},{8,9},{9,8},{10,11... | collective-permute-start | bytes 1376264 | tf_op jit(solution)/shard_map/ppermute | solution.py:235
  25.3 0.9 collective-permute-done.1
  26.2 0.9 pad_maximum_fusion.9
  27.1 4.4 %collective-permute-start.3 = (f32[64,1280]{1,0:T(8,128)S(1)}, f32[64,1280]{1,0:T(8,128)S(1)}, u32[]{:S(2)}, u32[]{:S(2)}) collective-permute-start(f32[64,1280]{1,0:T(8,128)S(1)} %pad_maximum_fusion.9), channel_id=1, source_target_pairs={{0,12},{1,13},{2,14},{3,15},{4,8},{5,9},{6,10},{7,11},{8,4},{9,5},... | collective-permute-start | bytes 983048 | tf_op jit(solution)/shard_map/ppermute | solution.py:235
  31.5 1.0 pad_maximum_fusion.2
  32.6 1.9 %collective-permute-start.2 = (f32[64,1792]{1,0:T(8,128)S(1)}, f32[64,1792]{1,0:T(8,128)S(1)}, u32[]{:S(2)}, u32[]{:S(2)}) collective-permute-start(f32[64,1792]{1,0:T(8,128)S(1)} %slice.16), channel_id=1, source_target_pairs={{0,4},{1,5},{2,6},{3,7},{4,0},{5,1},{6,2},{7,3},{8,12},{9,13},{10,... | collective-permute-start | bytes 1376264 | tf_op jit(solution)/shard_map/ppermute | solution.py:235
  34.5 0.9 pad_maximum_fusion.8
  35.4 3.7 %collective-permute-start.7 = (f32[64,1280]{1,0:T(8,128)S(1)}, f32[64,1280]{1,0:T(8,128)S(1)}, u32[]{:S(2)}, u32[]{:S(2)}) collective-permute-start(f32[64,1280]{1,0:T(8,128)S(1)} %pad_maximum_fusion.8), channel_id=1, source_target_pairs={{0,3},{1,2},{2,1},{3,0},{4,7},{5,6},{6,5},{7,4},{8,11},{9,10},{10,... | collective-permute-start | bytes 983048 | tf_op jit(solution)/shard_map/ppermute | solution.py:235
  39.2 0.0 collective-permute-done.6
  39.2 0.1 pad_maximum_fusion.1.refs_2_
  39.2 2.8 %collective-permute-start.9 = (f32[128,1792]{1,0:T(8,128)S(1)}, f32[128,1792]{1,0:T(8,128)}, u32[]{:S(2)}, u32[]{:S(2)}) collective-permute-start(f32[128,1792]{1,0:T(8,128)S(1)} %pad_maximum_fusion.1.refs_2_), channel_id=1, source_target_pairs={{0,3},{1,2},{2,1},{3,0},{4,7},{5,6},{6,5},{7,4},{8,11},{9,10},{10,... | collective-permute-start | bytes 2752520 | tf_op jit(solution)/shard_map/ppermute | solution.py:235
  42.0 0.6 collective-permute-done.2
  42.6 0.1 pad_maximum_fusion.refs_0_
  42.7 2.3 %collective-permute-start.8 = (f32[128,1792]{1,0:T(8,128)S(1)}, f32[128,1792]{1,0:T(8,128)}, u32[]{:S(2)}, u32[]{:S(2)}) collective-permute-start(f32[128,1792]{1,0:T(8,128)S(1)} %pad_maximum_fusion.refs_0_), channel_id=1, source_target_pairs={{0,12},{1,13},{2,14},{3,15},{4,8},{5,9},{6,10},{7,11},{8,4},{9,5},... | collective-permute-start | bytes 2752520 | tf_op jit(solution)/shard_map/ppermute | solution.py:235
  44.9 0.0 collective-permute-done.3
  45.0 2.8 %collective-permute-start.10 = (f32[128,1280]{1,0:T(8,128)S(1)}, f32[128,1280]{1,0:T(8,128)}, u32[]{:S(2)}, u32[]{:S(2)}) collective-permute-start(f32[128,1280]{1,0:T(8,128)S(1)} %pad_maximum_fusion.4.refs_1_), channel_id=1, source_target_pairs={{0,4},{1,5},{2,6},{3,7},{4,0},{5,1},{6,2},{7,3},{8,12},{9,13},{10,... | collective-permute-start | bytes 1966088 | tf_op jit(solution)/shard_map/ppermute | solution.py:235
  47.8 0.0 collective-permute-done.7
  47.8 1.9 %collective-permute-start.11 = (f32[128,1280]{1,0:T(8,128)S(1)}, f32[128,1280]{1,0:T(8,128)}, u32[]{:S(2)}, u32[]{:S(2)}) collective-permute-start(f32[128,1280]{1,0:T(8,128)S(1)} %pad_maximum_fusion.5.refs_3_), channel_id=1, source_target_pairs={{0,1},{1,0},{2,3},{3,2},{4,5},{5,4},{6,7},{7,6},{8,9},{9,8},{10,11... | collective-permute-start | bytes 1966088 | tf_op jit(solution)/shard_map/ppermute | solution.py:235
  49.8 0.0 copy-start
  49.8 1.4 copy-done
  51.2 2.6 %shard_map.55 = (f32[512,128]{1,0:T(8,128)S(1)}, bf16[3072,256]{1,0:T(8,128)(2,1)S(1)}, bf16[128,1792]{1,0:T(8,128)(2,1)S(1)}, bf16[128,1792]{1,0:T(8,128)(2,1)S...) custom-call(f32[3072,128]{1,0:T(8,128)S(1)} %copy-done, ...), custom_call_target="tpu_custom_call" | custom-call | flops 603979776 | bytes 12582912 | tf_op jit(solution)/shard_map/pallas_call | solution.py:104
  53.8 10.6 %collective-permute-done.9.refs_5_ = f32[128,1792]{1,0:T(8,128)} collective-permute-done((f32[128,1792]{1,0:T(8,128)S(1)}, f32[128,1792]{1,0:T(8,128)}, u32[]{:S(2)}, u32[]{:S(2)}) %collective-permute-start.9) | collective-permute-done | bytes 917536 | tf_op jit(solution)/shard_map/ppermute | solution.py:235
  64.3 0.0 collective-permute-done.8.refs_4_
  64.3 0.0 copy-start.1
  64.3 0.0 copy-start.2
  64.3 3.8 %shard_map.56 = (f32[1024,128]{1,0:T(8,128)S(1)}, bf16[6,1024,3072]{2,1,0:T(8,128)(2,1)}) custom-call(f32[512,128]{1,0:T(8,128)S(1)} %get-tuple-element.20.acc_ref, bf16[3072,256]{1,0:T(8,128)(2,1)S(1)} %get-tuple-element.21.zb_ref, bf16[128,1792]{1,0:T(8,128)(2,1)S(1)} %get-tuple-element.22.refs_0_, ...), custom_call_target="tpu_custom_call", output_to_operand_aliasing={{1}: (8, {})} | custom-call | tf_op jit(solution)/shard_map/pallas_call | solution.py:154
  68.2 0.0 collective-permute-done.10.refs_4_
  68.2 0.0 collective-permute-done.11.refs_5_
  68.2 3.1 %shard_map.57 = (f32[1024,128]{1,0:T(8,128)S(1)}, bf16[6,1024,3072]{2,1,0:T(8,128)(2,1)}) custom-call(f32[1024,128]{1,0:T(8,128)S(1)} %get-tuple-element.27.acc_ref, bf16[3072,256]{1,0:T(8,128)(2,1)S(1)} %get-tuple-element.21.zb_ref, bf16[128,1280]{1,0:T(8,128)(2,1)S(1)} %get-tuple-element.28.refs_0_, ...), custom_call_target="tpu_custom_call", output_to_operand_aliasing={{1}: (8, {})} | custom-call | tf_op jit(solution)/shard_map/pallas_call | solution.py:154
  71.3 6.3 %collective-permute-start.12 = (f32[512,128]{1,0:T(8,128)S(1)}, f32[512,128]{1,0:T(8,128)S(1)}, u32[]{:S(2)}, u32[]{:S(2)}) collective-permute-start(f32[512,128]{1,0:T(8,128)S(1)} %constant_dynamic-slice_fusion), channel_id=1, source_target_pairs={{0,16},{16,0},{32,48},{48,32},{64,80},{80,64},{96,112},{112,96},{1... | collective-permute-start | bytes 786440 | tf_op jit(solution)/shard_map/ppermute | solution.py:269
  77.6 1.1 collective-permute-done.12
  78.8 13.2 %all_to_all.15 = f32[4,128,128]{2,1,0:T(8,128)S(1)} all-to-all(f32[4,128,128]{2,1,0:T(8,128)S(1)} %bitcast.16), channel_id=1, replica_groups={{0,32,64,96},{16,48,80,112},{128,160,192,224},{144,176,208,240},{256,28..., dimensions={0} | all-to-all | bytes 524288 | tf_op jit(solution)/shard_map/all_to_all | solution.py:270
  92.1 26.9 %all_to_all.16 = f32[4,128,128]{2,1,0:T(8,128)S(1)} all-to-all(f32[4,128,128]{2,1,0:T(8,128)S(1)} %broadcast_in_dim.4), channel_id=1, replica_groups={{0,128,256,384},{16,144,272,400},{32,160,288,416},{48,176,304,432},{64,..., dimensions={0} | all-to-all | bytes 524288 | tf_op jit(solution)/shard_map/all_to_all | solution.py:272
  119.0 12.6 %all_to_all.17 = f32[4,128,128]{2,1,0:T(8,128)S(1)} all-to-all(f32[4,128,128]{2,1,0:T(8,128)S(1)} %broadcast_in_dim.5), channel_id=1, replica_groups={{0,32,64,96},{16,48,80,112},{128,160,192,224},{144,176,208,240},{256,28..., dimensions={0} | all-to-all | bytes 524288 | tf_op jit(solution)/shard_map/all_to_all | solution.py:276
  131.5 6.9 %collective-permute-start.13 = (f32[512,128]{1,0:T(8,128)S(1)}, f32[512,128]{1,0:T(8,128)S(1)}, u32[]{:S(2)}, u32[]{:S(2)}) collective-permute-start(f32[512,128]{1,0:T(8,128)S(1)} %bitcast.6), channel_id=1, source_target_pairs={{0,16},{16,0},{32,48},{48,32},{64,80},{80,64},{96,112},{112,96},{1... | collective-permute-start | bytes 786440 | tf_op jit(solution)/shard_map/ppermute | solution.py:280
  138.5 0.1 pad_add_fusion.place_ref
  138.6 1.1 collective-permute-done.13.other_ref
  139.6 0.0 copy-done.1
  139.6 0.0 copy-done.2
  139.6 0.0 copy-start.3
  139.6 0.9 copy-done.3
  140.6 5.7 %shard_map.58 = f32[3072,128]{1,0:T(8,128)} custom-call(s32[2]{0:T(128)S(1)} %pad_add_fusion.place_ref, f32[512,128]{1,0:T(8,128)S(1)} %bitcast.7, f32[512,128]{1,0:T(8,128)S(1)} %collective-permute-done.13.other_ref, f32[256,256]{1,0:T(8,128)S(1)} %copy-done.2, f32[256,256]{1,0:T(8,128)S(1)} %copy-done.3, f32[3072,128]{1,0:T(8,128)S(1)} %copy-done.1, ...), custom_call_target="tpu_custom_call" | custom-call | tf_op jit(solution)/shard_map/pallas_call | solution.py:222
  (10 shorter events, 0.3 us)
Async XLA Ops:
  0.0 7.3 %collective-permute-start.4 = (f32[16,3072]{1,0:T(8,128)}, f32[16,3072]{1,0:T(8,128)S(1)}, u32[]{:S(2)}, u32[]{:S(2)}) collective-permute-start(f32[16,3072]{1,0:T(8,128)} %bitcast.12), channel_id=1, source_target_pairs={{0,4},{1,5},{2,6},{3,7},{4,0},{5,1},{6,2},{7,3},{8,12},{9,13},{10,... | collective-permute-start | bytes 589832 | tf_op jit(solution)/shard_map/ppermute | solution.py:235
  4.0 10.3 %collective-permute-start = (f32[16,3072]{1,0:T(8,128)}, f32[16,3072]{1,0:T(8,128)S(1)}, u32[]{:S(2)}, u32[]{:S(2)}) collective-permute-start(f32[16,3072]{1,0:T(8,128)} %bitcast.8), channel_id=1, source_target_pairs={{0,1},{1,0},{2,3},{3,2},{4,5},{5,4},{6,7},{7,6},{8,9},{9,8},{10,11... | collective-permute-start | bytes 589832 | tf_op jit(solution)/shard_map/ppermute | solution.py:235
  8.2 11.5 %collective-permute-start.5 = (f32[32,3072]{1,0:T(8,128)S(1)}, f32[32,3072]{1,0:T(8,128)S(1)}, u32[]{:S(2)}, u32[]{:S(2)}) collective-permute-start(f32[32,3072]{1,0:T(8,128)S(1)} %pad_maximum_fusion.7), channel_id=1, source_target_pairs={{0,12},{1,13},{2,14},{3,15},{4,8},{5,9},{6,10},{7,11},{8,4},{9,5},... | collective-permute-start | bytes 1179656 | tf_op jit(solution)/shard_map/ppermute | solution.py:235
  15.3 11.0 %collective-permute-start.1 = (f32[32,3072]{1,0:T(8,128)S(1)}, f32[32,3072]{1,0:T(8,128)S(1)}, u32[]{:S(2)}, u32[]{:S(2)}) collective-permute-start(f32[32,3072]{1,0:T(8,128)S(1)} %pad_maximum_fusion.6), channel_id=1, source_target_pairs={{0,3},{1,2},{2,1},{3,0},{4,7},{5,6},{6,5},{7,4},{8,11},{9,10},{10,... | collective-permute-start | bytes 1179656 | tf_op jit(solution)/shard_map/ppermute | solution.py:235
  20.8 18.4 %collective-permute-start.6 = (f32[64,1792]{1,0:T(8,128)S(1)}, f32[64,1792]{1,0:T(8,128)S(1)}, u32[]{:S(2)}, u32[]{:S(2)}) collective-permute-start(f32[64,1792]{1,0:T(8,128)S(1)} %slice.17), channel_id=1, source_target_pairs={{0,1},{1,0},{2,3},{3,2},{4,5},{5,4},{6,7},{7,6},{8,9},{9,8},{10,11... | collective-permute-start | bytes 1376264 | tf_op jit(solution)/shard_map/ppermute | solution.py:235
  27.1 17.8 %collective-permute-start.3 = (f32[64,1280]{1,0:T(8,128)S(1)}, f32[64,1280]{1,0:T(8,128)S(1)}, u32[]{:S(2)}, u32[]{:S(2)}) collective-permute-start(f32[64,1280]{1,0:T(8,128)S(1)} %pad_maximum_fusion.9), channel_id=1, source_target_pairs={{0,12},{1,13},{2,14},{3,15},{4,8},{5,9},{6,10},{7,11},{8,4},{9,5},... | collective-permute-start | bytes 983048 | tf_op jit(solution)/shard_map/ppermute | solution.py:235
  32.6 10.0 %collective-permute-start.2 = (f32[64,1792]{1,0:T(8,128)S(1)}, f32[64,1792]{1,0:T(8,128)S(1)}, u32[]{:S(2)}, u32[]{:S(2)}) collective-permute-start(f32[64,1792]{1,0:T(8,128)S(1)} %slice.16), channel_id=1, source_target_pairs={{0,4},{1,5},{2,6},{3,7},{4,0},{5,1},{6,2},{7,3},{8,12},{9,13},{10,... | collective-permute-start | bytes 1376264 | tf_op jit(solution)/shard_map/ppermute | solution.py:235
  35.4 12.3 %collective-permute-start.7 = (f32[64,1280]{1,0:T(8,128)S(1)}, f32[64,1280]{1,0:T(8,128)S(1)}, u32[]{:S(2)}, u32[]{:S(2)}) collective-permute-start(f32[64,1280]{1,0:T(8,128)S(1)} %pad_maximum_fusion.8), channel_id=1, source_target_pairs={{0,3},{1,2},{2,1},{3,0},{4,7},{5,6},{6,5},{7,4},{8,11},{9,10},{10,... | collective-permute-start | bytes 983048 | tf_op jit(solution)/shard_map/ppermute | solution.py:235
  39.2 25.1 %collective-permute-start.9 = (f32[128,1792]{1,0:T(8,128)S(1)}, f32[128,1792]{1,0:T(8,128)}, u32[]{:S(2)}, u32[]{:S(2)}) collective-permute-start(f32[128,1792]{1,0:T(8,128)S(1)} %pad_maximum_fusion.1.refs_2_), channel_id=1, source_target_pairs={{0,3},{1,2},{2,1},{3,0},{4,7},{5,6},{6,5},{7,4},{8,11},{9,10},{10,... | collective-permute-start | bytes 2752520 | tf_op jit(solution)/shard_map/ppermute | solution.py:235
  42.7 21.7 %collective-permute-start.8 = (f32[128,1792]{1,0:T(8,128)S(1)}, f32[128,1792]{1,0:T(8,128)}, u32[]{:S(2)}, u32[]{:S(2)}) collective-permute-start(f32[128,1792]{1,0:T(8,128)S(1)} %pad_maximum_fusion.refs_0_), channel_id=1, source_target_pairs={{0,12},{1,13},{2,14},{3,15},{4,8},{5,9},{6,10},{7,11},{8,4},{9,5},... | collective-permute-start | bytes 2752520 | tf_op jit(solution)/shard_map/ppermute | solution.py:235
  45.0 23.2 %collective-permute-start.10 = (f32[128,1280]{1,0:T(8,128)S(1)}, f32[128,1280]{1,0:T(8,128)}, u32[]{:S(2)}, u32[]{:S(2)}) collective-permute-start(f32[128,1280]{1,0:T(8,128)S(1)} %pad_maximum_fusion.4.refs_1_), channel_id=1, source_target_pairs={{0,4},{1,5},{2,6},{3,7},{4,0},{5,1},{6,2},{7,3},{8,12},{9,13},{10,... | collective-permute-start | bytes 1966088 | tf_op jit(solution)/shard_map/ppermute | solution.py:235
  47.8 20.4 %collective-permute-start.11 = (f32[128,1280]{1,0:T(8,128)S(1)}, f32[128,1280]{1,0:T(8,128)}, u32[]{:S(2)}, u32[]{:S(2)}) collective-permute-start(f32[128,1280]{1,0:T(8,128)S(1)} %pad_maximum_fusion.5.refs_3_), channel_id=1, source_target_pairs={{0,1},{1,0},{2,3},{3,2},{4,5},{5,4},{6,7},{7,6},{8,9},{9,8},{10,11... | collective-permute-start | bytes 1966088 | tf_op jit(solution)/shard_map/ppermute | solution.py:235
  49.8 1.4 copy-start
  64.3 75.3 %copy-start.1 = (f32[3072,128]{1,0:T(8,128)S(1)}, f32[3072,128]{1,0:T(8,128)}, u32[]{:S(2)}) copy-start(f32[3072,128]{1,0:T(8,128)} %z_ref.3) | copy-start | bytes 4718596
  64.3 75.3 %copy-start.2 = (f32[256,256]{1,0:T(8,128)S(1)}, f32[256,256]{1,0:T(8,128)}, u32[]{:S(2)}) copy-start(f32[256,256]{1,0:T(8,128)} %t_one_ref.1) | copy-start | bytes 786436
  71.3 7.4 %collective-permute-start.12 = (f32[512,128]{1,0:T(8,128)S(1)}, f32[512,128]{1,0:T(8,128)S(1)}, u32[]{:S(2)}, u32[]{:S(2)}) collective-permute-start(f32[512,128]{1,0:T(8,128)S(1)} %constant_dynamic-slice_fusion), channel_id=1, source_target_pairs={{0,16},{16,0},{32,48},{48,32},{64,80},{80,64},{96,112},{112,96},{1... | collective-permute-start | bytes 786440 | tf_op jit(solution)/shard_map/ppermute | solution.py:269
  131.5 8.1 %collective-permute-start.13 = (f32[512,128]{1,0:T(8,128)S(1)}, f32[512,128]{1,0:T(8,128)S(1)}, u32[]{:S(2)}, u32[]{:S(2)}) collective-permute-start(f32[512,128]{1,0:T(8,128)S(1)} %bitcast.6), channel_id=1, source_target_pairs={{0,16},{16,0},{32,48},{48,32},{64,80},{80,64},{96,112},{112,96},{1... | collective-permute-start | bytes 786440 | tf_op jit(solution)/shard_map/ppermute | solution.py:280
  139.6 1.0 copy-start.3

commit v10 on v9

--- a/solution.py
+++ b/solution.py
@@ -10,8 +10,9 @@
 F32 = jnp.float32
 BF16 = jnp.bfloat16
 XA, XB, YA, YB = 1, 3, 4, 12
-RANGES = (14, 10)
-PARTS = 2
+RANGES = (12, 12)
+STEPS = (((XA, XB, YA, YB), (XB, XA, YB, YA)), ((YA, YB, XA, XB), (YB, YA, XB, XA)))
+LANES = 128
 PAIRS = 2
 NEAR = 4
 FAR = 4
@@ -39,8 +40,8 @@
 
 
 class Piece:
-    def __init__(self, panel, base, size, masks):
-        self.panel, self.base, self.size, self.masks = panel, base, size, masks
+    def __init__(self, panel, part, base, size, masks):
+        self.panel, self.part, self.base, self.size, self.masks = panel, part, base, size, masks
 
 
 def block(place, width, base=0):
@@ -66,18 +67,29 @@
     return copy
 
 
-def early_kernel(pieces, k, width, z_ref, *refs):
+def load_half(place_ref, piece, owns, others, raw, sem):
+    own = pltpu.make_async_copy(owns[piece.part].at[0], raw, sem)
+    other = pltpu.make_async_copy(others[piece.part], raw, sem)
+    pl.when(place_ref[1] == piece.panel)(own.start)
+    pl.when(place_ref[1] != piece.panel)(other.start)
+    return own
+
+
+def early_kernel(pieces, k, width, place_ref, z_ref, *refs):
     count = len(pieces)
-    halves, acc_ref, zb_ref, out = refs[:count], refs[count], refs[count + 1], refs[count + 2 : 3 * count + 2]
-    kept, sems = refs[3 * count + 2 :]
+    owns, others = refs[: count // 2], refs[count // 2 : count]
+    acc_ref, kept, sems, load_sems, zb_ref = refs[count : count + 5]
+    raw, out = refs[count + 5 : 2 * count + 5], refs[2 * count + 5 :]
     m = z_ref.shape[1]
+    loads = [load_half(place_ref, piece, owns, others, raw[p], load_sems.at[p]) for p, piece in enumerate(pieces)]
     acc_ref[...] = jnp.zeros_like(acc_ref)
     zb_ref[:, :m], zb_ref[:, m:] = split(z_ref[...])
     copies = []
     for p, piece in enumerate(pieces):
         rows = slice(piece.base, piece.base + piece.size)
         pair = out[2 * p : 2 * p + 2]
-        pair[0][...], pair[1][...] = split(halves[p][...])
+        loads[p].wait()
+        pair[0][...], pair[1][...] = split(raw[p][...])
         for i in range(2):
             copies.append(keep(pair[i], kept, (2 * i + piece.panel) * k, piece.base, sems.at[2 * p + i]))
         part = half_coeffs(pair[0][...], pair[1][...], zb_ref[rows, :])
@@ -97,71 +109,96 @@
 SMEM = [pl.BlockSpec(memory_space=pltpu.SMEM)]
 
 
-def early(z, halves, pieces, k, width):
+def early(place, z, owns, others, pieces, k, width):
     n, m = z.shape
-    pairs = [jax.ShapeDtypeStruct(half.shape, BF16) for half in halves for _ in range(2)]
-    shapes = [jax.ShapeDtypeStruct((2 * k, m), F32), jax.ShapeDtypeStruct((n, 2 * m), BF16)] + pairs
-    out = pl.pallas_call(
+    raw = [(k // 2, piece.size) for piece in pieces]
+    dma = pltpu.SemaphoreType.DMA
+    return pl.pallas_call(
         functools.partial(early_kernel, pieces, k, width),
-        out_shape=shapes + [jax.ShapeDtypeStruct((PLANES, 4 * k, n), BF16)],
-        in_specs=vmem_specs(1 + len(halves)),
-        out_specs=vmem_specs(len(shapes)) + any_specs(1),
-        scratch_shapes=[pltpu.SemaphoreType.DMA((len(pairs),))],
+        out_shape=[jax.ShapeDtypeStruct((2 * k, m), F32), jax.ShapeDtypeStruct((PLANES, 4 * k, n), BF16)],
+        in_specs=SMEM + vmem_specs(1) + any_specs(len(pieces)),
+        out_specs=vmem_specs(1) + any_specs(1),
+        scratch_shapes=[dma((2 * len(pieces),)), dma((len(pieces),)), pltpu.VMEM((n, 2 * m), BF16)]
+        + [pltpu.VMEM(shape, F32) for shape in raw]
+        + [pltpu.VMEM(shape, BF16) for shape in raw for _ in range(2)],
         compiler_params=pltpu.CompilerParams(vmem_limit_bytes=GRANT),
         cost_estimate=pl.CostEstimate(flops=6 * k * n * m, bytes_accessed=12 << 20, transcendentals=0),
-    )(z, *halves)
-    return out[0], out[1], out[2:-1], out[-1]
-
-
-def late_kernel(pieces, first, k, width, acc_ref, zb_ref, *refs):
-    firsts, gots, out_ref, kept = refs[:4], refs[4:6], refs[7], refs[8]
-    raw, pairs, load_sems, sems = refs[9:11], refs[11:15], refs[15], refs[16]
-    m = zb_ref.shape[1] // 2
+    )(place, z, *owns, *others)
+
+
+def late_kernel(pieces, k, width, place_ref, acc_ref, z_ref, *refs):
+    count = len(pieces)
+    owns, others, out_ref, kept = refs[: count // 2], refs[count // 2 : count], refs[count + 1], refs[count + 2]
+    z_sem, load_sems, first_sems, sems, z_held, zb_ref = refs[count + 3 : count + 9]
+    scratch = refs[count + 9 :]
+    raw, firsts, pairs = scratch[:count], scratch[count : 3 * count], scratch[3 * count :]
+    m = z_ref.shape[1]
     half = k // (2 * width)
-    loads = [pltpu.make_async_copy(gots[p], raw[p], load_sems.at[p]) for p in range(2)]
-    for load in loads:
-        load.start()
-    done = acc_ref.shape[0]
-    out_ref[:done, :] = acc_ref[...]
+    order = [p for r in range(count // 2) for p in (r, count // 2 + r)]
+    z_load = pltpu.make_async_copy(z_ref, z_held, z_sem)
+    loads, first_loads = {}, {}
+    for p in order:
+        piece = pieces[p]
+        loads[p] = load_half(place_ref, piece, owns, others, raw[p], load_sems.at[p])
+        if p == 0:
+            z_load.start()
+        for i in range(2):
+            rows, lanes = pl.ds((2 * i + piece.panel) * k, k // 2), pl.ds(piece.base, piece.size)
+            load = pltpu.make_async_copy(kept.at[0, rows, lanes], firsts[2 * p + i], first_sems.at[2 * p + i])
+            load.start()
+            first_loads[2 * p + i] = load
+    out_ref[: 2 * k, :] = acc_ref[...]
     copies, panels = [], []
-    for p, piece in enumerate(pieces):
-        own, got = firsts[2 * p : 2 * p + 2], pairs[2 * p : 2 * p + 2]
+    for p in order:
+        piece, own, got = pieces[p], firsts[2 * p : 2 * p + 2], pairs[2 * p : 2 * p + 2]
         loads[p].wait()
         got[0][...], got[1][...] = split(raw[p][...])
         for i in range(2):
             row = (2 * i + piece.panel) * k + k // 2
             copies.append(keep(got[i], kept, row, piece.base, sems.at[2 * p + i]))
+        if p == 0:
+            z_load.wait()
+            zb_ref[:, :m], zb_ref[:, m:] = split(z_held[...])
         part = half_coeffs(got[0][...], got[1][...], zb_ref[piece.base : piece.base + piece.size, :])
         add_coeffs(out_ref, part, piece.masks[half:], piece.panel * k, width)
+        first_loads[2 * p].wait()
+        first_loads[2 * p + 1].wait()
         for i in range(2):
             blocks = [None] * (2 * half)
             for pos, mask in enumerate(piece.masks):
                 ref, low = (own[i], got[i])[pos // half], pos % half * width
                 blocks[mask] = ref[low : low + width, :]
             panels.append(jnp.concatenate(blocks, 0))
-    one_h, one_l, two_h, two_l = panels
-    gram = dot_t(one_h, two_h) + (dot_t(one_h, two_l) + dot_t(one_l, two_h))
-    for i in range(k // m):
-        rows, part = slice((2 + i) * k, (3 + i) * k), gram[:, i * m : (i + 1) * m]
-        out_ref[rows, :] = part if first else out_ref[rows, :] + part
+        if piece.panel == 1:
+            one_h, one_l, two_h, two_l = panels
+            panels = []
+            gram = dot_t(one_h, two_h) + (dot_t(one_h, two_l) + dot_t(one_l, two_h))
+            for i in range(k // m):
+                rows, part = slice((2 + i) * k, (3 + i) * k), gram[:, i * m : (i + 1) * m]
+                out_ref[rows, :] = part if piece.base == 0 else out_ref[rows, :] + part
     for copy in copies:
         copy.wait()
 
 
-def late(acc, zb, firsts, gots, kept, pieces, first, k, width):
-    m = zb.shape[1] // 2
+def late(place, acc, z, owns, others, kept, pieces, k, width):
+    n, m = z.shape
+    count = len(pieces)
     dma = pltpu.SemaphoreType.DMA
+    raw = [(k // 2, piece.size) for piece in pieces]
+    pairs = [pltpu.VMEM(shape, BF16) for shape in raw for _ in range(2)]
     return pl.pallas_call(
-        functools.partial(late_kernel, pieces, first, k, width),
+        functools.partial(late_kernel, pieces, k, width),
         out_shape=[jax.ShapeDtypeStruct((2 * k + k * k // m, m), F32), jax.ShapeDtypeStruct(kept.shape, BF16)],
-        in_specs=vmem_specs(6) + any_specs(3),
+        in_specs=SMEM + vmem_specs(1) + any_specs(count + 2),
         out_specs=vmem_specs(1) + any_specs(1),
-        input_output_aliases={8: 1},
-        scratch_shapes=[pltpu.VMEM(got.shape, F32) for got in gots]
-        + [pltpu.VMEM(got.shape, BF16) for got in gots for _ in range(2)]
-        + [dma((2,)), dma((4,))],
+        input_output_aliases={3 + count: 1},
+        scratch_shapes=[dma, dma((count,)), dma((2 * count,)), dma((2 * count,))]
+        + [pltpu.VMEM((n, m), F32), pltpu.VMEM((n, 2 * m), BF16)]
+        + [pltpu.VMEM(shape, F32) for shape in raw]
+        + pairs
+        + pairs,
         compiler_params=pltpu.CompilerParams(vmem_limit_bytes=GRANT),
-    )(acc, zb, *firsts, *gots, kept)
+    )(place, acc, z, *owns, *others, kept)
 
 
 def apply_kernel(parts, width, place_ref, mine_ref, other_ref, t_one_ref, t_two_ref, z_ref, kept_ref, *refs):
@@ -231,28 +268,38 @@
     )(place, mine, other, t_one, t_two, z, kept)
 
 
-def widen(data, masks, mask, size):
-    got = lax.ppermute(data, "col", [(i, i ^ mask) for i in range(size)])
-    return got, masks + [m ^ mask for m in masks]
-
-
-def gather_pieces(owns, size):
-    unit = owns[0].shape[1] // sum(RANGES)
-    cut = unit * RANGES[0]
-    pieces, halves = [], []
-    for panel, early_steps, late_steps in ((0, (XA, XB), (YA, YB)), (1, (YA, YB), (XA, XB))):
-        data, masks = owns[panel], [0]
-        for step in early_steps:
-            got, masks = widen(data, masks, step, size)
-            data = jnp.concatenate([data, got], 0)
-        for low, high, steps in ((0, cut, late_steps), (cut, data.shape[1], late_steps[::-1])):
-            part = data[:, low:high]
-            got, held = widen(part, masks, steps[0], size)
-            part = jnp.concatenate([part, got], 0)
-            got, held = widen(part, held, steps[1], size)
-            pieces.append(Piece(panel, low, high - low, held))
-            halves.append((part, got))
-    return pieces, halves
+def exchange(data, masks, rows, cols):
+    pairs = [(r * cols + c, r * cols + (c ^ masks[r % PAIRS])) for r in range(rows) for c in range(cols)]
+    return lax.ppermute(data, ("row", "col"), pairs)
+
+
+def swap_cores(data, rows):
+    return lax.ppermute(data, "row", [(i, i ^ 1) for i in range(rows)])
+
+
+def gather_pieces(core, v_one, v_two, rows, cols):
+    n = v_one.shape[1]
+    cut = n // sum(RANGES) * RANGES[0]
+    bounds = ((0, cut), (cut, n))
+    stay, leave = jnp.where(core == 0, v_one, v_two), jnp.where(core == 0, v_two, v_one)
+    stay, leave = lax.optimization_barrier((stay, leave))
+    both = jnp.stack([stay, swap_cores(leave, rows)])
+    parts = [both[:, :, low:high] for low, high in bounds]
+    pieces = [[None] * len(parts) for _ in range(PAIRS)]
+    masks = [[[0] for _ in parts] for _ in range(PAIRS)]
+    gots = [None] * len(parts)
+    for step in range(len(STEPS[0][0])):
+        for r in range(len(parts)):
+            if step:
+                parts[r] = jnp.concatenate([parts[r], gots[r]], 1)
+            steps = [STEPS[panel][r][step] for panel in range(PAIRS)]
+            gots[r] = exchange(parts[r], steps, rows, cols)
+            for panel in range(PAIRS):
+                masks[panel][r] = masks[panel][r] + [m ^ steps[panel] for m in masks[panel][r]]
+    for panel in range(PAIRS):
+        for r, (low, high) in enumerate(bounds):
+            pieces[panel][r] = Piece(panel, r, low, high - low, masks[panel][r])
+    return pieces[0] + pieces[1], parts, gots
 
 
 def sum_over_row(part):
@@ -280,21 +327,23 @@
     return mine, lax.ppermute(mine, "row", pair)
 
 
-def body(size, z_slab, v_first, v_second, t_first, t_second):
+def body(sizes, z_slab, v_first, v_second, t_first, t_second):
     width = v_first.shape[1]
     k = t_first.shape[0]
-    pieces, halves = gather_pieces((v_first.T, v_second.T), size)
-    place = jnp.stack([lax.axis_index("col"), lax.axis_index("row") % PAIRS]).astype(jnp.int32)
-    place = lax.optimization_barrier(place)
-    part, z_both, firsts, kept = early(z_slab, [half[0] for half in halves], pieces, k, width)
+    core = lax.axis_index("row") % PAIRS
+    pieces, halves, gots = gather_pieces(core, v_first.T, v_second.T, *sizes)
+    place = lax.optimization_barrier(jnp.stack([lax.axis_index("col"), core]).astype(jnp.int32))
+    others = [swap_cores(half[1], sizes[0]) for half in halves]
+    part, kept = early(place, z_slab, halves, others, pieces, k, width)
+    gots = [lax.optimization_barrier((part, got))[1] for got in gots]
+    others = [swap_cores(half[1], sizes[0]) for half in gots]
+    part, kept = late(place, part, z_slab, gots, others, kept, pieces, k, width)
     parts = []
     for r in range(len(RANGES)):
-        both = (r, len(RANGES) + r)
-        pair = [pieces[p] for p in both]
-        two = [half for p in both for half in firsts[2 * p : 2 * p + 2]]
-        part, kept = late(part, z_both, two, [halves[p][1] for p in both], kept, pair, r == 0, k, width)
-        step = pair[0].size // PARTS
-        parts += [(pair[0].base + i * step, step, None if i else [piece.masks for piece in pair]) for i in range(PARTS)]
+        pair = [pieces[r], pieces[len(RANGES) + r]]
+        base, end = pair[0].base, pair[0].base + pair[0].size
+        middle = base + -(-pair[0].size // (2 * LANES)) * LANES
+        parts += [(base, middle - base, [piece.masks for piece in pair]), (middle, end - middle, None)]
     mine, other = sum_over_row(part)
     return apply(place, mine, other, t_first, t_second, z_slab, kept, parts, width)
 
@@ -302,7 +351,7 @@
 def solution(mesh):
     placed = (P("row", "col"), P("row", "col"), P("row", "col"), P(), P())
     return jax.shard_map(
-        functools.partial(body, mesh.shape["col"]),
+        functools.partial(body, (mesh.shape["row"], mesh.shape["col"])),
         mesh=mesh,
         in_specs=placed,
         out_specs=P("row", "col"),

time: 147 us -> 165 us (1.12)
  waiting for transfers between devices: 14.5 us -> 36.2 us
  blocking collectives: 52.6 us -> 46.7 us
  local copies, waits for them, and re-layouts: 2.49 us -> 8.09 us
  other arithmetic: 6.04 us -> 3.67 us
  starting transfers between devices: 55.1 us -> 53 us
    ppermute x12 -> x13, waiting for transfers between devices: 12.3 us -> 33.9 us  [the longest x8 28.3 us: exchange(): return lax.ppermute(data, ('row', 'col'), pairs)]
    squeeze x0 -> x4, local copies, waits for them, and re-layouts: none -> 7.23 us  [the longest x2 4.16 us: body(): others = [swap_cores(half[1], sizes[0]) for half in gots]]
    ppermute x1, starting transfers between devices: 6.29 us -> 2.4 us  [sum_over_row(): mine = kept + lax.ppermute(given, 'row', pair)]
    all_to_all x1, blocking collectives: 26.9 us -> 23.3 us  [sum_over_row(): lax.all_to_all(jnp.broadcast_to(mine[None], (FAR,) + mine.shape), 'row',...]
    concatenate x8 -> x6, other arithmetic: 4.08 us -> 1.51 us  [gather_pieces(): parts[r] = jnp.concatenate([parts[r], gots[r]], 1)]
    all_to_all x1, blocking collectives: 13.2 us -> 10.8 us  [sum_over_row(): lax.all_to_all(mine.reshape(NEAR, half // NEAR, m), 'row', 0, 0, axis_ind...]
    slice x2 -> x0, other arithmetic: 1.82 us -> none  [gather_pieces(): part = data[:, low:high]]
    ppermute x12 -> x13, starting transfers between devices: 41.9 us -> 43.7 us  [the longest x5 22.4 us: swap_cores(): return lax.ppermute(data, 'row', [(i, i ^ 1) for i in range(rows)])]
  transfers between devices with their start and end apart: 14 -> 15, of which waited for: 7 -> 12; matrix products, arithmetic and copies ran while one was open for 4% -> 5% of each run, Pallas kernels for 4% -> 3%
where the time goes in v10:
time: 165 us
  starting transfers between devices  53 us (32%)
  blocking collectives  46.7 us (28%)
  waiting for transfers between devices  36.2 us (22%)
  Pallas kernels  16.6 us (10%)
  local copies, waits for them, and re-layouts  8.09 us (5%)
  other arithmetic  3.67 us (2%)
    ppermute x8, waiting for transfers between devices, exchange(): return lax.ppermute(data, ('row', 'col'), pairs)  28.3 us
    all_to_all x1, blocking collectives, sum_over_row(): lax.all_to_all(jnp.broadcast_to(mine[None], (FAR,) + mine.shape), 'row',...  23.3 us
    ppermute x5, starting transfers between devices, swap_cores(): return lax.ppermute(data, 'row', [(i, i ^ 1) for i in range(rows)])  22.4 us
    ppermute x8, starting transfers between devices, exchange(): return lax.ppermute(data, ('row', 'col'), pairs)  21.3 us
    all_to_all x1, blocking collectives, sum_over_row(): lax.all_to_all(jnp.broadcast_to(mine[None], (NEAR,) + mine.shape), 'row',...  12.6 us
    all_to_all x1, blocking collectives, sum_over_row(): lax.all_to_all(mine.reshape(NEAR, half // NEAR, m), 'row', 0, 0, axis_ind...  10.8 us
    ppermute x1, starting transfers between devices, sum_over_row(): return (mine, lax.ppermute(mine, 'row', pair))  6.93 us
    pallas_call x1, Pallas kernels, late(): pl.pallas_call(functools.partial(late_kernel, pieces, k, width), out_shap...  6.6 us
  transfers between devices with their start and end apart: 15, of which 12 were waited for; matrix products, arithmetic and copies ran while one was open for 5% of the time, Pallas kernels for 3%

profile of v10, /device:TPU:1, one launch (start us, length us, event | category | flops | bytes accessed | tf_op | source)
XLA Modules:
  0.0 164.5 jit_solution(8251909701625574989)
XLA Ops:
  0.0 1.0 select_bitcast_fusion
  1.1 8.8 %collective-permute-start = (f32[16,3072]{1,0:T(8,128)S(1)}, f32[16,3072]{1,0:T(8,128)S(1)}, u32[]{:S(2)}, u32[]{:S(2)}) collective-permute-start(f32[16,3072]{1,0:T(8,128)S(1)} %get-tuple-element.14), channel_id=1, source_target_pairs={{0,16},{16,0},{32,48},{48,32},{64,80},{80,64},{96,112},{112,96},{1... | collective-permute-start | bytes 589832 | tf_op jit(solution)/shard_map/ppermute | solution.py:277
  9.8 1.0 collective-permute-done
  10.9 1.9 %collective-permute-start.4 = (f32[2,16,1536]{2,1,0:T(8,128)S(1)}, f32[2,16,1536]{2,1,0:T(8,128)S(1)}, u32[]{:S(2)}, u32[]{:S(2)}) collective-permute-start(f32[2,16,1536]{2,1,0:T(8,128)S(1)} %get-tuple-element.21), channel_id=1, source_target_pairs={{0,3},{1,2},{2,1},{3,0},{4,7},{5,6},{6,5},{7,4},{8,11},{9,10},{10,... | collective-permute-start | bytes 589832 | tf_op jit(solution)/shard_map/ppermute | solution.py:273
  12.9 6.0 %collective-permute-done.4 = f32[2,16,1536]{2,1,0:T(8,128)S(1)} collective-permute-done((f32[2,16,1536]{2,1,0:T(8,128)S(1)}, f32[2,16,1536]{2,1,0:T(8,128)S(1)}, u32[]{:S(2)}, u32[]{:S(2)}) %collective-permute-start.4) | collective-permute-done | bytes 196640 | tf_op jit(solution)/shard_map/ppermute | solution.py:273
  18.9 1.9 %collective-permute-start.5 = (f32[2,32,1536]{2,1,0:T(8,128)S(1)}, f32[2,32,1536]{2,1,0:T(8,128)S(1)}, u32[]{:S(2)}, u32[]{:S(2)}) collective-permute-start(f32[2,32,1536]{2,1,0:T(8,128)S(1)} %pad_maximum_fusion.5), channel_id=1, source_target_pairs={{0,1},{1,0},{2,3},{3,2},{4,5},{5,4},{6,7},{7,6},{8,9},{9,8},{10,11... | collective-permute-start | bytes 1179656 | tf_op jit(solution)/shard_map/ppermute | solution.py:273
  20.8 3.4 %collective-permute-start.1 = (f32[2,16,1536]{2,1,0:T(8,128)S(1)}, f32[2,16,1536]{2,1,0:T(8,128)S(1)}, u32[]{:S(2)}, u32[]{:S(2)}) collective-permute-start(f32[2,16,1536]{2,1,0:T(8,128)S(1)} %get-tuple-element.22), channel_id=1, source_target_pairs={{0,1},{1,0},{2,3},{3,2},{4,5},{5,4},{6,7},{7,6},{8,9},{9,8},{10,11... | collective-permute-start | bytes 589832 | tf_op jit(solution)/shard_map/ppermute | solution.py:273
  24.2 3.5 %collective-permute-done.5 = f32[2,32,1536]{2,1,0:T(8,128)S(1)} collective-permute-done((f32[2,32,1536]{2,1,0:T(8,128)S(1)}, f32[2,32,1536]{2,1,0:T(8,128)S(1)}, u32[]{:S(2)}, u32[]{:S(2)}) %collective-permute-start.5) | collective-permute-done | bytes 393248 | tf_op jit(solution)/shard_map/ppermute | solution.py:273
  27.7 0.1 pad_maximum_fusion.3
  27.7 1.9 %collective-permute-start.6 = (f32[2,64,1536]{2,1,0:T(8,128)S(1)}, f32[2,64,1536]{2,1,0:T(8,128)S(1)}, u32[]{:S(2)}, u32[]{:S(2)}) collective-permute-start(f32[2,64,1536]{2,1,0:T(8,128)S(1)} %pad_maximum_fusion.3), channel_id=1, source_target_pairs={{0,12},{1,13},{2,14},{3,15},{4,8},{5,9},{6,10},{7,11},{8,4},{9,5},... | collective-permute-start | bytes 2359304 | tf_op jit(solution)/shard_map/ppermute | solution.py:273
  29.7 0.1 collective-permute-done.1
  29.8 1.9 %collective-permute-start.2 = (f32[2,32,1536]{2,1,0:T(8,128)S(1)}, f32[2,32,1536]{2,1,0:T(8,128)S(1)}, u32[]{:S(2)}, u32[]{:S(2)}) collective-permute-start(f32[2,32,1536]{2,1,0:T(8,128)S(1)} %pad_maximum_fusion.4), channel_id=1, source_target_pairs={{0,3},{1,2},{2,1},{3,0},{4,7},{5,6},{6,5},{7,4},{8,11},{9,10},{10,... | collective-permute-start | bytes 1179656 | tf_op jit(solution)/shard_map/ppermute | solution.py:273
  31.8 11.9 %collective-permute-done.2 = f32[2,32,1536]{2,1,0:T(8,128)S(1)} collective-permute-done((f32[2,32,1536]{2,1,0:T(8,128)S(1)}, f32[2,32,1536]{2,1,0:T(8,128)S(1)}, u32[]{:S(2)}, u32[]{:S(2)}) %collective-permute-start.2) | collective-permute-done | bytes 393248 | tf_op jit(solution)/shard_map/ppermute | solution.py:273
  43.7 0.1 pad_maximum_fusion.2
  43.7 1.9 %collective-permute-start.3 = (f32[2,64,1536]{2,1,0:T(8,128)S(1)}, f32[2,64,1536]{2,1,0:T(8,128)S(1)}, u32[]{:S(2)}, u32[]{:S(2)}) collective-permute-start(f32[2,64,1536]{2,1,0:T(8,128)S(1)} %pad_maximum_fusion.2), channel_id=1, source_target_pairs={{0,4},{1,5},{2,6},{3,7},{4,0},{5,1},{6,2},{7,3},{8,12},{9,13},{10,... | collective-permute-start | bytes 2359304 | tf_op jit(solution)/shard_map/ppermute | solution.py:273
  45.7 0.1 collective-permute-done.6
  45.7 0.1 pad_maximum_fusion.1.refs_1_
  45.8 3.3 %collective-permute-start.10 = (f32[2,128,1536]{2,1,0:T(8,128)S(1)}, f32[2,128,1536]{2,1,0:T(8,128)}, u32[]{:S(2)}, u32[]{:S(2)}) collective-permute-start(f32[2,128,1536]{2,1,0:T(8,128)S(1)} %pad_maximum_fusion.1.refs_1_), channel_id=1, source_target_pairs={{0,4},{1,5},{2,6},{3,7},{4,0},{5,1},{6,2},{7,3},{8,12},{9,13},{10,... | collective-permute-start | bytes 4718600 | tf_op jit(solution)/shard_map/ppermute | solution.py:273
  49.2 1.0 slice_bitcast_fusion
  50.1 6.7 %collective-permute-done.3 = f32[2,64,1536]{2,1,0:T(8,128)S(1)} collective-permute-done((f32[2,64,1536]{2,1,0:T(8,128)S(1)}, f32[2,64,1536]{2,1,0:T(8,128)S(1)}, u32[]{:S(2)}, u32[]{:S(2)}) %collective-permute-start.3) | collective-permute-done | bytes 786464 | tf_op jit(solution)/shard_map/ppermute | solution.py:273
  56.8 1.3 pad_maximum_fusion.refs_0_
  58.0 0.0 copy-start
  58.0 5.0 %collective-permute-start.9 = (f32[2,128,1536]{2,1,0:T(8,128)}, f32[2,128,1536]{2,1,0:T(8,128)}, u32[]{:S(2)}, u32[]{:S(2)}) collective-permute-start(f32[2,128,1536]{2,1,0:T(8,128)} %pad_maximum_fusion.refs_0_), channel_id=1, source_target_pairs={{0,12},{1,13},{2,14},{3,15},{4,8},{5,9},{6,10},{7,11},{8,4},{9,5},... | collective-permute-start | bytes 4718600 | tf_op jit(solution)/shard_map/ppermute | solution.py:273
  63.1 2.1 %slice_bitcast_fusion.1 = f32[128,1536]{1,0:T(8,128)} fusion(f32[2,128,1536]{2,1,0:T(8,128)} %pad_maximum_fusion.refs_0_), kind=kLoop, calls=%fused_computation.3 | loop fusion | bytes 1572864 | tf_op jit(solution)/shard_map/squeeze | solution.py:336
  65.2 2.7 %collective-permute-start.8 = (f32[128,1536]{1,0:T(8,128)}, f32[128,1536]{1,0:T(8,128)}, u32[]{:S(2)}, u32[]{:S(2)}) collective-permute-start(f32[128,1536]{1,0:T(8,128)} %slice_bitcast_fusion), channel_id=1, source_target_pairs={{0,16},{16,0},{32,48},{48,32},{64,80},{80,64},{96,112},{112,96},{1... | collective-permute-start | bytes 2359304 | tf_op jit(solution)/shard_map/ppermute | solution.py:277
  67.9 1.9 %collective-permute-start.7 = (f32[128,1536]{1,0:T(8,128)}, f32[128,1536]{1,0:T(8,128)}, u32[]{:S(2)}, u32[]{:S(2)}) collective-permute-start(f32[128,1536]{1,0:T(8,128)} %slice_bitcast_fusion.1), channel_id=1, source_target_pairs={{0,16},{16,0},{32,48},{48,32},{64,80},{80,64},{96,112},{112,96},{1... | collective-permute-start | bytes 2359304 | tf_op jit(solution)/shard_map/ppermute | solution.py:277
  69.8 0.1 pad_add_fusion.place_ref
  69.9 0.2 collective-permute-done.8.refs_3_
  70.1 2.3 %collective-permute-done.7.refs_2_ = f32[128,1536]{1,0:T(8,128)} collective-permute-done((f32[128,1536]{1,0:T(8,128)}, f32[128,1536]{1,0:T(8,128)}, u32[]{:S(2)}, u32[]{:S(2)}) %collective-permute-start.7) | collective-permute-done | bytes 786464 | tf_op jit(solution)/shard_map/ppermute | solution.py:277
  72.4 0.0 copy-done
  72.4 4.1 %shard_map.55 = (f32[512,128]{1,0:T(8,128)S(1)}, bf16[6,1024,3072]{2,1,0:T(8,128)(2,1)}) custom-call(s32[2]{0:T(128)S(1)} %pad_add_fusion.place_ref, f32[3072,128]{1,0:T(8,128)S(1)} %copy-done, f32[2,128,1536]{2,1,0:T(8,128)} %pad_maximum_fusion.refs_0_, f32[2,128,1536]{2,1,0:T(8,128)S(1)} %pad_maximum_fusion.1.refs_1_, ...), custom_call_target="tpu_custom_call" | custom-call | flops 603979776 | bytes 12582912 | tf_op jit(solution)/shard_map/pallas_call | solution.py:116
  76.5 0.0 collective-permute-done.10.refs_1_
  76.5 2.1 %slice_bitcast_fusion.2 = f32[128,1536]{1,0:T(8,128)} fusion(f32[2,128,1536]{2,1,0:T(8,128)} %collective-permute-done.10.refs_1_), kind=kLoop, calls=%fused_computation.6 | loop fusion | bytes 1572864 | tf_op jit(solution)/shard_map/squeeze | solution.py:339
  78.6 2.9 %collective-permute-start.12 = (f32[128,1536]{1,0:T(8,128)}, f32[128,1536]{1,0:T(8,128)S(1)}, u32[]{:S(2)}, u32[]{:S(2)}) collective-permute-start(f32[128,1536]{1,0:T(8,128)} %slice_bitcast_fusion.2), channel_id=1, source_target_pairs={{0,16},{16,0},{32,48},{48,32},{64,80},{80,64},{96,112},{112,96},{1... | collective-permute-start | bytes 2359304 | tf_op jit(solution)/shard_map/ppermute | solution.py:277
  81.5 0.0 collective-permute-done.9.refs_0_
  81.5 2.1 %slice_bitcast_fusion.3 = f32[128,1536]{1,0:T(8,128)} fusion(f32[2,128,1536]{2,1,0:T(8,128)} %collective-permute-done.9.refs_0_), kind=kLoop, calls=%fused_computation.7 | loop fusion | bytes 1572864 | tf_op jit(solution)/shard_map/squeeze | solution.py:339
  83.6 6.1 %collective-permute-start.11 = (f32[128,1536]{1,0:T(8,128)}, f32[128,1536]{1,0:T(8,128)S(1)}, u32[]{:S(2)}, u32[]{:S(2)}) collective-permute-start(f32[128,1536]{1,0:T(8,128)} %slice_bitcast_fusion.3), channel_id=1, source_target_pairs={{0,16},{16,0},{32,48},{48,32},{64,80},{80,64},{96,112},{112,96},{1... | collective-permute-start | bytes 2359304 | tf_op jit(solution)/shard_map/ppermute | solution.py:277
  89.7 0.0 collective-permute-done.12.refs_3_
  89.7 2.1 %collective-permute-done.11.refs_2_ = f32[128,1536]{1,0:T(8,128)S(1)} collective-permute-done((f32[128,1536]{1,0:T(8,128)}, f32[128,1536]{1,0:T(8,128)S(1)}, u32[]{:S(2)}, u32[]{:S(2)}) %collective-permute-start.11) | collective-permute-done | bytes 786464 | tf_op jit(solution)/shard_map/ppermute | solution.py:277
  91.8 6.6 %shard_map.56 = (f32[1024,128]{1,0:T(8,128)S(1)}, bf16[6,1024,3072]{2,1,0:T(8,128)(2,1)}) custom-call(s32[2]{0:T(128)S(1)} %pad_add_fusion.place_ref, f32[512,128]{1,0:T(8,128)S(1)} %get-tuple-element.15.acc_ref, f32[3072,128]{1,0:T(8,128)S(1)} %copy-done, f32[2,128,1536]{2,1,0:T(8,128)} %collective-permute-done.9.refs_0_, ...), custom_call_target="tpu_custom_call", output_to_operand_aliasing={{1}: (7, {})} | custom-call | tf_op jit(solution)/shard_map/pallas_call | solution.py:189
  98.4 0.0 copy-start.1
  98.4 0.8 copy-done.1
  99.3 2.4 %collective-permute-start.13 = (f32[512,128]{1,0:T(8,128)S(1)}, f32[512,128]{1,0:T(8,128)S(1)}, u32[]{:S(2)}, u32[]{:S(2)}) collective-permute-start(f32[512,128]{1,0:T(8,128)S(1)} %constant_dynamic-slice_fusion), channel_id=1, source_target_pairs={{0,16},{16,0},{32,48},{48,32},{64,80},{80,64},{96,112},{112,96},{1... | collective-permute-start | bytes 786440 | tf_op jit(solution)/shard_map/ppermute | solution.py:316
  101.7 1.1 collective-permute-done.13
  102.8 1.0 dynamic-slice_add_fusion
  103.8 0.0 copy-start.2
  103.8 0.0 copy-start.3
  103.8 10.8 %all_to_all.15 = f32[4,128,128]{2,1,0:T(8,128)S(1)} all-to-all(f32[4,128,128]{2,1,0:T(8,128)S(1)} %bitcast.20), channel_id=1, replica_groups={{0,32,64,96},{16,48,80,112},{128,160,192,224},{144,176,208,240},{256,28..., dimensions={0} | all-to-all | bytes 524288 | tf_op jit(solution)/shard_map/all_to_all | solution.py:317
  114.6 23.3 %all_to_all.16 = f32[4,128,128]{2,1,0:T(8,128)S(1)} all-to-all(f32[4,128,128]{2,1,0:T(8,128)S(1)} %broadcast_in_dim.4), channel_id=1, replica_groups={{0,128,256,384},{16,144,272,400},{32,160,288,416},{48,176,304,432},{64,..., dimensions={0} | all-to-all | bytes 524288 | tf_op jit(solution)/shard_map/all_to_all | solution.py:319
  138.0 12.6 %all_to_all.17 = f32[4,128,128]{2,1,0:T(8,128)S(1)} all-to-all(f32[4,128,128]{2,1,0:T(8,128)S(1)} %broadcast_in_dim.5), channel_id=1, replica_groups={{0,32,64,96},{16,48,80,112},{128,160,192,224},{144,176,208,240},{256,28..., dimensions={0} | all-to-all | bytes 524288 | tf_op jit(solution)/shard_map/all_to_all | solution.py:323
  150.6 6.9 %collective-permute-start.14 = (f32[512,128]{1,0:T(8,128)S(1)}, f32[512,128]{1,0:T(8,128)S(1)}, u32[]{:S(2)}, u32[]{:S(2)}) collective-permute-start(f32[512,128]{1,0:T(8,128)S(1)} %bitcast.18), channel_id=1, source_target_pairs={{0,16},{16,0},{32,48},{48,32},{64,80},{80,64},{96,112},{112,96},{1... | collective-permute-start | bytes 786440 | tf_op jit(solution)/shard_map/ppermute | solution.py:327
  157.5 1.1 collective-permute-done.14.other_ref
  158.7 0.0 copy-done.2
  158.7 0.0 copy-done.3
  158.7 5.8 %shard_map.57 = f32[3072,128]{1,0:T(8,128)} custom-call(s32[2]{0:T(128)S(1)} %pad_add_fusion.place_ref, f32[512,128]{1,0:T(8,128)S(1)} %bitcast.19, f32[512,128]{1,0:T(8,128)S(1)} %collective-permute-done.14.other_ref, f32[256,256]{1,0:T(8,128)S(1)} %copy-done.2, f32[256,256]{1,0:T(8,128)S(1)} %copy-done.3, f32[3072,128]{1,0:T(8,128)S(1)} %copy-done, ...), custom_call_target="tpu_custom_call" | custom-call | tf_op jit(solution)/shard_map/pallas_call | solution.py:259
  (8 shorter events, 0.2 us)
Async XLA Ops:
  1.1 9.8 %collective-permute-start = (f32[16,3072]{1,0:T(8,128)S(1)}, f32[16,3072]{1,0:T(8,128)S(1)}, u32[]{:S(2)}, u32[]{:S(2)}) collective-permute-start(f32[16,3072]{1,0:T(8,128)S(1)} %get-tuple-element.14), channel_id=1, source_target_pairs={{0,16},{16,0},{32,48},{48,32},{64,80},{80,64},{96,112},{112,96},{1... | collective-permute-start | bytes 589832 | tf_op jit(solution)/shard_map/ppermute | solution.py:277
  10.9 7.9 %collective-permute-start.4 = (f32[2,16,1536]{2,1,0:T(8,128)S(1)}, f32[2,16,1536]{2,1,0:T(8,128)S(1)}, u32[]{:S(2)}, u32[]{:S(2)}) collective-permute-start(f32[2,16,1536]{2,1,0:T(8,128)S(1)} %get-tuple-element.21), channel_id=1, source_target_pairs={{0,3},{1,2},{2,1},{3,0},{4,7},{5,6},{6,5},{7,4},{8,11},{9,10},{10,... | collective-permute-start | bytes 589832 | tf_op jit(solution)/shard_map/ppermute | solution.py:273
  18.9 8.8 %collective-permute-start.5 = (f32[2,32,1536]{2,1,0:T(8,128)S(1)}, f32[2,32,1536]{2,1,0:T(8,128)S(1)}, u32[]{:S(2)}, u32[]{:S(2)}) collective-permute-start(f32[2,32,1536]{2,1,0:T(8,128)S(1)} %pad_maximum_fusion.5), channel_id=1, source_target_pairs={{0,1},{1,0},{2,3},{3,2},{4,5},{5,4},{6,7},{7,6},{8,9},{9,8},{10,11... | collective-permute-start | bytes 1179656 | tf_op jit(solution)/shard_map/ppermute | solution.py:273
  20.8 9.0 %collective-permute-start.1 = (f32[2,16,1536]{2,1,0:T(8,128)S(1)}, f32[2,16,1536]{2,1,0:T(8,128)S(1)}, u32[]{:S(2)}, u32[]{:S(2)}) collective-permute-start(f32[2,16,1536]{2,1,0:T(8,128)S(1)} %get-tuple-element.22), channel_id=1, source_target_pairs={{0,1},{1,0},{2,3},{3,2},{4,5},{5,4},{6,7},{7,6},{8,9},{9,8},{10,11... | collective-permute-start | bytes 589832 | tf_op jit(solution)/shard_map/ppermute | solution.py:273
  27.7 18.0 %collective-permute-start.6 = (f32[2,64,1536]{2,1,0:T(8,128)S(1)}, f32[2,64,1536]{2,1,0:T(8,128)S(1)}, u32[]{:S(2)}, u32[]{:S(2)}) collective-permute-start(f32[2,64,1536]{2,1,0:T(8,128)S(1)} %pad_maximum_fusion.3), channel_id=1, source_target_pairs={{0,12},{1,13},{2,14},{3,15},{4,8},{5,9},{6,10},{7,11},{8,4},{9,5},... | collective-permute-start | bytes 2359304 | tf_op jit(solution)/shard_map/ppermute | solution.py:273
  29.8 13.8 %collective-permute-start.2 = (f32[2,32,1536]{2,1,0:T(8,128)S(1)}, f32[2,32,1536]{2,1,0:T(8,128)S(1)}, u32[]{:S(2)}, u32[]{:S(2)}) collective-permute-start(f32[2,32,1536]{2,1,0:T(8,128)S(1)} %pad_maximum_fusion.4), channel_id=1, source_target_pairs={{0,3},{1,2},{2,1},{3,0},{4,7},{5,6},{6,5},{7,4},{8,11},{9,10},{10,... | collective-permute-start | bytes 1179656 | tf_op jit(solution)/shard_map/ppermute | solution.py:273
  43.7 13.0 %collective-permute-start.3 = (f32[2,64,1536]{2,1,0:T(8,128)S(1)}, f32[2,64,1536]{2,1,0:T(8,128)S(1)}, u32[]{:S(2)}, u32[]{:S(2)}) collective-permute-start(f32[2,64,1536]{2,1,0:T(8,128)S(1)} %pad_maximum_fusion.2), channel_id=1, source_target_pairs={{0,4},{1,5},{2,6},{3,7},{4,0},{5,1},{6,2},{7,3},{8,12},{9,13},{10,... | collective-permute-start | bytes 2359304 | tf_op jit(solution)/shard_map/ppermute | solution.py:273
  45.8 30.7 %collective-permute-start.10 = (f32[2,128,1536]{2,1,0:T(8,128)S(1)}, f32[2,128,1536]{2,1,0:T(8,128)}, u32[]{:S(2)}, u32[]{:S(2)}) collective-permute-start(f32[2,128,1536]{2,1,0:T(8,128)S(1)} %pad_maximum_fusion.1.refs_1_), channel_id=1, source_target_pairs={{0,4},{1,5},{2,6},{3,7},{4,0},{5,1},{6,2},{7,3},{8,12},{9,13},{10,... | collective-permute-start | bytes 4718600 | tf_op jit(solution)/shard_map/ppermute | solution.py:273
  58.0 14.4 %copy-start = (f32[3072,128]{1,0:T(8,128)S(1)}, f32[3072,128]{1,0:T(8,128)}, u32[]{:S(2)}) copy-start(f32[3072,128]{1,0:T(8,128)} %z_ref.5) | copy-start | bytes 4718596
  58.0 23.5 %collective-permute-start.9 = (f32[2,128,1536]{2,1,0:T(8,128)}, f32[2,128,1536]{2,1,0:T(8,128)}, u32[]{:S(2)}, u32[]{:S(2)}) collective-permute-start(f32[2,128,1536]{2,1,0:T(8,128)} %pad_maximum_fusion.refs_0_), channel_id=1, source_target_pairs={{0,12},{1,13},{2,14},{3,15},{4,8},{5,9},{6,10},{7,11},{8,4},{9,5},... | collective-permute-start | bytes 4718600 | tf_op jit(solution)/shard_map/ppermute | solution.py:273
  65.2 4.9 %collective-permute-start.8 = (f32[128,1536]{1,0:T(8,128)}, f32[128,1536]{1,0:T(8,128)}, u32[]{:S(2)}, u32[]{:S(2)}) collective-permute-start(f32[128,1536]{1,0:T(8,128)} %slice_bitcast_fusion), channel_id=1, source_target_pairs={{0,16},{16,0},{32,48},{48,32},{64,80},{80,64},{96,112},{112,96},{1... | collective-permute-start | bytes 2359304 | tf_op jit(solution)/shard_map/ppermute | solution.py:277
  67.9 4.5 %collective-permute-start.7 = (f32[128,1536]{1,0:T(8,128)}, f32[128,1536]{1,0:T(8,128)}, u32[]{:S(2)}, u32[]{:S(2)}) collective-permute-start(f32[128,1536]{1,0:T(8,128)} %slice_bitcast_fusion.1), channel_id=1, source_target_pairs={{0,16},{16,0},{32,48},{48,32},{64,80},{80,64},{96,112},{112,96},{1... | collective-permute-start | bytes 2359304 | tf_op jit(solution)/shard_map/ppermute | solution.py:277
  78.6 11.1 %collective-permute-start.12 = (f32[128,1536]{1,0:T(8,128)}, f32[128,1536]{1,0:T(8,128)S(1)}, u32[]{:S(2)}, u32[]{:S(2)}) collective-permute-start(f32[128,1536]{1,0:T(8,128)} %slice_bitcast_fusion.2), channel_id=1, source_target_pairs={{0,16},{16,0},{32,48},{48,32},{64,80},{80,64},{96,112},{112,96},{1... | collective-permute-start | bytes 2359304 | tf_op jit(solution)/shard_map/ppermute | solution.py:277
  83.6 8.2 %collective-permute-start.11 = (f32[128,1536]{1,0:T(8,128)}, f32[128,1536]{1,0:T(8,128)S(1)}, u32[]{:S(2)}, u32[]{:S(2)}) collective-permute-start(f32[128,1536]{1,0:T(8,128)} %slice_bitcast_fusion.3), channel_id=1, source_target_pairs={{0,16},{16,0},{32,48},{48,32},{64,80},{80,64},{96,112},{112,96},{1... | collective-permute-start | bytes 2359304 | tf_op jit(solution)/shard_map/ppermute | solution.py:277
  98.4 0.8 copy-start.1
  99.3 3.5 %collective-permute-start.13 = (f32[512,128]{1,0:T(8,128)S(1)}, f32[512,128]{1,0:T(8,128)S(1)}, u32[]{:S(2)}, u32[]{:S(2)}) collective-permute-start(f32[512,128]{1,0:T(8,128)S(1)} %constant_dynamic-slice_fusion), channel_id=1, source_target_pairs={{0,16},{16,0},{32,48},{48,32},{64,80},{80,64},{96,112},{112,96},{1... | collective-permute-start | bytes 786440 | tf_op jit(solution)/shard_map/ppermute | solution.py:316
  103.8 54.9 %copy-start.2 = (f32[256,256]{1,0:T(8,128)S(1)}, f32[256,256]{1,0:T(8,128)}, u32[]{:S(2)}) copy-start(f32[256,256]{1,0:T(8,128)} %t_one_ref.1) | copy-start | bytes 786436
  103.8 54.9 %copy-start.3 = (f32[256,256]{1,0:T(8,128)S(1)}, f32[256,256]{1,0:T(8,128)}, u32[]{:S(2)}) copy-start(f32[256,256]{1,0:T(8,128)} %t_two_ref.1) | copy-start | bytes 786436
  150.6 8.1 %collective-permute-start.14 = (f32[512,128]{1,0:T(8,128)S(1)}, f32[512,128]{1,0:T(8,128)S(1)}, u32[]{:S(2)}, u32[]{:S(2)}) collective-permute-start(f32[512,128]{1,0:T(8,128)S(1)} %bitcast.18), channel_id=1, source_target_pairs={{0,16},{16,0},{32,48},{48,32},{64,80},{80,64},{96,112},{112,96},{1... | collective-permute-start | bytes 786440 | tf_op jit(solution)/shard_map/ppermute | solution.py:327

commit v11 on v8

--- a/solution.py
+++ b/solution.py
@@ -11,6 +11,7 @@
 BF16 = jnp.bfloat16
 XA, XB, YA, YB = 1, 3, 4, 12
 SHARES = (7, 5, 7, 5)
+ORDER = ((0, 1), (2, 3))
 PAIRS = 2
 NEAR = 4
 FAR = 4
@@ -112,7 +113,7 @@
     return out[0], out[1], out[2:-1], out[-1]
 
 
-def late_kernel(pieces, k, width, acc_ref, zb_ref, *refs):
+def late_kernel(pieces, first, k, width, acc_ref, zb_ref, *refs):
     count = len(pieces)
     firsts, gots, out_ref, kept = refs[: 2 * count], refs[2 * count : 3 * count], refs[3 * count + 1], refs[3 * count + 2]
     scratch = refs[3 * count + 3 :]
@@ -122,7 +123,8 @@
     loads = [pltpu.make_async_copy(gots[p], raw[p], load_sems.at[p]) for p in range(count)]
     for load in loads:
         load.start()
-    out_ref[: 2 * k, :] = acc_ref[...]
+    done = acc_ref.shape[0]
+    out_ref[:done, :] = acc_ref[...]
     copies = []
     for p, piece in enumerate(pieces):
         got = pairs[2 * p : 2 * p + 2]
@@ -144,17 +146,17 @@
         gram = dot_t(one_h, two_h) + (dot_t(one_h, two_l) + dot_t(one_l, two_h))
         for i in range(k // m):
             rows, part = slice((2 + i) * k, (3 + i) * k), gram[:, i * m : (i + 1) * m]
-            out_ref[rows, :] = part if p == 0 else out_ref[rows, :] + part
+            out_ref[rows, :] = part if first and p == 0 else out_ref[rows, :] + part
     for copy in copies:
         copy.wait()
 
 
-def late(acc, zb, firsts, gots, kept, pieces, k, width):
+def late(acc, zb, firsts, gots, kept, pieces, first, k, width):
     m = zb.shape[1] // 2
     count = len(pieces)
     dma = pltpu.SemaphoreType.DMA
     return pl.pallas_call(
-        functools.partial(late_kernel, pieces, k, width),
+        functools.partial(late_kernel, pieces, first, k, width),
         out_shape=[jax.ShapeDtypeStruct((2 * k + k * k // m, m), F32), jax.ShapeDtypeStruct(kept.shape, BF16)],
         in_specs=vmem_specs(2 + 2 * count) + any_specs(count + 1),
         out_specs=vmem_specs(1) + any_specs(1),
@@ -292,7 +294,10 @@
     place = jnp.stack([lax.axis_index("col"), lax.axis_index("row") % PAIRS]).astype(jnp.int32)
     place = lax.optimization_barrier(place)
     part, z_both, firsts, kept = early(z_slab, [half[0] for half in halves], pieces, k, width)
-    part, kept = late(part, z_both, firsts, [half[1] for half in halves], kept, pieces, k, width)
+    for pair in ORDER:
+        two = [half for p in pair for half in firsts[2 * p : 2 * p + 2]]
+        some, gots = [pieces[p] for p in pair], [halves[p][1] for p in pair]
+        part, kept = late(part, z_both, two, gots, kept, some, pair == ORDER[0], k, width)
     mine, other = sum_over_row(part)
     return apply(place, mine, other, t_first, t_second, z_slab, kept, pieces, width)
 

time: 141 us -> 140 us (level)
  local copies, waits for them, and re-layouts: 0.18 us -> 2.52 us
  waiting for transfers between devices: 13.8 us -> 11.9 us
  other arithmetic: 3.29 us -> 1.61 us
    unnamed x6 -> x8, local copies, waits for them, and re-layouts: 0.02 us -> 2.36 us
    ppermute x12, waiting for transfers between devices: 11.6 us -> 9.68 us  [widen(): got = lax.ppermute(data, 'col', [(i, i ^ mask) for i in range(size)])]
    concatenate x4, other arithmetic: 1.89 us -> 0.21 us  [gather_pieces(): part = jnp.concatenate([part, got], 0)]
    pallas_call x1 -> x2, Pallas kernels: 5.4 us -> 6.82 us  [late(): pl.pallas_call(functools.partial(late_kernel, pieces, first, k, width), o...]
  transfers between devices with their start and end apart: 14 -> 14, of which waited for: 7 -> 7; matrix products, arithmetic and copies ran while one was open for 2% -> 0% of each run, Pallas kernels for 3% -> 4%
where the time goes in v11:
time: 140 us; the launch traced here: 139 us
  starting transfers between devices  55.8 us (40%)
  blocking collectives  51.9 us (37%)
  Pallas kernels  15.2 us (11%)
  waiting for transfers between devices  11.9 us (8%)
  local copies, waits for them, and re-layouts  2.52 us (2%)
  other arithmetic  1.61 us (1%)
    ppermute x12, starting transfers between devices, widen(): got = lax.ppermute(data, 'col', [(i, i ^ mask) for i in range(size)])  43.1 us
    all_to_all x1, blocking collectives, sum_over_row(): lax.all_to_all(jnp.broadcast_to(mine[None], (FAR,) + mine.shape), 'row',...  26.9 us
    all_to_all x1, blocking collectives, sum_over_row(): lax.all_to_all(jnp.broadcast_to(mine[None], (NEAR,) + mine.shape), 'row',...  12.6 us
    all_to_all x1, blocking collectives, sum_over_row(): lax.all_to_all(mine.reshape(NEAR, half // NEAR, m), 'row', 0, 0, axis_ind...  12.4 us
    ppermute x12, waiting for transfers between devices, widen(): got = lax.ppermute(data, 'col', [(i, i ^ mask) for i in range(size)])  9.68 us
    ppermute x1, starting transfers between devices, sum_over_row(): return (mine, lax.ppermute(mine, 'row', pair))  6.93 us
    pallas_call x2, Pallas kernels, late(): pl.pallas_call(functools.partial(late_kernel, pieces, first, k, width), o...  6.82 us
    pallas_call x1, Pallas kernels, apply(): pl.pallas_call(functools.partial(apply_kernel, pieces, width), out_shape=...  5.83 us
  transfers between devices with their start and end apart: 14, of which 7 were waited for; matrix products, arithmetic and copies ran while one was open for 0% of the time, Pallas kernels for 4%

profile of v11, /device:TPU:1, one launch (start us, length us, event | category | flops | bytes accessed | tf_op | source)
XLA Modules:
  0.0 139.3 jit_solution(11321557400071951140)
XLA Ops:
  0.0 1.0 pad_maximum_fusion.6
  1.1 3.9 %collective-permute-start = (f32[32,1536]{1,0:T(8,128)S(1)}, f32[32,1536]{1,0:T(8,128)S(1)}, u32[]{:S(2)}, u32[]{:S(2)}) collective-permute-start(f32[32,1536]{1,0:T(8,128)S(1)} %get-tuple-element.36), channel_id=1, source_target_pairs={{0,1},{1,0},{2,3},{3,2},{4,5},{5,4},{6,7},{7,6},{8,9},{9,8},{10,11... | collective-permute-start | bytes 589832 | tf_op jit(solution)/shard_map/ppermute | solution.py:239
  5.0 3.2 %collective-permute-start.4 = (f32[32,1536]{1,0:T(8,128)S(1)}, f32[32,1536]{1,0:T(8,128)S(1)}, u32[]{:S(2)}, u32[]{:S(2)}) collective-permute-start(f32[32,1536]{1,0:T(8,128)S(1)} %get-tuple-element.35), channel_id=1, source_target_pairs={{0,4},{1,5},{2,6},{3,7},{4,0},{5,1},{6,2},{7,3},{8,12},{9,13},{10,... | collective-permute-start | bytes 589832 | tf_op jit(solution)/shard_map/ppermute | solution.py:239
  8.3 0.0 collective-permute-done
  8.3 5.7 %collective-permute-start.1 = (f32[64,1536]{1,0:T(8,128)S(1)}, f32[64,1536]{1,0:T(8,128)S(1)}, u32[]{:S(2)}, u32[]{:S(2)}) collective-permute-start(f32[64,1536]{1,0:T(8,128)S(1)} %pad_maximum_fusion.7), channel_id=1, source_target_pairs={{0,3},{1,2},{2,1},{3,0},{4,7},{5,6},{6,5},{7,4},{8,11},{9,10},{10,... | collective-permute-start | bytes 1179656 | tf_op jit(solution)/shard_map/ppermute | solution.py:239
  14.0 0.0 collective-permute-done.4
  14.1 4.6 %collective-permute-start.5 = (f32[64,1536]{1,0:T(8,128)S(1)}, f32[64,1536]{1,0:T(8,128)S(1)}, u32[]{:S(2)}, u32[]{:S(2)}) collective-permute-start(f32[64,1536]{1,0:T(8,128)S(1)} %pad_maximum_fusion.8), channel_id=1, source_target_pairs={{0,12},{1,13},{2,14},{3,15},{4,8},{5,9},{6,10},{7,11},{8,4},{9,5},... | collective-permute-start | bytes 1179656 | tf_op jit(solution)/shard_map/ppermute | solution.py:239
  18.7 0.5 collective-permute-done.1
  19.2 0.1 pad_maximum_fusion.2
  19.3 4.9 %collective-permute-start.2 = (f32[128,896]{1,0:T(8,128)S(1)}, f32[128,896]{1,0:T(8,128)S(1)}, u32[]{:S(2)}, u32[]{:S(2)}) collective-permute-start(f32[128,896]{1,0:T(8,128)S(1)} %slice.25), channel_id=1, source_target_pairs={{0,4},{1,5},{2,6},{3,7},{4,0},{5,1},{6,2},{7,3},{8,12},{9,13},{10,... | collective-permute-start | bytes 1376264 | tf_op jit(solution)/shard_map/ppermute | solution.py:239
  24.2 1.1 collective-permute-done.5
  25.3 0.1 pad_maximum_fusion.3
  25.4 1.9 %collective-permute-start.6 = (f32[128,896]{1,0:T(8,128)S(1)}, f32[128,896]{1,0:T(8,128)S(1)}, u32[]{:S(2)}, u32[]{:S(2)}) collective-permute-start(f32[128,896]{1,0:T(8,128)S(1)} %slice.27), channel_id=1, source_target_pairs={{0,1},{1,0},{2,3},{3,2},{4,5},{5,4},{6,7},{7,6},{8,9},{9,8},{10,11... | collective-permute-start | bytes 1376264 | tf_op jit(solution)/shard_map/ppermute | solution.py:239
  27.3 5.3 %collective-permute-start.3 = (f32[128,640]{1,0:T(8,128)S(1)}, f32[128,640]{1,0:T(8,128)S(1)}, u32[]{:S(2)}, u32[]{:S(2)}) collective-permute-start(f32[128,640]{1,0:T(8,128)S(1)} %pad_maximum_fusion.10), channel_id=1, source_target_pairs={{0,12},{1,13},{2,14},{3,15},{4,8},{5,9},{6,10},{7,11},{8,4},{9,5},... | collective-permute-start | bytes 983048 | tf_op jit(solution)/shard_map/ppermute | solution.py:239
  32.7 3.0 %collective-permute-start.7 = (f32[128,640]{1,0:T(8,128)S(1)}, f32[128,640]{1,0:T(8,128)S(1)}, u32[]{:S(2)}, u32[]{:S(2)}) collective-permute-start(f32[128,640]{1,0:T(8,128)S(1)} %pad_maximum_fusion.9), channel_id=1, source_target_pairs={{0,3},{1,2},{2,1},{3,0},{4,7},{5,6},{6,5},{7,4},{8,11},{9,10},{10,... | collective-permute-start | bytes 983048 | tf_op jit(solution)/shard_map/ppermute | solution.py:239
  35.7 0.0 collective-permute-done.2
  35.7 0.1 pad_maximum_fusion.refs_0_
  35.7 2.4 %collective-permute-start.8 = (f32[256,896]{1,0:T(8,128)S(1)}, f32[256,896]{1,0:T(8,128)}, u32[]{:S(2)}, u32[]{:S(2)}) collective-permute-start(f32[256,896]{1,0:T(8,128)S(1)} %pad_maximum_fusion.refs_0_), channel_id=1, source_target_pairs={{0,12},{1,13},{2,14},{3,15},{4,8},{5,9},{6,10},{7,11},{8,4},{9,5},... | collective-permute-start | bytes 2752520 | tf_op jit(solution)/shard_map/ppermute | solution.py:239
  38.2 0.0 collective-permute-done.6
  38.2 0.1 pad_maximum_fusion.1.refs_2_
  38.3 4.2 %collective-permute-start.10 = (f32[256,896]{1,0:T(8,128)S(1)}, f32[256,896]{1,0:T(8,128)}, u32[]{:S(2)}, u32[]{:S(2)}) collective-permute-start(f32[256,896]{1,0:T(8,128)S(1)} %pad_maximum_fusion.1.refs_2_), channel_id=1, source_target_pairs={{0,3},{1,2},{2,1},{3,0},{4,7},{5,6},{6,5},{7,4},{8,11},{9,10},{10,... | collective-permute-start | bytes 2752520 | tf_op jit(solution)/shard_map/ppermute | solution.py:239
  42.5 0.0 collective-permute-done.3
  42.6 1.9 %collective-permute-start.9 = (f32[256,640]{1,0:T(8,128)S(1)}, f32[256,640]{1,0:T(8,128)}, u32[]{:S(2)}, u32[]{:S(2)}) collective-permute-start(f32[256,640]{1,0:T(8,128)S(1)} %pad_maximum_fusion.4.refs_1_), channel_id=1, source_target_pairs={{0,4},{1,5},{2,6},{3,7},{4,0},{5,1},{6,2},{7,3},{8,12},{9,13},{10,... | collective-permute-start | bytes 1966088 | tf_op jit(solution)/shard_map/ppermute | solution.py:239
  44.5 0.0 collective-permute-done.7
  44.6 1.9 %collective-permute-start.11 = (f32[256,640]{1,0:T(8,128)S(1)}, f32[256,640]{1,0:T(8,128)}, u32[]{:S(2)}, u32[]{:S(2)}) collective-permute-start(f32[256,640]{1,0:T(8,128)S(1)} %pad_maximum_fusion.5.refs_3_), channel_id=1, source_target_pairs={{0,1},{1,0},{2,3},{3,2},{4,5},{5,4},{6,7},{7,6},{8,9},{9,8},{10,11... | collective-permute-start | bytes 1966088 | tf_op jit(solution)/shard_map/ppermute | solution.py:239
  46.5 0.0 copy-start
  46.5 1.4 %copy-done = f32[3072,128]{1,0:T(8,128)S(1)} copy-done((f32[3072,128]{1,0:T(8,128)S(1)}, f32[3072,128]{1,0:T(8,128)}, u32[]{:S(2)}) %copy-start) | copy-done | bytes 1572888
  47.9 2.6 %shard_map.55 = (f32[512,128]{1,0:T(8,128)S(1)}, bf16[3072,256]{1,0:T(8,128)(2,1)S(1)}, bf16[256,896]{1,0:T(8,128)(2,1)S(1)}, bf16[256,896]{1,0:T(8,128)(2,1)S(1...) custom-call(f32[3072,128]{1,0:T(8,128)S(1)} %copy-done, ...), custom_call_target="tpu_custom_call" | custom-call | flops 603979776 | bytes 12582912 | tf_op jit(solution)/shard_map/pallas_call | solution.py:104
  50.5 6.0 %collective-permute-done.9.refs_5_ = f32[256,640]{1,0:T(8,128)} collective-permute-done((f32[256,640]{1,0:T(8,128)S(1)}, f32[256,640]{1,0:T(8,128)}, u32[]{:S(2)}, u32[]{:S(2)}) %collective-permute-start.9) | collective-permute-done | bytes 655392 | tf_op jit(solution)/shard_map/ppermute | solution.py:239
  56.5 2.0 %collective-permute-done.8.refs_4_ = f32[256,896]{1,0:T(8,128)} collective-permute-done((f32[256,896]{1,0:T(8,128)S(1)}, f32[256,896]{1,0:T(8,128)}, u32[]{:S(2)}, u32[]{:S(2)}) %collective-permute-start.8) | collective-permute-done | bytes 917536 | tf_op jit(solution)/shard_map/ppermute | solution.py:239
  58.5 0.0 copy-start.1
  58.5 0.0 copy-start.2
  58.5 3.4 %shard_map.56 = (f32[1024,128]{1,0:T(8,128)S(1)}, bf16[6,1024,3072]{2,1,0:T(8,128)(2,1)}) custom-call(f32[512,128]{1,0:T(8,128)S(1)} %get-tuple-element.20.acc_ref, bf16[3072,256]{1,0:T(8,128)(2,1)S(1)} %get-tuple-element.21.zb_ref, bf16[256,896]{1,0:T(8,128)(2,1)S(1)} %get-tuple-element.22.refs_0_, ...), custom_call_target="tpu_custom_call", output_to_operand_aliasing={{1}: (8, {})} | custom-call | tf_op jit(solution)/shard_map/pallas_call | solution.py:158
  61.9 0.0 collective-permute-done.11.refs_5_
  61.9 0.1 collective-permute-done.10.refs_4_
  62.0 3.4 %shard_map.57 = (f32[1024,128]{1,0:T(8,128)S(1)}, bf16[6,1024,3072]{2,1,0:T(8,128)(2,1)}) custom-call(f32[1024,128]{1,0:T(8,128)S(1)} %get-tuple-element.27.acc_ref, bf16[3072,256]{1,0:T(8,128)(2,1)S(1)} %get-tuple-element.21.zb_ref, bf16[256,896]{1,0:T(8,128)(2,1)S(1)} %get-tuple-element.28.refs_0_, ...), custom_call_target="tpu_custom_call", output_to_operand_aliasing={{1}: (8, {})} | custom-call | tf_op jit(solution)/shard_map/pallas_call | solution.py:158
  65.5 5.8 %collective-permute-start.12 = (f32[512,128]{1,0:T(8,128)S(1)}, f32[512,128]{1,0:T(8,128)S(1)}, u32[]{:S(2)}, u32[]{:S(2)}) collective-permute-start(f32[512,128]{1,0:T(8,128)S(1)} %constant_dynamic-slice_fusion), channel_id=1, source_target_pairs={{0,16},{16,0},{32,48},{48,32},{64,80},{80,64},{96,112},{112,96},{1... | collective-permute-start | bytes 786440 | tf_op jit(solution)/shard_map/ppermute | solution.py:275
  71.3 1.1 collective-permute-done.12
  72.5 12.4 %all_to_all.15 = f32[4,128,128]{2,1,0:T(8,128)S(1)} all-to-all(f32[4,128,128]{2,1,0:T(8,128)S(1)} %bitcast.8), channel_id=1, replica_groups={{0,32,64,96},{16,48,80,112},{128,160,192,224},{144,176,208,240},{256,28..., dimensions={0} | all-to-all | bytes 524288 | tf_op jit(solution)/shard_map/all_to_all | solution.py:276
  84.9 26.9 %all_to_all.16 = f32[4,128,128]{2,1,0:T(8,128)S(1)} all-to-all(f32[4,128,128]{2,1,0:T(8,128)S(1)} %broadcast_in_dim.4), channel_id=1, replica_groups={{0,128,256,384},{16,144,272,400},{32,160,288,416},{48,176,304,432},{64,..., dimensions={0} | all-to-all | bytes 524288 | tf_op jit(solution)/shard_map/all_to_all | solution.py:278
  111.8 12.6 %all_to_all.17 = f32[4,128,128]{2,1,0:T(8,128)S(1)} all-to-all(f32[4,128,128]{2,1,0:T(8,128)S(1)} %broadcast_in_dim.5), channel_id=1, replica_groups={{0,32,64,96},{16,48,80,112},{128,160,192,224},{144,176,208,240},{256,28..., dimensions={0} | all-to-all | bytes 524288 | tf_op jit(solution)/shard_map/all_to_all | solution.py:282
  124.4 6.9 %collective-permute-start.13 = (f32[512,128]{1,0:T(8,128)S(1)}, f32[512,128]{1,0:T(8,128)S(1)}, u32[]{:S(2)}, u32[]{:S(2)}) collective-permute-start(f32[512,128]{1,0:T(8,128)S(1)} %bitcast.6), channel_id=1, source_target_pairs={{0,16},{16,0},{32,48},{48,32},{64,80},{80,64},{96,112},{112,96},{1... | collective-permute-start | bytes 786440 | tf_op jit(solution)/shard_map/ppermute | solution.py:286
  131.4 0.1 pad_add_fusion.place_ref
  131.4 1.1 collective-permute-done.13.other_ref
  132.5 0.0 copy-done.1
  132.5 0.0 copy-done.2
  132.5 0.0 copy-start.3
  132.5 0.9 copy-done.3
  133.4 5.8 %shard_map.58 = f32[3072,128]{1,0:T(8,128)} custom-call(s32[2]{0:T(128)S(1)} %pad_add_fusion.place_ref, f32[512,128]{1,0:T(8,128)S(1)} %bitcast.7, f32[512,128]{1,0:T(8,128)S(1)} %collective-permute-done.13.other_ref, f32[256,256]{1,0:T(8,128)S(1)} %copy-done.2, f32[256,256]{1,0:T(8,128)S(1)} %copy-done.3, f32[3072,128]{1,0:T(8,128)S(1)} %copy-done.1, ...), custom_call_target="tpu_custom_call" | custom-call | tf_op jit(solution)/shard_map/pallas_call | solution.py:226
  (15 shorter events, 0.4 us)
Async XLA Ops:
  1.1 7.2 %collective-permute-start = (f32[32,1536]{1,0:T(8,128)S(1)}, f32[32,1536]{1,0:T(8,128)S(1)}, u32[]{:S(2)}, u32[]{:S(2)}) collective-permute-start(f32[32,1536]{1,0:T(8,128)S(1)} %get-tuple-element.36), channel_id=1, source_target_pairs={{0,1},{1,0},{2,3},{3,2},{4,5},{5,4},{6,7},{7,6},{8,9},{9,8},{10,11... | collective-permute-start | bytes 589832 | tf_op jit(solution)/shard_map/ppermute | solution.py:239
  5.0 9.0 %collective-permute-start.4 = (f32[32,1536]{1,0:T(8,128)S(1)}, f32[32,1536]{1,0:T(8,128)S(1)}, u32[]{:S(2)}, u32[]{:S(2)}) collective-permute-start(f32[32,1536]{1,0:T(8,128)S(1)} %get-tuple-element.35), channel_id=1, source_target_pairs={{0,4},{1,5},{2,6},{3,7},{4,0},{5,1},{6,2},{7,3},{8,12},{9,13},{10,... | collective-permute-start | bytes 589832 | tf_op jit(solution)/shard_map/ppermute | solution.py:239
  8.3 10.9 %collective-permute-start.1 = (f32[64,1536]{1,0:T(8,128)S(1)}, f32[64,1536]{1,0:T(8,128)S(1)}, u32[]{:S(2)}, u32[]{:S(2)}) collective-permute-start(f32[64,1536]{1,0:T(8,128)S(1)} %pad_maximum_fusion.7), channel_id=1, source_target_pairs={{0,3},{1,2},{2,1},{3,0},{4,7},{5,6},{6,5},{7,4},{8,11},{9,10},{10,... | collective-permute-start | bytes 1179656 | tf_op jit(solution)/shard_map/ppermute | solution.py:239
  14.1 11.2 %collective-permute-start.5 = (f32[64,1536]{1,0:T(8,128)S(1)}, f32[64,1536]{1,0:T(8,128)S(1)}, u32[]{:S(2)}, u32[]{:S(2)}) collective-permute-start(f32[64,1536]{1,0:T(8,128)S(1)} %pad_maximum_fusion.8), channel_id=1, source_target_pairs={{0,12},{1,13},{2,14},{3,15},{4,8},{5,9},{6,10},{7,11},{8,4},{9,5},... | collective-permute-start | bytes 1179656 | tf_op jit(solution)/shard_map/ppermute | solution.py:239
  19.3 16.4 %collective-permute-start.2 = (f32[128,896]{1,0:T(8,128)S(1)}, f32[128,896]{1,0:T(8,128)S(1)}, u32[]{:S(2)}, u32[]{:S(2)}) collective-permute-start(f32[128,896]{1,0:T(8,128)S(1)} %slice.25), channel_id=1, source_target_pairs={{0,4},{1,5},{2,6},{3,7},{4,0},{5,1},{6,2},{7,3},{8,12},{9,13},{10,... | collective-permute-start | bytes 1376264 | tf_op jit(solution)/shard_map/ppermute | solution.py:239
  25.4 12.8 %collective-permute-start.6 = (f32[128,896]{1,0:T(8,128)S(1)}, f32[128,896]{1,0:T(8,128)S(1)}, u32[]{:S(2)}, u32[]{:S(2)}) collective-permute-start(f32[128,896]{1,0:T(8,128)S(1)} %slice.27), channel_id=1, source_target_pairs={{0,1},{1,0},{2,3},{3,2},{4,5},{5,4},{6,7},{7,6},{8,9},{9,8},{10,11... | collective-permute-start | bytes 1376264 | tf_op jit(solution)/shard_map/ppermute | solution.py:239
  27.3 15.2 %collective-permute-start.3 = (f32[128,640]{1,0:T(8,128)S(1)}, f32[128,640]{1,0:T(8,128)S(1)}, u32[]{:S(2)}, u32[]{:S(2)}) collective-permute-start(f32[128,640]{1,0:T(8,128)S(1)} %pad_maximum_fusion.10), channel_id=1, source_target_pairs={{0,12},{1,13},{2,14},{3,15},{4,8},{5,9},{6,10},{7,11},{8,4},{9,5},... | collective-permute-start | bytes 983048 | tf_op jit(solution)/shard_map/ppermute | solution.py:239
  32.7 11.8 %collective-permute-start.7 = (f32[128,640]{1,0:T(8,128)S(1)}, f32[128,640]{1,0:T(8,128)S(1)}, u32[]{:S(2)}, u32[]{:S(2)}) collective-permute-start(f32[128,640]{1,0:T(8,128)S(1)} %pad_maximum_fusion.9), channel_id=1, source_target_pairs={{0,3},{1,2},{2,1},{3,0},{4,7},{5,6},{6,5},{7,4},{8,11},{9,10},{10,... | collective-permute-start | bytes 983048 | tf_op jit(solution)/shard_map/ppermute | solution.py:239
  35.7 22.8 %collective-permute-start.8 = (f32[256,896]{1,0:T(8,128)S(1)}, f32[256,896]{1,0:T(8,128)}, u32[]{:S(2)}, u32[]{:S(2)}) collective-permute-start(f32[256,896]{1,0:T(8,128)S(1)} %pad_maximum_fusion.refs_0_), channel_id=1, source_target_pairs={{0,12},{1,13},{2,14},{3,15},{4,8},{5,9},{6,10},{7,11},{8,4},{9,5},... | collective-permute-start | bytes 2752520 | tf_op jit(solution)/shard_map/ppermute | solution.py:239
  38.3 23.7 %collective-permute-start.10 = (f32[256,896]{1,0:T(8,128)S(1)}, f32[256,896]{1,0:T(8,128)}, u32[]{:S(2)}, u32[]{:S(2)}) collective-permute-start(f32[256,896]{1,0:T(8,128)S(1)} %pad_maximum_fusion.1.refs_2_), channel_id=1, source_target_pairs={{0,3},{1,2},{2,1},{3,0},{4,7},{5,6},{6,5},{7,4},{8,11},{9,10},{10,... | collective-permute-start | bytes 2752520 | tf_op jit(solution)/shard_map/ppermute | solution.py:239
  42.6 14.0 %collective-permute-start.9 = (f32[256,640]{1,0:T(8,128)S(1)}, f32[256,640]{1,0:T(8,128)}, u32[]{:S(2)}, u32[]{:S(2)}) collective-permute-start(f32[256,640]{1,0:T(8,128)S(1)} %pad_maximum_fusion.4.refs_1_), channel_id=1, source_target_pairs={{0,4},{1,5},{2,6},{3,7},{4,0},{5,1},{6,2},{7,3},{8,12},{9,13},{10,... | collective-permute-start | bytes 1966088 | tf_op jit(solution)/shard_map/ppermute | solution.py:239
  44.6 17.3 %collective-permute-start.11 = (f32[256,640]{1,0:T(8,128)S(1)}, f32[256,640]{1,0:T(8,128)}, u32[]{:S(2)}, u32[]{:S(2)}) collective-permute-start(f32[256,640]{1,0:T(8,128)S(1)} %pad_maximum_fusion.5.refs_3_), channel_id=1, source_target_pairs={{0,1},{1,0},{2,3},{3,2},{4,5},{5,4},{6,7},{7,6},{8,9},{9,8},{10,11... | collective-permute-start | bytes 1966088 | tf_op jit(solution)/shard_map/ppermute | solution.py:239
  46.5 1.4 %copy-start = (f32[3072,128]{1,0:T(8,128)S(1)}, f32[3072,128]{1,0:T(8,128)}, u32[]{:S(2)}) copy-start(f32[3072,128]{1,0:T(8,128)} %z_ref.3) | copy-start | bytes 4718596
  58.5 74.0 %copy-start.1 = (f32[3072,128]{1,0:T(8,128)S(1)}, f32[3072,128]{1,0:T(8,128)}, u32[]{:S(2)}) copy-start(f32[3072,128]{1,0:T(8,128)} %z_ref.3) | copy-start | bytes 4718596
  58.5 74.0 %copy-start.2 = (f32[256,256]{1,0:T(8,128)S(1)}, f32[256,256]{1,0:T(8,128)}, u32[]{:S(2)}) copy-start(f32[256,256]{1,0:T(8,128)} %t_one_ref.1) | copy-start | bytes 786436
  65.5 7.0 %collective-permute-start.12 = (f32[512,128]{1,0:T(8,128)S(1)}, f32[512,128]{1,0:T(8,128)S(1)}, u32[]{:S(2)}, u32[]{:S(2)}) collective-permute-start(f32[512,128]{1,0:T(8,128)S(1)} %constant_dynamic-slice_fusion), channel_id=1, source_target_pairs={{0,16},{16,0},{32,48},{48,32},{64,80},{80,64},{96,112},{112,96},{1... | collective-permute-start | bytes 786440 | tf_op jit(solution)/shard_map/ppermute | solution.py:275
  124.4 8.1 %collective-permute-start.13 = (f32[512,128]{1,0:T(8,128)S(1)}, f32[512,128]{1,0:T(8,128)S(1)}, u32[]{:S(2)}, u32[]{:S(2)}) collective-permute-start(f32[512,128]{1,0:T(8,128)S(1)} %bitcast.6), channel_id=1, source_target_pairs={{0,16},{16,0},{32,48},{48,32},{64,80},{80,64},{96,112},{112,96},{1... | collective-permute-start | bytes 786440 | tf_op jit(solution)/shard_map/ppermute | solution.py:286
  132.5 1.0 copy-start.3

commit v12 on v11

--- a/solution.py
+++ b/solution.py
@@ -169,16 +169,14 @@
 
 
 def apply_kernel(pieces, width, place_ref, mine_ref, other_ref, t_one_ref, t_two_ref, z_ref, kept_ref, *refs):
-    out_ref, held, z_held, out_held, total_ref, x_ref, slot_ref, sems, z_sems, out_sems = refs
+    out_ref, held, out_held, total_ref, x_ref, slot_ref, sems, out_sems = refs
     k = t_one_ref.shape[0]
     m = z_ref.shape[1]
-    loads, z_loads = [], []
+    loads = []
     for p, piece in enumerate(pieces):
         lanes = pl.ds(piece.base, piece.size)
         loads.append(pltpu.make_async_copy(kept_ref.at[0, :, lanes], held.at[:, lanes], sems.at[p]))
-        z_loads.append(pltpu.make_async_copy(z_ref.at[lanes, :], z_held.at[lanes, :], z_sems.at[p]))
         loads[p].start()
-        z_loads[p].start()
     core = place_ref[1]
     half = mine_ref.shape[0]
     total_ref[block(core, half), :] = mine_ref[...]
@@ -193,10 +191,8 @@
             x_ref[row + mask * width : row + (mask + 1) * width, :] = slot_ref[block(lax.bitwise_xor(col, mask), width), :]
 
     solve(t_two_ref, total_ref[k : 2 * k, :], k)
-    coeff = total_ref[:k, :]
-    for i in range(k // m):
-        row = (2 + i) * k
-        coeff = coeff - thrice(total_ref[row : row + k, :], x_ref[k + i * m : k + (i + 1) * m, :])
+    gram = jnp.concatenate([total_ref[(2 + i) * k : (3 + i) * k, :] for i in range(k // m)], 1)
+    coeff = total_ref[:k, :] - thrice(gram, x_ref[k:, :])
     solve(t_one_ref, coeff, 0)
     stores = []
     for p, piece in enumerate(pieces):
@@ -207,11 +203,10 @@
         x_h, x_l = split(slot_ref[...].T)
         x_both = jnp.concatenate([x_h, x_l], 0)
         loads[p].wait()
-        z_loads[p].wait()
         rows = slice(piece.base, piece.base + piece.size)
         wide = dot(x_both, held[: 2 * k, rows])
         moved = wide[:m, :] + (wide[m:, :] + dot(x_h, held[2 * k :, rows]))
-        out_held[rows, :] = z_held[rows, :] - moved.T
+        out_held[rows, :] = z_ref[rows, :] - moved.T
         lanes = pl.ds(piece.base, piece.size)
         stores.append(pltpu.make_async_copy(out_held.at[lanes, :], out_ref.at[lanes, :], out_sems.at[p]))
         stores[-1].start()
@@ -226,11 +221,11 @@
     return pl.pallas_call(
         functools.partial(apply_kernel, pieces, width),
         out_shape=jax.ShapeDtypeStruct(z.shape, F32),
-        in_specs=SMEM + vmem_specs(4) + any_specs(2),
+        in_specs=SMEM + vmem_specs(5) + any_specs(1),
         out_specs=pl.BlockSpec(memory_space=pl.ANY),
-        scratch_shapes=[pltpu.VMEM(kept.shape[1:], BF16), rows, rows, pltpu.VMEM((2 * mine.shape[0], m), F32)]
+        scratch_shapes=[pltpu.VMEM(kept.shape[1:], BF16), rows, pltpu.VMEM((2 * mine.shape[0], m), F32)]
         + [coeffs, coeffs]
-        + [pltpu.SemaphoreType.DMA((len(pieces),))] * 3,
+        + [pltpu.SemaphoreType.DMA((len(pieces),))] * 2,
         compiler_params=pltpu.CompilerParams(vmem_limit_bytes=GRANT),
     )(place, mine, other, t_one, t_two, z, kept)
 

time: 140 us -> 141 us (level)
  no operation moved by 1% of the time
where the time goes in v12:
time: 141 us; the launch traced here: 140 us
  starting transfers between devices  55.8 us (40%)
  blocking collectives  51.9 us (37%)
  Pallas kernels  15.8 us (11%)
  waiting for transfers between devices  11.9 us (8%)
  local copies, waits for them, and re-layouts  2.52 us (2%)
  other arithmetic  1.61 us (1%)
    ppermute x12, starting transfers between devices, widen(): got = lax.ppermute(data, 'col', [(i, i ^ mask) for i in range(size)])  43.1 us
    all_to_all x1, blocking collectives, sum_over_row(): lax.all_to_all(jnp.broadcast_to(mine[None], (FAR,) + mine.shape), 'row',...  26.9 us
    all_to_all x1, blocking collectives, sum_over_row(): lax.all_to_all(jnp.broadcast_to(mine[None], (NEAR,) + mine.shape), 'row',...  12.6 us
    all_to_all x1, blocking collectives, sum_over_row(): lax.all_to_all(mine.reshape(NEAR, half // NEAR, m), 'row', 0, 0, axis_ind...  12.4 us
    ppermute x12, waiting for transfers between devices, widen(): got = lax.ppermute(data, 'col', [(i, i ^ mask) for i in range(size)])  9.68 us
    ppermute x1, starting transfers between devices, sum_over_row(): return (mine, lax.ppermute(mine, 'row', pair))  6.93 us
    pallas_call x2, Pallas kernels, late(): pl.pallas_call(functools.partial(late_kernel, pieces, first, k, width), o...  6.82 us
    pallas_call x1, Pallas kernels, apply(): pl.pallas_call(functools.partial(apply_kernel, pieces, width), out_shape=...  6.44 us
  transfers between devices with their start and end apart: 14, of which 7 were waited for; matrix products, arithmetic and copies ran while one was open for 0% of the time, Pallas kernels for 4%

profile of v12, /device:TPU:1, one launch (start us, length us, event | category | flops | bytes accessed | tf_op | source)
XLA Modules:
  0.0 139.9 jit_solution(7526137755283075924)
XLA Ops:
  0.0 1.0 pad_maximum_fusion.6
  1.1 3.9 %collective-permute-start = (f32[32,1536]{1,0:T(8,128)S(1)}, f32[32,1536]{1,0:T(8,128)S(1)}, u32[]{:S(2)}, u32[]{:S(2)}) collective-permute-start(f32[32,1536]{1,0:T(8,128)S(1)} %get-tuple-element.36), channel_id=1, source_target_pairs={{0,1},{1,0},{2,3},{3,2},{4,5},{5,4},{6,7},{7,6},{8,9},{9,8},{10,11... | collective-permute-start | bytes 589832 | tf_op jit(solution)/shard_map/ppermute | solution.py:234
  5.0 3.2 %collective-permute-start.4 = (f32[32,1536]{1,0:T(8,128)S(1)}, f32[32,1536]{1,0:T(8,128)S(1)}, u32[]{:S(2)}, u32[]{:S(2)}) collective-permute-start(f32[32,1536]{1,0:T(8,128)S(1)} %get-tuple-element.35), channel_id=1, source_target_pairs={{0,4},{1,5},{2,6},{3,7},{4,0},{5,1},{6,2},{7,3},{8,12},{9,13},{10,... | collective-permute-start | bytes 589832 | tf_op jit(solution)/shard_map/ppermute | solution.py:234
  8.3 0.0 collective-permute-done
  8.3 5.7 %collective-permute-start.1 = (f32[64,1536]{1,0:T(8,128)S(1)}, f32[64,1536]{1,0:T(8,128)S(1)}, u32[]{:S(2)}, u32[]{:S(2)}) collective-permute-start(f32[64,1536]{1,0:T(8,128)S(1)} %pad_maximum_fusion.7), channel_id=1, source_target_pairs={{0,3},{1,2},{2,1},{3,0},{4,7},{5,6},{6,5},{7,4},{8,11},{9,10},{10,... | collective-permute-start | bytes 1179656 | tf_op jit(solution)/shard_map/ppermute | solution.py:234
  14.0 0.0 collective-permute-done.4
  14.1 4.6 %collective-permute-start.5 = (f32[64,1536]{1,0:T(8,128)S(1)}, f32[64,1536]{1,0:T(8,128)S(1)}, u32[]{:S(2)}, u32[]{:S(2)}) collective-permute-start(f32[64,1536]{1,0:T(8,128)S(1)} %pad_maximum_fusion.8), channel_id=1, source_target_pairs={{0,12},{1,13},{2,14},{3,15},{4,8},{5,9},{6,10},{7,11},{8,4},{9,5},... | collective-permute-start | bytes 1179656 | tf_op jit(solution)/shard_map/ppermute | solution.py:234
  18.7 0.5 collective-permute-done.1
  19.2 0.1 pad_maximum_fusion.2
  19.3 4.9 %collective-permute-start.2 = (f32[128,896]{1,0:T(8,128)S(1)}, f32[128,896]{1,0:T(8,128)S(1)}, u32[]{:S(2)}, u32[]{:S(2)}) collective-permute-start(f32[128,896]{1,0:T(8,128)S(1)} %slice.25), channel_id=1, source_target_pairs={{0,4},{1,5},{2,6},{3,7},{4,0},{5,1},{6,2},{7,3},{8,12},{9,13},{10,... | collective-permute-start | bytes 1376264 | tf_op jit(solution)/shard_map/ppermute | solution.py:234
  24.2 1.1 collective-permute-done.5
  25.3 0.1 pad_maximum_fusion.3
  25.4 1.9 %collective-permute-start.6 = (f32[128,896]{1,0:T(8,128)S(1)}, f32[128,896]{1,0:T(8,128)S(1)}, u32[]{:S(2)}, u32[]{:S(2)}) collective-permute-start(f32[128,896]{1,0:T(8,128)S(1)} %slice.27), channel_id=1, source_target_pairs={{0,1},{1,0},{2,3},{3,2},{4,5},{5,4},{6,7},{7,6},{8,9},{9,8},{10,11... | collective-permute-start | bytes 1376264 | tf_op jit(solution)/shard_map/ppermute | solution.py:234
  27.3 5.3 %collective-permute-start.3 = (f32[128,640]{1,0:T(8,128)S(1)}, f32[128,640]{1,0:T(8,128)S(1)}, u32[]{:S(2)}, u32[]{:S(2)}) collective-permute-start(f32[128,640]{1,0:T(8,128)S(1)} %pad_maximum_fusion.10), channel_id=1, source_target_pairs={{0,12},{1,13},{2,14},{3,15},{4,8},{5,9},{6,10},{7,11},{8,4},{9,5},... | collective-permute-start | bytes 983048 | tf_op jit(solution)/shard_map/ppermute | solution.py:234
  32.7 3.0 %collective-permute-start.7 = (f32[128,640]{1,0:T(8,128)S(1)}, f32[128,640]{1,0:T(8,128)S(1)}, u32[]{:S(2)}, u32[]{:S(2)}) collective-permute-start(f32[128,640]{1,0:T(8,128)S(1)} %pad_maximum_fusion.9), channel_id=1, source_target_pairs={{0,3},{1,2},{2,1},{3,0},{4,7},{5,6},{6,5},{7,4},{8,11},{9,10},{10,... | collective-permute-start | bytes 983048 | tf_op jit(solution)/shard_map/ppermute | solution.py:234
  35.7 0.0 collective-permute-done.2
  35.7 0.1 pad_maximum_fusion.refs_0_
  35.7 2.4 %collective-permute-start.8 = (f32[256,896]{1,0:T(8,128)S(1)}, f32[256,896]{1,0:T(8,128)}, u32[]{:S(2)}, u32[]{:S(2)}) collective-permute-start(f32[256,896]{1,0:T(8,128)S(1)} %pad_maximum_fusion.refs_0_), channel_id=1, source_target_pairs={{0,12},{1,13},{2,14},{3,15},{4,8},{5,9},{6,10},{7,11},{8,4},{9,5},... | collective-permute-start | bytes 2752520 | tf_op jit(solution)/shard_map/ppermute | solution.py:234
  38.2 0.0 collective-permute-done.6
  38.2 0.1 pad_maximum_fusion.1.refs_2_
  38.3 4.2 %collective-permute-start.10 = (f32[256,896]{1,0:T(8,128)S(1)}, f32[256,896]{1,0:T(8,128)}, u32[]{:S(2)}, u32[]{:S(2)}) collective-permute-start(f32[256,896]{1,0:T(8,128)S(1)} %pad_maximum_fusion.1.refs_2_), channel_id=1, source_target_pairs={{0,3},{1,2},{2,1},{3,0},{4,7},{5,6},{6,5},{7,4},{8,11},{9,10},{10,... | collective-permute-start | bytes 2752520 | tf_op jit(solution)/shard_map/ppermute | solution.py:234
  42.5 0.0 collective-permute-done.3
  42.6 1.9 %collective-permute-start.9 = (f32[256,640]{1,0:T(8,128)S(1)}, f32[256,640]{1,0:T(8,128)}, u32[]{:S(2)}, u32[]{:S(2)}) collective-permute-start(f32[256,640]{1,0:T(8,128)S(1)} %pad_maximum_fusion.4.refs_1_), channel_id=1, source_target_pairs={{0,4},{1,5},{2,6},{3,7},{4,0},{5,1},{6,2},{7,3},{8,12},{9,13},{10,... | collective-permute-start | bytes 1966088 | tf_op jit(solution)/shard_map/ppermute | solution.py:234
  44.5 0.0 collective-permute-done.7
  44.6 1.9 %collective-permute-start.11 = (f32[256,640]{1,0:T(8,128)S(1)}, f32[256,640]{1,0:T(8,128)}, u32[]{:S(2)}, u32[]{:S(2)}) collective-permute-start(f32[256,640]{1,0:T(8,128)S(1)} %pad_maximum_fusion.5.refs_3_), channel_id=1, source_target_pairs={{0,1},{1,0},{2,3},{3,2},{4,5},{5,4},{6,7},{7,6},{8,9},{9,8},{10,11... | collective-permute-start | bytes 1966088 | tf_op jit(solution)/shard_map/ppermute | solution.py:234
  46.5 0.0 copy-start
  46.5 1.4 %copy-done = f32[3072,128]{1,0:T(8,128)S(1)} copy-done((f32[3072,128]{1,0:T(8,128)S(1)}, f32[3072,128]{1,0:T(8,128)}, u32[]{:S(2)}) %copy-start) | copy-done | bytes 1572888
  47.9 2.6 %shard_map.55 = (f32[512,128]{1,0:T(8,128)S(1)}, bf16[3072,256]{1,0:T(8,128)(2,1)S(1)}, bf16[256,896]{1,0:T(8,128)(2,1)S(1)}, bf16[256,896]{1,0:T(8,128)(2,1)S(1...) custom-call(f32[3072,128]{1,0:T(8,128)S(1)} %copy-done, ...), custom_call_target="tpu_custom_call" | custom-call | flops 603979776 | bytes 12582912 | tf_op jit(solution)/shard_map/pallas_call | solution.py:104
  50.5 6.0 %collective-permute-done.9.refs_5_ = f32[256,640]{1,0:T(8,128)} collective-permute-done((f32[256,640]{1,0:T(8,128)S(1)}, f32[256,640]{1,0:T(8,128)}, u32[]{:S(2)}, u32[]{:S(2)}) %collective-permute-start.9) | collective-permute-done | bytes 655392 | tf_op jit(solution)/shard_map/ppermute | solution.py:234
  56.5 2.0 %collective-permute-done.8.refs_4_ = f32[256,896]{1,0:T(8,128)} collective-permute-done((f32[256,896]{1,0:T(8,128)S(1)}, f32[256,896]{1,0:T(8,128)}, u32[]{:S(2)}, u32[]{:S(2)}) %collective-permute-start.8) | collective-permute-done | bytes 917536 | tf_op jit(solution)/shard_map/ppermute | solution.py:234
  58.5 0.0 copy-start.1
  58.5 0.0 copy-start.2
  58.5 3.4 %shard_map.56 = (f32[1024,128]{1,0:T(8,128)S(1)}, bf16[6,1024,3072]{2,1,0:T(8,128)(2,1)}) custom-call(f32[512,128]{1,0:T(8,128)S(1)} %get-tuple-element.20.acc_ref, bf16[3072,256]{1,0:T(8,128)(2,1)S(1)} %get-tuple-element.21.zb_ref, bf16[256,896]{1,0:T(8,128)(2,1)S(1)} %get-tuple-element.22.refs_0_, ...), custom_call_target="tpu_custom_call", output_to_operand_aliasing={{1}: (8, {})} | custom-call | tf_op jit(solution)/shard_map/pallas_call | solution.py:158
  61.9 0.0 collective-permute-done.11.refs_5_
  61.9 0.1 collective-permute-done.10.refs_4_
  62.0 3.4 %shard_map.57 = (f32[1024,128]{1,0:T(8,128)S(1)}, bf16[6,1024,3072]{2,1,0:T(8,128)(2,1)}) custom-call(f32[1024,128]{1,0:T(8,128)S(1)} %get-tuple-element.27.acc_ref, bf16[3072,256]{1,0:T(8,128)(2,1)S(1)} %get-tuple-element.21.zb_ref, bf16[256,896]{1,0:T(8,128)(2,1)S(1)} %get-tuple-element.28.refs_0_, ...), custom_call_target="tpu_custom_call", output_to_operand_aliasing={{1}: (8, {})} | custom-call | tf_op jit(solution)/shard_map/pallas_call | solution.py:158
  65.5 5.8 %collective-permute-start.12 = (f32[512,128]{1,0:T(8,128)S(1)}, f32[512,128]{1,0:T(8,128)S(1)}, u32[]{:S(2)}, u32[]{:S(2)}) collective-permute-start(f32[512,128]{1,0:T(8,128)S(1)} %constant_dynamic-slice_fusion), channel_id=1, source_target_pairs={{0,16},{16,0},{32,48},{48,32},{64,80},{80,64},{96,112},{112,96},{1... | collective-permute-start | bytes 786440 | tf_op jit(solution)/shard_map/ppermute | solution.py:270
  71.3 1.1 collective-permute-done.12
  72.5 12.4 %all_to_all.15 = f32[4,128,128]{2,1,0:T(8,128)S(1)} all-to-all(f32[4,128,128]{2,1,0:T(8,128)S(1)} %bitcast.8), channel_id=1, replica_groups={{0,32,64,96},{16,48,80,112},{128,160,192,224},{144,176,208,240},{256,28..., dimensions={0} | all-to-all | bytes 524288 | tf_op jit(solution)/shard_map/all_to_all | solution.py:271
  84.9 26.9 %all_to_all.16 = f32[4,128,128]{2,1,0:T(8,128)S(1)} all-to-all(f32[4,128,128]{2,1,0:T(8,128)S(1)} %broadcast_in_dim.4), channel_id=1, replica_groups={{0,128,256,384},{16,144,272,400},{32,160,288,416},{48,176,304,432},{64,..., dimensions={0} | all-to-all | bytes 524288 | tf_op jit(solution)/shard_map/all_to_all | solution.py:273
  111.8 12.6 %all_to_all.17 = f32[4,128,128]{2,1,0:T(8,128)S(1)} all-to-all(f32[4,128,128]{2,1,0:T(8,128)S(1)} %broadcast_in_dim.5), channel_id=1, replica_groups={{0,32,64,96},{16,48,80,112},{128,160,192,224},{144,176,208,240},{256,28..., dimensions={0} | all-to-all | bytes 524288 | tf_op jit(solution)/shard_map/all_to_all | solution.py:277
  124.4 6.9 %collective-permute-start.13 = (f32[512,128]{1,0:T(8,128)S(1)}, f32[512,128]{1,0:T(8,128)S(1)}, u32[]{:S(2)}, u32[]{:S(2)}) collective-permute-start(f32[512,128]{1,0:T(8,128)S(1)} %bitcast.6), channel_id=1, source_target_pairs={{0,16},{16,0},{32,48},{48,32},{64,80},{80,64},{96,112},{112,96},{1... | collective-permute-start | bytes 786440 | tf_op jit(solution)/shard_map/ppermute | solution.py:281
  131.4 0.1 pad_add_fusion.place_ref
  131.4 1.1 collective-permute-done.13.other_ref
  132.5 0.0 copy-done.1
  132.5 0.0 copy-done.2
  132.5 0.0 copy-start.3
  132.5 0.9 copy-done.3
  133.4 6.4 %shard_map.58 = f32[3072,128]{1,0:T(8,128)} custom-call(s32[2]{0:T(128)S(1)} %pad_add_fusion.place_ref, f32[512,128]{1,0:T(8,128)S(1)} %bitcast.7, f32[512,128]{1,0:T(8,128)S(1)} %collective-permute-done.13.other_ref, f32[256,256]{1,0:T(8,128)S(1)} %copy-done.2, f32[256,256]{1,0:T(8,128)S(1)} %copy-done.3, f32[3072,128]{1,0:T(8,128)S(1)} %copy-done.1, ...), custom_call_target="tpu_custom_call" | custom-call | tf_op jit(solution)/shard_map/pallas_call | solution.py:221
  (15 shorter events, 0.4 us)
Async XLA Ops:
  1.1 7.2 %collective-permute-start = (f32[32,1536]{1,0:T(8,128)S(1)}, f32[32,1536]{1,0:T(8,128)S(1)}, u32[]{:S(2)}, u32[]{:S(2)}) collective-permute-start(f32[32,1536]{1,0:T(8,128)S(1)} %get-tuple-element.36), channel_id=1, source_target_pairs={{0,1},{1,0},{2,3},{3,2},{4,5},{5,4},{6,7},{7,6},{8,9},{9,8},{10,11... | collective-permute-start | bytes 589832 | tf_op jit(solution)/shard_map/ppermute | solution.py:234
  5.0 9.0 %collective-permute-start.4 = (f32[32,1536]{1,0:T(8,128)S(1)}, f32[32,1536]{1,0:T(8,128)S(1)}, u32[]{:S(2)}, u32[]{:S(2)}) collective-permute-start(f32[32,1536]{1,0:T(8,128)S(1)} %get-tuple-element.35), channel_id=1, source_target_pairs={{0,4},{1,5},{2,6},{3,7},{4,0},{5,1},{6,2},{7,3},{8,12},{9,13},{10,... | collective-permute-start | bytes 589832 | tf_op jit(solution)/shard_map/ppermute | solution.py:234
  8.3 10.9 %collective-permute-start.1 = (f32[64,1536]{1,0:T(8,128)S(1)}, f32[64,1536]{1,0:T(8,128)S(1)}, u32[]{:S(2)}, u32[]{:S(2)}) collective-permute-start(f32[64,1536]{1,0:T(8,128)S(1)} %pad_maximum_fusion.7), channel_id=1, source_target_pairs={{0,3},{1,2},{2,1},{3,0},{4,7},{5,6},{6,5},{7,4},{8,11},{9,10},{10,... | collective-permute-start | bytes 1179656 | tf_op jit(solution)/shard_map/ppermute | solution.py:234
  14.1 11.2 %collective-permute-start.5 = (f32[64,1536]{1,0:T(8,128)S(1)}, f32[64,1536]{1,0:T(8,128)S(1)}, u32[]{:S(2)}, u32[]{:S(2)}) collective-permute-start(f32[64,1536]{1,0:T(8,128)S(1)} %pad_maximum_fusion.8), channel_id=1, source_target_pairs={{0,12},{1,13},{2,14},{3,15},{4,8},{5,9},{6,10},{7,11},{8,4},{9,5},... | collective-permute-start | bytes 1179656 | tf_op jit(solution)/shard_map/ppermute | solution.py:234
  19.3 16.4 %collective-permute-start.2 = (f32[128,896]{1,0:T(8,128)S(1)}, f32[128,896]{1,0:T(8,128)S(1)}, u32[]{:S(2)}, u32[]{:S(2)}) collective-permute-start(f32[128,896]{1,0:T(8,128)S(1)} %slice.25), channel_id=1, source_target_pairs={{0,4},{1,5},{2,6},{3,7},{4,0},{5,1},{6,2},{7,3},{8,12},{9,13},{10,... | collective-permute-start | bytes 1376264 | tf_op jit(solution)/shard_map/ppermute | solution.py:234
  25.4 12.8 %collective-permute-start.6 = (f32[128,896]{1,0:T(8,128)S(1)}, f32[128,896]{1,0:T(8,128)S(1)}, u32[]{:S(2)}, u32[]{:S(2)}) collective-permute-start(f32[128,896]{1,0:T(8,128)S(1)} %slice.27), channel_id=1, source_target_pairs={{0,1},{1,0},{2,3},{3,2},{4,5},{5,4},{6,7},{7,6},{8,9},{9,8},{10,11... | collective-permute-start | bytes 1376264 | tf_op jit(solution)/shard_map/ppermute | solution.py:234
  27.3 15.2 %collective-permute-start.3 = (f32[128,640]{1,0:T(8,128)S(1)}, f32[128,640]{1,0:T(8,128)S(1)}, u32[]{:S(2)}, u32[]{:S(2)}) collective-permute-start(f32[128,640]{1,0:T(8,128)S(1)} %pad_maximum_fusion.10), channel_id=1, source_target_pairs={{0,12},{1,13},{2,14},{3,15},{4,8},{5,9},{6,10},{7,11},{8,4},{9,5},... | collective-permute-start | bytes 983048 | tf_op jit(solution)/shard_map/ppermute | solution.py:234
  32.7 11.8 %collective-permute-start.7 = (f32[128,640]{1,0:T(8,128)S(1)}, f32[128,640]{1,0:T(8,128)S(1)}, u32[]{:S(2)}, u32[]{:S(2)}) collective-permute-start(f32[128,640]{1,0:T(8,128)S(1)} %pad_maximum_fusion.9), channel_id=1, source_target_pairs={{0,3},{1,2},{2,1},{3,0},{4,7},{5,6},{6,5},{7,4},{8,11},{9,10},{10,... | collective-permute-start | bytes 983048 | tf_op jit(solution)/shard_map/ppermute | solution.py:234
  35.7 22.8 %collective-permute-start.8 = (f32[256,896]{1,0:T(8,128)S(1)}, f32[256,896]{1,0:T(8,128)}, u32[]{:S(2)}, u32[]{:S(2)}) collective-permute-start(f32[256,896]{1,0:T(8,128)S(1)} %pad_maximum_fusion.refs_0_), channel_id=1, source_target_pairs={{0,12},{1,13},{2,14},{3,15},{4,8},{5,9},{6,10},{7,11},{8,4},{9,5},... | collective-permute-start | bytes 2752520 | tf_op jit(solution)/shard_map/ppermute | solution.py:234
  38.3 23.7 %collective-permute-start.10 = (f32[256,896]{1,0:T(8,128)S(1)}, f32[256,896]{1,0:T(8,128)}, u32[]{:S(2)}, u32[]{:S(2)}) collective-permute-start(f32[256,896]{1,0:T(8,128)S(1)} %pad_maximum_fusion.1.refs_2_), channel_id=1, source_target_pairs={{0,3},{1,2},{2,1},{3,0},{4,7},{5,6},{6,5},{7,4},{8,11},{9,10},{10,... | collective-permute-start | bytes 2752520 | tf_op jit(solution)/shard_map/ppermute | solution.py:234
  42.6 14.0 %collective-permute-start.9 = (f32[256,640]{1,0:T(8,128)S(1)}, f32[256,640]{1,0:T(8,128)}, u32[]{:S(2)}, u32[]{:S(2)}) collective-permute-start(f32[256,640]{1,0:T(8,128)S(1)} %pad_maximum_fusion.4.refs_1_), channel_id=1, source_target_pairs={{0,4},{1,5},{2,6},{3,7},{4,0},{5,1},{6,2},{7,3},{8,12},{9,13},{10,... | collective-permute-start | bytes 1966088 | tf_op jit(solution)/shard_map/ppermute | solution.py:234
  44.6 17.3 %collective-permute-start.11 = (f32[256,640]{1,0:T(8,128)S(1)}, f32[256,640]{1,0:T(8,128)}, u32[]{:S(2)}, u32[]{:S(2)}) collective-permute-start(f32[256,640]{1,0:T(8,128)S(1)} %pad_maximum_fusion.5.refs_3_), channel_id=1, source_target_pairs={{0,1},{1,0},{2,3},{3,2},{4,5},{5,4},{6,7},{7,6},{8,9},{9,8},{10,11... | collective-permute-start | bytes 1966088 | tf_op jit(solution)/shard_map/ppermute | solution.py:234
  46.5 1.4 %copy-start = (f32[3072,128]{1,0:T(8,128)S(1)}, f32[3072,128]{1,0:T(8,128)}, u32[]{:S(2)}) copy-start(f32[3072,128]{1,0:T(8,128)} %z_ref.3) | copy-start | bytes 4718596
  58.5 74.0 %copy-start.1 = (f32[3072,128]{1,0:T(8,128)S(1)}, f32[3072,128]{1,0:T(8,128)}, u32[]{:S(2)}) copy-start(f32[3072,128]{1,0:T(8,128)} %z_ref.3) | copy-start | bytes 4718596
  58.5 74.0 %copy-start.2 = (f32[256,256]{1,0:T(8,128)S(1)}, f32[256,256]{1,0:T(8,128)}, u32[]{:S(2)}) copy-start(f32[256,256]{1,0:T(8,128)} %t_one_ref.1) | copy-start | bytes 786436
  65.5 7.0 %collective-permute-start.12 = (f32[512,128]{1,0:T(8,128)S(1)}, f32[512,128]{1,0:T(8,128)S(1)}, u32[]{:S(2)}, u32[]{:S(2)}) collective-permute-start(f32[512,128]{1,0:T(8,128)S(1)} %constant_dynamic-slice_fusion), channel_id=1, source_target_pairs={{0,16},{16,0},{32,48},{48,32},{64,80},{80,64},{96,112},{112,96},{1... | collective-permute-start | bytes 786440 | tf_op jit(solution)/shard_map/ppermute | solution.py:270
  124.4 8.1 %collective-permute-start.13 = (f32[512,128]{1,0:T(8,128)S(1)}, f32[512,128]{1,0:T(8,128)S(1)}, u32[]{:S(2)}, u32[]{:S(2)}) collective-permute-start(f32[512,128]{1,0:T(8,128)S(1)} %bitcast.6), channel_id=1, source_target_pairs={{0,16},{16,0},{32,48},{48,32},{64,80},{80,64},{96,112},{112,96},{1... | collective-permute-start | bytes 786440 | tf_op jit(solution)/shard_map/ppermute | solution.py:281
  132.5 1.0 copy-start.3

commit v13 on v11

--- a/solution.py
+++ b/solution.py
@@ -168,9 +168,10 @@
     )(acc, zb, *firsts, *gots, kept)
 
 
-def apply_kernel(pieces, width, place_ref, mine_ref, other_ref, t_one_ref, t_two_ref, z_ref, kept_ref, *refs):
+def apply_kernel(pieces, width, place_ref, mine_ref, other_ref, t_both, z_ref, kept_ref, *refs):
     out_ref, held, z_held, out_held, total_ref, x_ref, slot_ref, sems, z_sems, out_sems = refs
-    k = t_one_ref.shape[0]
+    t_one_ref, t_two_ref = t_both.at[0], t_both.at[1]
+    k = t_both.shape[1]
     m = z_ref.shape[1]
     loads, z_loads = [], []
     for p, piece in enumerate(pieces):
@@ -219,20 +220,20 @@
         store.wait()
 
 
-def apply(place, mine, other, t_one, t_two, z, kept, pieces, width):
-    k, m = t_one.shape[0], z.shape[1]
+def apply(place, mine, other, t_both, z, kept, pieces, width):
+    k, m = t_both.shape[1], z.shape[1]
     rows = pltpu.VMEM(z.shape, F32)
     coeffs = pltpu.VMEM((2 * k, m), F32)
     return pl.pallas_call(
         functools.partial(apply_kernel, pieces, width),
         out_shape=jax.ShapeDtypeStruct(z.shape, F32),
-        in_specs=SMEM + vmem_specs(4) + any_specs(2),
+        in_specs=SMEM + vmem_specs(3) + any_specs(2),
         out_specs=pl.BlockSpec(memory_space=pl.ANY),
         scratch_shapes=[pltpu.VMEM(kept.shape[1:], BF16), rows, rows, pltpu.VMEM((2 * mine.shape[0], m), F32)]
         + [coeffs, coeffs]
         + [pltpu.SemaphoreType.DMA((len(pieces),))] * 3,
         compiler_params=pltpu.CompilerParams(vmem_limit_bytes=GRANT),
-    )(place, mine, other, t_one, t_two, z, kept)
+    )(place, mine, other, t_both, z, kept)
 
 
 def widen(data, masks, mask, size):
@@ -298,8 +299,9 @@
         two = [half for p in pair for half in firsts[2 * p : 2 * p + 2]]
         some, gots = [pieces[p] for p in pair], [halves[p][1] for p in pair]
         part, kept = late(part, z_both, two, gots, kept, some, pair == ORDER[0], k, width)
+    t_both = lax.optimization_barrier(jnp.stack([t_first, t_second]))
     mine, other = sum_over_row(part)
-    return apply(place, mine, other, t_first, t_second, z_slab, kept, pieces, width)
+    return apply(place, mine, other, t_both, z_slab, kept, pieces, width)
 
 
 def solution(mesh):

time: 140 us -> 139 us (level)
  transfers between devices with their start and end apart: 14 -> 14, of which waited for: 7 -> 6; matrix products, arithmetic and copies ran while one was open for 0% -> 1% of each run, Pallas kernels for 4% -> 4%
where the time goes in v13:
time: 139 us; the launch traced here: 138 us
  starting transfers between devices  55.8 us (40%)
  blocking collectives  51.9 us (37%)
  Pallas kernels  15.3 us (11%)
  waiting for transfers between devices  10.8 us (8%)
  other arithmetic  2.6 us (2%)
  local copies, waits for them, and re-layouts  1.57 us (1%)
    ppermute x12, starting transfers between devices, widen(): got = lax.ppermute(data, 'col', [(i, i ^ mask) for i in range(size)])  43.1 us
    all_to_all x1, blocking collectives, sum_over_row(): lax.all_to_all(jnp.broadcast_to(mine[None], (FAR,) + mine.shape), 'row',...  26.9 us
    all_to_all x1, blocking collectives, sum_over_row(): lax.all_to_all(jnp.broadcast_to(mine[None], (NEAR,) + mine.shape), 'row',...  12.6 us
    all_to_all x1, blocking collectives, sum_over_row(): lax.all_to_all(mine.reshape(NEAR, half // NEAR, m), 'row', 0, 0, axis_ind...  12.4 us
    ppermute x12, waiting for transfers between devices, widen(): got = lax.ppermute(data, 'col', [(i, i ^ mask) for i in range(size)])  9.58 us
    ppermute x1, starting transfers between devices, sum_over_row(): return (mine, lax.ppermute(mine, 'row', pair))  6.93 us
    pallas_call x2, Pallas kernels, late(): pl.pallas_call(functools.partial(late_kernel, pieces, first, k, width), o...  6.87 us
    pallas_call x1, Pallas kernels, apply(): pl.pallas_call(functools.partial(apply_kernel, pieces, width), out_shape=...  5.82 us
  transfers between devices with their start and end apart: 14, of which 6 were waited for; matrix products, arithmetic and copies ran while one was open for 1% of the time, Pallas kernels for 4%

profile of v13, /device:TPU:1, one launch (start us, length us, event | category | flops | bytes accessed | tf_op | source)
XLA Modules:
  0.0 138.3 jit_solution(15203658958334419360)
XLA Ops:
  0.0 1.0 pad_maximum_fusion.7
  1.1 3.9 %collective-permute-start = (f32[32,1536]{1,0:T(8,128)S(1)}, f32[32,1536]{1,0:T(8,128)S(1)}, u32[]{:S(2)}, u32[]{:S(2)}) collective-permute-start(f32[32,1536]{1,0:T(8,128)S(1)} %get-tuple-element.36), channel_id=1, source_target_pairs={{0,1},{1,0},{2,3},{3,2},{4,5},{5,4},{6,7},{7,6},{8,9},{9,8},{10,11... | collective-permute-start | bytes 589832 | tf_op jit(solution)/shard_map/ppermute | solution.py:240
  5.0 3.2 %collective-permute-start.4 = (f32[32,1536]{1,0:T(8,128)S(1)}, f32[32,1536]{1,0:T(8,128)S(1)}, u32[]{:S(2)}, u32[]{:S(2)}) collective-permute-start(f32[32,1536]{1,0:T(8,128)S(1)} %get-tuple-element.35), channel_id=1, source_target_pairs={{0,4},{1,5},{2,6},{3,7},{4,0},{5,1},{6,2},{7,3},{8,12},{9,13},{10,... | collective-permute-start | bytes 589832 | tf_op jit(solution)/shard_map/ppermute | solution.py:240
  8.3 0.0 collective-permute-done
  8.3 5.7 %collective-permute-start.1 = (f32[64,1536]{1,0:T(8,128)S(1)}, f32[64,1536]{1,0:T(8,128)S(1)}, u32[]{:S(2)}, u32[]{:S(2)}) collective-permute-start(f32[64,1536]{1,0:T(8,128)S(1)} %pad_maximum_fusion.8), channel_id=1, source_target_pairs={{0,3},{1,2},{2,1},{3,0},{4,7},{5,6},{6,5},{7,4},{8,11},{9,10},{10,... | collective-permute-start | bytes 1179656 | tf_op jit(solution)/shard_map/ppermute | solution.py:240
  14.0 0.0 collective-permute-done.4
  14.1 4.6 %collective-permute-start.5 = (f32[64,1536]{1,0:T(8,128)S(1)}, f32[64,1536]{1,0:T(8,128)S(1)}, u32[]{:S(2)}, u32[]{:S(2)}) collective-permute-start(f32[64,1536]{1,0:T(8,128)S(1)} %pad_maximum_fusion.9), channel_id=1, source_target_pairs={{0,12},{1,13},{2,14},{3,15},{4,8},{5,9},{6,10},{7,11},{8,4},{9,5},... | collective-permute-start | bytes 1179656 | tf_op jit(solution)/shard_map/ppermute | solution.py:240
  18.7 0.5 collective-permute-done.1
  19.2 0.1 pad_maximum_fusion.2
  19.3 4.9 %collective-permute-start.2 = (f32[128,896]{1,0:T(8,128)S(1)}, f32[128,896]{1,0:T(8,128)S(1)}, u32[]{:S(2)}, u32[]{:S(2)}) collective-permute-start(f32[128,896]{1,0:T(8,128)S(1)} %slice.25), channel_id=1, source_target_pairs={{0,4},{1,5},{2,6},{3,7},{4,0},{5,1},{6,2},{7,3},{8,12},{9,13},{10,... | collective-permute-start | bytes 1376264 | tf_op jit(solution)/shard_map/ppermute | solution.py:240
  24.2 1.1 collective-permute-done.5
  25.3 0.1 pad_maximum_fusion.3
  25.4 1.9 %collective-permute-start.6 = (f32[128,896]{1,0:T(8,128)S(1)}, f32[128,896]{1,0:T(8,128)S(1)}, u32[]{:S(2)}, u32[]{:S(2)}) collective-permute-start(f32[128,896]{1,0:T(8,128)S(1)} %slice.27), channel_id=1, source_target_pairs={{0,1},{1,0},{2,3},{3,2},{4,5},{5,4},{6,7},{7,6},{8,9},{9,8},{10,11... | collective-permute-start | bytes 1376264 | tf_op jit(solution)/shard_map/ppermute | solution.py:240
  27.3 5.3 %collective-permute-start.3 = (f32[128,640]{1,0:T(8,128)S(1)}, f32[128,640]{1,0:T(8,128)S(1)}, u32[]{:S(2)}, u32[]{:S(2)}) collective-permute-start(f32[128,640]{1,0:T(8,128)S(1)} %pad_maximum_fusion.11), channel_id=1, source_target_pairs={{0,12},{1,13},{2,14},{3,15},{4,8},{5,9},{6,10},{7,11},{8,4},{9,5},... | collective-permute-start | bytes 983048 | tf_op jit(solution)/shard_map/ppermute | solution.py:240
  32.7 3.0 %collective-permute-start.7 = (f32[128,640]{1,0:T(8,128)S(1)}, f32[128,640]{1,0:T(8,128)S(1)}, u32[]{:S(2)}, u32[]{:S(2)}) collective-permute-start(f32[128,640]{1,0:T(8,128)S(1)} %pad_maximum_fusion.10), channel_id=1, source_target_pairs={{0,3},{1,2},{2,1},{3,0},{4,7},{5,6},{6,5},{7,4},{8,11},{9,10},{10,... | collective-permute-start | bytes 983048 | tf_op jit(solution)/shard_map/ppermute | solution.py:240
  35.7 0.0 collective-permute-done.2
  35.7 0.1 pad_maximum_fusion.refs_0_
  35.7 2.4 %collective-permute-start.8 = (f32[256,896]{1,0:T(8,128)S(1)}, f32[256,896]{1,0:T(8,128)}, u32[]{:S(2)}, u32[]{:S(2)}) collective-permute-start(f32[256,896]{1,0:T(8,128)S(1)} %pad_maximum_fusion.refs_0_), channel_id=1, source_target_pairs={{0,12},{1,13},{2,14},{3,15},{4,8},{5,9},{6,10},{7,11},{8,4},{9,5},... | collective-permute-start | bytes 2752520 | tf_op jit(solution)/shard_map/ppermute | solution.py:240
  38.2 0.0 collective-permute-done.6
  38.2 0.1 pad_maximum_fusion.1.refs_2_
  38.3 4.2 %collective-permute-start.10 = (f32[256,896]{1,0:T(8,128)S(1)}, f32[256,896]{1,0:T(8,128)}, u32[]{:S(2)}, u32[]{:S(2)}) collective-permute-start(f32[256,896]{1,0:T(8,128)S(1)} %pad_maximum_fusion.1.refs_2_), channel_id=1, source_target_pairs={{0,3},{1,2},{2,1},{3,0},{4,7},{5,6},{6,5},{7,4},{8,11},{9,10},{10,... | collective-permute-start | bytes 2752520 | tf_op jit(solution)/shard_map/ppermute | solution.py:240
  42.5 0.0 collective-permute-done.3
  42.6 1.9 %collective-permute-start.9 = (f32[256,640]{1,0:T(8,128)S(1)}, f32[256,640]{1,0:T(8,128)}, u32[]{:S(2)}, u32[]{:S(2)}) collective-permute-start(f32[256,640]{1,0:T(8,128)S(1)} %pad_maximum_fusion.4.refs_1_), channel_id=1, source_target_pairs={{0,4},{1,5},{2,6},{3,7},{4,0},{5,1},{6,2},{7,3},{8,12},{9,13},{10,... | collective-permute-start | bytes 1966088 | tf_op jit(solution)/shard_map/ppermute | solution.py:240
  44.5 0.0 collective-permute-done.7
  44.6 1.9 %collective-permute-start.11 = (f32[256,640]{1,0:T(8,128)S(1)}, f32[256,640]{1,0:T(8,128)}, u32[]{:S(2)}, u32[]{:S(2)}) collective-permute-start(f32[256,640]{1,0:T(8,128)S(1)} %pad_maximum_fusion.5.refs_3_), channel_id=1, source_target_pairs={{0,1},{1,0},{2,3},{3,2},{4,5},{5,4},{6,7},{7,6},{8,9},{9,8},{10,11... | collective-permute-start | bytes 1966088 | tf_op jit(solution)/shard_map/ppermute | solution.py:240
  46.5 0.0 copy-start
  46.5 1.4 %copy-done = f32[3072,128]{1,0:T(8,128)S(1)} copy-done((f32[3072,128]{1,0:T(8,128)S(1)}, f32[3072,128]{1,0:T(8,128)}, u32[]{:S(2)}) %copy-start) | copy-done | bytes 1572888
  47.9 2.6 %shard_map.55 = (f32[512,128]{1,0:T(8,128)S(1)}, bf16[3072,256]{1,0:T(8,128)(2,1)S(1)}, bf16[256,896]{1,0:T(8,128)(2,1)S(1)}, bf16[256,896]{1,0:T(8,128)(2,1)S(1...) custom-call(f32[3072,128]{1,0:T(8,128)S(1)} %copy-done, ...), custom_call_target="tpu_custom_call" | custom-call | flops 603979776 | bytes 12582912 | tf_op jit(solution)/shard_map/pallas_call | solution.py:104
  50.5 6.0 %collective-permute-done.9.refs_5_ = f32[256,640]{1,0:T(8,128)} collective-permute-done((f32[256,640]{1,0:T(8,128)S(1)}, f32[256,640]{1,0:T(8,128)}, u32[]{:S(2)}, u32[]{:S(2)}) %collective-permute-start.9) | collective-permute-done | bytes 655392 | tf_op jit(solution)/shard_map/ppermute | solution.py:240
  56.5 2.0 %collective-permute-done.8.refs_4_ = f32[256,896]{1,0:T(8,128)} collective-permute-done((f32[256,896]{1,0:T(8,128)S(1)}, f32[256,896]{1,0:T(8,128)}, u32[]{:S(2)}, u32[]{:S(2)}) %collective-permute-start.8) | collective-permute-done | bytes 917536 | tf_op jit(solution)/shard_map/ppermute | solution.py:240
  58.5 0.0 copy-start.2
  58.5 0.0 copy-start.1
  58.5 3.4 %shard_map.56 = (f32[1024,128]{1,0:T(8,128)S(1)}, bf16[6,1024,3072]{2,1,0:T(8,128)(2,1)}) custom-call(f32[512,128]{1,0:T(8,128)S(1)} %get-tuple-element.20.acc_ref, bf16[3072,256]{1,0:T(8,128)(2,1)S(1)} %get-tuple-element.21.zb_ref, bf16[256,896]{1,0:T(8,128)(2,1)S(1)} %get-tuple-element.22.refs_0_, ...), custom_call_target="tpu_custom_call", output_to_operand_aliasing={{1}: (8, {})} | custom-call | tf_op jit(solution)/shard_map/pallas_call | solution.py:158
  61.9 0.0 collective-permute-done.11.refs_5_
  62.0 0.0 collective-permute-done.10.refs_4_
  62.0 3.4 %shard_map.57 = (f32[1024,128]{1,0:T(8,128)S(1)}, bf16[6,1024,3072]{2,1,0:T(8,128)(2,1)}) custom-call(f32[1024,128]{1,0:T(8,128)S(1)} %get-tuple-element.27.acc_ref, bf16[3072,256]{1,0:T(8,128)(2,1)S(1)} %get-tuple-element.21.zb_ref, bf16[256,896]{1,0:T(8,128)(2,1)S(1)} %get-tuple-element.28.refs_0_, ...), custom_call_target="tpu_custom_call", output_to_operand_aliasing={{1}: (8, {})} | custom-call | tf_op jit(solution)/shard_map/pallas_call | solution.py:158
  65.4 5.8 %collective-permute-start.12 = (f32[512,128]{1,0:T(8,128)S(1)}, f32[512,128]{1,0:T(8,128)S(1)}, u32[]{:S(2)}, u32[]{:S(2)}) collective-permute-start(f32[512,128]{1,0:T(8,128)S(1)} %constant_dynamic-slice_fusion), channel_id=1, source_target_pairs={{0,16},{16,0},{32,48},{48,32},{64,80},{80,64},{96,112},{112,96},{1... | collective-permute-start | bytes 786440 | tf_op jit(solution)/shard_map/ppermute | solution.py:276
  71.3 1.1 collective-permute-done.12
  72.4 12.4 %all_to_all.15 = f32[4,128,128]{2,1,0:T(8,128)S(1)} all-to-all(f32[4,128,128]{2,1,0:T(8,128)S(1)} %bitcast.10), channel_id=1, replica_groups={{0,32,64,96},{16,48,80,112},{128,160,192,224},{144,176,208,240},{256,28..., dimensions={0} | all-to-all | bytes 524288 | tf_op jit(solution)/shard_map/all_to_all | solution.py:277
  84.9 26.9 %all_to_all.16 = f32[4,128,128]{2,1,0:T(8,128)S(1)} all-to-all(f32[4,128,128]{2,1,0:T(8,128)S(1)} %broadcast_in_dim.4), channel_id=1, replica_groups={{0,128,256,384},{16,144,272,400},{32,160,288,416},{48,176,304,432},{64,..., dimensions={0} | all-to-all | bytes 524288 | tf_op jit(solution)/shard_map/all_to_all | solution.py:279
  111.8 12.6 %all_to_all.17 = f32[4,128,128]{2,1,0:T(8,128)S(1)} all-to-all(f32[4,128,128]{2,1,0:T(8,128)S(1)} %broadcast_in_dim.5), channel_id=1, replica_groups={{0,32,64,96},{16,48,80,112},{128,160,192,224},{144,176,208,240},{256,28..., dimensions={0} | all-to-all | bytes 524288 | tf_op jit(solution)/shard_map/all_to_all | solution.py:283
  124.4 6.9 %collective-permute-start.13 = (f32[512,128]{1,0:T(8,128)S(1)}, f32[512,128]{1,0:T(8,128)S(1)}, u32[]{:S(2)}, u32[]{:S(2)}) collective-permute-start(f32[512,128]{1,0:T(8,128)S(1)} %bitcast.8), channel_id=1, source_target_pairs={{0,16},{16,0},{32,48},{48,32},{64,80},{80,64},{96,112},{112,96},{1... | collective-permute-start | bytes 786440 | tf_op jit(solution)/shard_map/ppermute | solution.py:287
  131.3 0.1 pad_add_fusion.place_ref
  131.4 0.0 copy-done.2
  131.4 1.0 pad_maximum_fusion.6.t_both
  132.4 0.1 collective-permute-done.13.other_ref
  132.5 0.0 copy-done.1
  132.5 5.8 %shard_map.58 = f32[3072,128]{1,0:T(8,128)} custom-call(s32[2]{0:T(128)S(1)} %pad_add_fusion.place_ref, f32[512,128]{1,0:T(8,128)S(1)} %bitcast.9, f32[512,128]{1,0:T(8,128)S(1)} %collective-permute-done.13.other_ref, f32[2,256,256]{2,1,0:T(8,128)S(1)} %pad_maximum_fusion.6.t_both, f32[3072,128]{1,0:T(8,128)S(1)} %copy-done.1, ...), custom_call_target="tpu_custom_call" | custom-call | tf_op jit(solution)/shard_map/pallas_call | solution.py:227
  (15 shorter events, 0.4 us)
Async XLA Ops:
  1.1 7.2 %collective-permute-start = (f32[32,1536]{1,0:T(8,128)S(1)}, f32[32,1536]{1,0:T(8,128)S(1)}, u32[]{:S(2)}, u32[]{:S(2)}) collective-permute-start(f32[32,1536]{1,0:T(8,128)S(1)} %get-tuple-element.36), channel_id=1, source_target_pairs={{0,1},{1,0},{2,3},{3,2},{4,5},{5,4},{6,7},{7,6},{8,9},{9,8},{10,11... | collective-permute-start | bytes 589832 | tf_op jit(solution)/shard_map/ppermute | solution.py:240
  5.0 9.0 %collective-permute-start.4 = (f32[32,1536]{1,0:T(8,128)S(1)}, f32[32,1536]{1,0:T(8,128)S(1)}, u32[]{:S(2)}, u32[]{:S(2)}) collective-permute-start(f32[32,1536]{1,0:T(8,128)S(1)} %get-tuple-element.35), channel_id=1, source_target_pairs={{0,4},{1,5},{2,6},{3,7},{4,0},{5,1},{6,2},{7,3},{8,12},{9,13},{10,... | collective-permute-start | bytes 589832 | tf_op jit(solution)/shard_map/ppermute | solution.py:240
  8.3 10.9 %collective-permute-start.1 = (f32[64,1536]{1,0:T(8,128)S(1)}, f32[64,1536]{1,0:T(8,128)S(1)}, u32[]{:S(2)}, u32[]{:S(2)}) collective-permute-start(f32[64,1536]{1,0:T(8,128)S(1)} %pad_maximum_fusion.8), channel_id=1, source_target_pairs={{0,3},{1,2},{2,1},{3,0},{4,7},{5,6},{6,5},{7,4},{8,11},{9,10},{10,... | collective-permute-start | bytes 1179656 | tf_op jit(solution)/shard_map/ppermute | solution.py:240
  14.1 11.2 %collective-permute-start.5 = (f32[64,1536]{1,0:T(8,128)S(1)}, f32[64,1536]{1,0:T(8,128)S(1)}, u32[]{:S(2)}, u32[]{:S(2)}) collective-permute-start(f32[64,1536]{1,0:T(8,128)S(1)} %pad_maximum_fusion.9), channel_id=1, source_target_pairs={{0,12},{1,13},{2,14},{3,15},{4,8},{5,9},{6,10},{7,11},{8,4},{9,5},... | collective-permute-start | bytes 1179656 | tf_op jit(solution)/shard_map/ppermute | solution.py:240
  19.3 16.4 %collective-permute-start.2 = (f32[128,896]{1,0:T(8,128)S(1)}, f32[128,896]{1,0:T(8,128)S(1)}, u32[]{:S(2)}, u32[]{:S(2)}) collective-permute-start(f32[128,896]{1,0:T(8,128)S(1)} %slice.25), channel_id=1, source_target_pairs={{0,4},{1,5},{2,6},{3,7},{4,0},{5,1},{6,2},{7,3},{8,12},{9,13},{10,... | collective-permute-start | bytes 1376264 | tf_op jit(solution)/shard_map/ppermute | solution.py:240
  25.4 12.8 %collective-permute-start.6 = (f32[128,896]{1,0:T(8,128)S(1)}, f32[128,896]{1,0:T(8,128)S(1)}, u32[]{:S(2)}, u32[]{:S(2)}) collective-permute-start(f32[128,896]{1,0:T(8,128)S(1)} %slice.27), channel_id=1, source_target_pairs={{0,1},{1,0},{2,3},{3,2},{4,5},{5,4},{6,7},{7,6},{8,9},{9,8},{10,11... | collective-permute-start | bytes 1376264 | tf_op jit(solution)/shard_map/ppermute | solution.py:240
  27.3 15.2 %collective-permute-start.3 = (f32[128,640]{1,0:T(8,128)S(1)}, f32[128,640]{1,0:T(8,128)S(1)}, u32[]{:S(2)}, u32[]{:S(2)}) collective-permute-start(f32[128,640]{1,0:T(8,128)S(1)} %pad_maximum_fusion.11), channel_id=1, source_target_pairs={{0,12},{1,13},{2,14},{3,15},{4,8},{5,9},{6,10},{7,11},{8,4},{9,5},... | collective-permute-start | bytes 983048 | tf_op jit(solution)/shard_map/ppermute | solution.py:240
  32.7 11.8 %collective-permute-start.7 = (f32[128,640]{1,0:T(8,128)S(1)}, f32[128,640]{1,0:T(8,128)S(1)}, u32[]{:S(2)}, u32[]{:S(2)}) collective-permute-start(f32[128,640]{1,0:T(8,128)S(1)} %pad_maximum_fusion.10), channel_id=1, source_target_pairs={{0,3},{1,2},{2,1},{3,0},{4,7},{5,6},{6,5},{7,4},{8,11},{9,10},{10,... | collective-permute-start | bytes 983048 | tf_op jit(solution)/shard_map/ppermute | solution.py:240
  35.7 22.8 %collective-permute-start.8 = (f32[256,896]{1,0:T(8,128)S(1)}, f32[256,896]{1,0:T(8,128)}, u32[]{:S(2)}, u32[]{:S(2)}) collective-permute-start(f32[256,896]{1,0:T(8,128)S(1)} %pad_maximum_fusion.refs_0_), channel_id=1, source_target_pairs={{0,12},{1,13},{2,14},{3,15},{4,8},{5,9},{6,10},{7,11},{8,4},{9,5},... | collective-permute-start | bytes 2752520 | tf_op jit(solution)/shard_map/ppermute | solution.py:240
  38.3 23.7 %collective-permute-start.10 = (f32[256,896]{1,0:T(8,128)S(1)}, f32[256,896]{1,0:T(8,128)}, u32[]{:S(2)}, u32[]{:S(2)}) collective-permute-start(f32[256,896]{1,0:T(8,128)S(1)} %pad_maximum_fusion.1.refs_2_), channel_id=1, source_target_pairs={{0,3},{1,2},{2,1},{3,0},{4,7},{5,6},{6,5},{7,4},{8,11},{9,10},{10,... | collective-permute-start | bytes 2752520 | tf_op jit(solution)/shard_map/ppermute | solution.py:240
  42.6 14.0 %collective-permute-start.9 = (f32[256,640]{1,0:T(8,128)S(1)}, f32[256,640]{1,0:T(8,128)}, u32[]{:S(2)}, u32[]{:S(2)}) collective-permute-start(f32[256,640]{1,0:T(8,128)S(1)} %pad_maximum_fusion.4.refs_1_), channel_id=1, source_target_pairs={{0,4},{1,5},{2,6},{3,7},{4,0},{5,1},{6,2},{7,3},{8,12},{9,13},{10,... | collective-permute-start | bytes 1966088 | tf_op jit(solution)/shard_map/ppermute | solution.py:240
  44.6 17.4 %collective-permute-start.11 = (f32[256,640]{1,0:T(8,128)S(1)}, f32[256,640]{1,0:T(8,128)}, u32[]{:S(2)}, u32[]{:S(2)}) collective-permute-start(f32[256,640]{1,0:T(8,128)S(1)} %pad_maximum_fusion.5.refs_3_), channel_id=1, source_target_pairs={{0,1},{1,0},{2,3},{3,2},{4,5},{5,4},{6,7},{7,6},{8,9},{9,8},{10,11... | collective-permute-start | bytes 1966088 | tf_op jit(solution)/shard_map/ppermute | solution.py:240
  46.5 1.4 %copy-start = (f32[3072,128]{1,0:T(8,128)S(1)}, f32[3072,128]{1,0:T(8,128)}, u32[]{:S(2)}) copy-start(f32[3072,128]{1,0:T(8,128)} %z_ref.3) | copy-start | bytes 4718596
  58.5 72.9 %copy-start.2 = (f32[256,256]{1,0:T(8,128)S(1)}, f32[256,256]{1,0:T(8,128)}, u32[]{:S(2)}) copy-start(f32[256,256]{1,0:T(8,128)} %param.9) | copy-start | bytes 786436
  58.5 74.0 %copy-start.1 = (f32[3072,128]{1,0:T(8,128)S(1)}, f32[3072,128]{1,0:T(8,128)}, u32[]{:S(2)}) copy-start(f32[3072,128]{1,0:T(8,128)} %z_ref.3) | copy-start | bytes 4718596
  65.4 7.0 %collective-permute-start.12 = (f32[512,128]{1,0:T(8,128)S(1)}, f32[512,128]{1,0:T(8,128)S(1)}, u32[]{:S(2)}, u32[]{:S(2)}) collective-permute-start(f32[512,128]{1,0:T(8,128)S(1)} %constant_dynamic-slice_fusion), channel_id=1, source_target_pairs={{0,16},{16,0},{32,48},{48,32},{64,80},{80,64},{96,112},{112,96},{1... | collective-permute-start | bytes 786440 | tf_op jit(solution)/shard_map/ppermute | solution.py:276
  124.4 8.1 %collective-permute-start.13 = (f32[512,128]{1,0:T(8,128)S(1)}, f32[512,128]{1,0:T(8,128)S(1)}, u32[]{:S(2)}, u32[]{:S(2)}) collective-permute-start(f32[512,128]{1,0:T(8,128)S(1)} %bitcast.8), channel_id=1, source_target_pairs={{0,16},{16,0},{32,48},{48,32},{64,80},{80,64},{96,112},{112,96},{1... | collective-permute-start | bytes 786440 | tf_op jit(solution)/shard_map/ppermute | solution.py:287
